TPU v7x, 32 devices: a whole 2x2x4 slice. The times are simulated.
32 devices in a mesh: req: 8 (over y, x, core), tp: 4 (over z).
Axes of the slice: x: 2, y: 2, z: 4, core: 2. Of those that a mesh axis runs over, the one named last changes fastest.
Arguments:
- queries: bfloat16 [1024, 8192], P('req', 'tp'), may hold values from -80 to 80
- incoming_key_value: bfloat16 [2, 1024, 1024], P(None, 'req', 'tp'), may hold values from -4 to 4
- key_value_pages: bfloat16 [4096, 32, 2, 1024], P('req', None, None, 'tp'), may hold values from -4 to 4
- page_request_home: int32 [4096], P('req'), may hold values from 0 to 4095, as said below
- lengths: int32 [256], P('req'), may hold values from 1 to 512, 65536 in all
- request_adapter_index: int32 [256], P('req'), may hold values from 0 to 15
- adapter_storage_slot: int32 [16], replicated, may hold values from 0 to 15, each once
- adapter_down_factor: bfloat16 [16, 8192, 64], P('req', 'tp'), may hold values from -0.25 to 0.25
- adapter_up_factor: bfloat16 [16, 64, 8192], P('req'), may hold values from -0.75 to 0.75
- output_projection_weight: bfloat16 [8192, 8192], P('tp', 'req'), may hold values from -0.75 to 0.75
Outputs:
- attn_out: bfloat16 [1024, 8192], P('tp', 'req')
Inputs may be any that keep to these rules, and one draw needn't show every extreme that they name: `page_request_home`: each value once. Pages p with p // 512 = a hold pages of requests i with i // 32 = b, b != a, for at most 2 pages p for every pair a, b; in every draw some a holds exactly 2 pages of every b != a.
All inputs are finite; a program needn't handle non-finite values. No bound on the sum of `lengths` on one device may be relied on, other than what follows from the above.
Results may differ from a plain program's by a relative error of at most 0.0058.
Values may be sent and summed in bfloat16 or wider, within the bound.
No kernel may reach another device: no remote copies, remote signals or barrier semaphores. Data moves between devices by JAX's collectives and lax.ppermute only.
A program may use at most 128 MiB of HBM per device.

v0:
```python
import math

import jax
import jax.numpy as jnp
from jax import lax
from jax.sharding import PartitionSpec as P

QUERY_HEADS = 64
KEY_VALUE_HEADS = 8
HEAD_WIDTH = 128
STEP_COUNT = 4
PAGE_LENGTH = 32
MAXP = 16
CAP = 2


def relocate(key_value_pages, page_request_home, my_req, req_count):
    per_dev = key_value_pages.shape[0]
    destination = page_request_home // per_dev
    remote = destination != my_req
    matches = (destination[:, None] == jnp.arange(req_count, dtype=jnp.int32)[None, :]) & remote[
        :, None
    ]
    before = jnp.cumsum(matches.astype(jnp.int32), axis=0) - 1
    placing = jnp.sum(jnp.where(matches, before, 0), axis=1)
    target = jnp.where(remote, destination * CAP + placing, req_count * CAP)
    page_numbers = jnp.arange(per_dev, dtype=jnp.int32)
    out_match = target[:, None] == jnp.arange(req_count * CAP, dtype=jnp.int32)[None, :]
    filled = jnp.any(out_match, axis=0)
    out_source = jnp.sum(jnp.where(out_match, page_numbers[:, None], 0), axis=0)
    out_label = jnp.sum(jnp.where(out_match, page_request_home[:, None], 0), axis=0)
    picked = jnp.take(key_value_pages, out_source, axis=0)
    outbox = jnp.where(filled[:, None, None, None], picked, jnp.zeros((), key_value_pages.dtype))
    labels = jnp.where(filled, out_label, -1)
    inbox_pages, arrived = (
        lax.all_to_all(outbox, "req", split_axis=0, concat_axis=0, tiled=True),
        lax.all_to_all(labels, "req", split_axis=0, concat_axis=0, tiled=True),
    )
    own_label = jnp.where(remote, -1, page_request_home - my_req * per_dev)
    in_label = jnp.where(arrived >= 0, arrived - my_req * per_dev, -1)
    candidate_label = jnp.concatenate([own_label, in_label], axis=0)
    candidates = jnp.concatenate([key_value_pages, inbox_pages], axis=0)
    candidate_numbers = jnp.arange(candidate_label.shape[0], dtype=jnp.int32)
    slot_match = candidate_label[:, None] == page_numbers[None, :]
    slot_source = jnp.sum(jnp.where(slot_match, candidate_numbers[:, None], 0), axis=0)
    return jnp.take(candidates, slot_source, axis=0)


def attend(queries, incoming_key_value, cache_pages, lengths):
    heads_kv = cache_pages.shape[-1] // HEAD_WIDTH
    query_group_count = QUERY_HEADS // KEY_VALUE_HEADS
    requests = lengths.shape[0]
    cache_extent = MAXP * PAGE_LENGTH
    score_scale = 1.0 / math.sqrt(HEAD_WIDTH)
    stored_entries = cache_pages.reshape(requests, cache_extent, 2, heads_kv, HEAD_WIDTH)
    fresh_key_value = incoming_key_value.reshape(2, requests, STEP_COUNT, heads_kv, HEAD_WIDTH)
    query_vectors = queries.reshape(requests, STEP_COUNT, heads_kv, query_group_count, HEAD_WIDTH)
    old_scores = (
        jnp.einsum(
            "rsgqd,rlgd->rgqsl",
            query_vectors,
            stored_entries[:, :, 0],
            preferred_element_type=jnp.float32,
        )
        * score_scale
    )
    new_scores = (
        jnp.einsum(
            "rsgqd,rtgd->rgqst",
            query_vectors,
            fresh_key_value[0],
            preferred_element_type=jnp.float32,
        )
        * score_scale
    )
    keep_old = jnp.arange(cache_extent, dtype=jnp.int32)[None, :] < lengths[:, None]
    keep_new = jnp.arange(STEP_COUNT)[None, :] <= jnp.arange(STEP_COUNT)[:, None]
    old_scores = jnp.where(keep_old[:, None, None, None, :], old_scores, -jnp.inf)
    new_scores = jnp.where(keep_new[None, None, None], new_scores, -jnp.inf)
    row_top = jnp.maximum(jnp.max(old_scores, axis=-1), jnp.max(new_scores, axis=-1))
    old_weights = jnp.exp(old_scores - row_top[..., None])
    new_weights = jnp.exp(new_scores - row_top[..., None])
    totals = jnp.sum(old_weights, axis=-1) + jnp.sum(new_weights, axis=-1)
    old_probs = (old_weights / totals[..., None]).astype(jnp.bfloat16)
    new_probs = (new_weights / totals[..., None]).astype(jnp.bfloat16)
    attention_mixed_output = jnp.einsum(
        "rgqsl,rlgd->rsgqd", old_probs, stored_entries[:, :, 1], preferred_element_type=jnp.float32
    )
    attention_mixed_output = attention_mixed_output + jnp.einsum(
        "rgqst,rtgd->rsgqd", new_probs, fresh_key_value[1], preferred_element_type=jnp.float32
    )
    return attention_mixed_output.astype(jnp.bfloat16).reshape(
        requests * STEP_COUNT, heads_kv * query_group_count * HEAD_WIDTH
    )


def on_device(
    queries,
    incoming_key_value,
    key_value_pages,
    page_request_home,
    lengths,
    request_adapter_index,
    adapter_storage_slot,
    adapter_down_factor,
    adapter_up_factor,
    output_projection_weight,
):
    req_count = lax.axis_size("req")
    tp_count = lax.axis_size("tp")
    my_req = lax.axis_index("req")
    my_lane = lax.axis_index("tp")
    cache_pages = relocate(key_value_pages, page_request_home, my_req, req_count)
    attention_mixed_output = attend(queries, incoming_key_value, cache_pages, lengths)
    own_tokens = attention_mixed_output.shape[0]
    everyone, adapters = (
        lax.all_gather(attention_mixed_output, "req", axis=0, tiled=True),
        lax.all_gather(request_adapter_index, "req", axis=0, tiled=True),
    )
    slot_count = adapter_storage_slot.shape[0]
    match_table = adapters[:, None] == jnp.arange(slot_count, dtype=jnp.int32)[None, :]
    req_slot = jnp.sum(jnp.where(match_table, adapter_storage_slot[None, :], 0), axis=1)
    token_slot = jnp.repeat(req_slot, STEP_COUNT)
    block_rows = everyone.shape[0] // tp_count
    plain_output_rows = lax.psum_scatter(
        jnp.dot(everyone, output_projection_weight, preferred_element_type=jnp.float32),
        "tp",
        scatter_dimension=0,
        tiled=True,
    )
    gathered_down_factors = lax.all_gather(adapter_down_factor, "req", axis=0, tiled=True)
    local_reduced_rows = jnp.einsum(
        "td,adr->tar",
        attention_mixed_output,
        gathered_down_factors,
        preferred_element_type=jnp.float32,
    )
    own_slot = lax.dynamic_slice_in_dim(token_slot, my_req * own_tokens, own_tokens)
    selected_pages = own_slot[:, None] == jnp.arange(slot_count, dtype=jnp.int32)[None, :]
    adapter_partial = jnp.sum(
        jnp.where(selected_pages[:, :, None], local_reduced_rows, 0.0), axis=1
    )
    distributed_terms = lax.all_gather(adapter_partial, "req", axis=0, tiled=True)
    low_rows = lax.psum_scatter(distributed_terms, "tp", scatter_dimension=0, tiled=True)
    up_factor_columns = lax.all_to_all(
        adapter_up_factor, "req", split_axis=2, concat_axis=0, tiled=True
    )
    low_bf = low_rows.astype(jnp.bfloat16)
    block_slot = lax.dynamic_slice_in_dim(token_slot, my_lane * block_rows, block_rows)
    selector = (block_slot[:, None] == jnp.arange(slot_count, dtype=jnp.int32)[None, :]).astype(
        jnp.bfloat16
    )
    expanded = (selector[:, :, None] * low_bf[:, None, :]).reshape(
        block_rows, slot_count * up_factor_columns.shape[1]
    )
    adapter_output_rows = jnp.dot(
        expanded,
        up_factor_columns.reshape(
            slot_count * up_factor_columns.shape[1], up_factor_columns.shape[2]
        ),
        preferred_element_type=jnp.float32,
    )
    return (plain_output_rows + adapter_output_rows).astype(jnp.bfloat16)


def solution(mesh):
    return jax.shard_map(
        on_device,
        mesh=mesh,
        in_specs=(
            P("req", "tp"),
            P(None, "req", "tp"),
            P("req", None, None, "tp"),
            P("req"),
            P("req"),
            P("req"),
            P(),
            P("req", "tp", None),
            P("req", None, None),
            P("tp", "req"),
        ),
        out_specs=P("tp", "req"),
        check_vma=False,
    )
```

profile of v0, /device:TPU:0, one launch (start us, length us, event | category | flops | bytes accessed | tf_op | source)
XLA Modules:
  0.0 354.8 jit_solution(8508082799168662368)
XLA Ops:
  10.4 5.2 %all-to-all-start = ((s32[8,2,1]{1,2,0:T(1,128)}), s32[8,2,1]{1,2,0:T(1,128)S(1)}, u32[]{:S(2)}, u32[]{:S(2)}) async-start(s32[8,2,1]{1,2,0:T(1,128)} %bitcast.4), calls=%async_computation | async-start | bytes 8192 | tf_op jit(solution)/shard_map/all_to_all | solution.py:37
  19.1 7.4 %gather_fusion = bf16[16,32,2,256]{3,2,1,0:T(2,128)(2,1)S(1)} fusion(bf16[512,32,2,256]{3,2,1,0:T(2,128)(2,1)} %param.12, s32[1024]{0:T(1024)S(1)} %pad_clamp_fusion.1), kind=kCustom, calls=%fused_computation | custom fusion | bytes 1048640 | tf_op jit(solution)/shard_map/jit(_take)/gather | solution.py:32
  27.9 2.4 fusion.35
  30.4 4.2 %all-to-all-start.1 = ((bf16[16,32,2,256]{3,2,1,0:T(2,128)(2,1)}), bf16[16,32,2,256]{3,2,1,0:T(2,128)(2,1)S(1)}, u32[]{:S(2)}, u32[]{:S(2)}) async-start(bf16[16,32,2,256]{3,2,1,0:T(2,128)(2,1)} %broadcast_select_fusion.1), calls=%async_computation.1 | async-start | bytes 1048576 | tf_op jit(solution)/shard_map/all_to_all | solution.py:36
  35.5 8.8 %all-to-all-done.1 = bf16[16,32,2,256]{3,2,1,0:T(2,128)(2,1)S(1)} async-done(((bf16[16,32,2,256]{3,2,1,0:T(2,128)(2,1)}), bf16[16,32,2,256]{3,2,1,0:T(2,128)(2,1)S(1)}, u32[]{:S(2)}, u32[]{:S(2)}) %all-to-all-start.1) | async-done | bytes 524320 | tf_op jit(solution)/shard_map/all_to_all | solution.py:36
  44.4 45.5 %pad_maximum_fusion = bf16[528,32,2,256]{3,2,1,0:T(2,128)(2,1)} fusion(bf16[16,32,2,256]{3,2,1,0:T(2,128)(2,1)S(1)} %all-to-all-done.1, bf16[512,32,2,256]{3,2,1,0:T(2,128)(2,1)} %param.12), kind=kLoop, calls=%fused_computation.2 | loop fusion | flops 8650752 | bytes 34603008 | tf_op jit(solution)/shard_map/concatenate | solution.py:42
  89.9 48.2 %gather_fusion.1 = bf16[512,32,2,256]{3,2,1,0:T(2,128)(2,1)} fusion(bf16[528,32,2,256]{3,2,1,0:T(2,128)(2,1)} %pad_maximum_fusion, s32[1024]{0:T(1024)S(1)} %pad_clamp_fusion), kind=kCustom, calls=%fused_computation.1 | custom fusion | bytes 33556480 | tf_op jit(solution)/shard_map/jit(_take)/gather | solution.py:46
  138.1 41.4 %reshape.244 = bf16[32,512,2,2,128]{4,3,2,1,0:T(2,128)(2,1)} reshape(bf16[512,32,2,256]{3,2,1,0:T(2,128)(2,1)} %gather_fusion.1) | data formatting | bytes 33554432 | tf_op jit(solution)/shard_map/jit(_take)/gather | solution.py:46
  179.5 15.5 %copy_select_fusion = bf16[32,512,2,2,128]{4,1,3,0,2:T(8,128)(2,1)} fusion(bf16[32,512,2,2,128]{4,3,2,1,0:T(2,128)(2,1)} %reshape.244, pred[32,512]{1,0:T(8,128)(4,1)S(1)} %broadcast_in_dim.174), kind=kLoop, calls=%fused_computation.3 | loop fusion | flops 8388608 | bytes 33570816 | tf_op jit(solution)/shard_map/jit(_take)/select_n | solution.py:46
  195.0 6.3 %bitcast_reduce_fusion = (f32[32,2,8,4]{2,3,1,0:T(4,128)S(1)}, f32[32,2,512,4,8]{2,4,3,1,0:T(8,128)S(1)}) fusion(pred[32,512]{1,0:T(8,128)(4,1)S(1)} %iota_compare_fusion.1, bf16[32,4,2,8,128]{4,3,2,1,0:T(8,128)(2,1)S(1)} %bitcast.89, bf16[32,512,2,2,128]{4,1,3,0,2:T(8,128)(2,1)} %copy_select_fusion), kind=kOutput, calls=%fused_computation.9 | convolution fusion | flops 271579136 | bytes 13131776 | tf_op jit(solution)/shard_map/rsgqd,rlgd->rgqsl/dot_general | solution.py:59
  203.6 4.7 %fusion.9 = f32[32,4,2,8,128]{4,3,1,2,0:T(8,128)S(1)} fusion(f32[32,2,512,4,8]{2,4,3,1,0:T(8,128)S(1)} %get-tuple-element.13, f32[32,2,8,4]{2,3,1,0:T(4,128)S(1)} %add.74, f32[32,2,8,4]{2,3,1,0:T(4,128)S(1)} %max.7, pred[32,512]{1,0:T(8,128)(4,1)S(1)} %iota_compare_fusion.1, bf16[32,512,2,2,128]{4,1,3,0,2:T(8,128)(2,1)} %copy_select_fusion), kind=kOutput, calls=%fused_computation.19 | convolution fusion | flops 273678336 | bytes 13664256 | tf_op jit(solution)/shard_map/rgqsl,rlgd->rsgqd/dot_general | solution.py:86
  211.7 6.4 %all-reduce = s32[256]{0:T(256)S(1)} all-reduce(s32[256]{0:T(256)S(1)} %dynamic-update-slice), channel_id=1, replica_groups=mesh['req'=8,'tp'=4] {'req'}, use_global_device_ids=true, to_apply=%add | all-reduce | flops 256 | bytes 2048
  218.5 3.6 %fusion.37 = f32[128,1024]{0,1:S(1)} fusion(bf16[128,2048]{1,0:T(8,128)(2,1)} %reshape.214, bf16[2048,1024]{0,1:T(8,128)(2,1)} %bitcast.84), kind=kOutput, calls=%fused_computation.90 | convolution fusion | flops 536870912 | bytes 5242880
  222.2 10.8 %all_gather.15 = f32[1024,64]{0,1:T(8,128)} all-gather(f32[128,64]{0,1:T(8,128)S(1)} %select_reduce_fusion.1), channel_id=1, replica_groups=mesh['req'=8,'tp'=4] {'req'}, dimensions={0}, use_global_device_ids=true | all-gather | bytes 294912 | tf_op jit(solution)/shard_map/all_gather | solution.py:143
  233.0 13.2 %all-gather.3.cloned.1.call-done = bf16[1024,2048]{1,0:T(8,128)(2,1)} async-done(((bf16[128,2048]{1,0:T(8,128)(2,1)}), bf16[1024,2048]{1,0:T(8,128)(2,1)}) %all-gather.3.cloned.1.call-update) | async-done | bytes 4194320 | tf_op jit(solution)/shard_map/all_gather | solution.py:117
  246.2 9.9 %fusion.36 = f32[1024,1024]{1,0:T(8,128)} fusion(bf16[1024,2048]{1,0:T(8,128)(2,1)} %all-gather.3.cloned.1.call-done, bf16[2048,1024]{1,0:T(8,128)(2,1)} %param.19), kind=kOutput, calls=%fused_computation.89 | convolution fusion | flops 4294967296 | bytes 12582912 | tf_op jit(solution)/shard_map/dot_general | solution.py:126
  257.7 6.9 %copy.47 = bf16[2,64,8192]{1,0,2:T(2,128)(2,1)} copy(bf16[2,64,8192]{2,1,0:T(8,128)(2,1)S(1)} %copy-done) | data formatting | bytes 4194304 | tf_op args[8]
  264.6 7.6 %reshape.253 = bf16[8,2,65536]{2,1,0:T(2,128)(2,1)} reshape(bf16[8192,2,64]{2,1,0:T(2,128)(2,1)} %bitcast.82) | data formatting | bytes 4194304
  272.2 3.7 %all-to-all-start.2 = ((bf16[8,2,65536]{2,1,0:T(2,128)(2,1)}), bf16[8,2,65536]{2,1,0:T(2,128)(2,1)S(1)}, u32[]{:S(2)}, u32[]{:S(2)}) async-start(bf16[8,2,65536]{2,1,0:T(2,128)(2,1)} %reshape.253), calls=%async_computation.4 | async-start | bytes 4194304 | tf_op jit(solution)/shard_map/all_to_all | solution.py:145
  275.9 26.5 %all-to-all-done.2 = bf16[8,2,65536]{2,1,0:T(2,128)(2,1)S(1)} async-done(((bf16[8,2,65536]{2,1,0:T(2,128)(2,1)}), bf16[8,2,65536]{2,1,0:T(2,128)(2,1)S(1)}, u32[]{:S(2)}, u32[]{:S(2)}) %all-to-all-start.2) | async-done | bytes 2097184 | tf_op jit(solution)/shard_map/all_to_all | solution.py:145
  302.4 5.0 %reshape.254 = bf16[8192,2,64]{2,1,0:T(2,128)(2,1)} reshape(bf16[8,2,65536]{2,1,0:T(2,128)(2,1)S(1)} %all-to-all-done.2) | data formatting | bytes 4194304
  307.4 9.1 %copy.61 = bf16[2,64,8,1024]{3,1,0,2:T(8,128)(2,1)S(1)} copy(bf16[2,64,8,1024]{1,0,3,2:T(2,128)(2,1)} %bitcast.81) | data formatting | bytes 4194304 | tf_op jit(solution)/shard_map/all_to_all | solution.py:145
  317.5 28.0 %reduce-scatter.3.cloned.1.call-done = f32[256,1024]{1,0:T(8,128)} async-done(((f32[1024,1024]{1,0:T(8,128)}), f32[256,1024]{1,0:T(8,128)}) %reduce-scatter.3.cloned.1.call-update) | async-done | bytes 1048592 | tf_op jit(solution)/shard_map/reduce_scatter | solution.py:125
  345.5 2.7 fusion.12
  (71 shorter events, 17.6 us)
Async XLA Ops:
  10.4 20.0 %all-to-all-start = ((s32[8,2,1]{1,2,0:T(1,128)}), s32[8,2,1]{1,2,0:T(1,128)S(1)}, u32[]{:S(2)}, u32[]{:S(2)}) async-start(s32[8,2,1]{1,2,0:T(1,128)} %bitcast.4), calls=%async_computation | async-start | bytes 8192 | tf_op jit(solution)/shard_map/all_to_all | solution.py:37
  15.5 203.0 %all-gather.5.cloned.1.call-start = ((), (), s32[]{:S(2)}) async-start(), calls=%async_computation.7 | async-start | bytes 4718592 | tf_op jit(solution)/shard_map/all_gather | solution.py:131
  30.4 14.0 %all-to-all-start.1 = ((bf16[16,32,2,256]{3,2,1,0:T(2,128)(2,1)}), bf16[16,32,2,256]{3,2,1,0:T(2,128)(2,1)S(1)}, u32[]{:S(2)}, u32[]{:S(2)}) async-start(bf16[16,32,2,256]{3,2,1,0:T(2,128)(2,1)} %broadcast_select_fusion.1), calls=%async_computation.1 | async-start | bytes 1048576 | tf_op jit(solution)/shard_map/all_to_all | solution.py:36
  34.6 211.7 %all-gather.3.cloned.1.call-start = ((), (), s32[]{:S(2)}) async-start(), calls=%async_computation.5 | async-start | bytes 4718592 | tf_op jit(solution)/shard_map/all_gather | solution.py:117
  208.3 1.7 copy-start.3
  208.3 3.1 copy-start.2
  208.3 9.8 %copy-start.1 = (s32[16]{0:T(128)S(1)}, s32[16]{0:T(128)}, u32[]{:S(2)}) copy-start(s32[16]{0:T(128)} %param.16) | copy-start | bytes 196
  210.0 106.6 %reduce-scatter.5.cloned.1.call-start = ((), (), s32[]{:S(2)}) async-start(), calls=%async_computation.8 | async-start | bytes 327680 | tf_op jit(solution)/shard_map/reduce_scatter | solution.py:144
  233.0 112.6 %reduce-scatter.3.cloned.1.call-start = ((), (), s32[]{:S(2)}) async-start(), calls=%async_computation.6 | async-start | bytes 5242880 | tf_op jit(solution)/shard_map/reduce_scatter | solution.py:125
  256.1 1.6 copy-start
  272.2 30.3 %all-to-all-start.2 = ((bf16[8,2,65536]{2,1,0:T(2,128)(2,1)}), bf16[8,2,65536]{2,1,0:T(2,128)(2,1)S(1)}, u32[]{:S(2)}, u32[]{:S(2)}) async-start(bf16[8,2,65536]{2,1,0:T(2,128)(2,1)} %reshape.253), calls=%async_computation.4 | async-start | bytes 4194304 | tf_op jit(solution)/shard_map/all_to_all | solution.py:145
Sparse Core Ops, SparseCore 0:
  18.2 38.9 all-gather.4
  210.1 36.1 all-gather.2
  248.5 19.6 reduce-scatter.4
  270.5 75.0 reduce-scatter.2
where the time goes:
time: 357 us; the launch traced here: 355 us
  local copies, waits for them, and re-layouts  133 us (37%)
  waiting for transfers between devices  77.4 us (22%)
  other arithmetic  69.7 us (20%)
  matrix products  30.2 us (8%)
  blocking collectives  17.2 us (5%)
  between operations  14.1 us (4%)
  starting transfers between devices  13.4 us (4%)
    gather x2, local copies, waits for them, and re-layouts, relocate(): return jnp.take(candidates, slot_source, axis=0)  89.6 us
    concatenate x1, other arithmetic, relocate(): candidates = jnp.concatenate([key_value_pages, inbox_pages], axis=0)  45.5 us
    reduce_scatter x1, waiting for transfers between devices, on_device(): lax.psum_scatter(jnp.dot(everyone, output_projection_weight, preferred_el...  28 us
    all_to_all x1, waiting for transfers between devices, on_device(): lax.all_to_all(adapter_up_factor, 'req', split_axis=2, concat_axis=0, til...  26.5 us
    unnamed x15, local copies, waits for them, and re-layouts  23.1 us
    select_n x2, other arithmetic, relocate(): return jnp.take(candidates, slot_source, axis=0)  15.5 us
    all_gather x1, waiting for transfers between devices, on_device(): lax.all_gather(attention_mixed_output, 'req', axis=0, tiled=True)  13.2 us
    all_gather x1, blocking collectives, on_device(): lax.all_gather(adapter_partial, 'req', axis=0, tiled=True)  10.8 us
  transfers between devices with their start and end apart: 7, of which 4 were waited for; matrix products, arithmetic and copies ran while one was open for 63% of the time, Pallas kernels for 0%

commit v1 on v0

v1 whole, which is shorter than its diff:
```python
import functools
import math

import jax
import jax.numpy as jnp
from jax import lax
from jax.experimental import pallas as pl
from jax.experimental.pallas import tpu as pltpu
from jax.sharding import PartitionSpec as P

QUERY_HEADS = 64
KEY_VALUE_HEADS = 8
GROUP = QUERY_HEADS // KEY_VALUE_HEADS
HEAD_WIDTH = 128
STEP_COUNT = 4
PAGE_LENGTH = 32
MAXP = 16
CAP = 2
BLOCK = CAP * PAGE_LENGTH + 1
LABEL_LANE = 64
DIGIT = 16
CHUNK_PAGES = 4
CHUNKS = MAXP // CHUNK_PAGES
PAGE_ROWS = PAGE_LENGTH * 2
CHUNK_ROWS = CHUNK_PAGES * PAGE_ROWS
NEW_ROWS = STEP_COUNT * 2
NEW_GROUP = 128 // NEW_ROWS
UNROLL = 2
SLOTS = 3
VMEM_LIMIT = 56 * 1024 * 1024

HBM = pl.BlockSpec(memory_space=pltpu.HBM)
VMEM = pl.BlockSpec(memory_space=pltpu.VMEM)
SMEM = pl.BlockSpec(memory_space=pltpu.SMEM)


def params():
    return pltpu.CompilerParams(vmem_limit_bytes=VMEM_LIMIT)


def dot(a, b, contract=((1,), (0,))):
    return lax.dot_general(a, b, (contract, ((), ())), preferred_element_type=jnp.float32)


def pack_kernel(req_count, per_dev, me_ref, home_ref, ids_ref, pages, outbox, info_v, info_s, ids_v, rows_v, sem, sems):
    me = me_ref[0]
    page = lax.broadcasted_iota(jnp.int32, (req_count, per_dev), 1)
    want = lax.broadcasted_iota(jnp.int32, (req_count, per_dev), 0)
    slots = jnp.broadcast_to(home_ref[...], (req_count, per_dev)) - want * per_dev
    hit = (slots >= 0) & (slots < per_dev) & (want != me)
    lane = lax.broadcasted_iota(jnp.int32, (req_count, 128), 1)
    info = jnp.full((req_count, 128), -1, jnp.int32)
    for k in range(CAP):
        first = jnp.min(jnp.where(hit, page, per_dev), axis=1, keepdims=True)
        here = hit & (page == first)
        slot = jnp.max(jnp.where(here, slots, -1), axis=1, keepdims=True)
        info = jnp.where(lane == k, first, info)
        info = jnp.where(lane == CAP + k, slot, info)
        hit = hit & (page != first)
    info_v[...] = info
    fetch = pltpu.make_async_copy(info_v, info_s, sem)
    fetch.start()
    ids_v[...] = jnp.zeros_like(ids_v)
    ids_v[:, 0:ids_ref.shape[1]] = ids_ref[...].astype(jnp.float32)
    ids = jnp.broadcast_to(ids_v[...], (2, 128))
    fetch.wait()

    def copy(d, k):
        return pltpu.make_async_copy(
            pages.at[info_s[d, k]],
            outbox.at[d, pl.ds(k * PAGE_LENGTH, PAGE_LENGTH)],
            sems.at[d, k],
        )

    for d in range(req_count):
        for k in range(CAP):

            @pl.when(info_s[d, k] < per_dev)
            def _():
                copy(d, k).start()

    at = lax.broadcasted_iota(jnp.int32, (2, 128), 1)
    row = lax.broadcasted_iota(jnp.int32, (2, 128), 0)
    for d in range(req_count):
        value = jnp.where(row == 0, ids, 0.0)
        for k in range(CAP):
            slot = info_s[d, CAP + k]
            high = ((slot + DIGIT) >> 4) - 1
            low = slot - high * DIGIT
            digit = jnp.where(row == 0, high, low).astype(jnp.float32)
            value = jnp.where(at == LABEL_LANE + k, digit, value)
        rows_v[d, 0, :, :] = jnp.zeros(rows_v.shape[2:], jnp.bfloat16)
        rows_v[d, 0, :, 0:128] = value.astype(jnp.bfloat16)
    rows = pltpu.make_async_copy(rows_v, outbox.at[:, pl.ds(BLOCK - 1, 1)], sem)
    rows.start()
    rows.wait()
    for d in range(req_count):
        for k in range(CAP):

            @pl.when(info_s[d, k] < per_dev)
            def _():
                copy(d, k).wait()


def pack(me, page_request_home, ids, key_value_pages, req_count):
    per_dev = key_value_pages.shape[0]
    columns = key_value_pages.shape[-1]
    return pl.pallas_call(
        functools.partial(pack_kernel, req_count, per_dev),
        out_shape=jax.ShapeDtypeStruct((req_count, BLOCK, 2, columns), jnp.bfloat16),
        in_specs=[SMEM, VMEM, VMEM, HBM],
        out_specs=HBM,
        scratch_shapes=[
            pltpu.VMEM((req_count, 128), jnp.int32),
            pltpu.SMEM((req_count, 128), jnp.int32),
            pltpu.VMEM((1, 128), jnp.float32),
            pltpu.VMEM((req_count, 1, 2, columns), jnp.bfloat16),
            pltpu.SemaphoreType.DMA,
            pltpu.SemaphoreType.DMA((req_count, CAP)),
        ],
        compiler_params=params(),
        name="pack_outbox",
    )(me, page_request_home.reshape(1, per_dev), ids.reshape(1, -1), key_value_pages)


def table_kernel(per_dev, requests, me_ref, home_ref, lengths_ref, table_ref, order_ref, chunks_ref):
    base = me_ref[0] * per_dev

    @pl.loop(0, per_dev)
    def _(s):
        table_ref[s] = 0

    @pl.loop(0, per_dev)
    def _(p):
        slot = home_ref[p] - base

        @pl.when((slot >= 0) & (slot < per_dev))
        def _():
            table_ref[slot] = p

    placed = jnp.int32(0)
    for c in range(CHUNKS, 0, -1):

        def step(r, placed):
            need = lax.shift_right_logical(lengths_ref[r] + (CHUNK_ROWS // 2 - 1), 7)
            mine = need == c

            @pl.when(mine)
            def _():
                order_ref[placed] = r
                chunks_ref[placed] = need

            return placed + jnp.where(mine, 1, 0)

        placed = lax.fori_loop(0, requests, step, placed)


def build_table(me, page_request_home, lengths):
    per_dev = page_request_home.shape[0]
    requests = lengths.shape[0]
    return pl.pallas_call(
        functools.partial(table_kernel, per_dev, requests),
        out_shape=(
            jax.ShapeDtypeStruct((per_dev,), jnp.int32),
            jax.ShapeDtypeStruct((requests,), jnp.int32),
            jax.ShapeDtypeStruct((requests,), jnp.int32),
        ),
        in_specs=[SMEM, SMEM, SMEM],
        out_specs=(SMEM, SMEM, SMEM),
        compiler_params=params(),
        name="page_table",
    )(me, page_request_home, lengths)


def attend_kernel(
    req_count,
    per_dev,
    requests,
    order_ref,
    chunks_ref,
    lengths_ref,
    table_in,
    q_ref,
    new_ref,
    pages,
    inbox,
    out_ref,
    table,
    labels_v,
    labels_w,
    labels_s,
    buf,
    acc,
    sem,
    sems,
):
    columns = pages.shape[-1]
    heads_kv = columns // HEAD_WIDTH
    half = STEP_COUNT * GROUP
    rows = heads_kv * half
    heads = heads_kv * GROUP
    scale = 1.0 / math.sqrt(HEAD_WIDTH)
    page_rows = pages.reshape(per_dev, PAGE_ROWS, columns)
    inbox_rows = inbox.reshape(req_count, BLOCK * 2, columns)

    first = pltpu.make_async_copy(inbox.at[:, pl.ds(BLOCK - 1, 1)], labels_v, sem)
    first.start()
    first.wait()
    tab = pltpu.make_async_copy(table_in, table, sem)
    tab.start()
    tab.wait()
    row = lax.broadcasted_iota(jnp.int32, (2, 128), 0)
    weight = jnp.where(row == 0, float(DIGIT), 1.0)
    for d in range(req_count):
        digits = labels_v[d, 0, :, 0:128].astype(jnp.float32) * weight
        labels_w[d : d + 1, :] = jnp.sum(digits, axis=0, keepdims=True).astype(jnp.int32)
    back = pltpu.make_async_copy(labels_w, labels_s, sem)
    back.start()
    back.wait()

    @pl.loop(0, req_count)
    def _(d):
        for k in range(CAP):
            slot = labels_s[d, LABEL_LANE + k]

            @pl.when(slot >= 0)
            def _():
                table[slot] = per_dev + d * CAP + k

    steps = requests // UNROLL

    def fetch(step):
        place = lax.rem(step, SLOTS)
        count = chunks_ref[step * UNROLL] * CHUNK_PAGES
        for u in range(UNROLL):
            first_slot = order_ref[step * UNROLL + u] * MAXP

            @pl.loop(0, count)
            def _(j):
                source = table[first_slot + j]
                target = buf.at[place, u, pl.ds(pl.multiple_of(j * PAGE_ROWS, PAGE_ROWS), PAGE_ROWS)]

                @pl.when(source < per_dev)
                def _():
                    pltpu.make_async_copy(page_rows.at[source], target, sems.at[place, u]).start()

                @pl.when(source >= per_dev)
                def _():
                    e = source - per_dev
                    d = lax.shift_right_logical(e, 1)
                    k = e - d * CAP
                    pltpu.make_async_copy(
                        inbox_rows.at[d, pl.ds(pl.multiple_of(k * PAGE_ROWS, PAGE_ROWS), PAGE_ROWS)],
                        target,
                        sems.at[place, u],
                    ).start()

    for s in range(SLOTS - 1):
        fetch(jnp.int32(s))

    def compute(step, n):
        place = lax.rem(step, SLOTS)
        width = n * CHUNK_ROWS
        for u in range(UNROLL):
            whole = buf.at[place, u, pl.ds(0, width)]
            pltpu.make_async_copy(whole, whole, sems.at[place, u]).wait()
        column = lax.broadcasted_iota(jnp.int32, (rows, width), 1)
        even = (column & 1) == 0
        new_column = lax.broadcasted_iota(jnp.int32, (rows, 128), 1)
        new_row = lax.broadcasted_iota(jnp.int32, (rows, 128), 0)
        new_ok = ((new_column & 1) == 0) & (((new_column & (NEW_ROWS - 1)) >> 1) <= (new_row & (STEP_COUNT - 1)))
        for u in range(UNROLL):
            r = order_ref[step * UNROLL + u]
            length = lengths_ref[r]
            q = q_ref[pl.ds(pl.multiple_of(r * rows, rows), rows), :]
            if heads_kv == 2:
                zero = jnp.zeros((half, HEAD_WIDTH), q.dtype)
                q = jnp.concatenate(
                    [jnp.concatenate([q[:half], zero], axis=1), jnp.concatenate([zero, q[half:]], axis=1)], axis=0
                )
            kv = buf[place, u, 0:width, :]
            group = r // NEW_GROUP
            new = new_ref[pl.ds(pl.multiple_of(group * 128, 128), 128), :]
            s = dot(q, kv, ((1,), (1,))) * scale
            sn = dot(q, new, ((1,), (1,))) * scale
            s = jnp.where(even & (column < 2 * length), s, -jnp.inf)
            mine = (new_column >> 3) == (r - group * NEW_GROUP)
            sn = jnp.where(new_ok & mine, sn, -jnp.inf)
            top = jnp.maximum(jnp.max(s, axis=1, keepdims=True), jnp.max(sn, axis=1, keepdims=True))
            w = jnp.exp(s - top)
            wn = jnp.exp(sn - top)
            total = jnp.sum(w, axis=1, keepdims=True) + jnp.sum(wn, axis=1, keepdims=True)
            p = pltpu.roll(w / total, 1, 1).astype(jnp.bfloat16)
            pn = pltpu.roll(wn / total, 1, 1).astype(jnp.bfloat16)
            o = dot(p, kv) + dot(pn, new)
            if heads_kv == 2:
                o = jnp.concatenate([o[:half, :HEAD_WIDTH], o[half:, HEAD_WIDTH:]], axis=0)
            for h in range(heads):
                acc[h, pl.ds(pl.multiple_of(r * STEP_COUNT, STEP_COUNT), STEP_COUNT), :] = o[
                    h * STEP_COUNT : (h + 1) * STEP_COUNT
                ]

    @pl.loop(0, steps)
    def _(step):
        @pl.when(step + (SLOTS - 1) < steps)
        def _():
            fetch(step + (SLOTS - 1))

        count = chunks_ref[step * UNROLL]
        for n in range(1, CHUNKS + 1):

            @pl.when(count == n)
            def _():
                compute(step, n)

    out_ref[...] = acc[...].astype(jnp.bfloat16)


def attend(order, chunks, lengths, table, q, new, pages, inbox):
    per_dev, _, _, columns = pages.shape
    req_count = inbox.shape[0]
    requests = lengths.shape[0]
    heads = columns // HEAD_WIDTH * GROUP
    tokens = requests * STEP_COUNT
    return pl.pallas_call(
        functools.partial(attend_kernel, req_count, per_dev, requests),
        out_shape=jax.ShapeDtypeStruct((heads, tokens, HEAD_WIDTH), jnp.bfloat16),
        in_specs=[SMEM, SMEM, SMEM, HBM, VMEM, VMEM, HBM, HBM],
        out_specs=VMEM,
        scratch_shapes=[
            pltpu.SMEM((per_dev,), jnp.int32),
            pltpu.VMEM((req_count, 1, 2, columns), jnp.bfloat16),
            pltpu.VMEM((req_count, 128), jnp.int32),
            pltpu.SMEM((req_count, 128), jnp.int32),
            pltpu.VMEM((SLOTS, UNROLL, MAXP * PAGE_ROWS, columns), jnp.bfloat16),
            pltpu.VMEM((heads, tokens, HEAD_WIDTH), jnp.float32),
            pltpu.SemaphoreType.DMA,
            pltpu.SemaphoreType.DMA((SLOTS, UNROLL)),
        ],
        compiler_params=params(),
        name="attend",
    )(order, chunks, lengths, table, q, new, pages, inbox)


def split_kernel(x_ref, o_ref):
    o_ref[0] = x_ref[...]


def split_columns(x, parts):
    rows, columns = x.shape
    block = columns // parts
    return pl.pallas_call(
        split_kernel,
        out_shape=jax.ShapeDtypeStruct((parts, rows, block), x.dtype),
        grid=(parts,),
        in_specs=[pl.BlockSpec((rows, block), lambda i: (0, i))],
        out_specs=pl.BlockSpec((1, rows, block), lambda i: (i, 0, 0)),
        compiler_params=params(),
        name="split_columns",
    )(x)


def project_kernel(x_ref, w_ref, down_ref, o_ref, low_ref):
    blocks, heads, tokens, _ = x_ref.shape
    for b in range(blocks):
        x = jnp.concatenate([x_ref[b, h] for h in range(heads)], axis=1)
        o_ref[b * tokens : (b + 1) * tokens, :] = dot(x, w_ref[...]).astype(jnp.bfloat16)

        @pl.when(pl.program_id(0) == 0)
        def _():
            low_ref[b * tokens : (b + 1) * tokens, :] = dot(x, down_ref[...], ((1,), (1,)))


def project(x, w, down):
    blocks, heads, tokens, width = x.shape
    columns = w.shape[1]
    tile = 256
    return pl.pallas_call(
        project_kernel,
        out_shape=(
            jax.ShapeDtypeStruct((blocks * tokens, columns), jnp.bfloat16),
            jax.ShapeDtypeStruct((blocks * tokens, down.shape[0]), jnp.float32),
        ),
        grid=(columns // tile,),
        in_specs=[
            pl.BlockSpec(x.shape, lambda i: (0, 0, 0, 0)),
            pl.BlockSpec((w.shape[0], tile), lambda i: (0, i)),
            pl.BlockSpec(down.shape, lambda i: (0, 0)),
        ],
        out_specs=(
            pl.BlockSpec((blocks * tokens, tile), lambda i: (0, i)),
            pl.BlockSpec((blocks * tokens, down.shape[0]), lambda i: (0, 0)),
        ),
        compiler_params=params(),
        name="project",
    )(x, w, down)


def finish_kernel(plain_ref, low_ref, up_ref, o_ref):
    o_ref[...] = (plain_ref[...].astype(jnp.float32) + dot(low_ref[...], up_ref[...])).astype(jnp.bfloat16)


def finish(plain, low, up):
    return pl.pallas_call(
        finish_kernel,
        out_shape=jax.ShapeDtypeStruct(plain.shape, jnp.bfloat16),
        in_specs=[VMEM, VMEM, VMEM],
        out_specs=VMEM,
        compiler_params=params(),
        name="finish",
    )(plain, low, up)


def on_device(
    queries,
    incoming_key_value,
    key_value_pages,
    page_request_home,
    lengths,
    request_adapter_index,
    adapter_storage_slot,
    adapter_down_factor,
    adapter_up_factor,
    output_projection_weight,
):
    req_count = lax.axis_size("req")
    my_req = lax.axis_index("req")
    my_lane = lax.axis_index("tp")
    tp_count = lax.axis_size("tp")
    me = my_req.astype(jnp.int32).reshape(1)
    requests = lengths.shape[0]
    columns = key_value_pages.shape[-1]
    heads = columns // HEAD_WIDTH * GROUP
    own_slots, rank, model = adapter_up_factor.shape

    outbox = pack(me, page_request_home, request_adapter_index, key_value_pages, req_count)
    inbox = lax.all_to_all(outbox, "req", split_axis=0, concat_axis=0, tiled=True)

    table, order, chunks = build_table(me, page_request_home, lengths)
    q = queries.reshape(requests, STEP_COUNT, heads, HEAD_WIDTH).transpose(0, 2, 1, 3)
    q = q.reshape(requests * heads * STEP_COUNT, HEAD_WIDTH)
    new = incoming_key_value.transpose(1, 0, 2).reshape(-1, columns)
    up = split_columns(adapter_up_factor.reshape(own_slots * rank, model), req_count)
    up = lax.all_to_all(up, "req", split_axis=0, concat_axis=0, tiled=True)
    up = up.reshape(req_count * own_slots * rank, -1)

    mixed = attend(order, chunks, lengths, table, q, new, key_value_pages, inbox)
    everyone = lax.all_gather(mixed, "req", axis=0)

    ids = inbox[:, BLOCK - 1, 0, :requests].astype(jnp.int32).reshape(-1)
    slot_count = adapter_storage_slot.shape[0]
    match = ids[:, None] == jnp.arange(slot_count, dtype=jnp.int32)[None, :]
    slot = jnp.sum(jnp.where(match, adapter_storage_slot[None, :], 0), axis=1)
    token_slot = jnp.repeat(slot, STEP_COUNT)

    down = adapter_down_factor.transpose(0, 2, 1).reshape(own_slots * rank, -1)
    partial, low = project(everyone, output_projection_weight, down)
    kept = jnp.zeros((low.shape[0], rank), jnp.float32)
    for k in range(own_slots):
        here = token_slot == my_req * own_slots + k
        kept = kept + jnp.where(here[:, None], low[:, k * rank : (k + 1) * rank], 0.0)
    low_rows = lax.psum_scatter(kept, "tp", scatter_dimension=0, tiled=True)
    low_rows = lax.psum(low_rows, "req").astype(jnp.bfloat16)
    plain = lax.psum_scatter(partial, "tp", scatter_dimension=0, tiled=True)

    block_rows = low_rows.shape[0]
    block_slot = lax.dynamic_slice_in_dim(token_slot, my_lane * block_rows, block_rows)
    selector = (block_slot[:, None] == jnp.arange(slot_count, dtype=jnp.int32)[None, :]).astype(jnp.bfloat16)
    expanded = (selector[:, :, None] * low_rows[:, None, :]).reshape(block_rows, slot_count * rank)
    return finish(plain, expanded, up)


def solution(mesh):
    return jax.shard_map(
        on_device,
        mesh=mesh,
        in_specs=(
            P("req", "tp"),
            P(None, "req", "tp"),
            P("req", None, None, "tp"),
            P("req"),
            P("req"),
            P("req"),
            P(),
            P("req", "tp", None),
            P("req", None, None),
            P("tp", "req"),
        ),
        out_specs=P("tp", "req"),
        check_vma=False,
    )
```

time: 357 us -> 209 us (0.59)
  local copies, waits for them, and re-layouts: 133 us -> 4.29 us
  Pallas kernels: 0 us -> 80.4 us
  other arithmetic: 69.7 us -> 3.41 us
  matrix products: 30.2 us -> 0 us
  blocking collectives: 17.2 us -> 32.9 us
  waiting for transfers between devices: 77.4 us -> 62.7 us
    gather x3 -> x0, local copies, waits for them, and re-layouts: 97 us -> none  [the longest x2 89.6 us: relocate(): return jnp.take(candidates, slot_source, axis=0)]
    pallas_call x0 -> x6, Pallas kernels: none -> 80.4 us  [the longest x1 32.3 us: attend(): pl.pallas_call(functools.partial(attend_kernel, req_count, per_dev, reque...]
    concatenate x2 -> x0, other arithmetic: 45.5 us -> none  [the longest x1 45.5 us: relocate(): candidates = jnp.concatenate([key_value_pages, inbox_pages], axis=0)]
    all_to_all x3 -> x2, waiting for transfers between devices: 35.3 us -> 0.01 us  [the longest x1 0.01 us: on_device(): lax.all_to_all(outbox, 'req', split_axis=0, concat_axis=0, tiled=True)]
    psum x0 -> x1, blocking collectives: none -> 32.9 us  [on_device(): low_rows = lax.psum(low_rows, 'req').astype(jnp.bfloat16)]
    all_gather x2 -> x1, waiting for transfers between devices: 13.2 us -> 39.9 us  [on_device(): everyone = lax.all_gather(mixed, 'req', axis=0)]
    dot_general x6 -> x0, matrix products: 26.5 us -> none  [the longest x1 9.88 us: on_device(): jnp.dot(everyone, output_projection_weight, preferred_element_type=jnp.fl...]
    unnamed x15 -> x11, local copies, waits for them, and re-layouts: 23.1 us -> 0.93 us
  transfers between devices with their start and end apart: 7 -> 5, of which waited for: 4 -> 3; matrix products, arithmetic and copies ran while one was open for 63% -> 2% of each run, Pallas kernels for 0% -> 8%
where the time goes in v1:
time: 209 us; the launch traced here: 208 us
  Pallas kernels  80.4 us (38%)
  waiting for transfers between devices  62.7 us (30%)
  blocking collectives  32.9 us (16%)
  between operations  13.2 us (6%)
  starting transfers between devices  11.4 us (5%)
  local copies, waits for them, and re-layouts  4.29 us (2%)
  other arithmetic  3.41 us (2%)
    all_gather x1, waiting for transfers between devices, on_device(): everyone = lax.all_gather(mixed, 'req', axis=0)  39.9 us
    psum x1, blocking collectives, on_device(): low_rows = lax.psum(low_rows, 'req').astype(jnp.bfloat16)  32.9 us
    pallas_call x1, Pallas kernels, attend(): pl.pallas_call(functools.partial(attend_kernel, req_count, per_dev, reque...  32.3 us
    pallas_call x1, Pallas kernels, project(): pl.pallas_call(project_kernel, out_shape=(jax.ShapeDtypeStruct((blocks *...  16.1 us
    pallas_call x1, Pallas kernels, build_table(): pl.pallas_call(functools.partial(table_kernel, per_dev, requests), out_sh...  11.8 us
    reduce_scatter x1, waiting for transfers between devices, on_device(): low_rows = lax.psum_scatter(kept, 'tp', scatter_dimension=0, tiled=True)  11.7 us
    pallas_call x1, Pallas kernels, pack(): pl.pallas_call(functools.partial(pack_kernel, req_count, per_dev), out_sh...  11 us
    reduce_scatter x1, waiting for transfers between devices, on_device(): plain = lax.psum_scatter(partial, 'tp', scatter_dimension=0, tiled=True)  10.4 us
  transfers between devices with their start and end apart: 5, of which 3 were waited for; matrix products, arithmetic and copies ran while one was open for 2% of the time, Pallas kernels for 8%

profile of v1, /device:TPU:0, one launch (start us, length us, event | category | flops | bytes accessed | tf_op | source)
XLA Modules:
  0.0 208.3 jit_solution(13359105815677158901)
XLA Ops:
  6.5 11.0 %pack_outbox.1 = bf16[8,65,2,256]{3,2,1,0:T(2,128)(2,1)} custom-call(s32[1]{0:T(128)} %bitcast.me_ref, s32[1,512]{1,0:T(1,128)} %bitcast.26, s32[1,32]{1,0:T(1,128)} %bitcast.27, bf16[512,32,2,256]{3,2,1,0:T(2,128)(2,1)} %pages.3), custom_call_target="tpu_custom_call" | custom-call | tf_op jit(solution)/shard_map/pack_outbox/pallas_call | solution.py:108
  17.6 7.7 %all-to-all-start = ((bf16[8,65,2,256]{3,2,1,0:T(2,128)(2,1)}), bf16[8,65,2,256]{3,2,1,0:T(2,128)(2,1)S(1)}, u32[]{:S(2)}, u32[]{:S(2)}) async-start(bf16[8,65,2,256]{3,2,1,0:T(2,128)(2,1)} %pack_outbox.1), calls=%async_computation | async-start | bytes 1064960 | tf_op jit(solution)/shard_map/all_to_all | solution.py:437
  25.3 11.8 %page_table.1 = (s32[512]{0:T(512)}, s32[32]{0:T(128)}, s32[32]{0:T(128)}) custom-call(s32[1]{0:T(128)} %bitcast.me_ref, s32[512]{0:T(512)} %home_ref.1, s32[32]{0:T(128)} %lengths_ref.3), custom_call_target="tpu_custom_call" | custom-call | tf_op jit(solution)/shard_map/page_table/pallas_call | solution.py:161
  37.1 0.1 copy.26
  37.3 0.7 reshape.78.new_ref
  38.0 0.1 copy.29
  38.1 1.1 copy.25
  39.1 0.8 copy-done.1
  40.0 32.3 %attend.1 = bf16[16,128,128]{2,1,0:T(8,128)(2,1)} custom-call(s32[32]{0:T(128)} %get-tuple-element.10.order_ref, s32[32]{0:T(128)} %get-tuple-element.11.chunks_ref, s32[32]{0:T(128)} %lengths_ref.3, s32[512]{0:T(512)} %get-tuple-element.12.table_in, bf16[2048,128]{1,0:T(8,128)(2,1)} %bitcast.19, bf16[256,256]{1,0:T(8,128)(2,1)} %reshape.78.new_ref, ...), custom_call_target="tpu_custom_call" | custom-call | tf_op jit(solution)/shard_map/attend/pallas_call | solution.py:325
  72.4 0.7 fusion.1
  73.2 0.1 broadcast_in_dim.43
  73.3 0.1 reshape.82
  73.5 39.9 %all-gather.3.cloned.1.call-done = bf16[128,128,128]{2,1,0:T(8,128)(2,1)} async-done(((bf16[16,128,128]{2,1,0:T(8,128)(2,1)}), bf16[128,128,128]{2,1,0:T(8,128)(2,1)}) %all-gather.3.cloned.1.call-update) | async-done | bytes 4194320 | tf_op jit(solution)/shard_map/all_gather | solution.py:448
  113.4 16.1 %project.1 = (bf16[1024,1024]{1,0:T(8,128)(2,1)}, f32[1024,128]{1,0:T(8,128)}) custom-call(bf16[8,16,128,128]{3,2,1,0:T(8,128)(2,1)} %bitcast.18, bf16[2048,1024]{1,0:T(8,128)(2,1)} %w_ref.1, bf16[128,2048]{1,0:T(8,128)(2,1)} %bitcast.23), custom_call_target="tpu_custom_call" | custom-call | tf_op jit(solution)/shard_map/project/pallas_call | solution.py:378
  129.5 2.5 %select_add_fusion = f32[1024,64]{1,0:T(8,128)} fusion(f32[1024,128]{1,0:T(8,128)} %get-tuple-element.14, pred[1024]{0:T(1024)(128)(4,1)S(1)} %get-tuple-element.16, pred[1024]{0:T(1024)(128)(4,1)S(1)} %get-tuple-element.15), kind=kLoop, calls=%fused_computation | loop fusion | flops 196608 | bytes 788480 | tf_op jit(solution)/shard_map/add | solution.py:461
  132.2 0.7 reduce-scatter.3.cloned.1.call-update
  132.8 5.6 %split_columns.1 = bf16[8,128,1024]{2,1,0:T(8,128)(2,1)} custom-call(bf16[128,8192]{1,0:T(8,128)(2,1)} %bitcast.20), custom_call_target="tpu_custom_call" | custom-call | tf_op jit(solution)/shard_map/split_columns/pallas_call | solution.py:352
  138.5 3.6 %all-to-all-start.1 = ((bf16[8,128,1024]{2,1,0:T(8,128)(2,1)}), bf16[8,128,1024]{2,1,0:T(8,128)(2,1)S(1)}, u32[]{:S(2)}, u32[]{:S(2)}) async-start(bf16[8,128,1024]{2,1,0:T(8,128)(2,1)} %split_columns.1), calls=%async_computation.3 | async-start | bytes 4194304 | tf_op jit(solution)/shard_map/all_to_all | solution.py:444
  142.2 11.7 %reduce-scatter.5.cloned.1.call-done = f32[256,64]{1,0:T(8,128)} async-done(((f32[1024,64]{1,0:T(8,128)}), f32[256,64]{1,0:T(8,128)}) %reduce-scatter.5.cloned.1.call-update) | async-done | bytes 65552 | tf_op jit(solution)/shard_map/reduce_scatter | solution.py:462
  153.9 32.9 %psum.7 = bf16[256,64]{1,0:T(8,128)(2,1)S(1)} all-reduce(f32[256,64]{1,0:T(8,128)} %reduce-scatter.5.cloned.1.call-done), channel_id=1, replica_groups=mesh['req'=8,'tp'=4] {'req'}, use_global_device_ids=true, to_apply=%region_3.4 | all-reduce | flops 16384 | bytes 98304 | tf_op jit(solution)/shard_map/psum | solution.py:463
  186.8 0.1 copy.27
  186.9 1.0 copy.28.low_ref
  187.9 10.4 %reduce-scatter.3.cloned.1.call-done.plain_ref = bf16[256,1024]{1,0:T(8,128)(2,1)} async-done(((bf16[1024,1024]{1,0:T(8,128)(2,1)}), bf16[256,1024]{1,0:T(8,128)(2,1)}) %reduce-scatter.3.cloned.1.call-update) | async-done | bytes 524304 | tf_op jit(solution)/shard_map/reduce_scatter | solution.py:464
  198.3 3.4 %finish.1 = bf16[256,1024]{1,0:T(8,128)(2,1)} custom-call(bf16[256,1024]{1,0:T(8,128)(2,1)} %reduce-scatter.3.cloned.1.call-done.plain_ref, bf16[256,1024]{1,0:T(8,128)(2,1)} %copy.28.low_ref, bf16[1024,1024]{1,0:T(8,128)(2,1)} %bitcast.17), custom_call_target="tpu_custom_call" | custom-call | tf_op jit(solution)/shard_map/finish/pallas_call | solution.py:404
  (22 shorter events, 0.5 us)
Async XLA Ops:
  6.5 30.6 %copy-start.3 = (bf16[2,128,256]{2,1,0:T(8,128)(2,1)S(1)}, bf16[2,128,256]{2,1,0:T(8,128)(2,1)}, u32[]{:S(2)}) copy-start(bf16[2,128,256]{2,1,0:T(8,128)(2,1)} %param.11) | copy-start | bytes 393220
  6.5 31.4 %copy-start.2 = (bf16[128,2048]{1,0:T(8,128)(2,1)S(1)}, bf16[128,2048]{1,0:T(8,128)(2,1)}, u32[]{:S(2)}) copy-start(bf16[128,2048]{1,0:T(8,128)(2,1)} %param.10) | copy-start | bytes 1572868
  17.6 21.6 %all-to-all-start = ((bf16[8,65,2,256]{3,2,1,0:T(2,128)(2,1)}), bf16[8,65,2,256]{3,2,1,0:T(2,128)(2,1)S(1)}, u32[]{:S(2)}, u32[]{:S(2)}) async-start(bf16[8,65,2,256]{3,2,1,0:T(2,128)(2,1)} %pack_outbox.1), calls=%async_computation | async-start | bytes 1064960 | tf_op jit(solution)/shard_map/all_to_all | solution.py:437
  25.3 88.1 %all-gather.3.cloned.1.call-start = ((), (), s32[]{:S(2)}) async-start(), calls=%async_computation.6 | async-start | bytes 4718592 | tf_op jit(solution)/shard_map/all_gather | solution.py:448
  39.1 0.8 copy-start.1
  39.9 33.2 %copy-start.4 = (s32[16]{0:T(128)S(1)}, s32[16]{0:T(128)}, u32[]{:S(2)}) copy-start(s32[16]{0:T(128)} %param.16) | copy-start | bytes 196
  72.3 81.6 %reduce-scatter.5.cloned.1.call-start = ((), (), s32[]{:S(2)}) async-start(), calls=%async_computation.5 | async-start | bytes 655360 | tf_op jit(solution)/shard_map/reduce_scatter | solution.py:462
  132.1 66.2 %reduce-scatter.3.cloned.1.call-start = ((), (), s32[]{:S(2)}) async-start(), calls=%async_computation.4 | async-start | bytes 2621440 | tf_op jit(solution)/shard_map/reduce_scatter | solution.py:464
  138.5 49.5 %all-to-all-start.1 = ((bf16[8,128,1024]{2,1,0:T(8,128)(2,1)}), bf16[8,128,1024]{2,1,0:T(8,128)(2,1)S(1)}, u32[]{:S(2)}, u32[]{:S(2)}) async-start(bf16[8,128,1024]{2,1,0:T(8,128)(2,1)} %split_columns.1), calls=%async_computation.3 | async-start | bytes 4194304 | tf_op jit(solution)/shard_map/all_to_all | solution.py:444
  187.9 10.4 %copy-start = (bf16[8,128,1024]{2,1,0:T(8,128)(2,1)}, bf16[8,128,1024]{2,1,0:T(8,128)(2,1)S(1)}, u32[]{:S(2)}) copy-start(bf16[8,128,1024]{2,1,0:T(8,128)(2,1)S(1)} %all-to-all-done.1) | copy-start | bytes 6291460
Sparse Core Ops, SparseCore 0:
  72.4 40.9 all-gather.2
  132.2 21.6 reduce-scatter.4
  156.2 42.1 reduce-scatter.2

commit v2 on v1

v2 whole, which is shorter than its diff:
```python
import functools
import math

import jax
import jax.numpy as jnp
from jax import lax
from jax.experimental import pallas as pl
from jax.experimental.pallas import tpu as pltpu
from jax.sharding import PartitionSpec as P

QUERY_HEADS = 64
KEY_VALUE_HEADS = 8
GROUP = QUERY_HEADS // KEY_VALUE_HEADS
HEAD_WIDTH = 128
STEP_COUNT = 4
PAGE_LENGTH = 32
MAXP = 16
CAP = 2
BLOCK = CAP * PAGE_LENGTH + 1
LABEL_LANE = 64
DIGIT = 16
CHUNK_PAGES = 4
CHUNKS = MAXP // CHUNK_PAGES
PAGE_ROWS = PAGE_LENGTH * 2
CHUNK_ROWS = CHUNK_PAGES * PAGE_ROWS
NEW_ROWS = STEP_COUNT * 2
NEW_GROUP = 128 // NEW_ROWS
UNROLL = 2
SLOTS = 6
HALVES = 2
VMEM_LIMIT = 56 * 1024 * 1024

HBM = pl.BlockSpec(memory_space=pltpu.HBM)
VMEM = pl.BlockSpec(memory_space=pltpu.VMEM)
SMEM = pl.BlockSpec(memory_space=pltpu.SMEM)


def params():
    return pltpu.CompilerParams(vmem_limit_bytes=VMEM_LIMIT)


def dot(a, b, contract=((1,), (0,))):
    return lax.dot_general(a, b, (contract, ((), ())), preferred_element_type=jnp.float32)


def pack_kernel(req_count, per_dev, me_ref, home_ref, ids_ref, pages, outbox, info_v, info_s, ids_v, rows_v, sem, sems):
    me = me_ref[0]
    page = lax.broadcasted_iota(jnp.int32, (req_count, per_dev), 1)
    want = lax.broadcasted_iota(jnp.int32, (req_count, per_dev), 0)
    slots = jnp.broadcast_to(home_ref[...], (req_count, per_dev)) - want * per_dev
    hit = (slots >= 0) & (slots < per_dev) & (want != me)
    lane = lax.broadcasted_iota(jnp.int32, (req_count, 128), 1)
    info = jnp.full((req_count, 128), -1, jnp.int32)
    for k in range(CAP):
        first = jnp.min(jnp.where(hit, page, per_dev), axis=1, keepdims=True)
        here = hit & (page == first)
        slot = jnp.max(jnp.where(here, slots, -1), axis=1, keepdims=True)
        info = jnp.where(lane == k, first, info)
        info = jnp.where(lane == CAP + k, slot, info)
        hit = hit & (page != first)
    info_v[...] = info
    fetch = pltpu.make_async_copy(info_v, info_s, sem)
    fetch.start()
    ids_v[...] = jnp.zeros_like(ids_v)
    ids_v[:, 0:ids_ref.shape[1]] = ids_ref[...].astype(jnp.float32)
    ids = jnp.broadcast_to(ids_v[...], (2, 128))
    fetch.wait()

    def copy(d, k):
        return pltpu.make_async_copy(
            pages.at[info_s[d, k]],
            outbox.at[d, pl.ds(k * PAGE_LENGTH, PAGE_LENGTH)],
            sems.at[d, k],
        )

    for d in range(req_count):
        for k in range(CAP):

            @pl.when(info_s[d, k] < per_dev)
            def _():
                copy(d, k).start()

    at = lax.broadcasted_iota(jnp.int32, (2, 128), 1)
    row = lax.broadcasted_iota(jnp.int32, (2, 128), 0)
    for d in range(req_count):
        value = jnp.where(row == 0, ids, 0.0)
        for k in range(CAP):
            slot = info_s[d, CAP + k]
            high = ((slot + DIGIT) >> 4) - 1
            low = slot - high * DIGIT
            digit = jnp.where(row == 0, high, low).astype(jnp.float32)
            value = jnp.where(at == LABEL_LANE + k, digit, value)
        rows_v[d, 0, :, :] = jnp.zeros(rows_v.shape[2:], jnp.bfloat16)
        rows_v[d, 0, :, 0:128] = value.astype(jnp.bfloat16)
    rows = pltpu.make_async_copy(rows_v, outbox.at[:, pl.ds(BLOCK - 1, 1)], sem)
    rows.start()
    rows.wait()
    for d in range(req_count):
        for k in range(CAP):

            @pl.when(info_s[d, k] < per_dev)
            def _():
                copy(d, k).wait()


def pack(me, page_request_home, ids, key_value_pages, req_count):
    per_dev = key_value_pages.shape[0]
    columns = key_value_pages.shape[-1]
    return pl.pallas_call(
        functools.partial(pack_kernel, req_count, per_dev),
        out_shape=jax.ShapeDtypeStruct((req_count, BLOCK, 2, columns), jnp.bfloat16),
        in_specs=[SMEM, VMEM, VMEM, HBM],
        out_specs=VMEM,
        scratch_shapes=[
            pltpu.VMEM((req_count, 128), jnp.int32),
            pltpu.SMEM((req_count, 128), jnp.int32),
            pltpu.VMEM((1, 128), jnp.float32),
            pltpu.VMEM((req_count, 1, 2, columns), jnp.bfloat16),
            pltpu.SemaphoreType.DMA,
            pltpu.SemaphoreType.DMA((req_count, CAP)),
        ],
        compiler_params=params(),
        name="pack_outbox",
    )(me, page_request_home.reshape(1, per_dev), ids.reshape(1, -1), key_value_pages)


def table_kernel(per_dev, requests, me_ref, home_ref, lengths_ref, table_ref, order_ref, len_v):
    base = me_ref[0] * per_dev
    lane = lax.broadcasted_iota(jnp.int32, (128, 128), 1)
    row = lax.broadcasted_iota(jnp.int32, (128, 128), 0)
    tiles = per_dev // 128
    columns = [
        jnp.transpose(jnp.broadcast_to(home_ref[i : i + 1, :] - base, (128, 128)).astype(jnp.float32))
        for i in range(tiles)
    ]
    for j in range(tiles):
        total = jnp.zeros((128, 128), jnp.float32)
        slot = (lane + j * 128).astype(jnp.float32)
        for i in range(tiles):
            total = total + jnp.where(columns[i] == slot, (row + i * 128).astype(jnp.float32), 0.0)
        table_ref[j : j + 1, :] = jnp.sum(total, axis=0, keepdims=True).astype(jnp.int32)
    half = requests // HALVES
    len_v[...] = jnp.zeros_like(len_v)
    len_v[:, 0:requests] = lengths_ref[...].astype(jnp.float32)
    along = jnp.broadcast_to(len_v[...], (128, 128))
    along = ((along.astype(jnp.int32) + (CHUNK_ROWS // 2 - 1)) >> 7).astype(jnp.float32)
    down = jnp.transpose(along)
    same = (lane // half) == (row // half)
    before = same & ((along > down) | ((along == down) & (lane < row)))
    rank = jnp.sum(jnp.where(before, 1.0, 0.0), axis=1, keepdims=True)
    place = rank + ((row // half) * half).astype(jnp.float32)
    at = place == lane.astype(jnp.float32)
    order = jnp.sum(jnp.where(at, row.astype(jnp.float32), 0.0), axis=0, keepdims=True)
    chunks = jnp.sum(jnp.where(at, down, 0.0), axis=0, keepdims=True)
    order_ref[0:1, :] = order.astype(jnp.int32)
    order_ref[1:2, :] = chunks.astype(jnp.int32)


def build_table(me, page_request_home, lengths):
    per_dev = page_request_home.shape[0]
    requests = lengths.shape[0]
    return pl.pallas_call(
        functools.partial(table_kernel, per_dev, requests),
        out_shape=(
            jax.ShapeDtypeStruct((per_dev // 128, 128), jnp.int32),
            jax.ShapeDtypeStruct((2, 128), jnp.int32),
        ),
        in_specs=[SMEM, VMEM, VMEM],
        out_specs=(VMEM, VMEM),
        scratch_shapes=[pltpu.VMEM((1, 128), jnp.float32)],
        compiler_params=params(),
        name="page_table",
    )(me, page_request_home.reshape(per_dev // 128, 128), lengths.reshape(1, requests))


def attend_kernel(
    req_count,
    per_dev,
    base,
    requests,
    order_ref,
    lengths_ref,
    table_in,
    q_ref,
    new_ref,
    pages,
    inbox,
    out_ref,
    table,
    labels_v,
    labels_w,
    labels_s,
    buf,
    acc,
    sem,
    sems,
):
    columns = pages.shape[-1]
    heads_kv = columns // HEAD_WIDTH
    half = STEP_COUNT * GROUP
    rows = heads_kv * half
    heads = heads_kv * GROUP
    scale = math.log2(math.e) / math.sqrt(HEAD_WIDTH)
    page_rows = pages.reshape(per_dev, PAGE_ROWS, columns)
    inbox_rows = inbox.reshape(req_count, BLOCK * 2, columns)

    tab = pltpu.make_async_copy(table_in, table, sem)
    tab.start()
    tab.wait()
    first = pltpu.make_async_copy(inbox.at[:, pl.ds(BLOCK - 1, 1)], labels_v, sem)
    first.start()
    first.wait()
    row = lax.broadcasted_iota(jnp.int32, (2, 128), 0)
    weight = jnp.where(row == 0, float(DIGIT), 1.0)
    for d in range(req_count):
        digits = labels_v[d, 0, :, 0:128].astype(jnp.float32) * weight
        labels_w[d : d + 1, :] = jnp.sum(digits, axis=0, keepdims=True).astype(jnp.int32)
    back = pltpu.make_async_copy(labels_w, labels_s, sem)
    back.start()
    back.wait()
    for d in range(req_count):
        for k in range(CAP):
            slot = labels_s[d, LABEL_LANE + k]

            @pl.when(slot >= 0)
            def _():
                table[lax.shift_right_logical(slot, 7), slot & 127] = per_dev + d * CAP + k

    steps = requests // UNROLL

    def fetch(step):
        place = lax.rem(step, SLOTS)
        count = order_ref[1, base + step * UNROLL]
        for u in range(UNROLL):
            slot = order_ref[0, base + step * UNROLL + u] * MAXP
            line = lax.shift_right_logical(slot, 7)
            at = slot & 127

            @pl.loop(0, count)
            def _(c):
                sources = [table[line, at + c * CHUNK_PAGES + j] for j in range(CHUNK_PAGES)]
                most = functools.reduce(jnp.maximum, sources)

                def target(j):
                    start = pl.multiple_of(c * CHUNK_ROWS + j * PAGE_ROWS, PAGE_ROWS)
                    return buf.at[place, u, pl.ds(start, PAGE_ROWS)]

                @pl.when(most < per_dev)
                def _():
                    for j in range(CHUNK_PAGES):
                        pltpu.make_async_copy(page_rows.at[sources[j]], target(j), sems.at[place, u]).start()

                @pl.when(most >= per_dev)
                def _():
                    for j in range(CHUNK_PAGES):
                        source = sources[j]

                        @pl.when(source < per_dev)
                        def _():
                            pltpu.make_async_copy(page_rows.at[source], target(j), sems.at[place, u]).start()

                        @pl.when(source >= per_dev)
                        def _():
                            e = source - per_dev
                            d = lax.shift_right_logical(e, 1)
                            k = e - d * CAP
                            start = pl.multiple_of(k * PAGE_ROWS, PAGE_ROWS)
                            pltpu.make_async_copy(
                                inbox_rows.at[d, pl.ds(start, PAGE_ROWS)], target(j), sems.at[place, u]
                            ).start()

    for s in range(min(SLOTS - 1, steps)):
        fetch(jnp.int32(s))

    def compute(step, n):
        place = lax.rem(step, SLOTS)
        width = n * CHUNK_ROWS
        for u in range(UNROLL):
            whole = buf.at[place, u, pl.ds(0, width)]
            pltpu.make_async_copy(whole, whole, sems.at[place, u]).wait()
        column = lax.broadcasted_iota(jnp.int32, (1, width), 1)
        column = jnp.where((column & 1) == 0, column, 2 * width * CHUNKS)
        new_column = lax.broadcasted_iota(jnp.int32, (rows, 128), 1)
        new_row = lax.broadcasted_iota(jnp.int32, (rows, 128), 0)
        new_ok = ((new_column & 1) == 0) & (((new_column & (NEW_ROWS - 1)) >> 1) <= (new_row & (STEP_COUNT - 1)))
        for u in range(UNROLL):
            r = order_ref[0, base + step * UNROLL + u]
            length = lengths_ref[r]
            q = q_ref[pl.ds(pl.multiple_of(r * rows, rows), rows), :]
            if heads_kv == 2:
                zero = jnp.zeros((half, HEAD_WIDTH), q.dtype)
                q = jnp.concatenate(
                    [jnp.concatenate([q[:half], zero], axis=1), jnp.concatenate([zero, q[half:]], axis=1)], axis=0
                )
            kv = buf[place, u, 0:width, :]
            group = r // NEW_GROUP
            new = new_ref[pl.ds(pl.multiple_of(group * 128, 128), 128), :]
            bias = jnp.where(column < 2 * length, 0.0, -jnp.inf)
            s = dot(q, kv, ((1,), (1,))) * scale + bias
            mine = (new_column >> 3) == (r - group * NEW_GROUP)
            sn = jnp.where(new_ok & mine, dot(q, new, ((1,), (1,))) * scale, -jnp.inf)
            top = jnp.maximum(jnp.max(s, axis=1, keepdims=True), jnp.max(sn, axis=1, keepdims=True))
            w = jnp.exp2(s - top)
            wn = jnp.exp2(sn - top)
            inverse = 1.0 / (jnp.sum(w, axis=1, keepdims=True) + jnp.sum(wn, axis=1, keepdims=True))
            p = pltpu.roll(w * inverse, 1, 1).astype(jnp.bfloat16)
            pn = pltpu.roll(wn * inverse, 1, 1).astype(jnp.bfloat16)
            o = dot(p, kv) + dot(pn, new)
            if heads_kv == 2:
                o = jnp.concatenate([o[:half, :HEAD_WIDTH], o[half:, HEAD_WIDTH:]], axis=0)
            at = pl.multiple_of((r - base) * STEP_COUNT, STEP_COUNT)
            for h in range(heads):
                acc[h, pl.ds(at, STEP_COUNT), :] = o[h * STEP_COUNT : (h + 1) * STEP_COUNT]

    @pl.loop(0, steps)
    def _(step):
        @pl.when(step + (SLOTS - 1) < steps)
        def _():
            fetch(step + (SLOTS - 1))

        count = order_ref[1, base + step * UNROLL]
        for n in range(1, CHUNKS + 1):

            @pl.when(count == n)
            def _():
                compute(step, n)

    out_ref[...] = acc[...].astype(jnp.bfloat16)


def attend(part, order, lengths, table, q, new, pages, inbox):
    per_dev, _, _, columns = pages.shape
    req_count = inbox.shape[0]
    requests = lengths.shape[0] // HALVES
    heads = columns // HEAD_WIDTH * GROUP
    tokens = requests * STEP_COUNT
    return pl.pallas_call(
        functools.partial(attend_kernel, req_count, per_dev, part * requests, requests),
        out_shape=jax.ShapeDtypeStruct((heads, tokens, HEAD_WIDTH), jnp.bfloat16),
        in_specs=[SMEM, SMEM, HBM, VMEM, VMEM, HBM, HBM],
        out_specs=VMEM,
        scratch_shapes=[
            pltpu.SMEM((per_dev // 128, 128), jnp.int32),
            pltpu.VMEM((req_count, 1, 2, columns), jnp.bfloat16),
            pltpu.VMEM((req_count, 128), jnp.int32),
            pltpu.SMEM((req_count, 128), jnp.int32),
            pltpu.VMEM((SLOTS, UNROLL, MAXP * PAGE_ROWS, columns), jnp.bfloat16),
            pltpu.VMEM((heads, tokens, HEAD_WIDTH), jnp.float32),
            pltpu.SemaphoreType.DMA,
            pltpu.SemaphoreType.DMA((SLOTS, UNROLL)),
        ],
        compiler_params=params(),
        cost_estimate=pl.CostEstimate(
            flops=16 * tokens * heads * HEAD_WIDTH * MAXP * PAGE_LENGTH,
            bytes_accessed=requests * MAXP * PAGE_ROWS * columns * 2,
            transcendentals=2 * tokens * heads * MAXP * PAGE_LENGTH,
        ),
        name="attend",
    )(order, lengths, table, q, new, pages, inbox)


def split_kernel(x_ref, o_ref):
    o_ref[0] = x_ref[...]


def split_columns(x, parts):
    rows, columns = x.shape
    block = columns // parts
    return pl.pallas_call(
        split_kernel,
        out_shape=jax.ShapeDtypeStruct((parts, rows, block), x.dtype),
        grid=(parts,),
        in_specs=[pl.BlockSpec((rows, block), lambda i: (0, i))],
        out_specs=pl.BlockSpec((1, rows, block), lambda i: (i, 0, 0)),
        compiler_params=params(),
        name="split_columns",
    )(x)


def project_kernel(count, roles, where_ref, *refs):
    xs, (w_ref, down_ref, mask_ref), rest = refs[:count], refs[count : count + 3], refs[count + 3 :]
    outs, low_ref, x_v = rest[:roles], rest[roles], rest[roles + 1]
    heads, tokens, width = xs[0].shape
    rows = count * tokens // roles

    @pl.when(pl.program_id(0) == 0)
    def _():
        for b in range(count):
            at = pl.multiple_of(where_ref[b] * tokens, tokens)
            for h in range(heads):
                x_v[pl.ds(at, tokens), h * width : (h + 1) * width] = xs[b][h]
        for j in range(roles):
            s = where_ref[count + j]
            low = dot(x_v[j * rows : (j + 1) * rows, :], down_ref[...], ((1,), (1,)))
            low_ref[s] = (low * mask_ref[s].astype(jnp.float32)).astype(jnp.bfloat16)

    y = dot(x_v[...], w_ref[...]).astype(jnp.bfloat16)
    for j in range(roles):
        outs[j][...] = y[j * rows : (j + 1) * rows, :]


def project(where, xs, w, down, mask, roles):
    count = len(xs)
    heads, tokens, width = xs[0].shape
    columns = w.shape[1]
    rows = count * tokens // roles
    tile = min(256, columns)
    return pl.pallas_call(
        functools.partial(project_kernel, count, roles),
        out_shape=[jax.ShapeDtypeStruct((rows, columns), jnp.bfloat16)] * roles
        + [jax.ShapeDtypeStruct((roles, rows, down.shape[0]), jnp.bfloat16)],
        grid=(columns // tile,),
        in_specs=[SMEM]
        + [pl.BlockSpec(xs[0].shape, lambda i: (0, 0, 0))] * count
        + [
            pl.BlockSpec((w.shape[0], tile), lambda i: (0, i)),
            pl.BlockSpec(down.shape, lambda i: (0, 0)),
            pl.BlockSpec(mask.shape, lambda i: (0, 0, 0)),
        ],
        out_specs=[pl.BlockSpec((rows, tile), lambda i: (0, i))] * roles
        + [pl.BlockSpec((roles, rows, down.shape[0]), lambda i: (0, 0, 0))],
        scratch_shapes=[pltpu.VMEM((count * tokens, heads * width), jnp.bfloat16)],
        compiler_params=params(),
        cost_estimate=pl.CostEstimate(
            flops=2 * count * tokens * heads * width * columns,
            bytes_accessed=w.size * 2 + count * tokens * (heads * width + columns) * 2,
            transcendentals=0,
        ),
        name="project",
    )(where, *xs, w, down, mask)


def add_kernel(a_ref, b_ref, o_ref):
    o_ref[...] = (a_ref[...].astype(jnp.float32) + b_ref[...].astype(jnp.float32)).astype(jnp.bfloat16)


def add(a, b):
    return pl.pallas_call(
        add_kernel,
        out_shape=jax.ShapeDtypeStruct(a.shape, a.dtype),
        in_specs=[VMEM, VMEM],
        out_specs=VMEM,
        compiler_params=params(),
        name="add",
    )(a, b)


def finish_kernel(counts, cores, low_ref, up_ref, *refs):
    terms, o_ref = refs[:-1], refs[-1]
    low = jnp.concatenate([low_ref[a] for a in range(low_ref.shape[0])], axis=1)
    extra = dot(low, up_ref[...])
    rows = terms[0].shape[0]
    tokens = rows // cores
    first = 0
    for h, count in enumerate(counts):
        total = extra[h * rows : (h + 1) * rows, :]
        for term in terms[first : first + count]:
            total = total + term[...].astype(jnp.float32)
        first = first + count
        for c in range(cores):
            at = (c * len(counts) + h) * tokens
            o_ref[at : at + tokens, :] = total[c * tokens : (c + 1) * tokens].astype(jnp.bfloat16)


def finish(terms, cores, low, up):
    flat = [t for half in terms for t in half]
    rows, columns = flat[0].shape
    tile = min(256, columns)
    return pl.pallas_call(
        functools.partial(finish_kernel, tuple(len(half) for half in terms), cores),
        out_shape=jax.ShapeDtypeStruct((len(terms) * rows, columns), jnp.bfloat16),
        grid=(columns // tile,),
        in_specs=[
            pl.BlockSpec(low.shape, lambda i: (0, 0, 0)),
            pl.BlockSpec((up.shape[0], tile), lambda i: (0, i)),
        ]
        + [pl.BlockSpec((rows, tile), lambda i: (0, i))] * len(flat),
        out_specs=pl.BlockSpec((len(terms) * rows, tile), lambda i: (0, i)),
        compiler_params=params(),
        name="finish",
    )(low, up, *flat)


def exchange(x, axis, distance):
    count = lax.axis_size(axis)
    return lax.ppermute(x, axis, [(i, i ^ distance) for i in range(count)])


def gather(x, my_req):
    count = lax.axis_size("req")
    if count != 8:
        whole = lax.all_gather(x, "req", axis=0)
        return [whole[b] for b in range(count)], [jnp.int32(b) for b in range(count)]
    far = [x] + [exchange(x, "req", d) for d in (2, 4, 6)]
    near = [exchange(block, "req", 1) for block in far]
    return far + near, [my_req ^ d for d in (0, 2, 4, 6, 1, 3, 5, 7)]


def scatter(blocks):
    if len(blocks) != 4:
        return [lax.psum_scatter(jnp.stack(blocks), "tp", scatter_dimension=0, tiled=False)]
    own, one, two, three = blocks
    onward = lax.ppermute(three, "tp", [(0, 1), (3, 2)])
    middle = lax.ppermute(three, "tp", [(1, 2), (2, 1)])
    return [own, exchange(one, "tp", 1), middle, exchange(add(two, onward), "tp", 2)]


def on_device(
    queries,
    incoming_key_value,
    key_value_pages,
    page_request_home,
    lengths,
    request_adapter_index,
    adapter_storage_slot,
    adapter_down_factor,
    adapter_up_factor,
    output_projection_weight,
):
    req_count = lax.axis_size("req")
    tp_count = lax.axis_size("tp")
    my_req = lax.axis_index("req").astype(jnp.int32)
    my_lane = lax.axis_index("tp").astype(jnp.int32)
    me = my_req.reshape(1)
    requests = lengths.shape[0]
    half = requests // HALVES
    columns = key_value_pages.shape[-1]
    heads = columns // HEAD_WIDTH * GROUP
    own_slots, rank, model = adapter_up_factor.shape
    cores = req_count // tp_count

    outbox = pack(me, page_request_home, request_adapter_index, key_value_pages, req_count)
    inbox = lax.all_to_all(outbox, "req", split_axis=0, concat_axis=0, tiled=True)

    table, order = build_table(me, page_request_home, lengths)
    q = queries.reshape(requests, STEP_COUNT, heads, HEAD_WIDTH).transpose(0, 2, 1, 3)
    q = q.reshape(requests * heads * STEP_COUNT, HEAD_WIDTH)
    new = incoming_key_value.transpose(1, 0, 2).reshape(-1, columns)
    down = adapter_down_factor.transpose(0, 2, 1).reshape(own_slots * rank, -1)
    up = split_columns(adapter_up_factor.reshape(own_slots * rank, model), req_count)
    up = lax.all_to_all(up, "req", split_axis=0, concat_axis=0, tiled=True)
    up = up.reshape(req_count * own_slots * rank, -1)

    slot_count = adapter_storage_slot.shape[0]
    ids = inbox[:, BLOCK - 1, 0, :requests].astype(jnp.int32)
    match = ids[:, :, None] == jnp.arange(slot_count, dtype=jnp.int32)
    slot = jnp.sum(jnp.where(match, adapter_storage_slot, 0), axis=2)
    mine = my_req * own_slots + jnp.arange(own_slots * rank, dtype=jnp.int32) // rank

    special = tp_count == 4
    roles = [my_lane ^ j if special else jnp.int32(j) for j in range(tp_count)]
    terms, lows = [], []
    for h in range(HALVES):
        mixed = attend(h, order, lengths, table, q, new, key_value_pages, inbox)
        blocks, origins = gather(mixed, my_req)
        where = []
        for origin in origins:
            s = origin // cores
            where.append((s ^ my_lane if special else s) * cores + origin % cores)
        where = jnp.stack(where + roles)
        token_slot = jnp.repeat(slot[:, h * half : (h + 1) * half], STEP_COUNT, axis=1)
        mask = (token_slot.reshape(tp_count, -1)[:, :, None] == mine).astype(jnp.bfloat16)
        *parts, low = project(where, blocks, output_projection_weight, down, mask, tp_count)
        lows.append(low)
        terms.append(scatter(parts))

    low = jnp.concatenate(lows, axis=1)
    low = lax.all_to_all(low, "tp", split_axis=0, concat_axis=0, tiled=True)
    low = jnp.sum(low.astype(jnp.float32), axis=0).astype(jnp.bfloat16)
    low = lax.all_gather(low, "req", axis=0)
    return finish(terms, cores, low, up)


def solution(mesh):
    return jax.shard_map(
        on_device,
        mesh=mesh,
        in_specs=(
            P("req", "tp"),
            P(None, "req", "tp"),
            P("req", None, None, "tp"),
            P("req"),
            P("req"),
            P("req"),
            P(),
            P("req", "tp", None),
            P("req", None, None),
            P("tp", "req"),
        ),
        out_specs=P("tp", "req"),
        check_vma=False,
    )
```

time: 209 us -> 160 us (0.77)
  waiting for transfers between devices: 62.7 us -> 35 us
  starting transfers between devices: 11.4 us -> 33.6 us
  blocking collectives: 32.9 us -> 11.3 us
  between operations: 13.2 us -> 0.38 us
  Pallas kernels: 80.4 us -> 67.6 us
  local copies, waits for them, and re-layouts: 4.29 us -> 6.85 us
    all_gather x1 -> x0, waiting for transfers between devices: 39.9 us -> none  [on_device(): everyone = lax.all_gather(mixed, 'req', axis=0)]
    psum x1 -> x0, blocking collectives: 32.9 us -> none  [on_device(): low_rows = lax.psum(low_rows, 'req').astype(jnp.bfloat16)]
    ppermute x0 -> x22, waiting for transfers between devices: none -> 25.7 us  [the longest x18 20.1 us: exchange(): return lax.ppermute(x, axis, [(i, i ^ distance) for i in range(count)])]
    reduce_scatter x2 -> x0, waiting for transfers between devices: 22.1 us -> none  [the longest x1 11.7 us: on_device(): low_rows = lax.psum_scatter(kept, 'tp', scatter_dimension=0, tiled=True)]
    ppermute x0 -> x22, starting transfers between devices: none -> 19.9 us  [the longest x18 15.2 us: exchange(): return lax.ppermute(x, axis, [(i, i ^ distance) for i in range(count)])]
    all_gather x0 -> x1, blocking collectives: none -> 11.3 us  [on_device(): low = lax.all_gather(low, 'req', axis=0)]
    pallas_call x1, Pallas kernels: 11.8 us -> 1.57 us  [build_table(): pl.pallas_call(functools.partial(table_kernel, per_dev, requests), out_sh...]
    pallas_call x1, Pallas kernels: 11 us -> 3.73 us  [pack(): pl.pallas_call(functools.partial(pack_kernel, req_count, per_dev), out_sh...]
  transfers between devices with their start and end apart: 5 -> 25, of which waited for: 3 -> 10; matrix products, arithmetic and copies ran while one was open for 2% -> 3% of each run, Pallas kernels for 8% -> 22%
where the time goes in v2:
time: 160 us; the launch traced here: 158 us
  Pallas kernels  67.6 us (42%)
  waiting for transfers between devices  35 us (22%)
  starting transfers between devices  33.6 us (21%)
  blocking collectives  11.3 us (7%)
  local copies, waits for them, and re-layouts  6.85 us (4%)
  other arithmetic  3.36 us (2%)
    pallas_call x2, Pallas kernels, attend(): pl.pallas_call(functools.partial(attend_kernel, req_count, per_dev, part...  33.5 us
    ppermute x18, waiting for transfers between devices, exchange(): return lax.ppermute(x, axis, [(i, i ^ distance) for i in range(count)])  20.1 us
    ppermute x18, starting transfers between devices, exchange(): return lax.ppermute(x, axis, [(i, i ^ distance) for i in range(count)])  15.2 us
    pallas_call x2, Pallas kernels, project(): pl.pallas_call(functools.partial(project_kernel, count, roles), out_shape...  14.8 us
    all_gather x1, blocking collectives, on_device(): low = lax.all_gather(low, 'req', axis=0)  11.3 us
    pallas_call x1, Pallas kernels, split_columns(): pl.pallas_call(split_kernel, out_shape=jax.ShapeDtypeStruct((parts, rows,...  5.63 us
    all_to_all x1, waiting for transfers between devices, on_device(): lax.all_to_all(outbox, 'req', split_axis=0, concat_axis=0, tiled=True)  5.59 us
    ppermute x2, waiting for transfers between devices, scatter(): onward = lax.ppermute(three, 'tp', [(0, 1), (3, 2)])  5.56 us
  transfers between devices with their start and end apart: 25, of which 10 were waited for; matrix products, arithmetic and copies ran while one was open for 3% of the time, Pallas kernels for 22%

profile of v2, /device:TPU:0, one launch (start us, length us, event | category | flops | bytes accessed | tf_op | source)
XLA Modules:
  0.0 158.1 jit_solution(7707586230337037384)
XLA Ops:
  0.0 3.7 %pack_outbox.1 = bf16[8,65,2,256]{3,2,1,0:T(2,128)(2,1)} custom-call(s32[1]{0:T(128)} %bitcast.12.me_ref, s32[1,512]{1,0:T(1,128)} %bitcast.40, s32[1,32]{1,0:T(1,128)} %bitcast.43, bf16[512,32,2,256]{3,2,1,0:T(2,128)(2,1)} %pages.5), custom_call_target="tpu_custom_call" | custom-call | tf_op jit(solution)/shard_map/pack_outbox/pallas_call | solution.py:109
  3.8 5.2 %all-to-all-start = ((bf16[8,65,2,256]{3,2,1,0:T(2,128)(2,1)}), bf16[8,65,2,256]{3,2,1,0:T(2,128)(2,1)S(1)}, u32[]{:S(2)}, u32[]{:S(2)}) async-start(bf16[8,65,2,256]{3,2,1,0:T(2,128)(2,1)} %pack_outbox.1), calls=%async_computation | async-start | bytes 1064960 | tf_op jit(solution)/shard_map/all_to_all | solution.py:533
  13.2 5.6 %all-to-all-done.inbox = bf16[8,65,2,256]{3,2,1,0:T(2,128)(2,1)S(1)} async-done(((bf16[8,65,2,256]{3,2,1,0:T(2,128)(2,1)}), bf16[8,65,2,256]{3,2,1,0:T(2,128)(2,1)S(1)}, u32[]{:S(2)}, u32[]{:S(2)}) %all-to-all-start) | async-done | bytes 532512 | tf_op jit(solution)/shard_map/all_to_all | solution.py:533
  19.6 16.8 %attend.2.refs_0_ = bf16[16,64,128]{2,1,0:T(8,128)(2,1)} custom-call(s32[2,128]{1,0:T(2,128)} %get-tuple-element.17.order_ref, s32[32]{0:T(128)} %lengths_ref.3, s32[4,128]{1,0:T(4,128)} %get-tuple-element.18.table_in, bf16[2048,128]{1,0:T(8,128)(2,1)} %bitcast.32, bf16[256,256]{1,0:T(8,128)(2,1)} %reshape.61.new_ref, bf16[512,32,2,256]{3,2,1,0:T(2,128)(2,1)} %pages.5, ...), custom_call_target="tpu_custom_call" | custom-call | flops 1073741824 | bytes 8388608 | tf_op jit(solution)/shard_map/attend/pallas_call | solution.py:337
  38.2 1.9 %collective-permute-start = (bf16[16,64,128]{2,1,0:T(8,128)(2,1)}, bf16[16,64,128]{2,1,0:T(8,128)(2,1)S(1)}, u32[]{:S(2)}, u32[]{:S(2)}) collective-permute-start(bf16[16,64,128]{2,1,0:T(8,128)(2,1)} %attend.2.refs_0_), channel_id=1, source_target_pairs={{0,8},{4,12},{8,0},{12,4},{16,24},{20,28},{24,16},{28,20},{1,9},{5... | collective-permute-start | bytes 786440 | tf_op jit(solution)/shard_map/ppermute | solution.py:486
  40.1 16.7 %attend.3.refs_0_ = bf16[16,64,128]{2,1,0:T(8,128)(2,1)} custom-call(s32[2,128]{1,0:T(2,128)} %get-tuple-element.17.order_ref, s32[32]{0:T(128)} %lengths_ref.3, s32[4,128]{1,0:T(4,128)} %get-tuple-element.18.table_in, bf16[2048,128]{1,0:T(8,128)(2,1)} %bitcast.33, bf16[256,256]{1,0:T(8,128)(2,1)} %reshape.61.new_ref, bf16[512,32,2,256]{3,2,1,0:T(2,128)(2,1)} %pages.5, ...), custom_call_target="tpu_custom_call" | custom-call | flops 1073741824 | bytes 8388608 | tf_op jit(solution)/shard_map/attend/pallas_call | solution.py:337
  58.2 1.9 %collective-permute-start.8 = (bf16[16,64,128]{2,1,0:T(8,128)(2,1)}, bf16[16,64,128]{2,1,0:T(8,128)(2,1)S(1)}, u32[]{:S(2)}, u32[]{:S(2)}) collective-permute-start(bf16[16,64,128]{2,1,0:T(8,128)(2,1)} %attend.3.refs_0_), channel_id=1, source_target_pairs={{0,16},{4,20},{8,24},{12,28},{16,0},{20,4},{24,8},{28,12},{1,17},{... | collective-permute-start | bytes 786440 | tf_op jit(solution)/shard_map/ppermute | solution.py:486
  61.8 5.5 %collective-permute-done.9.refs_3_ = bf16[16,64,128]{2,1,0:T(8,128)(2,1)S(1)} collective-permute-done((bf16[16,64,128]{2,1,0:T(8,128)(2,1)}, bf16[16,64,128]{2,1,0:T(8,128)(2,1)S(1)}, u32[]{:S(2)}, u32[]{:S(2)}) %collective-permute-start.9) | collective-permute-done | bytes 262176 | tf_op jit(solution)/shard_map/ppermute | solution.py:486
  67.7 3.0 %collective-permute-done.8.refs_2_ = bf16[16,64,128]{2,1,0:T(8,128)(2,1)S(1)} collective-permute-done((bf16[16,64,128]{2,1,0:T(8,128)(2,1)}, bf16[16,64,128]{2,1,0:T(8,128)(2,1)S(1)}, u32[]{:S(2)}, u32[]{:S(2)}) %collective-permute-start.8) | collective-permute-done | bytes 262176 | tf_op jit(solution)/shard_map/ppermute | solution.py:486
  73.5 7.4 %project.2 = (bf16[128,1024]{1,0:T(8,128)(2,1)}, bf16[128,1024]{1,0:T(8,128)(2,1)}, bf16[128,1024]{1,0:T(8,128)(2,1)}, bf16[128,1024]{1,0:T(8,128)(2,1)}, bf16[4,128,128]{2,1,0:T(8,128)(2,1)}) custom-call(s32[12]{0:T(128)} %stack.64.where_ref, bf16[16,64,128]{2,1,0:T(8,128)(2,1)} %attend.2.refs_0_, bf16[16,64,128]{2,1,0:T(8,128)(2,1)} %copy-done.18, ...), custom_call_target="tpu_custom_call" | custom-call | flops 2147483648 | bytes 7340032 | tf_op jit(solution)/shard_map/project/pallas_call | solution.py:408
  81.9 7.4 %project.3 = (bf16[128,1024]{1,0:T(8,128)(2,1)}, bf16[128,1024]{1,0:T(8,128)(2,1)}, bf16[128,1024]{1,0:T(8,128)(2,1)}, bf16[128,1024]{1,0:T(8,128)(2,1)}, bf16[4,128,128]{2,1,0:T(8,128)(2,1)}) custom-call(s32[12]{0:T(128)} %stack.64.where_ref, bf16[16,64,128]{2,1,0:T(8,128)(2,1)} %attend.3.refs_0_, bf16[16,64,128]{2,1,0:T(8,128)(2,1)} %copy-done.17, ...), custom_call_target="tpu_custom_call" | custom-call | flops 2147483648 | bytes 7340032 | tf_op jit(solution)/shard_map/project/pallas_call | solution.py:408
  91.0 4.9 %all-to-all-start.1 = ((bf16[4,256,128]{2,1,0:T(8,128)(2,1)}), bf16[4,256,128]{2,1,0:T(8,128)(2,1)S(1)}, u32[]{:S(2)}, u32[]{:S(2)}) async-start(bf16[4,256,128]{2,1,0:T(8,128)(2,1)} %pad_maximum_fusion), calls=%async_computation.1 | async-start | bytes 524288 | tf_op jit(solution)/shard_map/all_to_all | solution.py:568
  95.9 5.6 %split_columns.1 = bf16[8,128,1024]{2,1,0:T(8,128)(2,1)} custom-call(bf16[128,8192]{1,0:T(8,128)(2,1)} %bitcast.35), custom_call_target="tpu_custom_call" | custom-call | tf_op jit(solution)/shard_map/split_columns/pallas_call | solution.py:369
  101.5 3.8 %all-to-all-done.1 = bf16[4,256,128]{2,1,0:T(8,128)(2,1)S(1)} async-done(((bf16[4,256,128]{2,1,0:T(8,128)(2,1)}), bf16[4,256,128]{2,1,0:T(8,128)(2,1)S(1)}, u32[]{:S(2)}, u32[]{:S(2)}) %all-to-all-start.1) | async-done | bytes 262176 | tf_op jit(solution)/shard_map/all_to_all | solution.py:568
  105.3 3.6 %all-to-all-start.2 = ((bf16[8,128,1024]{2,1,0:T(8,128)(2,1)}), bf16[8,128,1024]{2,1,0:T(8,128)(2,1)S(1)}, u32[]{:S(2)}, u32[]{:S(2)}) async-start(bf16[8,128,1024]{2,1,0:T(8,128)(2,1)} %split_columns.1), calls=%async_computation.2 | async-start | bytes 4194304 | tf_op jit(solution)/shard_map/all_to_all | solution.py:541
  108.9 2.0 %collective-permute-start.16 = (bf16[128,1024]{1,0:T(8,128)(2,1)}, bf16[128,1024]{1,0:T(8,128)(2,1)S(1)}, u32[]{:S(2)}, u32[]{:S(2)}) collective-permute-start(bf16[128,1024]{1,0:T(8,128)(2,1)} %get-tuple-element.23), channel_id=1, source_target_pairs={{0,1},{3,2},{4,5},{7,6},{8,9},{11,10},{12,13},{15,14},{16,17},{19,... | collective-permute-start | bytes 786440 | tf_op jit(solution)/shard_map/ppermute | solution.py:503
  113.7 4.2 %collective-permute-done.16.b_ref = bf16[128,1024]{1,0:T(8,128)(2,1)S(1)} collective-permute-done((bf16[128,1024]{1,0:T(8,128)(2,1)}, bf16[128,1024]{1,0:T(8,128)(2,1)S(1)}, u32[]{:S(2)}, u32[]{:S(2)}) %collective-permute-start.16) | collective-permute-done | bytes 262176 | tf_op jit(solution)/shard_map/ppermute | solution.py:503
  117.8 2.4 %collective-permute-start.18 = (bf16[128,1024]{1,0:T(8,128)(2,1)}, bf16[128,1024]{1,0:T(8,128)(2,1)S(1)}, u32[]{:S(2)}, u32[]{:S(2)}) collective-permute-start(bf16[128,1024]{1,0:T(8,128)(2,1)} %get-tuple-element.26), channel_id=1, source_target_pairs={{0,1},{1,0},{2,3},{3,2},{4,5},{5,4},{6,7},{7,6},{8,9},{9,8},{10,11... | collective-permute-start | bytes 786440 | tf_op jit(solution)/shard_map/ppermute | solution.py:486
  123.5 2.2 %collective-permute-start.17 = (bf16[128,1024]{1,0:T(8,128)(2,1)}, bf16[128,1024]{1,0:T(8,128)(2,1)}, u32[]{:S(2)}, u32[]{:S(2)}) collective-permute-start(bf16[128,1024]{1,0:T(8,128)(2,1)} %add.110), channel_id=1, source_target_pairs={{0,2},{1,3},{2,0},{3,1},{4,6},{5,7},{6,4},{7,5},{8,10},{9,11},{10,... | collective-permute-start | bytes 786440 | tf_op jit(solution)/shard_map/ppermute | solution.py:486
  129.1 2.2 %collective-permute-start.21 = (bf16[128,1024]{1,0:T(8,128)(2,1)}, bf16[128,1024]{1,0:T(8,128)(2,1)}, u32[]{:S(2)}, u32[]{:S(2)}) collective-permute-start(bf16[128,1024]{1,0:T(8,128)(2,1)} %add.111), channel_id=1, source_target_pairs={{0,2},{1,3},{2,0},{3,1},{4,6},{5,7},{6,4},{7,5},{8,10},{9,11},{10,... | collective-permute-start | bytes 786440 | tf_op jit(solution)/shard_map/ppermute | solution.py:486
  131.3 11.3 %all-gather = bf16[2048,128]{1,0:T(8,128)(2,1)} all-gather(bf16[256,128]{1,0:T(8,128)(2,1)S(1)} %reduce_sum.22), channel_id=2, replica_groups=mesh['req'=8,'tp'=4] {'req'}, dimensions={0}, use_global_device_ids=true | all-gather | bytes 589824 | tf_op jit(solution)/shard_map/all_gather | solution.py:570
  142.6 5.0 %collective-permute-done.17.refs_3_ = bf16[128,1024]{1,0:T(8,128)(2,1)} collective-permute-done((bf16[128,1024]{1,0:T(8,128)(2,1)}, bf16[128,1024]{1,0:T(8,128)(2,1)}, u32[]{:S(2)}, u32[]{:S(2)}) %collective-permute-start.17) | collective-permute-done | bytes 262176 | tf_op jit(solution)/shard_map/ppermute | solution.py:486
  147.6 4.4 %collective-permute-done.21.refs_7_ = bf16[128,1024]{1,0:T(8,128)(2,1)} collective-permute-done((bf16[128,1024]{1,0:T(8,128)(2,1)}, bf16[128,1024]{1,0:T(8,128)(2,1)}, u32[]{:S(2)}, u32[]{:S(2)}) %collective-permute-start.21) | collective-permute-done | bytes 262176 | tf_op jit(solution)/shard_map/ppermute | solution.py:486
  153.4 4.7 %finish.1 = bf16[256,1024]{1,0:T(8,128)(2,1)} custom-call(bf16[8,256,128]{2,1,0:T(8,128)(2,1)} %bitcast.34, bf16[1024,1024]{1,0:T(8,128)(2,1)} %bitcast.31, bf16[128,1024]{1,0:T(8,128)(2,1)} %get-tuple-element.21.refs_0_, bf16[128,1024]{1,0:T(8,128)(2,1)} %copy-done.3, bf16[128,1024]{1,0:T(8,128)(2,1)} %copy-done.4, ...), custom_call_target="tpu_custom_call" | custom-call | tf_op jit(solution)/shard_map/finish/pallas_call | solution.py:469
  (105 shorter events, 26.3 us)
Async XLA Ops:
  3.8 15.1 %all-to-all-start = ((bf16[8,65,2,256]{3,2,1,0:T(2,128)(2,1)}), bf16[8,65,2,256]{3,2,1,0:T(2,128)(2,1)S(1)}, u32[]{:S(2)}, u32[]{:S(2)}) async-start(bf16[8,65,2,256]{3,2,1,0:T(2,128)(2,1)} %pack_outbox.1), calls=%async_computation | async-start | bytes 1064960 | tf_op jit(solution)/shard_map/all_to_all | solution.py:533
  36.4 21.7 %collective-permute-start.3 = (bf16[16,64,128]{2,1,0:T(8,128)(2,1)}, bf16[16,64,128]{2,1,0:T(8,128)(2,1)S(1)}, u32[]{:S(2)}, u32[]{:S(2)}) collective-permute-start(bf16[16,64,128]{2,1,0:T(8,128)(2,1)} %attend.2.refs_0_), channel_id=1, source_target_pairs={{0,4},{4,0},{8,12},{12,8},{16,20},{20,16},{24,28},{28,24},{1,5},{5... | collective-permute-start | bytes 786440 | tf_op jit(solution)/shard_map/ppermute | solution.py:486
  36.5 23.5 %collective-permute-start.2 = (bf16[16,64,128]{2,1,0:T(8,128)(2,1)}, bf16[16,64,128]{2,1,0:T(8,128)(2,1)S(1)}, u32[]{:S(2)}, u32[]{:S(2)}) collective-permute-start(bf16[16,64,128]{2,1,0:T(8,128)(2,1)} %attend.2.refs_0_), channel_id=1, source_target_pairs={{0,24},{4,28},{8,16},{12,20},{16,8},{20,12},{24,0},{28,4},{1,25},{... | collective-permute-start | bytes 786440 | tf_op jit(solution)/shard_map/ppermute | solution.py:486
  36.6 24.6 %collective-permute-start.1 = (bf16[16,64,128]{2,1,0:T(8,128)(2,1)}, bf16[16,64,128]{2,1,0:T(8,128)(2,1)S(1)}, u32[]{:S(2)}, u32[]{:S(2)}) collective-permute-start(bf16[16,64,128]{2,1,0:T(8,128)(2,1)} %attend.2.refs_0_), channel_id=1, source_target_pairs={{0,16},{4,20},{8,24},{12,28},{16,0},{20,4},{24,8},{28,12},{1,17},{... | collective-permute-start | bytes 786440 | tf_op jit(solution)/shard_map/ppermute | solution.py:486
  38.2 23.0 %collective-permute-start = (bf16[16,64,128]{2,1,0:T(8,128)(2,1)}, bf16[16,64,128]{2,1,0:T(8,128)(2,1)S(1)}, u32[]{:S(2)}, u32[]{:S(2)}) collective-permute-start(bf16[16,64,128]{2,1,0:T(8,128)(2,1)} %attend.2.refs_0_), channel_id=1, source_target_pairs={{0,8},{4,12},{8,0},{12,4},{16,24},{20,28},{24,16},{28,20},{1,9},{5... | collective-permute-start | bytes 786440 | tf_op jit(solution)/shard_map/ppermute | solution.py:486
  56.8 10.4 %collective-permute-start.9 = (bf16[16,64,128]{2,1,0:T(8,128)(2,1)}, bf16[16,64,128]{2,1,0:T(8,128)(2,1)S(1)}, u32[]{:S(2)}, u32[]{:S(2)}) collective-permute-start(bf16[16,64,128]{2,1,0:T(8,128)(2,1)} %attend.3.refs_0_), channel_id=1, source_target_pairs={{0,24},{4,28},{8,16},{12,20},{16,8},{20,12},{24,0},{28,4},{1,25},{... | collective-permute-start | bytes 786440 | tf_op jit(solution)/shard_map/ppermute | solution.py:486
  58.2 12.6 %collective-permute-start.8 = (bf16[16,64,128]{2,1,0:T(8,128)(2,1)}, bf16[16,64,128]{2,1,0:T(8,128)(2,1)S(1)}, u32[]{:S(2)}, u32[]{:S(2)}) collective-permute-start(bf16[16,64,128]{2,1,0:T(8,128)(2,1)} %attend.3.refs_0_), channel_id=1, source_target_pairs={{0,16},{4,20},{8,24},{12,28},{16,0},{20,4},{24,8},{28,12},{1,17},{... | collective-permute-start | bytes 786440 | tf_op jit(solution)/shard_map/ppermute | solution.py:486
  60.0 11.2 %collective-permute-start.7 = (bf16[16,64,128]{2,1,0:T(8,128)(2,1)}, bf16[16,64,128]{2,1,0:T(8,128)(2,1)S(1)}, u32[]{:S(2)}, u32[]{:S(2)}) collective-permute-start(bf16[16,64,128]{2,1,0:T(8,128)(2,1)} %attend.3.refs_0_), channel_id=1, source_target_pairs={{0,8},{4,12},{8,0},{12,4},{16,24},{20,28},{24,16},{28,20},{1,9},{5... | collective-permute-start | bytes 786440 | tf_op jit(solution)/shard_map/ppermute | solution.py:486
  61.1 10.2 %collective-permute-start.6 = (bf16[16,64,128]{2,1,0:T(8,128)(2,1)S(1)}, bf16[16,64,128]{2,1,0:T(8,128)(2,1)S(1)}, u32[]{:S(2)}, u32[]{:S(2)}) collective-permute-start(bf16[16,64,128]{2,1,0:T(8,128)(2,1)S(1)} %collective-permute-done.2.refs_3_), channel_id=1, source_target_pairs={{0,4},{4,0},{8,12},{12,8},{16,20},{20,16},{24,28},{28,24},{1,5},{5... | collective-permute-start | bytes 786440 | tf_op jit(solution)/shard_map/ppermute | solution.py:486
  61.2 10.6 %collective-permute-start.5 = (bf16[16,64,128]{2,1,0:T(8,128)(2,1)S(1)}, bf16[16,64,128]{2,1,0:T(8,128)(2,1)S(1)}, u32[]{:S(2)}, u32[]{:S(2)}) collective-permute-start(bf16[16,64,128]{2,1,0:T(8,128)(2,1)S(1)} %collective-permute-done.1.refs_2_), channel_id=1, source_target_pairs={{0,4},{4,0},{8,12},{12,8},{16,20},{20,16},{24,28},{28,24},{1,5},{5... | collective-permute-start | bytes 786440 | tf_op jit(solution)/shard_map/ppermute | solution.py:486
  70.7 10.2 %collective-permute-start.10 = (bf16[16,64,128]{2,1,0:T(8,128)(2,1)}, bf16[16,64,128]{2,1,0:T(8,128)(2,1)S(1)}, u32[]{:S(2)}, u32[]{:S(2)}) collective-permute-start(bf16[16,64,128]{2,1,0:T(8,128)(2,1)} %attend.3.refs_0_), channel_id=1, source_target_pairs={{0,4},{4,0},{8,12},{12,8},{16,20},{20,16},{24,28},{28,24},{1,5},{5... | collective-permute-start | bytes 786440 | tf_op jit(solution)/shard_map/ppermute | solution.py:486
  71.3 9.7 %collective-permute-start.13 = (bf16[16,64,128]{2,1,0:T(8,128)(2,1)S(1)}, bf16[16,64,128]{2,1,0:T(8,128)(2,1)S(1)}, u32[]{:S(2)}, u32[]{:S(2)}) collective-permute-start(bf16[16,64,128]{2,1,0:T(8,128)(2,1)S(1)} %collective-permute-done.9.refs_3_), channel_id=1, source_target_pairs={{0,4},{4,0},{8,12},{12,8},{16,20},{20,16},{24,28},{28,24},{1,5},{5... | collective-permute-start | bytes 786440 | tf_op jit(solution)/shard_map/ppermute | solution.py:486
  71.4 9.6 %collective-permute-start.12 = (bf16[16,64,128]{2,1,0:T(8,128)(2,1)S(1)}, bf16[16,64,128]{2,1,0:T(8,128)(2,1)S(1)}, u32[]{:S(2)}, u32[]{:S(2)}) collective-permute-start(bf16[16,64,128]{2,1,0:T(8,128)(2,1)S(1)} %collective-permute-done.8.refs_2_), channel_id=1, source_target_pairs={{0,4},{4,0},{8,12},{12,8},{16,20},{20,16},{24,28},{28,24},{1,5},{5... | collective-permute-start | bytes 786440 | tf_op jit(solution)/shard_map/ppermute | solution.py:486
  71.8 9.2 %collective-permute-start.11 = (bf16[16,64,128]{2,1,0:T(8,128)(2,1)S(1)}, bf16[16,64,128]{2,1,0:T(8,128)(2,1)S(1)}, u32[]{:S(2)}, u32[]{:S(2)}) collective-permute-start(bf16[16,64,128]{2,1,0:T(8,128)(2,1)S(1)} %collective-permute-done.7.refs_1_), channel_id=1, source_target_pairs={{0,4},{4,0},{8,12},{12,8},{16,20},{20,16},{24,28},{28,24},{1,5},{5... | collective-permute-start | bytes 786440 | tf_op jit(solution)/shard_map/ppermute | solution.py:486
  91.0 14.3 %all-to-all-start.1 = ((bf16[4,256,128]{2,1,0:T(8,128)(2,1)}), bf16[4,256,128]{2,1,0:T(8,128)(2,1)S(1)}, u32[]{:S(2)}, u32[]{:S(2)}) async-start(bf16[4,256,128]{2,1,0:T(8,128)(2,1)} %pad_maximum_fusion), calls=%async_computation.1 | async-start | bytes 524288 | tf_op jit(solution)/shard_map/all_to_all | solution.py:568
  105.3 46.8 %all-to-all-start.2 = ((bf16[8,128,1024]{2,1,0:T(8,128)(2,1)}), bf16[8,128,1024]{2,1,0:T(8,128)(2,1)S(1)}, u32[]{:S(2)}, u32[]{:S(2)}) async-start(bf16[8,128,1024]{2,1,0:T(8,128)(2,1)} %split_columns.1), calls=%async_computation.2 | async-start | bytes 4194304 | tf_op jit(solution)/shard_map/all_to_all | solution.py:541
  108.9 8.9 %collective-permute-start.16 = (bf16[128,1024]{1,0:T(8,128)(2,1)}, bf16[128,1024]{1,0:T(8,128)(2,1)S(1)}, u32[]{:S(2)}, u32[]{:S(2)}) collective-permute-start(bf16[128,1024]{1,0:T(8,128)(2,1)} %get-tuple-element.23), channel_id=1, source_target_pairs={{0,1},{3,2},{4,5},{7,6},{8,9},{11,10},{12,13},{15,14},{16,17},{19,... | collective-permute-start | bytes 786440 | tf_op jit(solution)/shard_map/ppermute | solution.py:503
  110.9 12.5 %collective-permute-start.20 = (bf16[128,1024]{1,0:T(8,128)(2,1)}, bf16[128,1024]{1,0:T(8,128)(2,1)S(1)}, u32[]{:S(2)}, u32[]{:S(2)}) collective-permute-start(bf16[128,1024]{1,0:T(8,128)(2,1)} %get-tuple-element.27), channel_id=1, source_target_pairs={{0,1},{3,2},{4,5},{7,6},{8,9},{11,10},{12,13},{15,14},{16,17},{19,... | collective-permute-start | bytes 786440 | tf_op jit(solution)/shard_map/ppermute | solution.py:503
  112.2 16.8 %collective-permute-start.14 = (bf16[128,1024]{1,0:T(8,128)(2,1)}, bf16[128,1024]{1,0:T(8,128)(2,1)S(1)}, u32[]{:S(2)}, u32[]{:S(2)}) collective-permute-start(bf16[128,1024]{1,0:T(8,128)(2,1)} %get-tuple-element.22), channel_id=1, source_target_pairs={{0,1},{1,0},{2,3},{3,2},{4,5},{5,4},{6,7},{7,6},{8,9},{9,8},{10,11... | collective-permute-start | bytes 786440 | tf_op jit(solution)/shard_map/ppermute | solution.py:486
  112.3 30.3 %collective-permute-start.15 = (bf16[128,1024]{1,0:T(8,128)(2,1)}, bf16[128,1024]{1,0:T(8,128)(2,1)S(1)}, u32[]{:S(2)}, u32[]{:S(2)}) collective-permute-start(bf16[128,1024]{1,0:T(8,128)(2,1)} %get-tuple-element.23), channel_id=1, source_target_pairs={{1,2},{2,1},{5,6},{6,5},{9,10},{10,9},{13,14},{14,13},{17,18},{18,... | collective-permute-start | bytes 786440 | tf_op jit(solution)/shard_map/ppermute | solution.py:504
  113.0 29.6 %collective-permute-start.19 = (bf16[128,1024]{1,0:T(8,128)(2,1)}, bf16[128,1024]{1,0:T(8,128)(2,1)S(1)}, u32[]{:S(2)}, u32[]{:S(2)}) collective-permute-start(bf16[128,1024]{1,0:T(8,128)(2,1)} %get-tuple-element.27), channel_id=1, source_target_pairs={{1,2},{2,1},{5,6},{6,5},{9,10},{10,9},{13,14},{14,13},{17,18},{18,... | collective-permute-start | bytes 786440 | tf_op jit(solution)/shard_map/ppermute | solution.py:504
  117.8 24.8 %collective-permute-start.18 = (bf16[128,1024]{1,0:T(8,128)(2,1)}, bf16[128,1024]{1,0:T(8,128)(2,1)S(1)}, u32[]{:S(2)}, u32[]{:S(2)}) collective-permute-start(bf16[128,1024]{1,0:T(8,128)(2,1)} %get-tuple-element.26), channel_id=1, source_target_pairs={{0,1},{1,0},{2,3},{3,2},{4,5},{5,4},{6,7},{7,6},{8,9},{9,8},{10,11... | collective-permute-start | bytes 786440 | tf_op jit(solution)/shard_map/ppermute | solution.py:486
  123.5 24.2 %collective-permute-start.17 = (bf16[128,1024]{1,0:T(8,128)(2,1)}, bf16[128,1024]{1,0:T(8,128)(2,1)}, u32[]{:S(2)}, u32[]{:S(2)}) collective-permute-start(bf16[128,1024]{1,0:T(8,128)(2,1)} %add.110), channel_id=1, source_target_pairs={{0,2},{1,3},{2,0},{3,1},{4,6},{5,7},{6,4},{7,5},{8,10},{9,11},{10,... | collective-permute-start | bytes 786440 | tf_op jit(solution)/shard_map/ppermute | solution.py:486
  129.1 23.0 %collective-permute-start.21 = (bf16[128,1024]{1,0:T(8,128)(2,1)}, bf16[128,1024]{1,0:T(8,128)(2,1)}, u32[]{:S(2)}, u32[]{:S(2)}) collective-permute-start(bf16[128,1024]{1,0:T(8,128)(2,1)} %add.111), channel_id=1, source_target_pairs={{0,2},{1,3},{2,0},{3,1},{4,6},{5,7},{6,4},{7,5},{8,10},{9,11},{10,... | collective-permute-start | bytes 786440 | tf_op jit(solution)/shard_map/ppermute | solution.py:486
  (27 other events, 202.4 us)

commit v3 on v2

--- a/solution.py
+++ b/solution.py
@@ -21,10 +21,7 @@
 DIGIT = 16
 CHUNK_PAGES = 4
 CHUNKS = MAXP // CHUNK_PAGES
-PAGE_ROWS = PAGE_LENGTH * 2
-CHUNK_ROWS = CHUNK_PAGES * PAGE_ROWS
-NEW_ROWS = STEP_COUNT * 2
-NEW_GROUP = 128 // NEW_ROWS
+CHUNK_POSITIONS = CHUNK_PAGES * PAGE_LENGTH
 UNROLL = 2
 SLOTS = 6
 HALVES = 2
@@ -143,7 +140,7 @@
     len_v[...] = jnp.zeros_like(len_v)
     len_v[:, 0:requests] = lengths_ref[...].astype(jnp.float32)
     along = jnp.broadcast_to(len_v[...], (128, 128))
-    along = ((along.astype(jnp.int32) + (CHUNK_ROWS // 2 - 1)) >> 7).astype(jnp.float32)
+    along = ((along.astype(jnp.int32) + (CHUNK_POSITIONS - 1)) >> 7).astype(jnp.float32)
     down = jnp.transpose(along)
     same = (lane // half) == (row // half)
     before = same & ((along > down) | ((along == down) & (lane < row)))
@@ -195,14 +192,17 @@
     sem,
     sems,
 ):
-    columns = pages.shape[-1]
-    heads_kv = columns // HEAD_WIDTH
+    heads_kv = pages.shape[2]
+    page_size = PAGE_LENGTH * heads_kv * 2
+    chunk_size = CHUNK_PAGES * page_size
+    new_rows = STEP_COUNT * heads_kv * 2
+    new_group = 128 // new_rows
     half = STEP_COUNT * GROUP
     rows = heads_kv * half
     heads = heads_kv * GROUP
     scale = math.log2(math.e) / math.sqrt(HEAD_WIDTH)
-    page_rows = pages.reshape(per_dev, PAGE_ROWS, columns)
-    inbox_rows = inbox.reshape(req_count, BLOCK * 2, columns)
+    page_rows = pages.reshape(per_dev, page_size, HEAD_WIDTH)
+    inbox_rows = inbox.reshape(req_count, BLOCK * heads_kv * 2, HEAD_WIDTH)
 
     tab = pltpu.make_async_copy(table_in, table, sem)
     tab.start()
@@ -213,7 +213,7 @@
     row = lax.broadcasted_iota(jnp.int32, (2, 128), 0)
     weight = jnp.where(row == 0, float(DIGIT), 1.0)
     for d in range(req_count):
-        digits = labels_v[d, 0, :, 0:128].astype(jnp.float32) * weight
+        digits = labels_v[d, 0, 0, :, :].astype(jnp.float32) * weight
         labels_w[d : d + 1, :] = jnp.sum(digits, axis=0, keepdims=True).astype(jnp.int32)
     back = pltpu.make_async_copy(labels_w, labels_s, sem)
     back.start()
@@ -242,8 +242,8 @@
                 most = functools.reduce(jnp.maximum, sources)
 
                 def target(j):
-                    start = pl.multiple_of(c * CHUNK_ROWS + j * PAGE_ROWS, PAGE_ROWS)
-                    return buf.at[place, u, pl.ds(start, PAGE_ROWS)]
+                    start = pl.multiple_of(c * chunk_size + j * page_size, page_size)
+                    return buf.at[place, u, pl.ds(start, page_size)]
 
                 @pl.when(most < per_dev)
                 def _():
@@ -264,9 +264,9 @@
                             e = source - per_dev
                             d = lax.shift_right_logical(e, 1)
                             k = e - d * CAP
-                            start = pl.multiple_of(k * PAGE_ROWS, PAGE_ROWS)
+                            start = pl.multiple_of(k * page_size, page_size)
                             pltpu.make_async_copy(
-                                inbox_rows.at[d, pl.ds(start, PAGE_ROWS)], target(j), sems.at[place, u]
+                                inbox_rows.at[d, pl.ds(start, page_size)], target(j), sems.at[place, u]
                             ).start()
 
     for s in range(min(SLOTS - 1, steps)):
@@ -274,40 +274,41 @@
 
     def compute(step, n):
         place = lax.rem(step, SLOTS)
-        width = n * CHUNK_ROWS
+        width = n * chunk_size
         for u in range(UNROLL):
             whole = buf.at[place, u, pl.ds(0, width)]
             pltpu.make_async_copy(whole, whole, sems.at[place, u]).wait()
         column = lax.broadcasted_iota(jnp.int32, (1, width), 1)
-        column = jnp.where((column & 1) == 0, column, 2 * width * CHUNKS)
-        new_column = lax.broadcasted_iota(jnp.int32, (rows, 128), 1)
-        new_row = lax.broadcasted_iota(jnp.int32, (rows, 128), 0)
-        new_ok = ((new_column & 1) == 0) & (((new_column & (NEW_ROWS - 1)) >> 1) <= (new_row & (STEP_COUNT - 1)))
+        new_column = lax.broadcasted_iota(jnp.int32, (half, 128), 1)
+        new_row = lax.broadcasted_iota(jnp.int32, (half, 128), 0)
+        new_step = (new_column & (new_rows - 1)) // (2 * heads_kv)
+        new_key = new_column & (2 * heads_kv - 1)
+        visible = new_step <= (new_row & (STEP_COUNT - 1))
         for u in range(UNROLL):
             r = order_ref[0, base + step * UNROLL + u]
             length = lengths_ref[r]
             q = q_ref[pl.ds(pl.multiple_of(r * rows, rows), rows), :]
-            if heads_kv == 2:
-                zero = jnp.zeros((half, HEAD_WIDTH), q.dtype)
-                q = jnp.concatenate(
-                    [jnp.concatenate([q[:half], zero], axis=1), jnp.concatenate([zero, q[half:]], axis=1)], axis=0
-                )
             kv = buf[place, u, 0:width, :]
-            group = r // NEW_GROUP
+            group = r // new_group
             new = new_ref[pl.ds(pl.multiple_of(group * 128, 128), 128), :]
-            bias = jnp.where(column < 2 * length, 0.0, -jnp.inf)
-            s = dot(q, kv, ((1,), (1,))) * scale + bias
-            mine = (new_column >> 3) == (r - group * NEW_GROUP)
-            sn = jnp.where(new_ok & mine, dot(q, new, ((1,), (1,))) * scale, -jnp.inf)
-            top = jnp.maximum(jnp.max(s, axis=1, keepdims=True), jnp.max(sn, axis=1, keepdims=True))
-            w = jnp.exp2(s - top)
-            wn = jnp.exp2(sn - top)
-            inverse = 1.0 / (jnp.sum(w, axis=1, keepdims=True) + jnp.sum(wn, axis=1, keepdims=True))
-            p = pltpu.roll(w * inverse, 1, 1).astype(jnp.bfloat16)
-            pn = pltpu.roll(wn * inverse, 1, 1).astype(jnp.bfloat16)
-            o = dot(p, kv) + dot(pn, new)
-            if heads_kv == 2:
-                o = jnp.concatenate([o[:half, :HEAD_WIDTH], o[half:, HEAD_WIDTH:]], axis=0)
+            seen = visible & (new_column // new_rows == r - group * new_group)
+            cached = column < 2 * heads_kv * length
+            whole_s = dot(q, kv, ((1,), (1,)))
+            whole_sn = dot(q, new, ((1,), (1,)))
+            ps, pns = [], []
+            for g in range(heads_kv):
+                key = (column & (2 * heads_kv - 1)) == 2 * g
+                bias = jnp.where(cached & key, 0.0, -jnp.inf)
+                s = whole_s[g * half : (g + 1) * half] * scale + bias
+                sn = whole_sn[g * half : (g + 1) * half] * scale
+                sn = jnp.where(seen & (new_key == 2 * g), sn, -jnp.inf)
+                top = jnp.maximum(jnp.max(s, axis=1, keepdims=True), jnp.max(sn, axis=1, keepdims=True))
+                w = jnp.exp2(s - top)
+                wn = jnp.exp2(sn - top)
+                inverse = 1.0 / (jnp.sum(w, axis=1, keepdims=True) + jnp.sum(wn, axis=1, keepdims=True))
+                ps.append(pltpu.roll(w * inverse, 1, 1).astype(jnp.bfloat16))
+                pns.append(pltpu.roll(wn * inverse, 1, 1).astype(jnp.bfloat16))
+            o = dot(jnp.concatenate(ps, axis=0), kv) + dot(jnp.concatenate(pns, axis=0), new)
             at = pl.multiple_of((r - base) * STEP_COUNT, STEP_COUNT)
             for h in range(heads):
                 acc[h, pl.ds(at, STEP_COUNT), :] = o[h * STEP_COUNT : (h + 1) * STEP_COUNT]
@@ -329,10 +330,11 @@
 
 
 def attend(part, order, lengths, table, q, new, pages, inbox):
-    per_dev, _, _, columns = pages.shape
+    per_dev, _, heads_kv, _, _ = pages.shape
     req_count = inbox.shape[0]
     requests = lengths.shape[0] // HALVES
-    heads = columns // HEAD_WIDTH * GROUP
+    heads = heads_kv * GROUP
+    extent = MAXP * PAGE_LENGTH * heads_kv * 2
     tokens = requests * STEP_COUNT
     return pl.pallas_call(
         functools.partial(attend_kernel, req_count, per_dev, part * requests, requests),
@@ -341,10 +343,10 @@
         out_specs=VMEM,
         scratch_shapes=[
             pltpu.SMEM((per_dev // 128, 128), jnp.int32),
-            pltpu.VMEM((req_count, 1, 2, columns), jnp.bfloat16),
+            pltpu.VMEM((req_count, 1, heads_kv, 2, HEAD_WIDTH), jnp.bfloat16),
             pltpu.VMEM((req_count, 128), jnp.int32),
             pltpu.SMEM((req_count, 128), jnp.int32),
-            pltpu.VMEM((SLOTS, UNROLL, MAXP * PAGE_ROWS, columns), jnp.bfloat16),
+            pltpu.VMEM((SLOTS, UNROLL, extent, HEAD_WIDTH), jnp.bfloat16),
             pltpu.VMEM((heads, tokens, HEAD_WIDTH), jnp.float32),
             pltpu.SemaphoreType.DMA,
             pltpu.SemaphoreType.DMA((SLOTS, UNROLL)),
@@ -352,26 +354,32 @@
         compiler_params=params(),
         cost_estimate=pl.CostEstimate(
             flops=16 * tokens * heads * HEAD_WIDTH * MAXP * PAGE_LENGTH,
-            bytes_accessed=requests * MAXP * PAGE_ROWS * columns * 2,
+            bytes_accessed=requests * extent * HEAD_WIDTH * 2,
             transcendentals=2 * tokens * heads * MAXP * PAGE_LENGTH,
         ),
         name="attend",
     )(order, lengths, table, q, new, pages, inbox)
 
 
-def split_kernel(x_ref, o_ref):
-    o_ref[0] = x_ref[...]
+def split_kernel(x_ref, o_ref, sems):
+    parts, _, block = o_ref.shape
+    copies = [
+        pltpu.make_async_copy(x_ref.at[:, pl.ds(i * block, block)], o_ref.at[i], sems.at[i]) for i in range(parts)
+    ]
+    for copy in copies:
+        copy.start()
+    for copy in copies:
+        copy.wait()
 
 
 def split_columns(x, parts):
     rows, columns = x.shape
-    block = columns // parts
     return pl.pallas_call(
         split_kernel,
-        out_shape=jax.ShapeDtypeStruct((parts, rows, block), x.dtype),
-        grid=(parts,),
-        in_specs=[pl.BlockSpec((rows, block), lambda i: (0, i))],
-        out_specs=pl.BlockSpec((1, rows, block), lambda i: (i, 0, 0)),
+        out_shape=jax.ShapeDtypeStruct((parts, rows, columns // parts), x.dtype),
+        in_specs=[HBM],
+        out_specs=VMEM,
+        scratch_shapes=[pltpu.SemaphoreType.DMA((parts,))],
         compiler_params=params(),
         name="split_columns",
     )(x)
@@ -486,23 +494,34 @@
     return lax.ppermute(x, axis, [(i, i ^ distance) for i in range(count)])
 
 
-def gather(x, my_req):
+def after(x, *others):
+    return lax.optimization_barrier((x, *others))[0]
+
+
+def gather(x, gates):
+    my_req = lax.axis_index("req").astype(jnp.int32)
     count = lax.axis_size("req")
     if count != 8:
         whole = lax.all_gather(x, "req", axis=0)
-        return [whole[b] for b in range(count)], [jnp.int32(b) for b in range(count)]
-    far = [x] + [exchange(x, "req", d) for d in (2, 4, 6)]
-    near = [exchange(block, "req", 1) for block in far]
-    return far + near, [my_req ^ d for d in (0, 2, 4, 6, 1, 3, 5, 7)]
+        return [whole[b] for b in range(count)], [jnp.int32(b) for b in range(count)], []
+    far = [exchange(x, "req", d) for d in (2, 4, 6)]
+    held = [x] + [after(block, *gates) for block in far] if gates else [x] + far
+    near = [exchange(block, "req", 1) for block in held]
+    return held + near, [my_req ^ d for d in (0, 2, 4, 6, 1, 3, 5, 7)], far
 
 
 def scatter(blocks):
     if len(blocks) != 4:
-        return [lax.psum_scatter(jnp.stack(blocks), "tp", scatter_dimension=0, tiled=False)]
+        return [lax.psum_scatter(jnp.stack(blocks), "tp", scatter_dimension=0, tiled=False)], blocks[0]
     own, one, two, three = blocks
     onward = lax.ppermute(three, "tp", [(0, 1), (3, 2)])
     middle = lax.ppermute(three, "tp", [(1, 2), (2, 1)])
-    return [own, exchange(one, "tp", 1), middle, exchange(add(two, onward), "tp", 2)]
+    passed = add(two, onward)
+    return [own, exchange(one, "tp", 1), middle, exchange(passed, "tp", 2)], passed
+
+
+def split_heads(x):
+    return x.reshape(*x.shape[:3], -1, HEAD_WIDTH).transpose(0, 1, 3, 2, 4)
 
 
 def on_device(
@@ -535,10 +554,14 @@
     table, order = build_table(me, page_request_home, lengths)
     q = queries.reshape(requests, STEP_COUNT, heads, HEAD_WIDTH).transpose(0, 2, 1, 3)
     q = q.reshape(requests * heads * STEP_COUNT, HEAD_WIDTH)
-    new = incoming_key_value.transpose(1, 0, 2).reshape(-1, columns)
+    up_blocks = split_columns(adapter_up_factor.reshape(own_slots * rank, model), req_count)
+    new = incoming_key_value.reshape(2, requests * STEP_COUNT, -1, HEAD_WIDTH).transpose(1, 2, 0, 3)
+    new = new.reshape(-1, HEAD_WIDTH)
+    q = after(q, up_blocks)
+    pages = split_heads(key_value_pages)
+    inbox_pages = split_heads(inbox)
     down = adapter_down_factor.transpose(0, 2, 1).reshape(own_slots * rank, -1)
-    up = split_columns(adapter_up_factor.reshape(own_slots * rank, model), req_count)
-    up = lax.all_to_all(up, "req", split_axis=0, concat_axis=0, tiled=True)
+    up = lax.all_to_all(up_blocks, "req", split_axis=0, concat_axis=0, tiled=True)
     up = up.reshape(req_count * own_slots * rank, -1)
 
     slot_count = adapter_storage_slot.shape[0]
@@ -549,10 +572,11 @@
 
     special = tp_count == 4
     roles = [my_lane ^ j if special else jnp.int32(j) for j in range(tp_count)]
-    terms, lows = [], []
+    terms, lows, early, gates = [], [], [], []
+    mixed = [attend(h, order, lengths, table, q, new, pages, inbox_pages) for h in range(HALVES)]
     for h in range(HALVES):
-        mixed = attend(h, order, lengths, table, q, new, key_value_pages, inbox)
-        blocks, origins = gather(mixed, my_req)
+        blocks, origins, far = gather(after(mixed[h], *early), gates)
+        early = far
         where = []
         for origin in origins:
             s = origin // cores
@@ -560,11 +584,14 @@
         where = jnp.stack(where + roles)
         token_slot = jnp.repeat(slot[:, h * half : (h + 1) * half], STEP_COUNT, axis=1)
         mask = (token_slot.reshape(tp_count, -1)[:, :, None] == mine).astype(jnp.bfloat16)
+        mask = after(mask, passed if h else up)
         *parts, low = project(where, blocks, output_projection_weight, down, mask, tp_count)
+        gates = [low]
         lows.append(low)
-        terms.append(scatter(parts))
-
-    low = jnp.concatenate(lows, axis=1)
+        sums, passed = scatter(parts)
+        terms.append(sums)
+
+    low = after(jnp.concatenate(lows, axis=1), passed)
     low = lax.all_to_all(low, "tp", split_axis=0, concat_axis=0, tiled=True)
     low = jnp.sum(low.astype(jnp.float32), axis=0).astype(jnp.bfloat16)
     low = lax.all_gather(low, "req", axis=0)

time: 160 us -> 175 us (1.094)
  waiting for transfers between devices: 35 us -> 47.7 us
  starting transfers between devices: 33.6 us -> 41.4 us
  Pallas kernels: 67.6 us -> 63.4 us
    ppermute x18, waiting for transfers between devices: 20.1 us -> 30.7 us  [exchange(): return lax.ppermute(x, axis, [(i, i ^ distance) for i in range(count)])]
    ppermute x2, waiting for transfers between devices: 5.56 us -> 10.1 us  [scatter(): onward = lax.ppermute(three, 'tp', [(0, 1), (3, 2)])]
    ppermute x2, starting transfers between devices: 3.31 us -> 7.78 us  [scatter(): onward = lax.ppermute(three, 'tp', [(0, 1), (3, 2)])]
    all_to_all x1, waiting for transfers between devices: 3.77 us -> 0.01 us  [on_device(): low = lax.all_to_all(low, 'tp', split_axis=0, concat_axis=0, tiled=True)]
    ppermute x18, starting transfers between devices: 15.2 us -> 18.8 us  [exchange(): return lax.ppermute(x, axis, [(i, i ^ distance) for i in range(count)])]
    pallas_call x1, Pallas kernels: 5.63 us -> 2.91 us  [split_columns(): pl.pallas_call(split_kernel, out_shape=jax.ShapeDtypeStruct((parts, rows,...]
    pallas_call x2, Pallas kernels: 33.5 us -> 31.6 us  [attend(): pl.pallas_call(functools.partial(attend_kernel, req_count, per_dev, part...]
  transfers between devices with their start and end apart: 25 -> 25, of which waited for: 10 -> 8; matrix products, arithmetic and copies ran while one was open for 3% -> 4% of each run, Pallas kernels for 22% -> 27%
where the time goes in v3:
time: 175 us; the launch traced here: 174 us
  Pallas kernels  63.4 us (36%)
  waiting for transfers between devices  47.7 us (27%)
  starting transfers between devices  41.4 us (24%)
  blocking collectives  10.6 us (6%)
  local copies, waits for them, and re-layouts  6.79 us (4%)
  other arithmetic  3.35 us (2%)
    pallas_call x2, Pallas kernels, attend(): pl.pallas_call(functools.partial(attend_kernel, req_count, per_dev, part...  31.6 us
    ppermute x18, waiting for transfers between devices, exchange(): return lax.ppermute(x, axis, [(i, i ^ distance) for i in range(count)])  30.7 us
    ppermute x18, starting transfers between devices, exchange(): return lax.ppermute(x, axis, [(i, i ^ distance) for i in range(count)])  18.8 us
    pallas_call x2, Pallas kernels, project(): pl.pallas_call(functools.partial(project_kernel, count, roles), out_shape...  15.4 us
    all_gather x1, blocking collectives, on_device(): low = lax.all_gather(low, 'req', axis=0)  10.6 us
    ppermute x2, waiting for transfers between devices, scatter(): onward = lax.ppermute(three, 'tp', [(0, 1), (3, 2)])  10.1 us
    ppermute x2, starting transfers between devices, scatter(): onward = lax.ppermute(three, 'tp', [(0, 1), (3, 2)])  7.78 us
    all_to_all x1, waiting for transfers between devices, on_device(): lax.all_to_all(outbox, 'req', split_axis=0, concat_axis=0, tiled=True)  6.89 us
  transfers between devices with their start and end apart: 25, of which 8 were waited for; matrix products, arithmetic and copies ran while one was open for 4% of the time, Pallas kernels for 27%

profile of v3, /device:TPU:0, one launch (start us, length us, event | category | flops | bytes accessed | tf_op | source)
XLA Modules:
  0.0 173.9 jit_solution(11241019111705226772)
XLA Ops:
  0.0 3.6 %pack_outbox.1 = bf16[8,65,2,256]{3,2,1,0:T(2,128)(2,1)} custom-call(s32[1]{0:T(128)} %bitcast.12.me_ref, s32[1,512]{1,0:T(1,128)} %bitcast.53, s32[1,32]{1,0:T(1,128)} %bitcast.56, bf16[512,32,2,256]{3,2,1,0:T(2,128)(2,1)} %pages.1), custom_call_target="tpu_custom_call" | custom-call | tf_op jit(solution)/shard_map/pack_outbox/pallas_call | solution.py:106
  3.6 5.2 %all-to-all-start = ((bf16[8,65,2,256]{3,2,1,0:T(2,128)(2,1)}), bf16[8,65,2,256]{3,2,1,0:T(2,128)(2,1)S(1)}, u32[]{:S(2)}, u32[]{:S(2)}) async-start(bf16[8,65,2,256]{3,2,1,0:T(2,128)(2,1)} %pack_outbox.1), calls=%async_computation | async-start | bytes 1064960 | tf_op jit(solution)/shard_map/all_to_all | solution.py:552
  8.8 2.9 %split_columns.1 = bf16[8,128,1024]{2,1,0:T(8,128)(2,1)} custom-call(bf16[128,8192]{1,0:T(8,128)(2,1)} %bitcast.47), custom_call_target="tpu_custom_call" | custom-call | tf_op jit(solution)/shard_map/split_columns/pallas_call | solution.py:377
  11.8 6.9 %all-to-all-done = bf16[8,65,2,256]{3,2,1,0:T(2,128)(2,1)S(1)} async-done(((bf16[8,65,2,256]{3,2,1,0:T(2,128)(2,1)}), bf16[8,65,2,256]{3,2,1,0:T(2,128)(2,1)S(1)}, u32[]{:S(2)}, u32[]{:S(2)}) %all-to-all-start) | async-done | bytes 532512 | tf_op jit(solution)/shard_map/all_to_all | solution.py:552
  18.7 3.6 %all-to-all-start.1 = ((bf16[8,128,1024]{2,1,0:T(8,128)(2,1)}), bf16[8,128,1024]{2,1,0:T(8,128)(2,1)S(1)}, u32[]{:S(2)}, u32[]{:S(2)}) async-start(bf16[8,128,1024]{2,1,0:T(8,128)(2,1)} %split_columns.1), calls=%async_computation.1 | async-start | bytes 4194304 | tf_op jit(solution)/shard_map/all_to_all | solution.py:564
  26.9 15.8 %attend.2.refs_0_ = bf16[16,64,128]{2,1,0:T(8,128)(2,1)} custom-call(s32[2,128]{1,0:T(2,128)} %get-tuple-element.25.order_ref, s32[32]{0:T(128)} %lengths_ref.3, s32[4,128]{1,0:T(4,128)} %get-tuple-element.26.table_in, bf16[2048,128]{1,0:T(8,128)(2,1)} %bitcast.44, bf16[512,128]{1,0:T(8,128)(2,1)} %bitcast.49, bf16[512,32,2,2,128]{4,3,2,1,0:T(2,128)(2,1)} %bitcast.39, ...), custom_call_target="tpu_custom_call" | custom-call | flops 1073741824 | bytes 8388608 | tf_op jit(solution)/shard_map/attend/pallas_call | solution.py:339
  43.6 2.8 %collective-permute-start.2 = (bf16[16,64,128]{2,1,0:T(8,128)(2,1)}, bf16[16,64,128]{2,1,0:T(8,128)(2,1)S(1)}, u32[]{:S(2)}, u32[]{:S(2)}) collective-permute-start(bf16[16,64,128]{2,1,0:T(8,128)(2,1)} %attend.2.refs_0_), channel_id=1, source_target_pairs={{0,24},{4,28},{8,16},{12,20},{16,8},{20,12},{24,0},{28,4},{1,25},{... | collective-permute-start | bytes 786440 | tf_op jit(solution)/shard_map/ppermute | solution.py:494
  47.8 7.2 %collective-permute-done.2.refs_3_ = bf16[16,64,128]{2,1,0:T(8,128)(2,1)S(1)} collective-permute-done((bf16[16,64,128]{2,1,0:T(8,128)(2,1)}, bf16[16,64,128]{2,1,0:T(8,128)(2,1)S(1)}, u32[]{:S(2)}, u32[]{:S(2)}) %collective-permute-start.2) | collective-permute-done | bytes 262176 | tf_op jit(solution)/shard_map/ppermute | solution.py:494
  55.1 5.1 %collective-permute-done.1.refs_2_ = bf16[16,64,128]{2,1,0:T(8,128)(2,1)} collective-permute-done((bf16[16,64,128]{2,1,0:T(8,128)(2,1)}, bf16[16,64,128]{2,1,0:T(8,128)(2,1)}, u32[]{:S(2)}, u32[]{:S(2)}) %collective-permute-start.1) | collective-permute-done | bytes 262176 | tf_op jit(solution)/shard_map/ppermute | solution.py:494
  60.7 15.8 %attend.3.refs_0_ = bf16[16,64,128]{2,1,0:T(8,128)(2,1)} custom-call(s32[2,128]{1,0:T(2,128)} %get-tuple-element.25.order_ref, s32[32]{0:T(128)} %lengths_ref.3, s32[4,128]{1,0:T(4,128)} %get-tuple-element.26.table_in, bf16[2048,128]{1,0:T(8,128)(2,1)} %bitcast.45, bf16[512,128]{1,0:T(8,128)(2,1)} %bitcast.50, bf16[512,32,2,2,128]{4,3,2,1,0:T(2,128)(2,1)} %bitcast.40, ...), custom_call_target="tpu_custom_call" | custom-call | flops 1073741824 | bytes 8388608 | tf_op jit(solution)/shard_map/attend/pallas_call | solution.py:339
  81.6 8.0 %project.2 = (bf16[128,1024]{1,0:T(8,128)(2,1)}, bf16[128,1024]{1,0:T(8,128)(2,1)}, bf16[128,1024]{1,0:T(8,128)(2,1)}, bf16[128,1024]{1,0:T(8,128)(2,1)}, bf16[4,128,128]{2,1,0:T(8,128)(2,1)}) custom-call(s32[12]{0:T(128)} %stack.64.where_ref, bf16[16,64,128]{2,1,0:T(8,128)(2,1)} %attend.2.refs_0_, bf16[16,64,128]{2,1,0:T(8,128)(2,1)} %collective-permute-done.refs_1_, ...), custom_call_target="tpu_custom_call" | custom-call | flops 2147483648 | bytes 7340032 | tf_op jit(solution)/shard_map/project/pallas_call | solution.py:416
  89.6 2.1 %collective-permute-done.8.refs_2_ = bf16[16,64,128]{2,1,0:T(8,128)(2,1)S(1)} collective-permute-done((bf16[16,64,128]{2,1,0:T(8,128)(2,1)}, bf16[16,64,128]{2,1,0:T(8,128)(2,1)S(1)}, u32[]{:S(2)}, u32[]{:S(2)}) %collective-permute-start.8) | collective-permute-done | bytes 262176 | tf_op jit(solution)/shard_map/ppermute | solution.py:494
  91.7 3.5 %collective-permute-start.14 = (bf16[128,1024]{1,0:T(8,128)(2,1)}, bf16[128,1024]{1,0:T(8,128)(2,1)S(1)}, u32[]{:S(2)}, u32[]{:S(2)}) collective-permute-start(bf16[128,1024]{1,0:T(8,128)(2,1)} %get-tuple-element.35), channel_id=1, source_target_pairs={{0,1},{3,2},{4,5},{7,6},{8,9},{11,10},{12,13},{15,14},{16,17},{19,... | collective-permute-start | bytes 786440 | tf_op jit(solution)/shard_map/ppermute | solution.py:517
  95.9 4.8 %collective-permute-done.14.b_ref = bf16[128,1024]{1,0:T(8,128)(2,1)S(1)} collective-permute-done((bf16[128,1024]{1,0:T(8,128)(2,1)}, bf16[128,1024]{1,0:T(8,128)(2,1)S(1)}, u32[]{:S(2)}, u32[]{:S(2)}) %collective-permute-start.14) | collective-permute-done | bytes 262176 | tf_op jit(solution)/shard_map/ppermute | solution.py:517
  104.8 7.4 %project.3 = (bf16[128,1024]{1,0:T(8,128)(2,1)}, bf16[128,1024]{1,0:T(8,128)(2,1)}, bf16[128,1024]{1,0:T(8,128)(2,1)}, bf16[128,1024]{1,0:T(8,128)(2,1)}, bf16[4,128,128]{2,1,0:T(8,128)(2,1)}) custom-call(s32[12]{0:T(128)} %stack.64.where_ref, bf16[16,64,128]{2,1,0:T(8,128)(2,1)} %attend.3.refs_0_, bf16[16,64,128]{2,1,0:T(8,128)(2,1)} %copy-done.21, ...), custom_call_target="tpu_custom_call" | custom-call | flops 2147483648 | bytes 7340032 | tf_op jit(solution)/shard_map/project/pallas_call | solution.py:416
  112.2 4.3 %collective-permute-start.15 = (bf16[128,1024]{1,0:T(8,128)(2,1)}, bf16[128,1024]{1,0:T(8,128)(2,1)S(1)}, u32[]{:S(2)}, u32[]{:S(2)}) collective-permute-start(bf16[128,1024]{1,0:T(8,128)(2,1)} %get-tuple-element.39), channel_id=1, source_target_pairs={{0,1},{3,2},{4,5},{7,6},{8,9},{11,10},{12,13},{15,14},{16,17},{19,... | collective-permute-start | bytes 786440 | tf_op jit(solution)/shard_map/ppermute | solution.py:517
  118.2 5.3 %collective-permute-done.15.b_ref = bf16[128,1024]{1,0:T(8,128)(2,1)S(1)} collective-permute-done((bf16[128,1024]{1,0:T(8,128)(2,1)}, bf16[128,1024]{1,0:T(8,128)(2,1)S(1)}, u32[]{:S(2)}, u32[]{:S(2)}) %collective-permute-start.15) | collective-permute-done | bytes 262176 | tf_op jit(solution)/shard_map/ppermute | solution.py:517
  126.0 4.7 %all-to-all-start.2 = ((bf16[4,256,128]{2,1,0:T(8,128)(2,1)}), bf16[4,256,128]{2,1,0:T(8,128)(2,1)S(1)}, u32[]{:S(2)}, u32[]{:S(2)}) async-start(bf16[4,256,128]{2,1,0:T(8,128)(2,1)} %pad_maximum_fusion), calls=%async_computation.2 | async-start | bytes 524288 | tf_op jit(solution)/shard_map/all_to_all | solution.py:595
  132.0 6.6 %collective-permute-start.19 = (bf16[128,1024]{1,0:T(8,128)(2,1)}, bf16[128,1024]{1,0:T(8,128)(2,1)S(1)}, u32[]{:S(2)}, u32[]{:S(2)}) collective-permute-start(bf16[128,1024]{1,0:T(8,128)(2,1)} %get-tuple-element.44), channel_id=1, source_target_pairs={{0,1},{1,0},{2,3},{3,2},{4,5},{5,4},{6,7},{7,6},{8,9},{9,8},{10,11... | collective-permute-start | bytes 786440 | tf_op jit(solution)/shard_map/ppermute | solution.py:494
  139.6 1.9 %collective-permute-start.21 = (bf16[128,1024]{1,0:T(8,128)(2,1)}, bf16[128,1024]{1,0:T(8,128)(2,1)S(1)}, u32[]{:S(2)}, u32[]{:S(2)}) collective-permute-start(bf16[128,1024]{1,0:T(8,128)(2,1)} %add.111), channel_id=1, source_target_pairs={{0,2},{1,3},{2,0},{3,1},{4,6},{5,7},{6,4},{7,5},{8,10},{9,11},{10,... | collective-permute-start | bytes 786440 | tf_op jit(solution)/shard_map/ppermute | solution.py:494
  141.6 10.6 %all-gather = bf16[2048,128]{1,0:T(8,128)(2,1)} all-gather(bf16[256,128]{1,0:T(8,128)(2,1)S(1)} %reduce_sum.22), channel_id=2, replica_groups=mesh['req'=8,'tp'=4] {'req'}, dimensions={0}, use_global_device_ids=true | all-gather | bytes 589824 | tf_op jit(solution)/shard_map/all_gather | solution.py:597
  152.2 13.4 %collective-permute-done.18.refs_3_ = bf16[128,1024]{1,0:T(8,128)(2,1)S(1)} collective-permute-done((bf16[128,1024]{1,0:T(8,128)(2,1)S(1)}, bf16[128,1024]{1,0:T(8,128)(2,1)S(1)}, u32[]{:S(2)}, u32[]{:S(2)}) %collective-permute-start.18) | collective-permute-done | bytes 262176 | tf_op jit(solution)/shard_map/ppermute | solution.py:494
  165.7 2.8 %collective-permute-done.21.refs_7_ = bf16[128,1024]{1,0:T(8,128)(2,1)S(1)} collective-permute-done((bf16[128,1024]{1,0:T(8,128)(2,1)}, bf16[128,1024]{1,0:T(8,128)(2,1)S(1)}, u32[]{:S(2)}, u32[]{:S(2)}) %collective-permute-start.21) | collective-permute-done | bytes 262176 | tf_op jit(solution)/shard_map/ppermute | solution.py:494
  169.2 4.7 %finish.1 = bf16[256,1024]{1,0:T(8,128)(2,1)} custom-call(bf16[8,256,128]{2,1,0:T(8,128)(2,1)} %bitcast.46, bf16[1024,1024]{1,0:T(8,128)(2,1)} %bitcast.41, bf16[128,1024]{1,0:T(8,128)(2,1)} %get-tuple-element.41.refs_0_, bf16[128,1024]{1,0:T(8,128)(2,1)} %copy-done.4, bf16[128,1024]{1,0:T(8,128)(2,1)} %copy-done.5, bf16[128,1024]{1,0:T(8,128)(2,1)} %copy-done.8, ...), custom_call_target="tpu_custom_call" | custom-call | tf_op jit(solution)/shard_map/finish/pallas_call | solution.py:477
  (105 shorter events, 24.2 us)
Async XLA Ops:
  3.6 15.0 %all-to-all-start = ((bf16[8,65,2,256]{3,2,1,0:T(2,128)(2,1)}), bf16[8,65,2,256]{3,2,1,0:T(2,128)(2,1)S(1)}, u32[]{:S(2)}, u32[]{:S(2)}) async-start(bf16[8,65,2,256]{3,2,1,0:T(2,128)(2,1)} %pack_outbox.1), calls=%async_computation | async-start | bytes 1064960 | tf_op jit(solution)/shard_map/all_to_all | solution.py:552
  18.7 62.8 %all-to-all-start.1 = ((bf16[8,128,1024]{2,1,0:T(8,128)(2,1)}), bf16[8,128,1024]{2,1,0:T(8,128)(2,1)S(1)}, u32[]{:S(2)}, u32[]{:S(2)}) async-start(bf16[8,128,1024]{2,1,0:T(8,128)(2,1)} %split_columns.1), calls=%async_computation.1 | async-start | bytes 4194304 | tf_op jit(solution)/shard_map/all_to_all | solution.py:564
  42.7 35.7 %collective-permute-start.3 = (bf16[16,64,128]{2,1,0:T(8,128)(2,1)}, bf16[16,64,128]{2,1,0:T(8,128)(2,1)S(1)}, u32[]{:S(2)}, u32[]{:S(2)}) collective-permute-start(bf16[16,64,128]{2,1,0:T(8,128)(2,1)} %attend.2.refs_0_), channel_id=1, source_target_pairs={{0,4},{4,0},{8,12},{12,8},{16,20},{20,16},{24,28},{28,24},{1,5},{5... | collective-permute-start | bytes 786440 | tf_op jit(solution)/shard_map/ppermute | solution.py:494
  43.6 11.4 %collective-permute-start.2 = (bf16[16,64,128]{2,1,0:T(8,128)(2,1)}, bf16[16,64,128]{2,1,0:T(8,128)(2,1)S(1)}, u32[]{:S(2)}, u32[]{:S(2)}) collective-permute-start(bf16[16,64,128]{2,1,0:T(8,128)(2,1)} %attend.2.refs_0_), channel_id=1, source_target_pairs={{0,24},{4,28},{8,16},{12,20},{16,8},{20,12},{24,0},{28,4},{1,25},{... | collective-permute-start | bytes 786440 | tf_op jit(solution)/shard_map/ppermute | solution.py:494
  46.3 13.9 %collective-permute-start.1 = (bf16[16,64,128]{2,1,0:T(8,128)(2,1)}, bf16[16,64,128]{2,1,0:T(8,128)(2,1)}, u32[]{:S(2)}, u32[]{:S(2)}) collective-permute-start(bf16[16,64,128]{2,1,0:T(8,128)(2,1)} %attend.2.refs_0_), channel_id=1, source_target_pairs={{0,16},{4,20},{8,24},{12,28},{16,0},{20,4},{24,8},{28,12},{1,17},{... | collective-permute-start | bytes 786440 | tf_op jit(solution)/shard_map/ppermute | solution.py:494
  46.8 13.5 %collective-permute-start = (bf16[16,64,128]{2,1,0:T(8,128)(2,1)}, bf16[16,64,128]{2,1,0:T(8,128)(2,1)}, u32[]{:S(2)}, u32[]{:S(2)}) collective-permute-start(bf16[16,64,128]{2,1,0:T(8,128)(2,1)} %attend.2.refs_0_), channel_id=1, source_target_pairs={{0,8},{4,12},{8,0},{12,4},{16,24},{20,28},{24,16},{28,20},{1,9},{5... | collective-permute-start | bytes 786440 | tf_op jit(solution)/shard_map/ppermute | solution.py:494
  55.0 24.2 %collective-permute-start.6 = (bf16[16,64,128]{2,1,0:T(8,128)(2,1)S(1)}, bf16[16,64,128]{2,1,0:T(8,128)(2,1)}, u32[]{:S(2)}, u32[]{:S(2)}) collective-permute-start(bf16[16,64,128]{2,1,0:T(8,128)(2,1)S(1)} %collective-permute-done.2.refs_3_), channel_id=1, source_target_pairs={{0,4},{4,0},{8,12},{12,8},{16,20},{20,16},{24,28},{28,24},{1,5},{5... | collective-permute-start | bytes 786440 | tf_op jit(solution)/shard_map/ppermute | solution.py:494
  60.2 21.2 %collective-permute-start.5 = (bf16[16,64,128]{2,1,0:T(8,128)(2,1)}, bf16[16,64,128]{2,1,0:T(8,128)(2,1)}, u32[]{:S(2)}, u32[]{:S(2)}) collective-permute-start(bf16[16,64,128]{2,1,0:T(8,128)(2,1)} %collective-permute-done.1.refs_2_), channel_id=1, source_target_pairs={{0,4},{4,0},{8,12},{12,8},{16,20},{20,16},{24,28},{28,24},{1,5},{5... | collective-permute-start | bytes 786440 | tf_op jit(solution)/shard_map/ppermute | solution.py:494
  60.2 21.3 %collective-permute-start.4 = (bf16[16,64,128]{2,1,0:T(8,128)(2,1)}, bf16[16,64,128]{2,1,0:T(8,128)(2,1)}, u32[]{:S(2)}, u32[]{:S(2)}) collective-permute-start(bf16[16,64,128]{2,1,0:T(8,128)(2,1)} %collective-permute-done.refs_1_), channel_id=1, source_target_pairs={{0,4},{4,0},{8,12},{12,8},{16,20},{20,16},{24,28},{28,24},{1,5},{5... | collective-permute-start | bytes 786440 | tf_op jit(solution)/shard_map/ppermute | solution.py:494
  77.0 12.6 %collective-permute-start.9 = (bf16[16,64,128]{2,1,0:T(8,128)(2,1)}, bf16[16,64,128]{2,1,0:T(8,128)(2,1)S(1)}, u32[]{:S(2)}, u32[]{:S(2)}) collective-permute-start(bf16[16,64,128]{2,1,0:T(8,128)(2,1)} %attend.3.refs_0_), channel_id=1, source_target_pairs={{0,24},{4,28},{8,16},{12,20},{16,8},{20,12},{24,0},{28,4},{1,25},{... | collective-permute-start | bytes 786440 | tf_op jit(solution)/shard_map/ppermute | solution.py:494
  78.4 13.3 %collective-permute-start.8 = (bf16[16,64,128]{2,1,0:T(8,128)(2,1)}, bf16[16,64,128]{2,1,0:T(8,128)(2,1)S(1)}, u32[]{:S(2)}, u32[]{:S(2)}) collective-permute-start(bf16[16,64,128]{2,1,0:T(8,128)(2,1)} %attend.3.refs_0_), channel_id=1, source_target_pairs={{0,16},{4,20},{8,24},{12,28},{16,0},{20,4},{24,8},{28,12},{1,17},{... | collective-permute-start | bytes 786440 | tf_op jit(solution)/shard_map/ppermute | solution.py:494
  79.2 16.0 %collective-permute-start.7 = (bf16[16,64,128]{2,1,0:T(8,128)(2,1)}, bf16[16,64,128]{2,1,0:T(8,128)(2,1)S(1)}, u32[]{:S(2)}, u32[]{:S(2)}) collective-permute-start(bf16[16,64,128]{2,1,0:T(8,128)(2,1)} %attend.3.refs_0_), channel_id=1, source_target_pairs={{0,8},{4,12},{8,0},{12,4},{16,24},{20,28},{24,16},{28,20},{1,9},{5... | collective-permute-start | bytes 786440 | tf_op jit(solution)/shard_map/ppermute | solution.py:494
  81.5 21.7 %collective-permute-start.10 = (bf16[16,64,128]{2,1,0:T(8,128)(2,1)}, bf16[16,64,128]{2,1,0:T(8,128)(2,1)S(1)}, u32[]{:S(2)}, u32[]{:S(2)}) collective-permute-start(bf16[16,64,128]{2,1,0:T(8,128)(2,1)} %attend.3.refs_0_), channel_id=1, source_target_pairs={{0,4},{4,0},{8,12},{12,8},{16,20},{20,16},{24,28},{28,24},{1,5},{5... | collective-permute-start | bytes 786440 | tf_op jit(solution)/shard_map/ppermute | solution.py:494
  91.7 8.9 %collective-permute-start.14 = (bf16[128,1024]{1,0:T(8,128)(2,1)}, bf16[128,1024]{1,0:T(8,128)(2,1)S(1)}, u32[]{:S(2)}, u32[]{:S(2)}) collective-permute-start(bf16[128,1024]{1,0:T(8,128)(2,1)} %get-tuple-element.35), channel_id=1, source_target_pairs={{0,1},{3,2},{4,5},{7,6},{8,9},{11,10},{12,13},{15,14},{16,17},{19,... | collective-permute-start | bytes 786440 | tf_op jit(solution)/shard_map/ppermute | solution.py:517
  95.2 7.9 %collective-permute-start.11 = (bf16[16,64,128]{2,1,0:T(8,128)(2,1)S(1)}, bf16[16,64,128]{2,1,0:T(8,128)(2,1)S(1)}, u32[]{:S(2)}, u32[]{:S(2)}) collective-permute-start(bf16[16,64,128]{2,1,0:T(8,128)(2,1)S(1)} %collective-permute-done.7.refs_1_), channel_id=1, source_target_pairs={{0,4},{4,0},{8,12},{12,8},{16,20},{20,16},{24,28},{28,24},{1,5},{5... | collective-permute-start | bytes 786440 | tf_op jit(solution)/shard_map/ppermute | solution.py:494
  95.3 7.9 %collective-permute-start.12 = (bf16[16,64,128]{2,1,0:T(8,128)(2,1)S(1)}, bf16[16,64,128]{2,1,0:T(8,128)(2,1)S(1)}, u32[]{:S(2)}, u32[]{:S(2)}) collective-permute-start(bf16[16,64,128]{2,1,0:T(8,128)(2,1)S(1)} %collective-permute-done.8.refs_2_), channel_id=1, source_target_pairs={{0,4},{4,0},{8,12},{12,8},{16,20},{20,16},{24,28},{28,24},{1,5},{5... | collective-permute-start | bytes 786440 | tf_op jit(solution)/shard_map/ppermute | solution.py:494
  112.2 11.3 %collective-permute-start.15 = (bf16[128,1024]{1,0:T(8,128)(2,1)}, bf16[128,1024]{1,0:T(8,128)(2,1)S(1)}, u32[]{:S(2)}, u32[]{:S(2)}) collective-permute-start(bf16[128,1024]{1,0:T(8,128)(2,1)} %get-tuple-element.39), channel_id=1, source_target_pairs={{0,1},{3,2},{4,5},{7,6},{8,9},{11,10},{12,13},{15,14},{16,17},{19,... | collective-permute-start | bytes 786440 | tf_op jit(solution)/shard_map/ppermute | solution.py:517
  116.5 23.1 %collective-permute-start.16 = (bf16[128,1024]{1,0:T(8,128)(2,1)S(1)}, bf16[128,1024]{1,0:T(8,128)(2,1)S(1)}, u32[]{:S(2)}, u32[]{:S(2)}) collective-permute-start(bf16[128,1024]{1,0:T(8,128)(2,1)S(1)} %copy-done.16), channel_id=1, source_target_pairs={{0,1},{1,0},{2,3},{3,2},{4,5},{5,4},{6,7},{7,6},{8,9},{9,8},{10,11... | collective-permute-start | bytes 786440 | tf_op jit(solution)/shard_map/ppermute | solution.py:494
  126.0 15.5 %all-to-all-start.2 = ((bf16[4,256,128]{2,1,0:T(8,128)(2,1)}), bf16[4,256,128]{2,1,0:T(8,128)(2,1)S(1)}, u32[]{:S(2)}, u32[]{:S(2)}) async-start(bf16[4,256,128]{2,1,0:T(8,128)(2,1)} %pad_maximum_fusion), calls=%async_computation.2 | async-start | bytes 524288 | tf_op jit(solution)/shard_map/all_to_all | solution.py:595
  130.7 21.5 %collective-permute-start.17 = (bf16[128,1024]{1,0:T(8,128)(2,1)S(1)}, bf16[128,1024]{1,0:T(8,128)(2,1)S(1)}, u32[]{:S(2)}, u32[]{:S(2)}) collective-permute-start(bf16[128,1024]{1,0:T(8,128)(2,1)S(1)} %copy-done.15), channel_id=1, source_target_pairs={{1,2},{2,1},{5,6},{6,5},{9,10},{10,9},{13,14},{14,13},{17,18},{18,... | collective-permute-start | bytes 786440 | tf_op jit(solution)/shard_map/ppermute | solution.py:518
  131.3 20.9 %collective-permute-start.20 = (bf16[128,1024]{1,0:T(8,128)(2,1)}, bf16[128,1024]{1,0:T(8,128)(2,1)S(1)}, u32[]{:S(2)}, u32[]{:S(2)}) collective-permute-start(bf16[128,1024]{1,0:T(8,128)(2,1)} %get-tuple-element.39), channel_id=1, source_target_pairs={{1,2},{2,1},{5,6},{6,5},{9,10},{10,9},{13,14},{14,13},{17,18},{18,... | collective-permute-start | bytes 786440 | tf_op jit(solution)/shard_map/ppermute | solution.py:518
  132.0 20.2 %collective-permute-start.19 = (bf16[128,1024]{1,0:T(8,128)(2,1)}, bf16[128,1024]{1,0:T(8,128)(2,1)S(1)}, u32[]{:S(2)}, u32[]{:S(2)}) collective-permute-start(bf16[128,1024]{1,0:T(8,128)(2,1)} %get-tuple-element.44), channel_id=1, source_target_pairs={{0,1},{1,0},{2,3},{3,2},{4,5},{5,4},{6,7},{7,6},{8,9},{9,8},{10,11... | collective-permute-start | bytes 786440 | tf_op jit(solution)/shard_map/ppermute | solution.py:494
  138.6 27.1 %collective-permute-start.18 = (bf16[128,1024]{1,0:T(8,128)(2,1)S(1)}, bf16[128,1024]{1,0:T(8,128)(2,1)S(1)}, u32[]{:S(2)}, u32[]{:S(2)}) collective-permute-start(bf16[128,1024]{1,0:T(8,128)(2,1)S(1)} %copy-done.3), channel_id=1, source_target_pairs={{0,2},{1,3},{2,0},{3,1},{4,6},{5,7},{6,4},{7,5},{8,10},{9,11},{10,... | collective-permute-start | bytes 786440 | tf_op jit(solution)/shard_map/ppermute | solution.py:494
  139.6 28.9 %collective-permute-start.21 = (bf16[128,1024]{1,0:T(8,128)(2,1)}, bf16[128,1024]{1,0:T(8,128)(2,1)S(1)}, u32[]{:S(2)}, u32[]{:S(2)}) collective-permute-start(bf16[128,1024]{1,0:T(8,128)(2,1)} %add.111), channel_id=1, source_target_pairs={{0,2},{1,3},{2,0},{3,1},{4,6},{5,7},{6,4},{7,5},{8,10},{9,11},{10,... | collective-permute-start | bytes 786440 | tf_op jit(solution)/shard_map/ppermute | solution.py:494
  (27 other events, 296.0 us)

commit v4 on v3

--- a/solution.py
+++ b/solution.py
@@ -27,6 +27,9 @@
 HALVES = 2
 VMEM_LIMIT = 56 * 1024 * 1024
 
+SMALL = pl.CostEstimate(flops=1, bytes_accessed=1, transcendentals=0)
+
+ANY = pl.BlockSpec(memory_space=pl.ANY)
 HBM = pl.BlockSpec(memory_space=pltpu.HBM)
 VMEM = pl.BlockSpec(memory_space=pltpu.VMEM)
 SMEM = pl.BlockSpec(memory_space=pltpu.SMEM)
@@ -117,6 +120,7 @@
             pltpu.SemaphoreType.DMA((req_count, CAP)),
         ],
         compiler_params=params(),
+        cost_estimate=SMALL,
         name="pack_outbox",
     )(me, page_request_home.reshape(1, per_dev), ids.reshape(1, -1), key_value_pages)
 
@@ -166,6 +170,7 @@
         out_specs=(VMEM, VMEM),
         scratch_shapes=[pltpu.VMEM((1, 128), jnp.float32)],
         compiler_params=params(),
+        cost_estimate=SMALL,
         name="page_table",
     )(me, page_request_home.reshape(per_dev // 128, 128), lengths.reshape(1, requests))
 
@@ -201,8 +206,9 @@
     rows = heads_kv * half
     heads = heads_kv * GROUP
     scale = math.log2(math.e) / math.sqrt(HEAD_WIDTH)
-    page_rows = pages.reshape(per_dev, page_size, HEAD_WIDTH)
-    inbox_rows = inbox.reshape(req_count, BLOCK * heads_kv * 2, HEAD_WIDTH)
+    pairs = PAGE_LENGTH * heads_kv
+    page_rows = pages.reshape(per_dev, pairs, 2, HEAD_WIDTH)
+    inbox_rows = inbox.reshape(req_count, BLOCK * heads_kv, 2, HEAD_WIDTH)
 
     tab = pltpu.make_async_copy(table_in, table, sem)
     tab.start()
@@ -227,6 +233,7 @@
                 table[lax.shift_right_logical(slot, 7), slot & 127] = per_dev + d * CAP + k
 
     steps = requests // UNROLL
+    flat = buf.reshape(SLOTS, UNROLL, MAXP * page_size, HEAD_WIDTH)
 
     def fetch(step):
         place = lax.rem(step, SLOTS)
@@ -242,8 +249,7 @@
                 most = functools.reduce(jnp.maximum, sources)
 
                 def target(j):
-                    start = pl.multiple_of(c * chunk_size + j * page_size, page_size)
-                    return buf.at[place, u, pl.ds(start, page_size)]
+                    return buf.at[place, u, pl.ds((c * CHUNK_PAGES + j) * pairs, pairs)]
 
                 @pl.when(most < per_dev)
                 def _():
@@ -264,9 +270,8 @@
                             e = source - per_dev
                             d = lax.shift_right_logical(e, 1)
                             k = e - d * CAP
-                            start = pl.multiple_of(k * page_size, page_size)
                             pltpu.make_async_copy(
-                                inbox_rows.at[d, pl.ds(start, page_size)], target(j), sems.at[place, u]
+                                inbox_rows.at[d, pl.ds(k * pairs, pairs)], target(j), sems.at[place, u]
                             ).start()
 
     for s in range(min(SLOTS - 1, steps)):
@@ -276,7 +281,7 @@
         place = lax.rem(step, SLOTS)
         width = n * chunk_size
         for u in range(UNROLL):
-            whole = buf.at[place, u, pl.ds(0, width)]
+            whole = buf.at[place, u, pl.ds(0, width // 2)]
             pltpu.make_async_copy(whole, whole, sems.at[place, u]).wait()
         column = lax.broadcasted_iota(jnp.int32, (1, width), 1)
         new_column = lax.broadcasted_iota(jnp.int32, (half, 128), 1)
@@ -288,7 +293,7 @@
             r = order_ref[0, base + step * UNROLL + u]
             length = lengths_ref[r]
             q = q_ref[pl.ds(pl.multiple_of(r * rows, rows), rows), :]
-            kv = buf[place, u, 0:width, :]
+            kv = flat[place, u, 0:width, :]
             group = r // new_group
             new = new_ref[pl.ds(pl.multiple_of(group * 128, 128), 128), :]
             seen = visible & (new_column // new_rows == r - group * new_group)
@@ -326,7 +331,8 @@
             def _():
                 compute(step, n)
 
-    out_ref[...] = acc[...].astype(jnp.bfloat16)
+    for h in range(heads):
+        out_ref[:, h * HEAD_WIDTH : (h + 1) * HEAD_WIDTH] = acc[h].astype(jnp.bfloat16)
 
 
 def attend(part, order, lengths, table, q, new, pages, inbox):
@@ -338,7 +344,7 @@
     tokens = requests * STEP_COUNT
     return pl.pallas_call(
         functools.partial(attend_kernel, req_count, per_dev, part * requests, requests),
-        out_shape=jax.ShapeDtypeStruct((heads, tokens, HEAD_WIDTH), jnp.bfloat16),
+        out_shape=jax.ShapeDtypeStruct((tokens, heads * HEAD_WIDTH), jnp.bfloat16),
         in_specs=[SMEM, SMEM, HBM, VMEM, VMEM, HBM, HBM],
         out_specs=VMEM,
         scratch_shapes=[
@@ -346,17 +352,13 @@
             pltpu.VMEM((req_count, 1, heads_kv, 2, HEAD_WIDTH), jnp.bfloat16),
             pltpu.VMEM((req_count, 128), jnp.int32),
             pltpu.SMEM((req_count, 128), jnp.int32),
-            pltpu.VMEM((SLOTS, UNROLL, extent, HEAD_WIDTH), jnp.bfloat16),
+            pltpu.VMEM((SLOTS, UNROLL, extent // 2, 2, HEAD_WIDTH), jnp.bfloat16),
             pltpu.VMEM((heads, tokens, HEAD_WIDTH), jnp.float32),
             pltpu.SemaphoreType.DMA,
             pltpu.SemaphoreType.DMA((SLOTS, UNROLL)),
         ],
         compiler_params=params(),
-        cost_estimate=pl.CostEstimate(
-            flops=16 * tokens * heads * HEAD_WIDTH * MAXP * PAGE_LENGTH,
-            bytes_accessed=requests * extent * HEAD_WIDTH * 2,
-            transcendentals=2 * tokens * heads * MAXP * PAGE_LENGTH,
-        ),
+        cost_estimate=SMALL,
         name="attend",
     )(order, lengths, table, q, new, pages, inbox)
 
@@ -381,26 +383,31 @@
         out_specs=VMEM,
         scratch_shapes=[pltpu.SemaphoreType.DMA((parts,))],
         compiler_params=params(),
+        cost_estimate=SMALL,
         name="split_columns",
     )(x)
 
 
 def project_kernel(count, roles, where_ref, *refs):
     xs, (w_ref, down_ref, mask_ref), rest = refs[:count], refs[count : count + 3], refs[count + 3 :]
-    outs, low_ref, x_v = rest[:roles], rest[roles], rest[roles + 1]
-    heads, tokens, width = xs[0].shape
+    outs, low_ref, x_v, sems = rest[:roles], rest[roles], rest[roles + 1], rest[roles + 2]
+    tokens = xs[0].shape[0]
     rows = count * tokens // roles
 
     @pl.when(pl.program_id(0) == 0)
     def _():
+        copies = []
         for b in range(count):
             at = pl.multiple_of(where_ref[b] * tokens, tokens)
-            for h in range(heads):
-                x_v[pl.ds(at, tokens), h * width : (h + 1) * width] = xs[b][h]
+            copies.append(pltpu.make_async_copy(xs[b], x_v.at[pl.ds(at, tokens)], sems.at[b]))
+        for copy in copies:
+            copy.start()
+        for copy in copies:
+            copy.wait()
+        low = dot(x_v[...], down_ref[...], ((1,), (1,)))
         for j in range(roles):
             s = where_ref[count + j]
-            low = dot(x_v[j * rows : (j + 1) * rows, :], down_ref[...], ((1,), (1,)))
-            low_ref[s] = (low * mask_ref[s].astype(jnp.float32)).astype(jnp.bfloat16)
+            low_ref[s] = (low[j * rows : (j + 1) * rows] * mask_ref[s].astype(jnp.float32)).astype(jnp.bfloat16)
 
     y = dot(x_v[...], w_ref[...]).astype(jnp.bfloat16)
     for j in range(roles):
@@ -409,7 +416,7 @@
 
 def project(where, xs, w, down, mask, roles):
     count = len(xs)
-    heads, tokens, width = xs[0].shape
+    tokens, width = xs[0].shape
     columns = w.shape[1]
     rows = count * tokens // roles
     tile = min(256, columns)
@@ -419,21 +426,17 @@
         + [jax.ShapeDtypeStruct((roles, rows, down.shape[0]), jnp.bfloat16)],
         grid=(columns // tile,),
         in_specs=[SMEM]
-        + [pl.BlockSpec(xs[0].shape, lambda i: (0, 0, 0))] * count
+        + [ANY] * count
         + [
-            pl.BlockSpec((w.shape[0], tile), lambda i: (0, i)),
+            pl.BlockSpec((width, tile), lambda i: (0, i)),
             pl.BlockSpec(down.shape, lambda i: (0, 0)),
             pl.BlockSpec(mask.shape, lambda i: (0, 0, 0)),
         ],
         out_specs=[pl.BlockSpec((rows, tile), lambda i: (0, i))] * roles
         + [pl.BlockSpec((roles, rows, down.shape[0]), lambda i: (0, 0, 0))],
-        scratch_shapes=[pltpu.VMEM((count * tokens, heads * width), jnp.bfloat16)],
-        compiler_params=params(),
-        cost_estimate=pl.CostEstimate(
-            flops=2 * count * tokens * heads * width * columns,
-            bytes_accessed=w.size * 2 + count * tokens * (heads * width + columns) * 2,
-            transcendentals=0,
-        ),
+        scratch_shapes=[pltpu.VMEM((count * tokens, width), jnp.bfloat16), pltpu.SemaphoreType.DMA((count,))],
+        compiler_params=params(),
+        cost_estimate=SMALL,
         name="project",
     )(where, *xs, w, down, mask)
 
@@ -449,19 +452,41 @@
         in_specs=[VMEM, VMEM],
         out_specs=VMEM,
         compiler_params=params(),
+        cost_estimate=SMALL,
         name="add",
     )(a, b)
 
 
-def finish_kernel(counts, cores, low_ref, up_ref, *refs):
+def adapt_kernel(low_ref, up_ref, o_ref):
+    low = jnp.concatenate([low_ref[a] for a in range(low_ref.shape[0])], axis=1)
+    o_ref[...] = dot(low, up_ref[...])
+
+
+def adapt(low, up):
+    columns = up.shape[1]
+    tile = min(256, columns)
+    return pl.pallas_call(
+        adapt_kernel,
+        out_shape=jax.ShapeDtypeStruct((low.shape[1], columns), jnp.float32),
+        grid=(columns // tile,),
+        in_specs=[
+            pl.BlockSpec(low.shape, lambda i: (0, 0, 0)),
+            pl.BlockSpec((up.shape[0], tile), lambda i: (0, i)),
+        ],
+        out_specs=pl.BlockSpec((low.shape[1], tile), lambda i: (0, i)),
+        compiler_params=params(),
+        cost_estimate=SMALL,
+        name="adapt",
+    )(low, up)
+
+
+def finish_kernel(counts, cores, extra_ref, *refs):
     terms, o_ref = refs[:-1], refs[-1]
-    low = jnp.concatenate([low_ref[a] for a in range(low_ref.shape[0])], axis=1)
-    extra = dot(low, up_ref[...])
     rows = terms[0].shape[0]
     tokens = rows // cores
     first = 0
     for h, count in enumerate(counts):
-        total = extra[h * rows : (h + 1) * rows, :]
+        total = extra_ref[h * rows : (h + 1) * rows, :]
         for term in terms[first : first + count]:
             total = total + term[...].astype(jnp.float32)
         first = first + count
@@ -470,23 +495,17 @@
             o_ref[at : at + tokens, :] = total[c * tokens : (c + 1) * tokens].astype(jnp.bfloat16)
 
 
-def finish(terms, cores, low, up):
+def finish(terms, cores, extra):
     flat = [t for half in terms for t in half]
-    rows, columns = flat[0].shape
-    tile = min(256, columns)
     return pl.pallas_call(
         functools.partial(finish_kernel, tuple(len(half) for half in terms), cores),
-        out_shape=jax.ShapeDtypeStruct((len(terms) * rows, columns), jnp.bfloat16),
-        grid=(columns // tile,),
-        in_specs=[
-            pl.BlockSpec(low.shape, lambda i: (0, 0, 0)),
-            pl.BlockSpec((up.shape[0], tile), lambda i: (0, i)),
-        ]
-        + [pl.BlockSpec((rows, tile), lambda i: (0, i))] * len(flat),
-        out_specs=pl.BlockSpec((len(terms) * rows, tile), lambda i: (0, i)),
-        compiler_params=params(),
+        out_shape=jax.ShapeDtypeStruct(extra.shape, jnp.bfloat16),
+        in_specs=[VMEM] * (1 + len(flat)),
+        out_specs=VMEM,
+        compiler_params=params(),
+        cost_estimate=SMALL,
         name="finish",
-    )(low, up, *flat)
+    )(extra, *flat)
 
 
 def exchange(x, axis, distance):
@@ -574,6 +593,7 @@
     roles = [my_lane ^ j if special else jnp.int32(j) for j in range(tp_count)]
     terms, lows, early, gates = [], [], [], []
     mixed = [attend(h, order, lengths, table, q, new, pages, inbox_pages) for h in range(HALVES)]
+    gates = [mixed[-1]]
     for h in range(HALVES):
         blocks, origins, far = gather(after(mixed[h], *early), gates)
         early = far
@@ -595,7 +615,7 @@
     low = lax.all_to_all(low, "tp", split_axis=0, concat_axis=0, tiled=True)
     low = jnp.sum(low.astype(jnp.float32), axis=0).astype(jnp.bfloat16)
     low = lax.all_gather(low, "req", axis=0)
-    return finish(terms, cores, low, up)
+    return finish(terms, cores, adapt(low, up))
 
 
 def solution(mesh):

time: 175 us -> 172 us (0.983)
  waiting for transfers between devices: 47.7 us -> 38.1 us
  Pallas kernels: 63.4 us -> 69.8 us
  local copies, waits for them, and re-layouts: 6.79 us -> 8.92 us
    ppermute x18, waiting for transfers between devices: 30.7 us -> 18.3 us  [exchange(): return lax.ppermute(x, axis, [(i, i ^ distance) for i in range(count)])]
    pallas_call x0 -> x1, Pallas kernels: none -> 4.4 us  [adapt(): pl.pallas_call(adapt_kernel, out_shape=jax.ShapeDtypeStruct((low.shape[1]...]
    pallas_call x2, Pallas kernels: 31.6 us -> 34.8 us  [attend(): pl.pallas_call(functools.partial(attend_kernel, req_count, per_dev, part...]
    all_to_all x1, waiting for transfers between devices: 0.01 us -> 2.4 us  [on_device(): low = lax.all_to_all(low, 'tp', split_axis=0, concat_axis=0, tiled=True)]
    unnamed x53 -> x59, local copies, waits for them, and re-layouts: 3.77 us -> 5.84 us
    pallas_call x1, Pallas kernels: 4.74 us -> 2.9 us  [finish(): pl.pallas_call(functools.partial(finish_kernel, tuple((len(half) for half...]
  transfers between devices with their start and end apart: 25 -> 25, of which waited for: 8 -> 7; matrix products, arithmetic and copies ran while one was open for 4% -> 4% of each run, Pallas kernels for 27% -> 32%
where the time goes in v4:
time: 172 us
  Pallas kernels  69.8 us (41%)
  starting transfers between devices  39.9 us (23%)
  waiting for transfers between devices  38.1 us (22%)
  blocking collectives  11.1 us (6%)
  local copies, waits for them, and re-layouts  8.92 us (5%)
  other arithmetic  3.37 us (2%)
    pallas_call x2, Pallas kernels, attend(): pl.pallas_call(functools.partial(attend_kernel, req_count, per_dev, part...  34.8 us
    ppermute x18, waiting for transfers between devices, exchange(): return lax.ppermute(x, axis, [(i, i ^ distance) for i in range(count)])  18.3 us
    ppermute x18, starting transfers between devices, exchange(): return lax.ppermute(x, axis, [(i, i ^ distance) for i in range(count)])  17.3 us
    pallas_call x2, Pallas kernels, project(): pl.pallas_call(functools.partial(project_kernel, count, roles), out_shape...  16 us
    all_gather x1, blocking collectives, on_device(): low = lax.all_gather(low, 'req', axis=0)  11.1 us
    ppermute x2, waiting for transfers between devices, scatter(): onward = lax.ppermute(three, 'tp', [(0, 1), (3, 2)])  10.5 us
    ppermute x2, starting transfers between devices, scatter(): onward = lax.ppermute(three, 'tp', [(0, 1), (3, 2)])  7.79 us
    all_to_all x1, waiting for transfers between devices, on_device(): lax.all_to_all(outbox, 'req', split_axis=0, concat_axis=0, tiled=True)  6.88 us
  transfers between devices with their start and end apart: 25, of which 7 were waited for; matrix products, arithmetic and copies ran while one was open for 4% of the time, Pallas kernels for 32%

profile of v4, /device:TPU:0, one launch (start us, length us, event | category | flops | bytes accessed | tf_op | source)
XLA Modules:
  0.0 171.6 jit_solution(17982979914287880416)
XLA Ops:
  0.0 3.6 %pack_outbox.1 = bf16[8,65,2,256]{3,2,1,0:T(2,128)(2,1)} custom-call(s32[1]{0:T(128)} %bitcast.12.me_ref, s32[1,512]{1,0:T(1,128)} %bitcast.55, s32[1,32]{1,0:T(1,128)} %bitcast.58, bf16[512,32,2,256]{3,2,1,0:T(2,128)(2,1)} %pages.1), custom_call_target="tpu_custom_call" | custom-call | flops 1 | bytes 1 | tf_op jit(solution)/shard_map/pack_outbox/pallas_call | solution.py:109
  3.6 5.3 %all-to-all-start = ((bf16[8,65,2,256]{3,2,1,0:T(2,128)(2,1)}), bf16[8,65,2,256]{3,2,1,0:T(2,128)(2,1)S(1)}, u32[]{:S(2)}, u32[]{:S(2)}) async-start(bf16[8,65,2,256]{3,2,1,0:T(2,128)(2,1)} %pack_outbox.1), calls=%async_computation | async-start | bytes 1064960 | tf_op jit(solution)/shard_map/all_to_all | solution.py:571
  8.9 2.9 %split_columns.1 = bf16[8,128,1024]{2,1,0:T(8,128)(2,1)} custom-call(bf16[128,8192]{1,0:T(8,128)(2,1)} %bitcast.47), custom_call_target="tpu_custom_call" | custom-call | flops 1 | bytes 1 | tf_op jit(solution)/shard_map/split_columns/pallas_call | solution.py:379
  11.8 6.9 %all-to-all-done = bf16[8,65,2,256]{3,2,1,0:T(2,128)(2,1)S(1)} async-done(((bf16[8,65,2,256]{3,2,1,0:T(2,128)(2,1)}), bf16[8,65,2,256]{3,2,1,0:T(2,128)(2,1)S(1)}, u32[]{:S(2)}, u32[]{:S(2)}) %all-to-all-start) | async-done | bytes 532512 | tf_op jit(solution)/shard_map/all_to_all | solution.py:571
  18.7 3.6 %all-to-all-start.1 = ((bf16[8,128,1024]{2,1,0:T(8,128)(2,1)}), bf16[8,128,1024]{2,1,0:T(8,128)(2,1)S(1)}, u32[]{:S(2)}, u32[]{:S(2)}) async-start(bf16[8,128,1024]{2,1,0:T(8,128)(2,1)} %split_columns.1), calls=%async_computation.1 | async-start | bytes 4194304 | tf_op jit(solution)/shard_map/all_to_all | solution.py:583
  26.0 16.5 %attend.2.refs_0_ = bf16[64,2048]{1,0:T(8,128)(2,1)} custom-call(s32[2,128]{1,0:T(2,128)} %get-tuple-element.28.order_ref, s32[32]{0:T(128)} %lengths_ref.3, s32[4,128]{1,0:T(4,128)} %get-tuple-element.29.table_in, bf16[2048,128]{1,0:T(8,128)(2,1)} %bitcast.44, bf16[512,128]{1,0:T(8,128)(2,1)} %bitcast.51, bf16[512,32,2,2,128]{4,3,2,1,0:T(2,128)(2,1)} %bitcast.39, ...), custom_call_target="tpu_custom_call" | custom-call | flops 1 | bytes 1 | tf_op jit(solution)/shard_map/attend/pallas_call | solution.py:345
  42.5 3.8 %collective-permute-start.2 = (bf16[64,2048]{1,0:T(8,128)(2,1)}, bf16[64,2048]{1,0:T(8,128)(2,1)S(1)}, u32[]{:S(2)}, u32[]{:S(2)}) collective-permute-start(bf16[64,2048]{1,0:T(8,128)(2,1)} %attend.2.refs_0_), channel_id=1, source_target_pairs={{0,24},{4,28},{8,16},{12,20},{16,8},{20,12},{24,0},{28,4},{1,25},{... | collective-permute-start | bytes 786440 | tf_op jit(solution)/shard_map/ppermute | solution.py:513
  47.0 18.3 %attend.3.refs_0_ = bf16[64,2048]{1,0:T(8,128)(2,1)} custom-call(s32[2,128]{1,0:T(2,128)} %get-tuple-element.28.order_ref, s32[32]{0:T(128)} %lengths_ref.3, s32[4,128]{1,0:T(4,128)} %get-tuple-element.29.table_in, bf16[2048,128]{1,0:T(8,128)(2,1)} %bitcast.45, bf16[512,128]{1,0:T(8,128)(2,1)} %bitcast.52, bf16[512,32,2,2,128]{4,3,2,1,0:T(2,128)(2,1)} %bitcast.40, ...), custom_call_target="tpu_custom_call" | custom-call | flops 1 | bytes 1 | tf_op jit(solution)/shard_map/attend/pallas_call | solution.py:345
  67.5 6.7 %collective-permute-done.1.refs_2_ = bf16[64,2048]{1,0:T(8,128)(2,1)} collective-permute-done((bf16[64,2048]{1,0:T(8,128)(2,1)S(1)}, bf16[64,2048]{1,0:T(8,128)(2,1)}, u32[]{:S(2)}, u32[]{:S(2)}) %collective-permute-start.1) | collective-permute-done | bytes 262176 | tf_op jit(solution)/shard_map/ppermute | solution.py:513
  74.2 2.3 %collective-permute-start.9 = (bf16[64,2048]{1,0:T(8,128)(2,1)}, bf16[64,2048]{1,0:T(8,128)(2,1)S(1)}, u32[]{:S(2)}, u32[]{:S(2)}) collective-permute-start(bf16[64,2048]{1,0:T(8,128)(2,1)} %attend.3.refs_0_), channel_id=1, source_target_pairs={{0,24},{4,28},{8,16},{12,20},{16,8},{20,12},{24,0},{28,4},{1,25},{... | collective-permute-start | bytes 786440 | tf_op jit(solution)/shard_map/ppermute | solution.py:513
  81.2 8.0 %project.2 = (bf16[128,1024]{1,0:T(8,128)(2,1)}, bf16[128,1024]{1,0:T(8,128)(2,1)}, bf16[128,1024]{1,0:T(8,128)(2,1)}, bf16[128,1024]{1,0:T(8,128)(2,1)}, bf16[4,128,128]{2,1,0:T(8,128)(2,1)}) custom-call(s32[12]{0:T(128)} %stack.64.where_ref, bf16[64,2048]{1,0:T(8,128)(2,1)} %attend.2.refs_0_, bf16[64,2048]{1,0:T(8,128)(2,1)} %collective-permute-done.refs_1_, ...), custom_call_target="tpu_custom_call" | custom-call | flops 1 | bytes 1 | tf_op jit(solution)/shard_map/project/pallas_call | solution.py:423
  89.3 3.5 %collective-permute-start.14 = (bf16[128,1024]{1,0:T(8,128)(2,1)}, bf16[128,1024]{1,0:T(8,128)(2,1)S(1)}, u32[]{:S(2)}, u32[]{:S(2)}) collective-permute-start(bf16[128,1024]{1,0:T(8,128)(2,1)} %get-tuple-element.41), channel_id=1, source_target_pairs={{0,1},{3,2},{4,5},{7,6},{8,9},{11,10},{12,13},{15,14},{16,17},{19,... | collective-permute-start | bytes 786440 | tf_op jit(solution)/shard_map/ppermute | solution.py:536
  93.5 5.1 %collective-permute-done.14.b_ref = bf16[128,1024]{1,0:T(8,128)(2,1)S(1)} collective-permute-done((bf16[128,1024]{1,0:T(8,128)(2,1)}, bf16[128,1024]{1,0:T(8,128)(2,1)S(1)}, u32[]{:S(2)}, u32[]{:S(2)}) %collective-permute-start.14) | collective-permute-done | bytes 262176 | tf_op jit(solution)/shard_map/ppermute | solution.py:536
  102.8 8.0 %project.3 = (bf16[128,1024]{1,0:T(8,128)(2,1)}, bf16[128,1024]{1,0:T(8,128)(2,1)}, bf16[128,1024]{1,0:T(8,128)(2,1)}, bf16[128,1024]{1,0:T(8,128)(2,1)}, bf16[4,128,128]{2,1,0:T(8,128)(2,1)}) custom-call(s32[12]{0:T(128)} %stack.64.where_ref, bf16[64,2048]{1,0:T(8,128)(2,1)} %attend.3.refs_0_, bf16[64,2048]{1,0:T(8,128)(2,1)} %copy-done.13, ...), custom_call_target="tpu_custom_call" | custom-call | flops 1 | bytes 1 | tf_op jit(solution)/shard_map/project/pallas_call | solution.py:423
  110.8 4.3 %collective-permute-start.15 = (bf16[128,1024]{1,0:T(8,128)(2,1)}, bf16[128,1024]{1,0:T(8,128)(2,1)S(1)}, u32[]{:S(2)}, u32[]{:S(2)}) collective-permute-start(bf16[128,1024]{1,0:T(8,128)(2,1)} %get-tuple-element.45), channel_id=1, source_target_pairs={{0,1},{3,2},{4,5},{7,6},{8,9},{11,10},{12,13},{15,14},{16,17},{19,... | collective-permute-start | bytes 786440 | tf_op jit(solution)/shard_map/ppermute | solution.py:536
  116.9 5.3 %collective-permute-done.15.b_ref = bf16[128,1024]{1,0:T(8,128)(2,1)S(1)} collective-permute-done((bf16[128,1024]{1,0:T(8,128)(2,1)}, bf16[128,1024]{1,0:T(8,128)(2,1)S(1)}, u32[]{:S(2)}, u32[]{:S(2)}) %collective-permute-start.15) | collective-permute-done | bytes 262176 | tf_op jit(solution)/shard_map/ppermute | solution.py:536
  124.6 4.7 %all-to-all-start.2 = ((bf16[4,256,128]{2,1,0:T(8,128)(2,1)}), bf16[4,256,128]{2,1,0:T(8,128)(2,1)S(1)}, u32[]{:S(2)}, u32[]{:S(2)}) async-start(bf16[4,256,128]{2,1,0:T(8,128)(2,1)} %pad_maximum_fusion), calls=%async_computation.2 | async-start | bytes 524288 | tf_op jit(solution)/shard_map/all_to_all | solution.py:615
  130.0 4.8 %collective-permute-start.18 = (bf16[128,1024]{1,0:T(8,128)(2,1)S(1)}, bf16[128,1024]{1,0:T(8,128)(2,1)S(1)}, u32[]{:S(2)}, u32[]{:S(2)}) collective-permute-start(bf16[128,1024]{1,0:T(8,128)(2,1)S(1)} %copy-done.14), channel_id=1, source_target_pairs={{0,2},{1,3},{2,0},{3,1},{4,6},{5,7},{6,4},{7,5},{8,10},{9,11},{10,... | collective-permute-start | bytes 786440 | tf_op jit(solution)/shard_map/ppermute | solution.py:513
  138.4 2.4 %all-to-all-done.2 = bf16[4,256,128]{2,1,0:T(8,128)(2,1)S(1)} async-done(((bf16[4,256,128]{2,1,0:T(8,128)(2,1)}), bf16[4,256,128]{2,1,0:T(8,128)(2,1)S(1)}, u32[]{:S(2)}, u32[]{:S(2)}) %all-to-all-start.2) | async-done | bytes 262176 | tf_op jit(solution)/shard_map/all_to_all | solution.py:615
  140.9 11.1 %all-gather = bf16[2048,128]{1,0:T(8,128)(2,1)} all-gather(bf16[256,128]{1,0:T(8,128)(2,1)S(1)} %reduce_sum.22), channel_id=2, replica_groups=mesh['req'=8,'tp'=4] {'req'}, dimensions={0}, use_global_device_ids=true | all-gather | bytes 589824 | tf_op jit(solution)/shard_map/all_gather | solution.py:617
  152.0 4.4 %adapt.1.extra_ref = f32[256,1024]{1,0:T(8,128)} custom-call(bf16[8,256,128]{2,1,0:T(8,128)(2,1)} %bitcast.46, bf16[1024,1024]{1,0:T(8,128)(2,1)} %bitcast.41), custom_call_target="tpu_custom_call" | custom-call | flops 1 | bytes 1 | tf_op jit(solution)/shard_map/adapt/pallas_call | solution.py:468
  156.4 3.2 %collective-permute-done.18.refs_3_ = bf16[128,1024]{1,0:T(8,128)(2,1)S(1)} collective-permute-done((bf16[128,1024]{1,0:T(8,128)(2,1)S(1)}, bf16[128,1024]{1,0:T(8,128)(2,1)S(1)}, u32[]{:S(2)}, u32[]{:S(2)}) %collective-permute-start.18) | collective-permute-done | bytes 262176 | tf_op jit(solution)/shard_map/ppermute | solution.py:513
  159.7 8.3 %collective-permute-done.21.refs_7_ = bf16[128,1024]{1,0:T(8,128)(2,1)S(1)} collective-permute-done((bf16[128,1024]{1,0:T(8,128)(2,1)}, bf16[128,1024]{1,0:T(8,128)(2,1)S(1)}, u32[]{:S(2)}, u32[]{:S(2)}) %collective-permute-start.21) | collective-permute-done | bytes 262176 | tf_op jit(solution)/shard_map/ppermute | solution.py:513
  168.7 2.9 %finish.1 = bf16[256,1024]{1,0:T(8,128)(2,1)} custom-call(f32[256,1024]{1,0:T(8,128)} %adapt.1.extra_ref, bf16[128,1024]{1,0:T(8,128)(2,1)} %get-tuple-element.47.refs_0_, bf16[128,1024]{1,0:T(8,128)(2,1)} %copy-done.4, bf16[128,1024]{1,0:T(8,128)(2,1)} %copy-done.5, bf16[128,1024]{1,0:T(8,128)(2,1)} %copy-done.6, ...), custom_call_target="tpu_custom_call" | custom-call | flops 1 | bytes 1 | tf_op jit(solution)/shard_map/finish/pallas_call | solution.py:500
  (112 shorter events, 25.2 us)
Async XLA Ops:
  3.6 15.1 %all-to-all-start = ((bf16[8,65,2,256]{3,2,1,0:T(2,128)(2,1)}), bf16[8,65,2,256]{3,2,1,0:T(2,128)(2,1)S(1)}, u32[]{:S(2)}, u32[]{:S(2)}) async-start(bf16[8,65,2,256]{3,2,1,0:T(2,128)(2,1)} %pack_outbox.1), calls=%async_computation | async-start | bytes 1064960 | tf_op jit(solution)/shard_map/all_to_all | solution.py:571
  18.7 61.8 %all-to-all-start.1 = ((bf16[8,128,1024]{2,1,0:T(8,128)(2,1)}), bf16[8,128,1024]{2,1,0:T(8,128)(2,1)S(1)}, u32[]{:S(2)}, u32[]{:S(2)}) async-start(bf16[8,128,1024]{2,1,0:T(8,128)(2,1)} %split_columns.1), calls=%async_computation.1 | async-start | bytes 4194304 | tf_op jit(solution)/shard_map/all_to_all | solution.py:583
  42.5 24.1 %collective-permute-start.2 = (bf16[64,2048]{1,0:T(8,128)(2,1)}, bf16[64,2048]{1,0:T(8,128)(2,1)S(1)}, u32[]{:S(2)}, u32[]{:S(2)}) collective-permute-start(bf16[64,2048]{1,0:T(8,128)(2,1)} %attend.2.refs_0_), channel_id=1, source_target_pairs={{0,24},{4,28},{8,16},{12,20},{16,8},{20,12},{24,0},{28,4},{1,25},{... | collective-permute-start | bytes 786440 | tf_op jit(solution)/shard_map/ppermute | solution.py:513
  65.3 12.4 %collective-permute-start.3 = (bf16[64,2048]{1,0:T(8,128)(2,1)S(1)}, bf16[64,2048]{1,0:T(8,128)(2,1)S(1)}, u32[]{:S(2)}, u32[]{:S(2)}) collective-permute-start(bf16[64,2048]{1,0:T(8,128)(2,1)S(1)} %copy-done.2), channel_id=1, source_target_pairs={{0,4},{4,0},{8,12},{12,8},{16,20},{20,16},{24,28},{28,24},{1,5},{5... | collective-permute-start | bytes 786440 | tf_op jit(solution)/shard_map/ppermute | solution.py:513
  65.4 8.8 %collective-permute-start.1 = (bf16[64,2048]{1,0:T(8,128)(2,1)S(1)}, bf16[64,2048]{1,0:T(8,128)(2,1)}, u32[]{:S(2)}, u32[]{:S(2)}) collective-permute-start(bf16[64,2048]{1,0:T(8,128)(2,1)S(1)} %copy-done.2), channel_id=1, source_target_pairs={{0,16},{4,20},{8,24},{12,28},{16,0},{20,4},{24,8},{28,12},{1,17},{... | collective-permute-start | bytes 786440 | tf_op jit(solution)/shard_map/ppermute | solution.py:513
  65.4 8.8 %collective-permute-start = (bf16[64,2048]{1,0:T(8,128)(2,1)S(1)}, bf16[64,2048]{1,0:T(8,128)(2,1)}, u32[]{:S(2)}, u32[]{:S(2)}) collective-permute-start(bf16[64,2048]{1,0:T(8,128)(2,1)S(1)} %copy-done.2), channel_id=1, source_target_pairs={{0,8},{4,12},{8,0},{12,4},{16,24},{20,28},{24,16},{28,20},{1,9},{5... | collective-permute-start | bytes 786440 | tf_op jit(solution)/shard_map/ppermute | solution.py:513
  66.6 11.1 %collective-permute-start.6 = (bf16[64,2048]{1,0:T(8,128)(2,1)S(1)}, bf16[64,2048]{1,0:T(8,128)(2,1)S(1)}, u32[]{:S(2)}, u32[]{:S(2)}) collective-permute-start(bf16[64,2048]{1,0:T(8,128)(2,1)S(1)} %collective-permute-done.2.refs_3_), channel_id=1, source_target_pairs={{0,4},{4,0},{8,12},{12,8},{16,20},{20,16},{24,28},{28,24},{1,5},{5... | collective-permute-start | bytes 786440 | tf_op jit(solution)/shard_map/ppermute | solution.py:513
  74.2 18.6 %collective-permute-start.9 = (bf16[64,2048]{1,0:T(8,128)(2,1)}, bf16[64,2048]{1,0:T(8,128)(2,1)S(1)}, u32[]{:S(2)}, u32[]{:S(2)}) collective-permute-start(bf16[64,2048]{1,0:T(8,128)(2,1)} %attend.3.refs_0_), channel_id=1, source_target_pairs={{0,24},{4,28},{8,16},{12,20},{16,8},{20,12},{24,0},{28,4},{1,25},{... | collective-permute-start | bytes 786440 | tf_op jit(solution)/shard_map/ppermute | solution.py:513
  76.5 16.5 %collective-permute-start.8 = (bf16[64,2048]{1,0:T(8,128)(2,1)}, bf16[64,2048]{1,0:T(8,128)(2,1)S(1)}, u32[]{:S(2)}, u32[]{:S(2)}) collective-permute-start(bf16[64,2048]{1,0:T(8,128)(2,1)} %attend.3.refs_0_), channel_id=1, source_target_pairs={{0,16},{4,20},{8,24},{12,28},{16,0},{20,4},{24,8},{28,12},{1,17},{... | collective-permute-start | bytes 786440 | tf_op jit(solution)/shard_map/ppermute | solution.py:513
  76.7 16.7 %collective-permute-start.7 = (bf16[64,2048]{1,0:T(8,128)(2,1)}, bf16[64,2048]{1,0:T(8,128)(2,1)S(1)}, u32[]{:S(2)}, u32[]{:S(2)}) collective-permute-start(bf16[64,2048]{1,0:T(8,128)(2,1)} %attend.3.refs_0_), channel_id=1, source_target_pairs={{0,8},{4,12},{8,0},{12,4},{16,24},{20,28},{24,16},{28,20},{1,9},{5... | collective-permute-start | bytes 786440 | tf_op jit(solution)/shard_map/ppermute | solution.py:513
  77.7 2.8 %collective-permute-start.5 = (bf16[64,2048]{1,0:T(8,128)(2,1)}, bf16[64,2048]{1,0:T(8,128)(2,1)S(1)}, u32[]{:S(2)}, u32[]{:S(2)}) collective-permute-start(bf16[64,2048]{1,0:T(8,128)(2,1)} %collective-permute-done.1.refs_2_), channel_id=1, source_target_pairs={{0,4},{4,0},{8,12},{12,8},{16,20},{20,16},{24,28},{28,24},{1,5},{5... | collective-permute-start | bytes 786440 | tf_op jit(solution)/shard_map/ppermute | solution.py:513
  80.5 20.7 %collective-permute-start.10 = (bf16[64,2048]{1,0:T(8,128)(2,1)}, bf16[64,2048]{1,0:T(8,128)(2,1)S(1)}, u32[]{:S(2)}, u32[]{:S(2)}) collective-permute-start(bf16[64,2048]{1,0:T(8,128)(2,1)} %attend.3.refs_0_), channel_id=1, source_target_pairs={{0,4},{4,0},{8,12},{12,8},{16,20},{20,16},{24,28},{28,24},{1,5},{5... | collective-permute-start | bytes 786440 | tf_op jit(solution)/shard_map/ppermute | solution.py:513
  89.3 9.3 %collective-permute-start.14 = (bf16[128,1024]{1,0:T(8,128)(2,1)}, bf16[128,1024]{1,0:T(8,128)(2,1)S(1)}, u32[]{:S(2)}, u32[]{:S(2)}) collective-permute-start(bf16[128,1024]{1,0:T(8,128)(2,1)} %get-tuple-element.41), channel_id=1, source_target_pairs={{0,1},{3,2},{4,5},{7,6},{8,9},{11,10},{12,13},{15,14},{16,17},{19,... | collective-permute-start | bytes 786440 | tf_op jit(solution)/shard_map/ppermute | solution.py:536
  92.8 8.4 %collective-permute-start.13 = (bf16[64,2048]{1,0:T(8,128)(2,1)S(1)}, bf16[64,2048]{1,0:T(8,128)(2,1)S(1)}, u32[]{:S(2)}, u32[]{:S(2)}) collective-permute-start(bf16[64,2048]{1,0:T(8,128)(2,1)S(1)} %collective-permute-done.9.refs_3_), channel_id=1, source_target_pairs={{0,4},{4,0},{8,12},{12,8},{16,20},{20,16},{24,28},{28,24},{1,5},{5... | collective-permute-start | bytes 786440 | tf_op jit(solution)/shard_map/ppermute | solution.py:513
  92.9 8.3 %collective-permute-start.12 = (bf16[64,2048]{1,0:T(8,128)(2,1)S(1)}, bf16[64,2048]{1,0:T(8,128)(2,1)S(1)}, u32[]{:S(2)}, u32[]{:S(2)}) collective-permute-start(bf16[64,2048]{1,0:T(8,128)(2,1)S(1)} %collective-permute-done.8.refs_2_), channel_id=1, source_target_pairs={{0,4},{4,0},{8,12},{12,8},{16,20},{20,16},{24,28},{28,24},{1,5},{5... | collective-permute-start | bytes 786440 | tf_op jit(solution)/shard_map/ppermute | solution.py:513
  93.4 7.8 %collective-permute-start.11 = (bf16[64,2048]{1,0:T(8,128)(2,1)S(1)}, bf16[64,2048]{1,0:T(8,128)(2,1)S(1)}, u32[]{:S(2)}, u32[]{:S(2)}) collective-permute-start(bf16[64,2048]{1,0:T(8,128)(2,1)S(1)} %collective-permute-done.7.refs_1_), channel_id=1, source_target_pairs={{0,4},{4,0},{8,12},{12,8},{16,20},{20,16},{24,28},{28,24},{1,5},{5... | collective-permute-start | bytes 786440 | tf_op jit(solution)/shard_map/ppermute | solution.py:513
  110.8 11.4 %collective-permute-start.15 = (bf16[128,1024]{1,0:T(8,128)(2,1)}, bf16[128,1024]{1,0:T(8,128)(2,1)S(1)}, u32[]{:S(2)}, u32[]{:S(2)}) collective-permute-start(bf16[128,1024]{1,0:T(8,128)(2,1)} %get-tuple-element.45), channel_id=1, source_target_pairs={{0,1},{3,2},{4,5},{7,6},{8,9},{11,10},{12,13},{15,14},{16,17},{19,... | collective-permute-start | bytes 786440 | tf_op jit(solution)/shard_map/ppermute | solution.py:536
  115.1 22.2 %collective-permute-start.16 = (bf16[128,1024]{1,0:T(8,128)(2,1)S(1)}, bf16[128,1024]{1,0:T(8,128)(2,1)S(1)}, u32[]{:S(2)}, u32[]{:S(2)}) collective-permute-start(bf16[128,1024]{1,0:T(8,128)(2,1)S(1)} %copy-done.28), channel_id=1, source_target_pairs={{0,1},{1,0},{2,3},{3,2},{4,5},{5,4},{6,7},{7,6},{8,9},{9,8},{10,11... | collective-permute-start | bytes 786440 | tf_op jit(solution)/shard_map/ppermute | solution.py:513
  124.6 16.2 %all-to-all-start.2 = ((bf16[4,256,128]{2,1,0:T(8,128)(2,1)}), bf16[4,256,128]{2,1,0:T(8,128)(2,1)S(1)}, u32[]{:S(2)}, u32[]{:S(2)}) async-start(bf16[4,256,128]{2,1,0:T(8,128)(2,1)} %pad_maximum_fusion), calls=%async_computation.2 | async-start | bytes 524288 | tf_op jit(solution)/shard_map/all_to_all | solution.py:615
  129.3 27.1 %collective-permute-start.17 = (bf16[128,1024]{1,0:T(8,128)(2,1)S(1)}, bf16[128,1024]{1,0:T(8,128)(2,1)S(1)}, u32[]{:S(2)}, u32[]{:S(2)}) collective-permute-start(bf16[128,1024]{1,0:T(8,128)(2,1)S(1)} %copy-done.27), channel_id=1, source_target_pairs={{1,2},{2,1},{5,6},{6,5},{9,10},{10,9},{13,14},{14,13},{17,18},{18,... | collective-permute-start | bytes 786440 | tf_op jit(solution)/shard_map/ppermute | solution.py:537
  130.0 29.7 %collective-permute-start.18 = (bf16[128,1024]{1,0:T(8,128)(2,1)S(1)}, bf16[128,1024]{1,0:T(8,128)(2,1)S(1)}, u32[]{:S(2)}, u32[]{:S(2)}) collective-permute-start(bf16[128,1024]{1,0:T(8,128)(2,1)S(1)} %copy-done.14), channel_id=1, source_target_pairs={{0,2},{1,3},{2,0},{3,1},{4,6},{5,7},{6,4},{7,5},{8,10},{9,11},{10,... | collective-permute-start | bytes 786440 | tf_op jit(solution)/shard_map/ppermute | solution.py:513
  134.8 24.9 %collective-permute-start.20 = (bf16[128,1024]{1,0:T(8,128)(2,1)}, bf16[128,1024]{1,0:T(8,128)(2,1)S(1)}, u32[]{:S(2)}, u32[]{:S(2)}) collective-permute-start(bf16[128,1024]{1,0:T(8,128)(2,1)} %get-tuple-element.45), channel_id=1, source_target_pairs={{1,2},{2,1},{5,6},{6,5},{9,10},{10,9},{13,14},{14,13},{17,18},{18,... | collective-permute-start | bytes 786440 | tf_op jit(solution)/shard_map/ppermute | solution.py:537
  135.4 24.2 %collective-permute-start.19 = (bf16[128,1024]{1,0:T(8,128)(2,1)}, bf16[128,1024]{1,0:T(8,128)(2,1)S(1)}, u32[]{:S(2)}, u32[]{:S(2)}) collective-permute-start(bf16[128,1024]{1,0:T(8,128)(2,1)} %get-tuple-element.50), channel_id=1, source_target_pairs={{0,1},{1,0},{2,3},{3,2},{4,5},{5,4},{6,7},{7,6},{8,9},{9,8},{10,11... | collective-permute-start | bytes 786440 | tf_op jit(solution)/shard_map/ppermute | solution.py:513
  137.3 30.7 %collective-permute-start.21 = (bf16[128,1024]{1,0:T(8,128)(2,1)}, bf16[128,1024]{1,0:T(8,128)(2,1)S(1)}, u32[]{:S(2)}, u32[]{:S(2)}) collective-permute-start(bf16[128,1024]{1,0:T(8,128)(2,1)} %add.111), channel_id=1, source_target_pairs={{0,2},{1,3},{2,0},{3,1},{4,6},{5,7},{6,4},{7,5},{8,10},{9,11},{10,... | collective-permute-start | bytes 786440 | tf_op jit(solution)/shard_map/ppermute | solution.py:513
  (30 other events, 265.0 us)

commit v5 on v4

--- a/solution.py
+++ b/solution.py
@@ -22,10 +22,12 @@
 CHUNK_PAGES = 4
 CHUNKS = MAXP // CHUNK_PAGES
 CHUNK_POSITIONS = CHUNK_PAGES * PAGE_LENGTH
-UNROLL = 2
-SLOTS = 6
+BUFFERS = 12
+UNROLLS = (2, 4)
+PRIORITIES = (2, 1)
 HALVES = 2
-VMEM_LIMIT = 56 * 1024 * 1024
+VMEM_LIMIT = 24 * 1024 * 1024
+WHOLE_VMEM = 60 * 1024 * 1024
 
 SMALL = pl.CostEstimate(flops=1, bytes_accessed=1, transcendentals=0)
 
@@ -35,8 +37,8 @@
 SMEM = pl.BlockSpec(memory_space=pltpu.SMEM)
 
 
-def params():
-    return pltpu.CompilerParams(vmem_limit_bytes=VMEM_LIMIT)
+def params(limit=VMEM_LIMIT):
+    return pltpu.CompilerParams(vmem_limit_bytes=limit)
 
 
 def dot(a, b, contract=((1,), (0,))):
@@ -119,7 +121,7 @@
             pltpu.SemaphoreType.DMA,
             pltpu.SemaphoreType.DMA((req_count, CAP)),
         ],
-        compiler_params=params(),
+        compiler_params=params(WHOLE_VMEM),
         cost_estimate=SMALL,
         name="pack_outbox",
     )(me, page_request_home.reshape(1, per_dev), ids.reshape(1, -1), key_value_pages)
@@ -180,6 +182,8 @@
     per_dev,
     base,
     requests,
+    unroll,
+    priorities,
     order_ref,
     lengths_ref,
     table_in,
@@ -232,14 +236,15 @@
             def _():
                 table[lax.shift_right_logical(slot, 7), slot & 127] = per_dev + d * CAP + k
 
-    steps = requests // UNROLL
-    flat = buf.reshape(SLOTS, UNROLL, MAXP * page_size, HEAD_WIDTH)
+    slots = BUFFERS // unroll
+    steps = requests // unroll
+    flat = buf.reshape(slots, unroll, MAXP * page_size, HEAD_WIDTH)
 
     def fetch(step):
-        place = lax.rem(step, SLOTS)
-        count = order_ref[1, base + step * UNROLL]
-        for u in range(UNROLL):
-            slot = order_ref[0, base + step * UNROLL + u] * MAXP
+        place = lax.rem(step, slots)
+        count = order_ref[1, base + step * unroll]
+        for u in range(unroll):
+            slot = order_ref[0, base + step * unroll + u] * MAXP
             line = lax.shift_right_logical(slot, 7)
             at = slot & 127
 
@@ -254,7 +259,9 @@
                 @pl.when(most < per_dev)
                 def _():
                     for j in range(CHUNK_PAGES):
-                        pltpu.make_async_copy(page_rows.at[sources[j]], target(j), sems.at[place, u]).start()
+                        pltpu.make_async_copy(page_rows.at[sources[j]], target(j), sems.at[place, u]).start(
+                            priority=j % priorities
+                        )
 
                 @pl.when(most >= per_dev)
                 def _():
@@ -274,13 +281,13 @@
                                 inbox_rows.at[d, pl.ds(k * pairs, pairs)], target(j), sems.at[place, u]
                             ).start()
 
-    for s in range(min(SLOTS - 1, steps)):
+    for s in range(min(slots - 1, steps)):
         fetch(jnp.int32(s))
 
     def compute(step, n):
-        place = lax.rem(step, SLOTS)
+        place = lax.rem(step, slots)
         width = n * chunk_size
-        for u in range(UNROLL):
+        for u in range(unroll):
             whole = buf.at[place, u, pl.ds(0, width // 2)]
             pltpu.make_async_copy(whole, whole, sems.at[place, u]).wait()
         column = lax.broadcasted_iota(jnp.int32, (1, width), 1)
@@ -289,8 +296,8 @@
         new_step = (new_column & (new_rows - 1)) // (2 * heads_kv)
         new_key = new_column & (2 * heads_kv - 1)
         visible = new_step <= (new_row & (STEP_COUNT - 1))
-        for u in range(UNROLL):
-            r = order_ref[0, base + step * UNROLL + u]
+        for u in range(unroll):
+            r = order_ref[0, base + step * unroll + u]
             length = lengths_ref[r]
             q = q_ref[pl.ds(pl.multiple_of(r * rows, rows), rows), :]
             kv = flat[place, u, 0:width, :]
@@ -320,11 +327,11 @@
 
     @pl.loop(0, steps)
     def _(step):
-        @pl.when(step + (SLOTS - 1) < steps)
+        @pl.when(step + (slots - 1) < steps)
         def _():
-            fetch(step + (SLOTS - 1))
-
-        count = order_ref[1, base + step * UNROLL]
+            fetch(step + (slots - 1))
+
+        count = order_ref[1, base + step * unroll]
         for n in range(1, CHUNKS + 1):
 
             @pl.when(count == n)
@@ -341,9 +348,10 @@
     requests = lengths.shape[0] // HALVES
     heads = heads_kv * GROUP
     extent = MAXP * PAGE_LENGTH * heads_kv * 2
+    unroll = UNROLLS[part]
     tokens = requests * STEP_COUNT
     return pl.pallas_call(
-        functools.partial(attend_kernel, req_count, per_dev, part * requests, requests),
+        functools.partial(attend_kernel, req_count, per_dev, part * requests, requests, unroll, PRIORITIES[part]),
         out_shape=jax.ShapeDtypeStruct((tokens, heads * HEAD_WIDTH), jnp.bfloat16),
         in_specs=[SMEM, SMEM, HBM, VMEM, VMEM, HBM, HBM],
         out_specs=VMEM,
@@ -352,13 +360,17 @@
             pltpu.VMEM((req_count, 1, heads_kv, 2, HEAD_WIDTH), jnp.bfloat16),
             pltpu.VMEM((req_count, 128), jnp.int32),
             pltpu.SMEM((req_count, 128), jnp.int32),
-            pltpu.VMEM((SLOTS, UNROLL, extent // 2, 2, HEAD_WIDTH), jnp.bfloat16),
+            pltpu.VMEM((BUFFERS // unroll, unroll, extent // 2, 2, HEAD_WIDTH), jnp.bfloat16),
             pltpu.VMEM((heads, tokens, HEAD_WIDTH), jnp.float32),
             pltpu.SemaphoreType.DMA,
-            pltpu.SemaphoreType.DMA((SLOTS, UNROLL)),
+            pltpu.SemaphoreType.DMA((BUFFERS // unroll, unroll)),
         ],
         compiler_params=params(),
-        cost_estimate=SMALL,
+        cost_estimate=pl.CostEstimate(
+            flops=16 * tokens * heads * HEAD_WIDTH * MAXP * PAGE_LENGTH,
+            bytes_accessed=requests * extent * HEAD_WIDTH * 2,
+            transcendentals=2 * tokens * heads * MAXP * PAGE_LENGTH,
+        ),
         name="attend",
     )(order, lengths, table, q, new, pages, inbox)
 
@@ -388,30 +400,24 @@
     )(x)
 
 
-def project_kernel(count, roles, where_ref, *refs):
+def project_kernel(count, roles, tile, where_ref, *refs):
     xs, (w_ref, down_ref, mask_ref), rest = refs[:count], refs[count : count + 3], refs[count + 3 :]
-    outs, low_ref, x_v, sems = rest[:roles], rest[roles], rest[roles + 1], rest[roles + 2]
+    outs, low_ref, x_v = rest[:roles], rest[roles], rest[roles + 1]
     tokens = xs[0].shape[0]
     rows = count * tokens // roles
-
-    @pl.when(pl.program_id(0) == 0)
-    def _():
-        copies = []
-        for b in range(count):
-            at = pl.multiple_of(where_ref[b] * tokens, tokens)
-            copies.append(pltpu.make_async_copy(xs[b], x_v.at[pl.ds(at, tokens)], sems.at[b]))
-        for copy in copies:
-            copy.start()
-        for copy in copies:
-            copy.wait()
-        low = dot(x_v[...], down_ref[...], ((1,), (1,)))
+    for b in range(count):
+        x_v[pl.ds(pl.multiple_of(where_ref[b] * tokens, tokens), tokens), :] = xs[b][...]
+    low = dot(x_v[...], down_ref[...], ((1,), (1,)))
+    for j in range(roles):
+        s = where_ref[count + j]
+        low_ref[s] = (low[j * rows : (j + 1) * rows] * mask_ref[s].astype(jnp.float32)).astype(jnp.bfloat16)
+
+    @pl.loop(0, w_ref.shape[1] // tile)
+    def _(i):
+        at = pl.ds(pl.multiple_of(i * tile, tile), tile)
+        y = dot(x_v[...], w_ref[:, at]).astype(jnp.bfloat16)
         for j in range(roles):
-            s = where_ref[count + j]
-            low_ref[s] = (low[j * rows : (j + 1) * rows] * mask_ref[s].astype(jnp.float32)).astype(jnp.bfloat16)
-
-    y = dot(x_v[...], w_ref[...]).astype(jnp.bfloat16)
-    for j in range(roles):
-        outs[j][...] = y[j * rows : (j + 1) * rows, :]
+            outs[j][:, at] = y[j * rows : (j + 1) * rows, :]
 
 
 def project(where, xs, w, down, mask, roles):
@@ -419,22 +425,13 @@
     tokens, width = xs[0].shape
     columns = w.shape[1]
     rows = count * tokens // roles
-    tile = min(256, columns)
-    return pl.pallas_call(
-        functools.partial(project_kernel, count, roles),
+    return pl.pallas_call(
+        functools.partial(project_kernel, count, roles, min(256, columns)),
         out_shape=[jax.ShapeDtypeStruct((rows, columns), jnp.bfloat16)] * roles
         + [jax.ShapeDtypeStruct((roles, rows, down.shape[0]), jnp.bfloat16)],
-        grid=(columns // tile,),
-        in_specs=[SMEM]
-        + [ANY] * count
-        + [
-            pl.BlockSpec((width, tile), lambda i: (0, i)),
-            pl.BlockSpec(down.shape, lambda i: (0, 0)),
-            pl.BlockSpec(mask.shape, lambda i: (0, 0, 0)),
-        ],
-        out_specs=[pl.BlockSpec((rows, tile), lambda i: (0, i))] * roles
-        + [pl.BlockSpec((roles, rows, down.shape[0]), lambda i: (0, 0, 0))],
-        scratch_shapes=[pltpu.VMEM((count * tokens, width), jnp.bfloat16), pltpu.SemaphoreType.DMA((count,))],
+        in_specs=[SMEM] + [VMEM] * (count + 3),
+        out_specs=[VMEM] * (roles + 1),
+        scratch_shapes=[pltpu.VMEM((count * tokens, width), jnp.bfloat16)],
         compiler_params=params(),
         cost_estimate=SMALL,
         name="project",
@@ -463,17 +460,11 @@
 
 
 def adapt(low, up):
-    columns = up.shape[1]
-    tile = min(256, columns)
     return pl.pallas_call(
         adapt_kernel,
-        out_shape=jax.ShapeDtypeStruct((low.shape[1], columns), jnp.float32),
-        grid=(columns // tile,),
-        in_specs=[
-            pl.BlockSpec(low.shape, lambda i: (0, 0, 0)),
-            pl.BlockSpec((up.shape[0], tile), lambda i: (0, i)),
-        ],
-        out_specs=pl.BlockSpec((low.shape[1], tile), lambda i: (0, i)),
+        out_shape=jax.ShapeDtypeStruct((low.shape[1], up.shape[1]), jnp.float32),
+        in_specs=[VMEM, VMEM],
+        out_specs=VMEM,
         compiler_params=params(),
         cost_estimate=SMALL,
         name="adapt",
@@ -576,12 +567,9 @@
     up_blocks = split_columns(adapter_up_factor.reshape(own_slots * rank, model), req_count)
     new = incoming_key_value.reshape(2, requests * STEP_COUNT, -1, HEAD_WIDTH).transpose(1, 2, 0, 3)
     new = new.reshape(-1, HEAD_WIDTH)
-    q = after(q, up_blocks)
     pages = split_heads(key_value_pages)
     inbox_pages = split_heads(inbox)
     down = adapter_down_factor.transpose(0, 2, 1).reshape(own_slots * rank, -1)
-    up = lax.all_to_all(up_blocks, "req", split_axis=0, concat_axis=0, tiled=True)
-    up = up.reshape(req_count * own_slots * rank, -1)
 
     slot_count = adapter_storage_slot.shape[0]
     ids = inbox[:, BLOCK - 1, 0, :requests].astype(jnp.int32)
@@ -604,16 +592,20 @@
         where = jnp.stack(where + roles)
         token_slot = jnp.repeat(slot[:, h * half : (h + 1) * half], STEP_COUNT, axis=1)
         mask = (token_slot.reshape(tp_count, -1)[:, :, None] == mine).astype(jnp.bfloat16)
-        mask = after(mask, passed if h else up)
+        if h:
+            mask = after(mask, passed)
         *parts, low = project(where, blocks, output_projection_weight, down, mask, tp_count)
         gates = [low]
         lows.append(low)
         sums, passed = scatter(parts)
         terms.append(sums)
 
-    low = after(jnp.concatenate(lows, axis=1), passed)
+    up = lax.all_to_all(after(up_blocks, lows[0]), "req", split_axis=0, concat_axis=0, tiled=True)
+    up = up.reshape(req_count * own_slots * rank, -1)
+    low = after(jnp.concatenate(lows, axis=1), *terms[0])
     low = lax.all_to_all(low, "tp", split_axis=0, concat_axis=0, tiled=True)
     low = jnp.sum(low.astype(jnp.float32), axis=0).astype(jnp.bfloat16)
+    low = after(low, *terms[1][:3])
     low = lax.all_gather(low, "req", axis=0)
     return finish(terms, cores, adapt(low, up))
 

time: 172 us -> 168 us (0.977)
  Pallas kernels: 69.8 us -> 58.9 us
  local copies, waits for them, and re-layouts: 8.92 us -> 15.6 us
  waiting for transfers between devices: 38.1 us -> 35.1 us
  blocking collectives: 11.1 us -> 13.7 us
    unnamed x59 -> x57, local copies, waits for them, and re-layouts: 5.84 us -> 14.6 us
    ppermute x18, waiting for transfers between devices: 18.3 us -> 10.9 us  [exchange(): return lax.ppermute(x, axis, [(i, i ^ distance) for i in range(count)])]
    pallas_call x2, Pallas kernels: 34.8 us -> 41.2 us  [attend(): pl.pallas_call(functools.partial(attend_kernel, req_count, per_dev, part...]
    pallas_call x2, Pallas kernels: 16 us -> 9.94 us  [project(): pl.pallas_call(functools.partial(project_kernel, count, roles, min(256, c...]
    pallas_call x1, Pallas kernels: 4.4 us -> 0.7 us  [adapt(): pl.pallas_call(adapt_kernel, out_shape=jax.ShapeDtypeStruct((low.shape[1]...]
    all_to_all x1, waiting for transfers between devices: 2.4 us -> 5.2 us  [on_device(): low = lax.all_to_all(low, 'tp', split_axis=0, concat_axis=0, tiled=True)]
    ppermute x18, starting transfers between devices: 17.3 us -> 20 us  [exchange(): return lax.ppermute(x, axis, [(i, i ^ distance) for i in range(count)])]
    pallas_call x2, Pallas kernels: 3.58 us -> 0.83 us  [add(): pl.pallas_call(add_kernel, out_shape=jax.ShapeDtypeStruct(a.shape, a.dtyp...]
  transfers between devices with their start and end apart: 25 -> 25, of which waited for: 7 -> 6; matrix products, arithmetic and copies ran while one was open for 4% -> 2% of each run, Pallas kernels for 32% -> 20%
where the time goes in v5:
time: 168 us; the launch traced here: 167 us
  Pallas kernels  58.9 us (35%)
  starting transfers between devices  41.2 us (25%)
  waiting for transfers between devices  35.1 us (21%)
  local copies, waits for them, and re-layouts  15.6 us (9%)
  blocking collectives  13.7 us (8%)
  other arithmetic  2.07 us (1%)
    pallas_call x2, Pallas kernels, attend(): pl.pallas_call(functools.partial(attend_kernel, req_count, per_dev, part...  41.2 us
    ppermute x18, starting transfers between devices, exchange(): return lax.ppermute(x, axis, [(i, i ^ distance) for i in range(count)])  20 us
    unnamed x57, local copies, waits for them, and re-layouts  14.6 us
    all_gather x1, blocking collectives, on_device(): low = lax.all_gather(low, 'req', axis=0)  13.7 us
    ppermute x18, waiting for transfers between devices, exchange(): return lax.ppermute(x, axis, [(i, i ^ distance) for i in range(count)])  10.9 us
    ppermute x2, waiting for transfers between devices, scatter(): onward = lax.ppermute(three, 'tp', [(0, 1), (3, 2)])  10.6 us
    pallas_call x2, Pallas kernels, project(): pl.pallas_call(functools.partial(project_kernel, count, roles, min(256, c...  9.94 us
    all_to_all x1, waiting for transfers between devices, on_device(): lax.all_to_all(outbox, 'req', split_axis=0, concat_axis=0, tiled=True)  8.38 us
  transfers between devices with their start and end apart: 25, of which 6 were waited for; matrix products, arithmetic and copies ran while one was open for 2% of the time, Pallas kernels for 20%

profile of v5, /device:TPU:0, one launch (start us, length us, event | category | flops | bytes accessed | tf_op | source)
XLA Modules:
  0.0 167.3 jit_solution(6265035092402210160)
XLA Ops:
  0.0 3.6 %pack_outbox.1 = bf16[8,65,2,256]{3,2,1,0:T(2,128)(2,1)} custom-call(s32[1]{0:T(128)} %bitcast.12.me_ref, s32[1,512]{1,0:T(1,128)} %bitcast.52, s32[1,32]{1,0:T(1,128)} %bitcast.58, bf16[512,32,2,256]{3,2,1,0:T(2,128)(2,1)} %pages.1), custom_call_target="tpu_custom_call" | custom-call | flops 1 | bytes 1 | tf_op jit(solution)/shard_map/pack_outbox/pallas_call | solution.py:111
  3.7 5.3 %all-to-all-start = ((bf16[8,65,2,256]{3,2,1,0:T(2,128)(2,1)}), bf16[8,65,2,256]{3,2,1,0:T(2,128)(2,1)S(1)}, u32[]{:S(2)}, u32[]{:S(2)}) async-start(bf16[8,65,2,256]{3,2,1,0:T(2,128)(2,1)} %pack_outbox.1), calls=%async_computation | async-start | bytes 1064960 | tf_op jit(solution)/shard_map/all_to_all | solution.py:562
  10.4 8.4 %all-to-all-done = bf16[8,65,2,256]{3,2,1,0:T(2,128)(2,1)S(1)} async-done(((bf16[8,65,2,256]{3,2,1,0:T(2,128)(2,1)}), bf16[8,65,2,256]{3,2,1,0:T(2,128)(2,1)S(1)}, u32[]{:S(2)}, u32[]{:S(2)}) %all-to-all-start) | async-done | bytes 532512 | tf_op jit(solution)/shard_map/all_to_all | solution.py:562
  18.8 5.8 %copy-done = bf16[512,32,2,256]{3,2,1,0:T(2,128)(2,1)S(1)} copy-done((bf16[512,32,2,256]{3,2,1,0:T(2,128)(2,1)S(1)}, bf16[512,32,2,256]{3,2,1,0:T(2,128)(2,1)}, u32[]{:S(2)}) %copy-start) | copy-done | bytes 16777240
  24.6 20.4 %attend.2.refs_0_ = bf16[64,2048]{1,0:T(8,128)(2,1)S(1)} custom-call(s32[2,128]{1,0:T(2,128)S(1)} %get-tuple-element.28.order_ref, s32[32]{0:T(128)S(1)} %copy-done.23, s32[4,128]{1,0:T(4,128)S(1)} %get-tuple-element.29.table_in, bf16[2048,128]{1,0:T(8,128)(2,1)S(1)} %bitcast.44, bf16[512,128]{1,0:T(8,128)(2,1)S(1)} %bitcast.50, ...), custom_call_target="tpu_custom_call" | custom-call | flops 1073741824 | bytes 8388608 | tf_op jit(solution)/shard_map/attend/pallas_call | solution.py:353
  46.7 2.2 %collective-permute-start.1 = (bf16[64,2048]{1,0:T(8,128)(2,1)S(1)}, bf16[64,2048]{1,0:T(8,128)(2,1)S(1)}, u32[]{:S(2)}, u32[]{:S(2)}) collective-permute-start(bf16[64,2048]{1,0:T(8,128)(2,1)S(1)} %attend.2.refs_0_), channel_id=1, source_target_pairs={{0,16},{4,20},{8,24},{12,28},{16,0},{20,4},{24,8},{28,12},{1,17},{... | collective-permute-start | bytes 786440 | tf_op jit(solution)/shard_map/ppermute | solution.py:504
  50.3 20.9 %attend.3.refs_0_ = bf16[64,2048]{1,0:T(8,128)(2,1)S(1)} custom-call(s32[2,128]{1,0:T(2,128)S(1)} %get-tuple-element.28.order_ref, s32[32]{0:T(128)S(1)} %copy-done.23, s32[4,128]{1,0:T(4,128)S(1)} %get-tuple-element.29.table_in, bf16[2048,128]{1,0:T(8,128)(2,1)S(1)} %bitcast.45, bf16[512,128]{1,0:T(8,128)(2,1)S(1)} %bitcast.51, ...), custom_call_target="tpu_custom_call" | custom-call | flops 1073741824 | bytes 8388608 | tf_op jit(solution)/shard_map/attend/pallas_call | solution.py:353
  73.1 3.9 %collective-permute-start.9 = (bf16[64,2048]{1,0:T(8,128)(2,1)S(1)}, bf16[64,2048]{1,0:T(8,128)(2,1)S(1)}, u32[]{:S(2)}, u32[]{:S(2)}) collective-permute-start(bf16[64,2048]{1,0:T(8,128)(2,1)S(1)} %attend.3.refs_0_), channel_id=1, source_target_pairs={{0,24},{4,28},{8,16},{12,20},{16,8},{20,12},{24,0},{28,4},{1,25},{... | collective-permute-start | bytes 786440 | tf_op jit(solution)/shard_map/ppermute | solution.py:504
  78.6 2.2 %copy-done.1 = bf16[2048,1024]{1,0:T(8,128)(2,1)S(1)} copy-done((bf16[2048,1024]{1,0:T(8,128)(2,1)S(1)}, bf16[2048,1024]{1,0:T(8,128)(2,1)}, u32[]{:S(2)}) %copy-start.1) | copy-done | bytes 4194328
  81.7 4.9 %project.2 = (bf16[128,1024]{1,0:T(8,128)(2,1)S(1)}, bf16[128,1024]{1,0:T(8,128)(2,1)S(1)}, bf16[128,1024]{1,0:T(8,128)(2,1)S(1)}, bf16[128,1024]{1,0:T(8,128)(2,1)S(1)}, bf16[4,128,128]{2,1,0:T(8,128)(2,1)S(1)}) custom-call(s32[12]{0:T(128)S(1)} %stack.64.where_ref, bf16[64,2048]{1,0:T(8,128)(2,1)S(1)} %attend.2.refs_0_, ...), custom_call_target="tpu_custom_call" | custom-call | flops 1 | bytes 1 | tf_op jit(solution)/shard_map/project/pallas_call | solution.py:428
  86.6 3.5 %collective-permute-start.14 = (bf16[128,1024]{1,0:T(8,128)(2,1)S(1)}, bf16[128,1024]{1,0:T(8,128)(2,1)S(1)}, u32[]{:S(2)}, u32[]{:S(2)}) collective-permute-start(bf16[128,1024]{1,0:T(8,128)(2,1)S(1)} %get-tuple-element.39), channel_id=1, source_target_pairs={{0,1},{3,2},{4,5},{7,6},{8,9},{11,10},{12,13},{15,14},{16,17},{19,... | collective-permute-start | bytes 786440 | tf_op jit(solution)/shard_map/ppermute | solution.py:527
  91.2 4.5 %collective-permute-done.14.b_ref = bf16[128,1024]{1,0:T(8,128)(2,1)S(1)} collective-permute-done((bf16[128,1024]{1,0:T(8,128)(2,1)S(1)}, bf16[128,1024]{1,0:T(8,128)(2,1)S(1)}, u32[]{:S(2)}, u32[]{:S(2)}) %collective-permute-start.14) | collective-permute-done | bytes 262176 | tf_op jit(solution)/shard_map/ppermute | solution.py:527
  96.5 5.4 %collective-permute-start.15 = (bf16[128,1024]{1,0:T(8,128)(2,1)S(1)}, bf16[128,1024]{1,0:T(8,128)(2,1)S(1)}, u32[]{:S(2)}, u32[]{:S(2)}) collective-permute-start(bf16[128,1024]{1,0:T(8,128)(2,1)S(1)} %get-tuple-element.43), channel_id=1, source_target_pairs={{0,1},{1,0},{2,3},{3,2},{4,5},{5,4},{6,7},{7,6},{8,9},{9,8},{10,11... | collective-permute-start | bytes 786440 | tf_op jit(solution)/shard_map/ppermute | solution.py:504
  102.8 5.0 %project.3 = (bf16[128,1024]{1,0:T(8,128)(2,1)S(1)}, bf16[128,1024]{1,0:T(8,128)(2,1)}, bf16[128,1024]{1,0:T(8,128)(2,1)S(1)}, bf16[128,1024]{1,0:T(8,128)(2,1)}, bf16[4,128,128]{2,1,0:T(8,128)(2,1)S(1)}) custom-call(s32[12]{0:T(128)S(1)} %stack.64.where_ref, bf16[64,2048]{1,0:T(8,128)(2,1)S(1)} %attend.3.refs_0_, ...), custom_call_target="tpu_custom_call" | custom-call | flops 1 | bytes 1 | tf_op jit(solution)/shard_map/project/pallas_call | solution.py:428
  109.3 8.6 %collective-permute-done.17.refs_3_ = bf16[128,1024]{1,0:T(8,128)(2,1)S(1)} collective-permute-done((bf16[128,1024]{1,0:T(8,128)(2,1)S(1)}, bf16[128,1024]{1,0:T(8,128)(2,1)S(1)}, u32[]{:S(2)}, u32[]{:S(2)}) %collective-permute-start.17) | collective-permute-done | bytes 262176 | tf_op jit(solution)/shard_map/ppermute | solution.py:504
  118.7 4.0 %all-to-all-start.1 = ((bf16[4,256,128]{2,1,0:T(8,128)(2,1)}), bf16[4,256,128]{2,1,0:T(8,128)(2,1)S(1)}, u32[]{:S(2)}, u32[]{:S(2)}) async-start(bf16[4,256,128]{2,1,0:T(8,128)(2,1)} %pad_maximum_fusion), calls=%async_computation.1 | async-start | bytes 524288 | tf_op jit(solution)/shard_map/all_to_all | solution.py:606
  124.2 5.2 %all-to-all-done.1 = bf16[4,256,128]{2,1,0:T(8,128)(2,1)S(1)} async-done(((bf16[4,256,128]{2,1,0:T(8,128)(2,1)}), bf16[4,256,128]{2,1,0:T(8,128)(2,1)S(1)}, u32[]{:S(2)}, u32[]{:S(2)}) %all-to-all-start.1) | async-done | bytes 262176 | tf_op jit(solution)/shard_map/all_to_all | solution.py:606
  129.4 3.6 %all-to-all-start.2 = ((bf16[8,128,1024]{2,1,0:T(8,128)(2,1)}), bf16[8,128,1024]{2,1,0:T(8,128)(2,1)S(1)}, u32[]{:S(2)}, u32[]{:S(2)}) async-start(bf16[8,128,1024]{2,1,0:T(8,128)(2,1)} %copy-done.3), calls=%async_computation.2 | async-start | bytes 4194304 | tf_op jit(solution)/shard_map/all_to_all | solution.py:603
  133.0 3.4 %collective-permute-start.20 = (bf16[128,1024]{1,0:T(8,128)(2,1)}, bf16[128,1024]{1,0:T(8,128)(2,1)S(1)}, u32[]{:S(2)}, u32[]{:S(2)}) collective-permute-start(bf16[128,1024]{1,0:T(8,128)(2,1)} %get-tuple-element.47), channel_id=1, source_target_pairs={{0,1},{3,2},{4,5},{7,6},{8,9},{11,10},{12,13},{15,14},{16,17},{19,... | collective-permute-start | bytes 786440 | tf_op jit(solution)/shard_map/ppermute | solution.py:527
  137.2 6.1 %collective-permute-done.20.b_ref = bf16[128,1024]{1,0:T(8,128)(2,1)S(1)} collective-permute-done((bf16[128,1024]{1,0:T(8,128)(2,1)}, bf16[128,1024]{1,0:T(8,128)(2,1)S(1)}, u32[]{:S(2)}, u32[]{:S(2)}) %collective-permute-start.20) | collective-permute-done | bytes 262176 | tf_op jit(solution)/shard_map/ppermute | solution.py:527
  144.1 1.7 %collective-permute-start.21 = (bf16[128,1024]{1,0:T(8,128)(2,1)}, bf16[128,1024]{1,0:T(8,128)(2,1)}, u32[]{:S(2)}, u32[]{:S(2)}) collective-permute-start(bf16[128,1024]{1,0:T(8,128)(2,1)} %add.111), channel_id=1, source_target_pairs={{0,2},{1,3},{2,0},{3,1},{4,6},{5,7},{6,4},{7,5},{8,10},{9,11},{10,... | collective-permute-start | bytes 786440 | tf_op jit(solution)/shard_map/ppermute | solution.py:504
  146.8 2.2 %collective-permute-done.18.refs_5_ = bf16[128,1024]{1,0:T(8,128)(2,1)S(1)} collective-permute-done((bf16[128,1024]{1,0:T(8,128)(2,1)}, bf16[128,1024]{1,0:T(8,128)(2,1)S(1)}, u32[]{:S(2)}, u32[]{:S(2)}) %collective-permute-start.18) | collective-permute-done | bytes 262176 | tf_op jit(solution)/shard_map/ppermute | solution.py:504
  150.4 13.7 %all-gather = bf16[2048,128]{1,0:T(8,128)(2,1)S(1)} all-gather(bf16[256,128]{1,0:T(8,128)(2,1)S(1)} %reduce_sum.22), channel_id=2, replica_groups=mesh['req'=8,'tp'=4] {'req'}, dimensions={0}, use_global_device_ids=true | all-gather | bytes 589824 | tf_op jit(solution)/shard_map/all_gather | solution.py:609
  165.3 2.0 %finish.1 = bf16[256,1024]{1,0:T(8,128)(2,1)} custom-call(f32[256,1024]{1,0:T(8,128)S(1)} %adapt.1.extra_ref, bf16[128,1024]{1,0:T(8,128)(2,1)S(1)} %get-tuple-element.42.refs_0_, bf16[128,1024]{1,0:T(8,128)(2,1)S(1)} %copy-done.7, bf16[128,1024]{1,0:T(8,128)(2,1)S(1)} %collective-permute-done.16.refs_2_, bf16[128,1024]{1,0:T(8,128)(2,1)S(1)} %copy-done.9, ...), custom_call_target="tpu_custom_call" | custom-call | flops 1 | bytes 1 | tf_op jit(solution)/shard_map/finish/pallas_call | solution.py:491
  (110 shorter events, 20.1 us)
Async XLA Ops:
  3.7 15.1 %all-to-all-start = ((bf16[8,65,2,256]{3,2,1,0:T(2,128)(2,1)}), bf16[8,65,2,256]{3,2,1,0:T(2,128)(2,1)S(1)}, u32[]{:S(2)}, u32[]{:S(2)}) async-start(bf16[8,65,2,256]{3,2,1,0:T(2,128)(2,1)} %pack_outbox.1), calls=%async_computation | async-start | bytes 1064960 | tf_op jit(solution)/shard_map/all_to_all | solution.py:562
  44.9 32.5 %collective-permute-start.3 = (bf16[64,2048]{1,0:T(8,128)(2,1)S(1)}, bf16[64,2048]{1,0:T(8,128)(2,1)S(1)}, u32[]{:S(2)}, u32[]{:S(2)}) collective-permute-start(bf16[64,2048]{1,0:T(8,128)(2,1)S(1)} %attend.2.refs_0_), channel_id=1, source_target_pairs={{0,4},{4,0},{8,12},{12,8},{16,20},{20,16},{24,28},{28,24},{1,5},{5... | collective-permute-start | bytes 786440 | tf_op jit(solution)/shard_map/ppermute | solution.py:504
  45.0 26.1 %collective-permute-start.2 = (bf16[64,2048]{1,0:T(8,128)(2,1)S(1)}, bf16[64,2048]{1,0:T(8,128)(2,1)S(1)}, u32[]{:S(2)}, u32[]{:S(2)}) collective-permute-start(bf16[64,2048]{1,0:T(8,128)(2,1)S(1)} %attend.2.refs_0_), channel_id=1, source_target_pairs={{0,24},{4,28},{8,16},{12,20},{16,8},{20,12},{24,0},{28,4},{1,25},{... | collective-permute-start | bytes 786440 | tf_op jit(solution)/shard_map/ppermute | solution.py:504
  46.7 25.8 %collective-permute-start.1 = (bf16[64,2048]{1,0:T(8,128)(2,1)S(1)}, bf16[64,2048]{1,0:T(8,128)(2,1)S(1)}, u32[]{:S(2)}, u32[]{:S(2)}) collective-permute-start(bf16[64,2048]{1,0:T(8,128)(2,1)S(1)} %attend.2.refs_0_), channel_id=1, source_target_pairs={{0,16},{4,20},{8,24},{12,28},{16,0},{20,4},{24,8},{28,12},{1,17},{... | collective-permute-start | bytes 786440 | tf_op jit(solution)/shard_map/ppermute | solution.py:504
  48.9 23.7 %collective-permute-start = (bf16[64,2048]{1,0:T(8,128)(2,1)S(1)}, bf16[64,2048]{1,0:T(8,128)(2,1)}, u32[]{:S(2)}, u32[]{:S(2)}) collective-permute-start(bf16[64,2048]{1,0:T(8,128)(2,1)S(1)} %attend.2.refs_0_), channel_id=1, source_target_pairs={{0,8},{4,12},{8,0},{12,4},{16,24},{20,28},{24,16},{28,20},{1,9},{5... | collective-permute-start | bytes 786440 | tf_op jit(solution)/shard_map/ppermute | solution.py:504
  71.2 7.2 %collective-permute-start.6 = (bf16[64,2048]{1,0:T(8,128)(2,1)S(1)}, bf16[64,2048]{1,0:T(8,128)(2,1)S(1)}, u32[]{:S(2)}, u32[]{:S(2)}) collective-permute-start(bf16[64,2048]{1,0:T(8,128)(2,1)S(1)} %collective-permute-done.2.refs_3_), channel_id=1, source_target_pairs={{0,4},{4,0},{8,12},{12,8},{16,20},{20,16},{24,28},{28,24},{1,5},{5... | collective-permute-start | bytes 786440 | tf_op jit(solution)/shard_map/ppermute | solution.py:504
  72.5 6.0 %collective-permute-start.5 = (bf16[64,2048]{1,0:T(8,128)(2,1)S(1)}, bf16[64,2048]{1,0:T(8,128)(2,1)S(1)}, u32[]{:S(2)}, u32[]{:S(2)}) collective-permute-start(bf16[64,2048]{1,0:T(8,128)(2,1)S(1)} %collective-permute-done.1.refs_2_), channel_id=1, source_target_pairs={{0,4},{4,0},{8,12},{12,8},{16,20},{20,16},{24,28},{28,24},{1,5},{5... | collective-permute-start | bytes 786440 | tf_op jit(solution)/shard_map/ppermute | solution.py:504
  73.1 17.1 %collective-permute-start.9 = (bf16[64,2048]{1,0:T(8,128)(2,1)S(1)}, bf16[64,2048]{1,0:T(8,128)(2,1)S(1)}, u32[]{:S(2)}, u32[]{:S(2)}) collective-permute-start(bf16[64,2048]{1,0:T(8,128)(2,1)S(1)} %attend.3.refs_0_), channel_id=1, source_target_pairs={{0,24},{4,28},{8,16},{12,20},{16,8},{20,12},{24,0},{28,4},{1,25},{... | collective-permute-start | bytes 786440 | tf_op jit(solution)/shard_map/ppermute | solution.py:504
  77.4 13.3 %collective-permute-start.8 = (bf16[64,2048]{1,0:T(8,128)(2,1)S(1)}, bf16[64,2048]{1,0:T(8,128)(2,1)S(1)}, u32[]{:S(2)}, u32[]{:S(2)}) collective-permute-start(bf16[64,2048]{1,0:T(8,128)(2,1)S(1)} %attend.3.refs_0_), channel_id=1, source_target_pairs={{0,16},{4,20},{8,24},{12,28},{16,0},{20,4},{24,8},{28,12},{1,17},{... | collective-permute-start | bytes 786440 | tf_op jit(solution)/shard_map/ppermute | solution.py:504
  78.3 12.5 %collective-permute-start.7 = (bf16[64,2048]{1,0:T(8,128)(2,1)S(1)}, bf16[64,2048]{1,0:T(8,128)(2,1)S(1)}, u32[]{:S(2)}, u32[]{:S(2)}) collective-permute-start(bf16[64,2048]{1,0:T(8,128)(2,1)S(1)} %attend.3.refs_0_), channel_id=1, source_target_pairs={{0,8},{4,12},{8,0},{12,4},{16,24},{20,28},{24,16},{28,20},{1,9},{5... | collective-permute-start | bytes 786440 | tf_op jit(solution)/shard_map/ppermute | solution.py:504
  86.6 9.1 %collective-permute-start.14 = (bf16[128,1024]{1,0:T(8,128)(2,1)S(1)}, bf16[128,1024]{1,0:T(8,128)(2,1)S(1)}, u32[]{:S(2)}, u32[]{:S(2)}) collective-permute-start(bf16[128,1024]{1,0:T(8,128)(2,1)S(1)} %get-tuple-element.39), channel_id=1, source_target_pairs={{0,1},{3,2},{4,5},{7,6},{8,9},{11,10},{12,13},{15,14},{16,17},{19,... | collective-permute-start | bytes 786440 | tf_op jit(solution)/shard_map/ppermute | solution.py:527
  90.1 6.3 %collective-permute-start.10 = (bf16[64,2048]{1,0:T(8,128)(2,1)S(1)}, bf16[64,2048]{1,0:T(8,128)(2,1)S(1)}, u32[]{:S(2)}, u32[]{:S(2)}) collective-permute-start(bf16[64,2048]{1,0:T(8,128)(2,1)S(1)} %attend.3.refs_0_), channel_id=1, source_target_pairs={{0,4},{4,0},{8,12},{12,8},{16,20},{20,16},{24,28},{28,24},{1,5},{5... | collective-permute-start | bytes 786440 | tf_op jit(solution)/shard_map/ppermute | solution.py:504
  90.2 11.6 %collective-permute-start.13 = (bf16[64,2048]{1,0:T(8,128)(2,1)S(1)}, bf16[64,2048]{1,0:T(8,128)(2,1)S(1)}, u32[]{:S(2)}, u32[]{:S(2)}) collective-permute-start(bf16[64,2048]{1,0:T(8,128)(2,1)S(1)} %collective-permute-done.9.refs_3_), channel_id=1, source_target_pairs={{0,4},{4,0},{8,12},{12,8},{16,20},{20,16},{24,28},{28,24},{1,5},{5... | collective-permute-start | bytes 786440 | tf_op jit(solution)/shard_map/ppermute | solution.py:504
  90.7 11.1 %collective-permute-start.12 = (bf16[64,2048]{1,0:T(8,128)(2,1)S(1)}, bf16[64,2048]{1,0:T(8,128)(2,1)S(1)}, u32[]{:S(2)}, u32[]{:S(2)}) collective-permute-start(bf16[64,2048]{1,0:T(8,128)(2,1)S(1)} %collective-permute-done.8.refs_2_), channel_id=1, source_target_pairs={{0,4},{4,0},{8,12},{12,8},{16,20},{20,16},{24,28},{28,24},{1,5},{5... | collective-permute-start | bytes 786440 | tf_op jit(solution)/shard_map/ppermute | solution.py:504
  90.8 11.0 %collective-permute-start.11 = (bf16[64,2048]{1,0:T(8,128)(2,1)S(1)}, bf16[64,2048]{1,0:T(8,128)(2,1)S(1)}, u32[]{:S(2)}, u32[]{:S(2)}) collective-permute-start(bf16[64,2048]{1,0:T(8,128)(2,1)S(1)} %collective-permute-done.7.refs_1_), channel_id=1, source_target_pairs={{0,4},{4,0},{8,12},{12,8},{16,20},{20,16},{24,28},{28,24},{1,5},{5... | collective-permute-start | bytes 786440 | tf_op jit(solution)/shard_map/ppermute | solution.py:504
  95.7 13.6 %collective-permute-start.16 = (bf16[128,1024]{1,0:T(8,128)(2,1)S(1)}, bf16[128,1024]{1,0:T(8,128)(2,1)S(1)}, u32[]{:S(2)}, u32[]{:S(2)}) collective-permute-start(bf16[128,1024]{1,0:T(8,128)(2,1)S(1)} %get-tuple-element.39), channel_id=1, source_target_pairs={{1,2},{2,1},{5,6},{6,5},{9,10},{10,9},{13,14},{14,13},{17,18},{18,... | collective-permute-start | bytes 786440 | tf_op jit(solution)/shard_map/ppermute | solution.py:528
  96.5 12.2 %collective-permute-start.15 = (bf16[128,1024]{1,0:T(8,128)(2,1)S(1)}, bf16[128,1024]{1,0:T(8,128)(2,1)S(1)}, u32[]{:S(2)}, u32[]{:S(2)}) collective-permute-start(bf16[128,1024]{1,0:T(8,128)(2,1)S(1)} %get-tuple-element.43), channel_id=1, source_target_pairs={{0,1},{1,0},{2,3},{3,2},{4,5},{5,4},{6,7},{7,6},{8,9},{9,8},{10,11... | collective-permute-start | bytes 786440 | tf_op jit(solution)/shard_map/ppermute | solution.py:504
  101.8 16.1 %collective-permute-start.17 = (bf16[128,1024]{1,0:T(8,128)(2,1)S(1)}, bf16[128,1024]{1,0:T(8,128)(2,1)S(1)}, u32[]{:S(2)}, u32[]{:S(2)}) collective-permute-start(bf16[128,1024]{1,0:T(8,128)(2,1)S(1)} %add.110), channel_id=1, source_target_pairs={{0,2},{1,3},{2,0},{3,1},{4,6},{5,7},{6,4},{7,5},{8,10},{9,11},{10,... | collective-permute-start | bytes 786440 | tf_op jit(solution)/shard_map/ppermute | solution.py:504
  118.7 10.7 %all-to-all-start.1 = ((bf16[4,256,128]{2,1,0:T(8,128)(2,1)}), bf16[4,256,128]{2,1,0:T(8,128)(2,1)S(1)}, u32[]{:S(2)}, u32[]{:S(2)}) async-start(bf16[4,256,128]{2,1,0:T(8,128)(2,1)} %pad_maximum_fusion), calls=%async_computation.1 | async-start | bytes 524288 | tf_op jit(solution)/shard_map/all_to_all | solution.py:606
  129.4 34.7 %all-to-all-start.2 = ((bf16[8,128,1024]{2,1,0:T(8,128)(2,1)}), bf16[8,128,1024]{2,1,0:T(8,128)(2,1)S(1)}, u32[]{:S(2)}, u32[]{:S(2)}) async-start(bf16[8,128,1024]{2,1,0:T(8,128)(2,1)} %copy-done.3), calls=%async_computation.2 | async-start | bytes 4194304 | tf_op jit(solution)/shard_map/all_to_all | solution.py:603
  133.0 10.3 %collective-permute-start.20 = (bf16[128,1024]{1,0:T(8,128)(2,1)}, bf16[128,1024]{1,0:T(8,128)(2,1)S(1)}, u32[]{:S(2)}, u32[]{:S(2)}) collective-permute-start(bf16[128,1024]{1,0:T(8,128)(2,1)} %get-tuple-element.47), channel_id=1, source_target_pairs={{0,1},{3,2},{4,5},{7,6},{8,9},{11,10},{12,13},{15,14},{16,17},{19,... | collective-permute-start | bytes 786440 | tf_op jit(solution)/shard_map/ppermute | solution.py:527
  136.5 12.5 %collective-permute-start.18 = (bf16[128,1024]{1,0:T(8,128)(2,1)}, bf16[128,1024]{1,0:T(8,128)(2,1)S(1)}, u32[]{:S(2)}, u32[]{:S(2)}) collective-permute-start(bf16[128,1024]{1,0:T(8,128)(2,1)} %get-tuple-element.46), channel_id=1, source_target_pairs={{0,1},{1,0},{2,3},{3,2},{4,5},{5,4},{6,7},{7,6},{8,9},{9,8},{10,11... | collective-permute-start | bytes 786440 | tf_op jit(solution)/shard_map/ppermute | solution.py:504
  136.5 13.2 %collective-permute-start.19 = (bf16[128,1024]{1,0:T(8,128)(2,1)}, bf16[128,1024]{1,0:T(8,128)(2,1)S(1)}, u32[]{:S(2)}, u32[]{:S(2)}) collective-permute-start(bf16[128,1024]{1,0:T(8,128)(2,1)} %get-tuple-element.47), channel_id=1, source_target_pairs={{1,2},{2,1},{5,6},{6,5},{9,10},{10,9},{13,14},{14,13},{17,18},{18,... | collective-permute-start | bytes 786440 | tf_op jit(solution)/shard_map/ppermute | solution.py:528
  144.1 20.7 %collective-permute-start.21 = (bf16[128,1024]{1,0:T(8,128)(2,1)}, bf16[128,1024]{1,0:T(8,128)(2,1)}, u32[]{:S(2)}, u32[]{:S(2)}) collective-permute-start(bf16[128,1024]{1,0:T(8,128)(2,1)} %add.111), channel_id=1, source_target_pairs={{0,2},{1,3},{2,0},{3,1},{4,6},{5,7},{6,4},{7,5},{8,10},{9,11},{10,... | collective-permute-start | bytes 786440 | tf_op jit(solution)/shard_map/ppermute | solution.py:504
  (29 other events, 226.9 us)

commit v6 on v5

--- a/solution.py
+++ b/solution.py
@@ -22,9 +22,8 @@
 CHUNK_PAGES = 4
 CHUNKS = MAXP // CHUNK_PAGES
 CHUNK_POSITIONS = CHUNK_PAGES * PAGE_LENGTH
-BUFFERS = 12
-UNROLLS = (2, 4)
-PRIORITIES = (2, 1)
+UNROLL = 4
+STAGE_PARTS = 8
 HALVES = 2
 VMEM_LIMIT = 24 * 1024 * 1024
 WHOLE_VMEM = 60 * 1024 * 1024
@@ -177,13 +176,36 @@
     )(me, page_request_home.reshape(per_dev // 128, 128), lengths.reshape(1, requests))
 
 
+def stage_kernel(x_ref, o_ref, sems):
+    step = x_ref.shape[0] // STAGE_PARTS
+    copies = []
+    for i in range(STAGE_PARTS):
+        at = pl.ds(i * step, step)
+        copies.append(pltpu.make_async_copy(x_ref.at[at], o_ref.at[at], sems.at[i]))
+    for copy in copies:
+        copy.start()
+    for copy in copies:
+        copy.wait()
+
+
+def stage(pages):
+    return pl.pallas_call(
+        stage_kernel,
+        out_shape=jax.ShapeDtypeStruct(pages.shape, pages.dtype),
+        in_specs=[HBM],
+        out_specs=VMEM,
+        scratch_shapes=[pltpu.SemaphoreType.DMA((STAGE_PARTS,))],
+        compiler_params=params(),
+        cost_estimate=pl.CostEstimate(flops=0, bytes_accessed=2 * pages.size * 2, transcendentals=0),
+        name="stage",
+    )(pages)
+
+
 def attend_kernel(
     req_count,
     per_dev,
     base,
     requests,
-    unroll,
-    priorities,
     order_ref,
     lengths_ref,
     table_in,
@@ -193,13 +215,11 @@
     inbox,
     out_ref,
     table,
-    labels_v,
     labels_w,
     labels_s,
     buf,
     acc,
     sem,
-    sems,
 ):
     heads_kv = pages.shape[2]
     page_size = PAGE_LENGTH * heads_kv * 2
@@ -210,20 +230,16 @@
     rows = heads_kv * half
     heads = heads_kv * GROUP
     scale = math.log2(math.e) / math.sqrt(HEAD_WIDTH)
-    pairs = PAGE_LENGTH * heads_kv
-    page_rows = pages.reshape(per_dev, pairs, 2, HEAD_WIDTH)
-    inbox_rows = inbox.reshape(req_count, BLOCK * heads_kv, 2, HEAD_WIDTH)
+    page_rows = pages.reshape(per_dev, page_size, HEAD_WIDTH)
+    inbox_rows = inbox.reshape(req_count, BLOCK * heads_kv * 2, HEAD_WIDTH)
 
     tab = pltpu.make_async_copy(table_in, table, sem)
     tab.start()
     tab.wait()
-    first = pltpu.make_async_copy(inbox.at[:, pl.ds(BLOCK - 1, 1)], labels_v, sem)
-    first.start()
-    first.wait()
     row = lax.broadcasted_iota(jnp.int32, (2, 128), 0)
     weight = jnp.where(row == 0, float(DIGIT), 1.0)
     for d in range(req_count):
-        digits = labels_v[d, 0, 0, :, :].astype(jnp.float32) * weight
+        digits = inbox[d, BLOCK - 1, 0, :, :].astype(jnp.float32) * weight
         labels_w[d : d + 1, :] = jnp.sum(digits, axis=0, keepdims=True).astype(jnp.int32)
     back = pltpu.make_async_copy(labels_w, labels_s, sem)
     back.start()
@@ -236,15 +252,12 @@
             def _():
                 table[lax.shift_right_logical(slot, 7), slot & 127] = per_dev + d * CAP + k
 
-    slots = BUFFERS // unroll
-    steps = requests // unroll
-    flat = buf.reshape(slots, unroll, MAXP * page_size, HEAD_WIDTH)
+    steps = requests // UNROLL
 
     def fetch(step):
-        place = lax.rem(step, slots)
-        count = order_ref[1, base + step * unroll]
-        for u in range(unroll):
-            slot = order_ref[0, base + step * unroll + u] * MAXP
+        count = order_ref[1, base + step * UNROLL]
+        for u in range(UNROLL):
+            slot = order_ref[0, base + step * UNROLL + u] * MAXP
             line = lax.shift_right_logical(slot, 7)
             at = slot & 127
 
@@ -253,15 +266,14 @@
                 sources = [table[line, at + c * CHUNK_PAGES + j] for j in range(CHUNK_PAGES)]
                 most = functools.reduce(jnp.maximum, sources)
 
-                def target(j):
-                    return buf.at[place, u, pl.ds((c * CHUNK_PAGES + j) * pairs, pairs)]
+                def put(j, page):
+                    start = pl.multiple_of(c * chunk_size + j * page_size, page_size)
+                    buf[u, pl.ds(start, page_size), :] = page
 
                 @pl.when(most < per_dev)
                 def _():
                     for j in range(CHUNK_PAGES):
-                        pltpu.make_async_copy(page_rows.at[sources[j]], target(j), sems.at[place, u]).start(
-                            priority=j % priorities
-                        )
+                        put(j, page_rows[sources[j]])
 
                 @pl.when(most >= per_dev)
                 def _():
@@ -270,37 +282,35 @@
 
                         @pl.when(source < per_dev)
                         def _():
-                            pltpu.make_async_copy(page_rows.at[source], target(j), sems.at[place, u]).start()
+                            put(j, page_rows[source])
 
                         @pl.when(source >= per_dev)
                         def _():
                             e = source - per_dev
                             d = lax.shift_right_logical(e, 1)
                             k = e - d * CAP
-                            pltpu.make_async_copy(
-                                inbox_rows.at[d, pl.ds(k * pairs, pairs)], target(j), sems.at[place, u]
-                            ).start()
-
-    for s in range(min(slots - 1, steps)):
-        fetch(jnp.int32(s))
+
+                            @pl.when(k == 0)
+                            def _():
+                                put(j, inbox_rows[d, 0:page_size])
+
+                            @pl.when(k == 1)
+                            def _():
+                                put(j, inbox_rows[d, page_size : 2 * page_size])
 
     def compute(step, n):
-        place = lax.rem(step, slots)
         width = n * chunk_size
-        for u in range(unroll):
-            whole = buf.at[place, u, pl.ds(0, width // 2)]
-            pltpu.make_async_copy(whole, whole, sems.at[place, u]).wait()
         column = lax.broadcasted_iota(jnp.int32, (1, width), 1)
         new_column = lax.broadcasted_iota(jnp.int32, (half, 128), 1)
         new_row = lax.broadcasted_iota(jnp.int32, (half, 128), 0)
         new_step = (new_column & (new_rows - 1)) // (2 * heads_kv)
         new_key = new_column & (2 * heads_kv - 1)
         visible = new_step <= (new_row & (STEP_COUNT - 1))
-        for u in range(unroll):
-            r = order_ref[0, base + step * unroll + u]
+        for u in range(UNROLL):
+            r = order_ref[0, base + step * UNROLL + u]
             length = lengths_ref[r]
             q = q_ref[pl.ds(pl.multiple_of(r * rows, rows), rows), :]
-            kv = flat[place, u, 0:width, :]
+            kv = buf[u, 0:width, :]
             group = r // new_group
             new = new_ref[pl.ds(pl.multiple_of(group * 128, 128), 128), :]
             seen = visible & (new_column // new_rows == r - group * new_group)
@@ -327,11 +337,8 @@
 
     @pl.loop(0, steps)
     def _(step):
-        @pl.when(step + (slots - 1) < steps)
-        def _():
-            fetch(step + (slots - 1))
-
-        count = order_ref[1, base + step * unroll]
+        fetch(step)
+        count = order_ref[1, base + step * UNROLL]
         for n in range(1, CHUNKS + 1):
 
             @pl.when(count == n)
@@ -348,22 +355,19 @@
     requests = lengths.shape[0] // HALVES
     heads = heads_kv * GROUP
     extent = MAXP * PAGE_LENGTH * heads_kv * 2
-    unroll = UNROLLS[part]
     tokens = requests * STEP_COUNT
     return pl.pallas_call(
-        functools.partial(attend_kernel, req_count, per_dev, part * requests, requests, unroll, PRIORITIES[part]),
+        functools.partial(attend_kernel, req_count, per_dev, part * requests, requests),
         out_shape=jax.ShapeDtypeStruct((tokens, heads * HEAD_WIDTH), jnp.bfloat16),
-        in_specs=[SMEM, SMEM, HBM, VMEM, VMEM, HBM, HBM],
+        in_specs=[SMEM, SMEM, ANY, VMEM, VMEM, VMEM, VMEM],
         out_specs=VMEM,
         scratch_shapes=[
             pltpu.SMEM((per_dev // 128, 128), jnp.int32),
-            pltpu.VMEM((req_count, 1, heads_kv, 2, HEAD_WIDTH), jnp.bfloat16),
             pltpu.VMEM((req_count, 128), jnp.int32),
             pltpu.SMEM((req_count, 128), jnp.int32),
-            pltpu.VMEM((BUFFERS // unroll, unroll, extent // 2, 2, HEAD_WIDTH), jnp.bfloat16),
+            pltpu.VMEM((UNROLL, extent, HEAD_WIDTH), jnp.bfloat16),
             pltpu.VMEM((heads, tokens, HEAD_WIDTH), jnp.float32),
             pltpu.SemaphoreType.DMA,
-            pltpu.SemaphoreType.DMA((BUFFERS // unroll, unroll)),
         ],
         compiler_params=params(),
         cost_estimate=pl.CostEstimate(
@@ -567,10 +571,12 @@
     up_blocks = split_columns(adapter_up_factor.reshape(own_slots * rank, model), req_count)
     new = incoming_key_value.reshape(2, requests * STEP_COUNT, -1, HEAD_WIDTH).transpose(1, 2, 0, 3)
     new = new.reshape(-1, HEAD_WIDTH)
-    pages = split_heads(key_value_pages)
+    pages = stage(split_heads(after(key_value_pages, outbox)))
     inbox_pages = split_heads(inbox)
     down = adapter_down_factor.transpose(0, 2, 1).reshape(own_slots * rank, -1)
 
+    up = lax.all_to_all(up_blocks, "req", split_axis=0, concat_axis=0, tiled=True)
+    up = up.reshape(req_count * own_slots * rank, -1)
     slot_count = adapter_storage_slot.shape[0]
     ids = inbox[:, BLOCK - 1, 0, :requests].astype(jnp.int32)
     match = ids[:, :, None] == jnp.arange(slot_count, dtype=jnp.int32)
@@ -592,21 +598,18 @@
         where = jnp.stack(where + roles)
         token_slot = jnp.repeat(slot[:, h * half : (h + 1) * half], STEP_COUNT, axis=1)
         mask = (token_slot.reshape(tp_count, -1)[:, :, None] == mine).astype(jnp.bfloat16)
-        if h:
-            mask = after(mask, passed)
+        mask = after(mask, *([passed, *terms[0][:3]] if h else [up]))
         *parts, low = project(where, blocks, output_projection_weight, down, mask, tp_count)
         gates = [low]
         lows.append(low)
         sums, passed = scatter(parts)
         terms.append(sums)
 
-    up = lax.all_to_all(after(up_blocks, lows[0]), "req", split_axis=0, concat_axis=0, tiled=True)
-    up = up.reshape(req_count * own_slots * rank, -1)
-    low = after(jnp.concatenate(lows, axis=1), *terms[0])
+    low = after(jnp.concatenate(lows, axis=1), passed, *terms[0])
     low = lax.all_to_all(low, "tp", split_axis=0, concat_axis=0, tiled=True)
     low = jnp.sum(low.astype(jnp.float32), axis=0).astype(jnp.bfloat16)
     low = after(low, *terms[1][:3])
-    low = lax.all_gather(low, "req", axis=0)
+    low = after(lax.all_gather(low, "req", axis=0), *terms[1])
     return finish(terms, cores, adapt(low, up))
 
 

time: 168 us -> 176 us (1.048)
  the two profiles are of different devices: /device:TPU:0 before, /device:TPU:9 now
where the time goes in v6:
time: 176 us
  Pallas kernels  55.6 us (32%)
  starting transfers between devices  47.6 us (27%)
  waiting for transfers between devices  28.5 us (16%)
  local copies, waits for them, and re-layouts  23.7 us (13%)
  blocking collectives  16.3 us (9%)
  other arithmetic  3.28 us (2%)
    pallas_call x2, Pallas kernels, attend(): pl.pallas_call(functools.partial(attend_kernel, req_count, per_dev, part...  32.9 us
    unnamed x51, local copies, waits for them, and re-layouts  22.2 us
    ppermute x18, starting transfers between devices, exchange(): return lax.ppermute(x, axis, [(i, i ^ distance) for i in range(count)])  21.9 us
    all_gather x1, blocking collectives, on_device(): low = after(lax.all_gather(low, 'req', axis=0), *terms[1])  16.3 us
    ppermute x18, waiting for transfers between devices, exchange(): return lax.ppermute(x, axis, [(i, i ^ distance) for i in range(count)])  12 us
    pallas_call x2, Pallas kernels, project(): pl.pallas_call(functools.partial(project_kernel, count, roles, min(256, c...  9.5 us
    ppermute x2, starting transfers between devices, scatter(): middle = lax.ppermute(three, 'tp', [(1, 2), (2, 1)])  7.42 us
    all_to_all x1, starting transfers between devices, on_device(): lax.all_to_all(up_blocks, 'req', split_axis=0, concat_axis=0, tiled=True)  6.57 us
  transfers between devices with their start and end apart: 25, of which 9 were waited for; matrix products, arithmetic and copies ran while one was open for 3% of the time, Pallas kernels for 25%

profile of v6, /device:TPU:9, one launch (start us, length us, event | category | flops | bytes accessed | tf_op | source)
XLA Modules:
  0.0 175.8 jit_solution(6174300260237828453)
XLA Ops:
  0.0 3.7 %pack_outbox.1 = bf16[8,65,2,256]{3,2,1,0:T(2,128)(2,1)} custom-call(s32[1]{0:T(128)} %bitcast.12.me_ref, s32[1,512]{1,0:T(1,128)} %bitcast.50, s32[1,32]{1,0:T(1,128)} %bitcast.57, bf16[512,32,2,256]{3,2,1,0:T(2,128)(2,1)} %pages.1), custom_call_target="tpu_custom_call" | custom-call | flops 1 | bytes 1 | tf_op jit(solution)/shard_map/pack_outbox/pallas_call | solution.py:110
  3.7 4.5 %all-to-all-start = ((bf16[8,65,2,256]{3,2,1,0:T(2,128)(2,1)}), bf16[8,65,2,256]{3,2,1,0:T(2,128)(2,1)S(1)}, u32[]{:S(2)}, u32[]{:S(2)}) async-start(bf16[8,65,2,256]{3,2,1,0:T(2,128)(2,1)} %pack_outbox.1), calls=%async_computation | async-start | bytes 1064960 | tf_op jit(solution)/shard_map/all_to_all | solution.py:566
  9.8 5.2 %all-to-all-done = bf16[8,65,2,256]{3,2,1,0:T(2,128)(2,1)S(1)} async-done(((bf16[8,65,2,256]{3,2,1,0:T(2,128)(2,1)}), bf16[8,65,2,256]{3,2,1,0:T(2,128)(2,1)S(1)}, u32[]{:S(2)}, u32[]{:S(2)}) %all-to-all-start) | async-done | bytes 532512 | tf_op jit(solution)/shard_map/all_to_all | solution.py:566
  15.0 6.6 %all-to-all-start.1 = ((bf16[8,128,1024]{2,1,0:T(8,128)(2,1)}), bf16[8,128,1024]{2,1,0:T(8,128)(2,1)S(1)}, u32[]{:S(2)}, u32[]{:S(2)}) async-start(bf16[8,128,1024]{2,1,0:T(8,128)(2,1)} %copy-done.4), calls=%async_computation.1 | async-start | bytes 4194304 | tf_op jit(solution)/shard_map/all_to_all | solution.py:578
  22.8 5.9 %stage.1.pages = bf16[512,32,2,2,128]{4,3,2,1,0:T(2,128)(2,1)S(1)} custom-call(bf16[512,32,2,2,128]{4,3,2,1,0:T(2,128)(2,1)} %bitcast.53), custom_call_target="tpu_custom_call" | custom-call | bytes 33554432 | tf_op jit(solution)/shard_map/stage/pallas_call | solution.py:192
  28.8 5.8 %copy-done = bf16[512,32,2,2,128]{4,3,2,1,0:T(2,128)(2,1)} copy-done((bf16[512,32,2,2,128]{4,3,2,1,0:T(2,128)(2,1)}, bf16[512,32,2,2,128]{4,3,2,1,0:T(2,128)(2,1)S(1)}, u32[]{:S(2)}) %copy-start) | copy-done | bytes 16777240
  35.7 5.8 %copy-done.1 = bf16[512,32,2,2,128]{4,3,2,1,0:T(2,128)(2,1)S(1)} copy-done((bf16[512,32,2,2,128]{4,3,2,1,0:T(2,128)(2,1)S(1)}, bf16[512,32,2,2,128]{4,3,2,1,0:T(2,128)(2,1)}, u32[]{:S(2)}) %copy-start.1) | copy-done | bytes 16777240
  41.5 16.4 %attend.2.refs_0_ = bf16[64,2048]{1,0:T(8,128)(2,1)} custom-call(s32[2,128]{1,0:T(2,128)S(1)} %get-tuple-element.30.order_ref, s32[32]{0:T(128)S(1)} %copy-done.15, s32[4,128]{1,0:T(4,128)S(1)} %get-tuple-element.31.table_in, bf16[2048,128]{1,0:T(8,128)(2,1)S(1)} %bitcast.42, bf16[512,128]{1,0:T(8,128)(2,1)S(1)} %bitcast.48, ...), custom_call_target="tpu_custom_call" | custom-call | flops 1073741824 | bytes 8388608 | tf_op jit(solution)/shard_map/attend/pallas_call | solution.py:359
  64.2 16.5 %attend.3.refs_0_ = bf16[64,2048]{1,0:T(8,128)(2,1)S(1)} custom-call(s32[2,128]{1,0:T(2,128)S(1)} %copy-done.19, s32[32]{0:T(128)S(1)} %copy-done.15, s32[4,128]{1,0:T(4,128)S(1)} %get-tuple-element.31.table_in, bf16[2048,128]{1,0:T(8,128)(2,1)S(1)} %bitcast.43, bf16[512,128]{1,0:T(8,128)(2,1)S(1)} %bitcast.49, bf16[512,32,2,2,128]{4,3,2,1,0:T(2,128)(2,1)S(1)} %copy-done.1, ...), custom_call_target="tpu_custom_call" | custom-call | flops 1073741824 | bytes 8388608 | tf_op jit(solution)/shard_map/attend/pallas_call | solution.py:359
  87.6 2.2 %copy-done.2 = bf16[2048,1024]{1,0:T(8,128)(2,1)S(1)} copy-done((bf16[2048,1024]{1,0:T(8,128)(2,1)S(1)}, bf16[2048,1024]{1,0:T(8,128)(2,1)}, u32[]{:S(2)}) %copy-start.2) | copy-done | bytes 4194328
  93.3 5.2 %project.2 = (bf16[128,1024]{1,0:T(8,128)(2,1)S(1)}, bf16[128,1024]{1,0:T(8,128)(2,1)S(1)}, bf16[128,1024]{1,0:T(8,128)(2,1)S(1)}, bf16[128,1024]{1,0:T(8,128)(2,1)S(1)}, bf16[4,128,128]{2,1,0:T(8,128)(2,1)S(1)}) custom-call(s32[12]{0:T(128)S(1)} %copy-done.16, bf16[64,2048]{1,0:T(8,128)(2,1)} %attend.2.refs_0_, ...), custom_call_target="tpu_custom_call" | custom-call | flops 1 | bytes 1 | tf_op jit(solution)/shard_map/project/pallas_call | solution.py:432
  103.5 3.2 %collective-permute-start.16 = (bf16[128,1024]{1,0:T(8,128)(2,1)S(1)}, bf16[128,1024]{1,0:T(8,128)(2,1)S(1)}, u32[]{:S(2)}, u32[]{:S(2)}) collective-permute-start(bf16[128,1024]{1,0:T(8,128)(2,1)S(1)} %get-tuple-element.43), channel_id=1, source_target_pairs={{1,2},{2,1},{5,6},{6,5},{9,10},{10,9},{13,14},{14,13},{17,18},{18,... | collective-permute-start | bytes 786440 | tf_op jit(solution)/shard_map/ppermute | solution.py:532
  107.4 3.2 %collective-permute-start.12 = (bf16[64,2048]{1,0:T(8,128)(2,1)S(1)}, bf16[64,2048]{1,0:T(8,128)(2,1)S(1)}, u32[]{:S(2)}, u32[]{:S(2)}) collective-permute-start(bf16[64,2048]{1,0:T(8,128)(2,1)S(1)} %collective-permute-done.8.refs_2_), channel_id=1, source_target_pairs={{0,4},{4,0},{8,12},{12,8},{16,20},{20,16},{24,28},{28,24},{1,5},{5... | collective-permute-start | bytes 786440 | tf_op jit(solution)/shard_map/ppermute | solution.py:508
  110.6 2.4 %collective-permute-done.15.refs_1_ = bf16[128,1024]{1,0:T(8,128)(2,1)S(1)} collective-permute-done((bf16[128,1024]{1,0:T(8,128)(2,1)S(1)}, bf16[128,1024]{1,0:T(8,128)(2,1)S(1)}, u32[]{:S(2)}, u32[]{:S(2)}) %collective-permute-start.15) | collective-permute-done | bytes 262176 | tf_op jit(solution)/shard_map/ppermute | solution.py:508
  116.0 4.3 %project.3 = (bf16[128,1024]{1,0:T(8,128)(2,1)S(1)}, bf16[128,1024]{1,0:T(8,128)(2,1)S(1)}, bf16[128,1024]{1,0:T(8,128)(2,1)S(1)}, bf16[128,1024]{1,0:T(8,128)(2,1)S(1)}, bf16[4,128,128]{2,1,0:T(8,128)(2,1)S(1)}) custom-call(s32[12]{0:T(128)S(1)} %copy-done.17, bf16[64,2048]{1,0:T(8,128)(2,1)S(1)} %attend.3.refs_0_, ...), custom_call_target="tpu_custom_call" | custom-call | flops 1 | bytes 1 | tf_op jit(solution)/shard_map/project/pallas_call | solution.py:432
  122.4 3.2 %collective-permute-start.18 = (bf16[128,1024]{1,0:T(8,128)(2,1)S(1)}, bf16[128,1024]{1,0:T(8,128)(2,1)S(1)}, u32[]{:S(2)}, u32[]{:S(2)}) collective-permute-start(bf16[128,1024]{1,0:T(8,128)(2,1)S(1)} %add.110), channel_id=1, source_target_pairs={{0,2},{1,3},{2,0},{3,1},{4,6},{5,7},{6,4},{7,5},{8,10},{9,11},{10,... | collective-permute-start | bytes 786440 | tf_op jit(solution)/shard_map/ppermute | solution.py:508
  126.3 4.2 %collective-permute-done.17.b_ref = bf16[128,1024]{1,0:T(8,128)(2,1)S(1)} collective-permute-done((bf16[128,1024]{1,0:T(8,128)(2,1)S(1)}, bf16[128,1024]{1,0:T(8,128)(2,1)S(1)}, u32[]{:S(2)}, u32[]{:S(2)}) %collective-permute-start.17) | collective-permute-done | bytes 262176 | tf_op jit(solution)/shard_map/ppermute | solution.py:531
  131.3 5.9 %collective-permute-done.18.refs_3_ = bf16[128,1024]{1,0:T(8,128)(2,1)S(1)} collective-permute-done((bf16[128,1024]{1,0:T(8,128)(2,1)S(1)}, bf16[128,1024]{1,0:T(8,128)(2,1)S(1)}, u32[]{:S(2)}, u32[]{:S(2)}) %collective-permute-start.18) | collective-permute-done | bytes 262176 | tf_op jit(solution)/shard_map/ppermute | solution.py:508
  137.2 4.5 %all-to-all-start.2 = ((bf16[4,256,128]{2,1,0:T(8,128)(2,1)}), bf16[4,256,128]{2,1,0:T(8,128)(2,1)}, u32[]{:S(2)}, u32[]{:S(2)}) async-start(bf16[4,256,128]{2,1,0:T(8,128)(2,1)} %pad_maximum_fusion), calls=%async_computation.2 | async-start | bytes 524288 | tf_op jit(solution)/shard_map/all_to_all | solution.py:609
  141.7 4.2 %collective-permute-start.20 = (bf16[128,1024]{1,0:T(8,128)(2,1)}, bf16[128,1024]{1,0:T(8,128)(2,1)}, u32[]{:S(2)}, u32[]{:S(2)}) collective-permute-start(bf16[128,1024]{1,0:T(8,128)(2,1)} %copy-done.20), channel_id=1, source_target_pairs={{1,2},{2,1},{5,6},{6,5},{9,10},{10,9},{13,14},{14,13},{17,18},{18,... | collective-permute-start | bytes 786440 | tf_op jit(solution)/shard_map/ppermute | solution.py:532
  148.2 2.6 %collective-permute-done.19.refs_5_ = bf16[128,1024]{1,0:T(8,128)(2,1)} collective-permute-done((bf16[128,1024]{1,0:T(8,128)(2,1)}, bf16[128,1024]{1,0:T(8,128)(2,1)}, u32[]{:S(2)}, u32[]{:S(2)}) %collective-permute-start.19) | collective-permute-done | bytes 262176 | tf_op jit(solution)/shard_map/ppermute | solution.py:508
  150.8 5.7 %collective-permute-done.20.refs_6_ = bf16[128,1024]{1,0:T(8,128)(2,1)} collective-permute-done((bf16[128,1024]{1,0:T(8,128)(2,1)}, bf16[128,1024]{1,0:T(8,128)(2,1)}, u32[]{:S(2)}, u32[]{:S(2)}) %collective-permute-start.20) | collective-permute-done | bytes 262176 | tf_op jit(solution)/shard_map/ppermute | solution.py:532
  156.5 16.3 %all-gather = bf16[2048,128]{1,0:T(8,128)(2,1)S(1)} all-gather(bf16[256,128]{1,0:T(8,128)(2,1)S(1)} %reduce_sum.22), channel_id=2, replica_groups=mesh['req'=8,'tp'=4] {'req'}, dimensions={0}, use_global_device_ids=true | all-gather | bytes 589824 | tf_op jit(solution)/shard_map/all_gather | solution.py:612
  173.6 2.2 %finish.1 = bf16[256,1024]{1,0:T(8,128)(2,1)} custom-call(f32[256,1024]{1,0:T(8,128)S(1)} %adapt.1.extra_ref, bf16[128,1024]{1,0:T(8,128)(2,1)S(1)} %get-tuple-element.44.refs_0_, bf16[128,1024]{1,0:T(8,128)(2,1)S(1)} %collective-permute-done.15.refs_1_, bf16[128,1024]{1,0:T(8,128)(2,1)S(1)} %collective-permute-done.16.refs_2_, ...), custom_call_target="tpu_custom_call" | custom-call | flops 1 | bytes 1 | tf_op jit(solution)/shard_map/finish/pallas_call | solution.py:495
  (105 shorter events, 35.4 us)
Async XLA Ops:
  3.7 11.2 %all-to-all-start = ((bf16[8,65,2,256]{3,2,1,0:T(2,128)(2,1)}), bf16[8,65,2,256]{3,2,1,0:T(2,128)(2,1)S(1)}, u32[]{:S(2)}, u32[]{:S(2)}) async-start(bf16[8,65,2,256]{3,2,1,0:T(2,128)(2,1)} %pack_outbox.1), calls=%async_computation | async-start | bytes 1064960 | tf_op jit(solution)/shard_map/all_to_all | solution.py:566
  15.0 69.7 %all-to-all-start.1 = ((bf16[8,128,1024]{2,1,0:T(8,128)(2,1)}), bf16[8,128,1024]{2,1,0:T(8,128)(2,1)S(1)}, u32[]{:S(2)}, u32[]{:S(2)}) async-start(bf16[8,128,1024]{2,1,0:T(8,128)(2,1)} %copy-done.4), calls=%async_computation.1 | async-start | bytes 4194304 | tf_op jit(solution)/shard_map/all_to_all | solution.py:578
  58.0 22.8 %collective-permute-start = (bf16[64,2048]{1,0:T(8,128)(2,1)}, bf16[64,2048]{1,0:T(8,128)(2,1)}, u32[]{:S(2)}, u32[]{:S(2)}) collective-permute-start(bf16[64,2048]{1,0:T(8,128)(2,1)} %attend.2.refs_0_), channel_id=1, source_target_pairs={{0,8},{4,12},{8,0},{12,4},{16,24},{20,28},{24,16},{28,20},{1,9},{5... | collective-permute-start | bytes 786440 | tf_op jit(solution)/shard_map/ppermute | solution.py:508
  60.0 20.7 %collective-permute-start.1 = (bf16[64,2048]{1,0:T(8,128)(2,1)}, bf16[64,2048]{1,0:T(8,128)(2,1)}, u32[]{:S(2)}, u32[]{:S(2)}) collective-permute-start(bf16[64,2048]{1,0:T(8,128)(2,1)} %attend.2.refs_0_), channel_id=1, source_target_pairs={{0,16},{4,20},{8,24},{12,28},{16,0},{20,4},{24,8},{28,12},{1,17},{... | collective-permute-start | bytes 786440 | tf_op jit(solution)/shard_map/ppermute | solution.py:508
  61.5 19.2 %collective-permute-start.2 = (bf16[64,2048]{1,0:T(8,128)(2,1)}, bf16[64,2048]{1,0:T(8,128)(2,1)}, u32[]{:S(2)}, u32[]{:S(2)}) collective-permute-start(bf16[64,2048]{1,0:T(8,128)(2,1)} %attend.2.refs_0_), channel_id=1, source_target_pairs={{0,24},{4,28},{8,16},{12,20},{16,8},{20,12},{24,0},{28,4},{1,25},{... | collective-permute-start | bytes 786440 | tf_op jit(solution)/shard_map/ppermute | solution.py:508
  62.6 22.0 %collective-permute-start.3 = (bf16[64,2048]{1,0:T(8,128)(2,1)}, bf16[64,2048]{1,0:T(8,128)(2,1)}, u32[]{:S(2)}, u32[]{:S(2)}) collective-permute-start(bf16[64,2048]{1,0:T(8,128)(2,1)} %attend.2.refs_0_), channel_id=1, source_target_pairs={{0,4},{4,0},{8,12},{12,8},{16,20},{20,16},{24,28},{28,24},{1,5},{5... | collective-permute-start | bytes 786440 | tf_op jit(solution)/shard_map/ppermute | solution.py:508
  80.8 4.3 %collective-permute-start.4 = (bf16[64,2048]{1,0:T(8,128)(2,1)}, bf16[64,2048]{1,0:T(8,128)(2,1)S(1)}, u32[]{:S(2)}, u32[]{:S(2)}) collective-permute-start(bf16[64,2048]{1,0:T(8,128)(2,1)} %collective-permute-done.refs_1_), channel_id=1, source_target_pairs={{0,4},{4,0},{8,12},{12,8},{16,20},{20,16},{24,28},{28,24},{1,5},{5... | collective-permute-start | bytes 786440 | tf_op jit(solution)/shard_map/ppermute | solution.py:508
  81.6 5.3 %collective-permute-start.5 = (bf16[64,2048]{1,0:T(8,128)(2,1)}, bf16[64,2048]{1,0:T(8,128)(2,1)S(1)}, u32[]{:S(2)}, u32[]{:S(2)}) collective-permute-start(bf16[64,2048]{1,0:T(8,128)(2,1)} %collective-permute-done.1.refs_2_), channel_id=1, source_target_pairs={{0,4},{4,0},{8,12},{12,8},{16,20},{20,16},{24,28},{28,24},{1,5},{5... | collective-permute-start | bytes 786440 | tf_op jit(solution)/shard_map/ppermute | solution.py:508
  81.7 5.9 %collective-permute-start.6 = (bf16[64,2048]{1,0:T(8,128)(2,1)}, bf16[64,2048]{1,0:T(8,128)(2,1)}, u32[]{:S(2)}, u32[]{:S(2)}) collective-permute-start(bf16[64,2048]{1,0:T(8,128)(2,1)} %collective-permute-done.2.refs_3_), channel_id=1, source_target_pairs={{0,4},{4,0},{8,12},{12,8},{16,20},{20,16},{24,28},{28,24},{1,5},{5... | collective-permute-start | bytes 786440 | tf_op jit(solution)/shard_map/ppermute | solution.py:508
  83.5 18.6 %collective-permute-start.7 = (bf16[64,2048]{1,0:T(8,128)(2,1)S(1)}, bf16[64,2048]{1,0:T(8,128)(2,1)S(1)}, u32[]{:S(2)}, u32[]{:S(2)}) collective-permute-start(bf16[64,2048]{1,0:T(8,128)(2,1)S(1)} %attend.3.refs_0_), channel_id=1, source_target_pairs={{0,8},{4,12},{8,0},{12,4},{16,24},{20,28},{24,16},{28,20},{1,9},{5... | collective-permute-start | bytes 786440 | tf_op jit(solution)/shard_map/ppermute | solution.py:508
  84.6 18.9 %collective-permute-start.8 = (bf16[64,2048]{1,0:T(8,128)(2,1)S(1)}, bf16[64,2048]{1,0:T(8,128)(2,1)S(1)}, u32[]{:S(2)}, u32[]{:S(2)}) collective-permute-start(bf16[64,2048]{1,0:T(8,128)(2,1)S(1)} %attend.3.refs_0_), channel_id=1, source_target_pairs={{0,16},{4,20},{8,24},{12,28},{16,0},{20,4},{24,8},{28,12},{1,17},{... | collective-permute-start | bytes 786440 | tf_op jit(solution)/shard_map/ppermute | solution.py:508
  85.8 20.9 %collective-permute-start.9 = (bf16[64,2048]{1,0:T(8,128)(2,1)S(1)}, bf16[64,2048]{1,0:T(8,128)(2,1)S(1)}, u32[]{:S(2)}, u32[]{:S(2)}) collective-permute-start(bf16[64,2048]{1,0:T(8,128)(2,1)S(1)} %attend.3.refs_0_), channel_id=1, source_target_pairs={{0,24},{4,28},{8,16},{12,20},{16,8},{20,12},{24,0},{28,4},{1,25},{... | collective-permute-start | bytes 786440 | tf_op jit(solution)/shard_map/ppermute | solution.py:508
  98.6 8.8 %collective-permute-start.14 = (bf16[128,1024]{1,0:T(8,128)(2,1)S(1)}, bf16[128,1024]{1,0:T(8,128)(2,1)S(1)}, u32[]{:S(2)}, u32[]{:S(2)}) collective-permute-start(bf16[128,1024]{1,0:T(8,128)(2,1)S(1)} %get-tuple-element.43), channel_id=1, source_target_pairs={{0,1},{3,2},{4,5},{7,6},{8,9},{11,10},{12,13},{15,14},{16,17},{19,... | collective-permute-start | bytes 786440 | tf_op jit(solution)/shard_map/ppermute | solution.py:531
  99.9 13.1 %collective-permute-start.15 = (bf16[128,1024]{1,0:T(8,128)(2,1)S(1)}, bf16[128,1024]{1,0:T(8,128)(2,1)S(1)}, u32[]{:S(2)}, u32[]{:S(2)}) collective-permute-start(bf16[128,1024]{1,0:T(8,128)(2,1)S(1)} %get-tuple-element.45), channel_id=1, source_target_pairs={{0,1},{1,0},{2,3},{3,2},{4,5},{5,4},{6,7},{7,6},{8,9},{9,8},{10,11... | collective-permute-start | bytes 786440 | tf_op jit(solution)/shard_map/ppermute | solution.py:508
  102.0 12.8 %collective-permute-start.10 = (bf16[64,2048]{1,0:T(8,128)(2,1)S(1)}, bf16[64,2048]{1,0:T(8,128)(2,1)S(1)}, u32[]{:S(2)}, u32[]{:S(2)}) collective-permute-start(bf16[64,2048]{1,0:T(8,128)(2,1)S(1)} %attend.3.refs_0_), channel_id=1, source_target_pairs={{0,4},{4,0},{8,12},{12,8},{16,20},{20,16},{24,28},{28,24},{1,5},{5... | collective-permute-start | bytes 786440 | tf_op jit(solution)/shard_map/ppermute | solution.py:508
  103.5 11.4 %collective-permute-start.16 = (bf16[128,1024]{1,0:T(8,128)(2,1)S(1)}, bf16[128,1024]{1,0:T(8,128)(2,1)S(1)}, u32[]{:S(2)}, u32[]{:S(2)}) collective-permute-start(bf16[128,1024]{1,0:T(8,128)(2,1)S(1)} %get-tuple-element.43), channel_id=1, source_target_pairs={{1,2},{2,1},{5,6},{6,5},{9,10},{10,9},{13,14},{14,13},{17,18},{18,... | collective-permute-start | bytes 786440 | tf_op jit(solution)/shard_map/ppermute | solution.py:532
  106.7 8.2 %collective-permute-start.11 = (bf16[64,2048]{1,0:T(8,128)(2,1)S(1)}, bf16[64,2048]{1,0:T(8,128)(2,1)S(1)}, u32[]{:S(2)}, u32[]{:S(2)}) collective-permute-start(bf16[64,2048]{1,0:T(8,128)(2,1)S(1)} %collective-permute-done.7.refs_1_), channel_id=1, source_target_pairs={{0,4},{4,0},{8,12},{12,8},{16,20},{20,16},{24,28},{28,24},{1,5},{5... | collective-permute-start | bytes 786440 | tf_op jit(solution)/shard_map/ppermute | solution.py:508
  107.4 7.5 %collective-permute-start.12 = (bf16[64,2048]{1,0:T(8,128)(2,1)S(1)}, bf16[64,2048]{1,0:T(8,128)(2,1)S(1)}, u32[]{:S(2)}, u32[]{:S(2)}) collective-permute-start(bf16[64,2048]{1,0:T(8,128)(2,1)S(1)} %collective-permute-done.8.refs_2_), channel_id=1, source_target_pairs={{0,4},{4,0},{8,12},{12,8},{16,20},{20,16},{24,28},{28,24},{1,5},{5... | collective-permute-start | bytes 786440 | tf_op jit(solution)/shard_map/ppermute | solution.py:508
  121.0 9.5 %collective-permute-start.17 = (bf16[128,1024]{1,0:T(8,128)(2,1)S(1)}, bf16[128,1024]{1,0:T(8,128)(2,1)S(1)}, u32[]{:S(2)}, u32[]{:S(2)}) collective-permute-start(bf16[128,1024]{1,0:T(8,128)(2,1)S(1)} %get-tuple-element.49), channel_id=1, source_target_pairs={{0,1},{3,2},{4,5},{7,6},{8,9},{11,10},{12,13},{15,14},{16,17},{19,... | collective-permute-start | bytes 786440 | tf_op jit(solution)/shard_map/ppermute | solution.py:531
  122.4 14.8 %collective-permute-start.18 = (bf16[128,1024]{1,0:T(8,128)(2,1)S(1)}, bf16[128,1024]{1,0:T(8,128)(2,1)S(1)}, u32[]{:S(2)}, u32[]{:S(2)}) collective-permute-start(bf16[128,1024]{1,0:T(8,128)(2,1)S(1)} %add.110), channel_id=1, source_target_pairs={{0,2},{1,3},{2,0},{3,1},{4,6},{5,7},{6,4},{7,5},{8,10},{9,11},{10,... | collective-permute-start | bytes 786440 | tf_op jit(solution)/shard_map/ppermute | solution.py:508
  137.2 10.1 %all-to-all-start.2 = ((bf16[4,256,128]{2,1,0:T(8,128)(2,1)}), bf16[4,256,128]{2,1,0:T(8,128)(2,1)}, u32[]{:S(2)}, u32[]{:S(2)}) async-start(bf16[4,256,128]{2,1,0:T(8,128)(2,1)} %pad_maximum_fusion), calls=%async_computation.2 | async-start | bytes 524288 | tf_op jit(solution)/shard_map/all_to_all | solution.py:609
  141.7 9.1 %collective-permute-start.19 = (bf16[128,1024]{1,0:T(8,128)(2,1)}, bf16[128,1024]{1,0:T(8,128)(2,1)}, u32[]{:S(2)}, u32[]{:S(2)}) collective-permute-start(bf16[128,1024]{1,0:T(8,128)(2,1)} %copy-done.21), channel_id=1, source_target_pairs={{0,1},{1,0},{2,3},{3,2},{4,5},{5,4},{6,7},{7,6},{8,9},{9,8},{10,11... | collective-permute-start | bytes 786440 | tf_op jit(solution)/shard_map/ppermute | solution.py:508
  141.7 14.8 %collective-permute-start.20 = (bf16[128,1024]{1,0:T(8,128)(2,1)}, bf16[128,1024]{1,0:T(8,128)(2,1)}, u32[]{:S(2)}, u32[]{:S(2)}) collective-permute-start(bf16[128,1024]{1,0:T(8,128)(2,1)} %copy-done.20), channel_id=1, source_target_pairs={{1,2},{2,1},{5,6},{6,5},{9,10},{10,9},{13,14},{14,13},{17,18},{18,... | collective-permute-start | bytes 786440 | tf_op jit(solution)/shard_map/ppermute | solution.py:532
  146.0 26.9 %collective-permute-start.21 = (bf16[128,1024]{1,0:T(8,128)(2,1)}, bf16[128,1024]{1,0:T(8,128)(2,1)}, u32[]{:S(2)}, u32[]{:S(2)}) collective-permute-start(bf16[128,1024]{1,0:T(8,128)(2,1)} %copy-done.13), channel_id=1, source_target_pairs={{0,2},{1,3},{2,0},{3,1},{4,6},{5,7},{6,4},{7,5},{8,10},{9,11},{10,... | collective-permute-start | bytes 786440 | tf_op jit(solution)/shard_map/ppermute | solution.py:508
  (26 other events, 246.8 us)

commit v7 on v5

--- a/solution.py
+++ b/solution.py
@@ -22,12 +22,12 @@
 CHUNK_PAGES = 4
 CHUNKS = MAXP // CHUNK_PAGES
 CHUNK_POSITIONS = CHUNK_PAGES * PAGE_LENGTH
-BUFFERS = 12
-UNROLLS = (2, 4)
-PRIORITIES = (2, 1)
+LANES = 128
+SLOTS = 6
 HALVES = 2
 VMEM_LIMIT = 24 * 1024 * 1024
 WHOLE_VMEM = 60 * 1024 * 1024
+ATTEND_VMEM = 48 * 1024 * 1024
 
 SMALL = pl.CostEstimate(flops=1, bytes_accessed=1, transcendentals=0)
 
@@ -127,7 +127,7 @@
     )(me, page_request_home.reshape(1, per_dev), ids.reshape(1, -1), key_value_pages)
 
 
-def table_kernel(per_dev, requests, me_ref, home_ref, lengths_ref, table_ref, order_ref, len_v):
+def table_kernel(per_dev, requests, pack_size, me_ref, home_ref, lengths_ref, table_ref, order_ref, len_v):
     base = me_ref[0] * per_dev
     lane = lax.broadcasted_iota(jnp.int32, (128, 128), 1)
     row = lax.broadcasted_iota(jnp.int32, (128, 128), 0)
@@ -148,10 +148,10 @@
     along = jnp.broadcast_to(len_v[...], (128, 128))
     along = ((along.astype(jnp.int32) + (CHUNK_POSITIONS - 1)) >> 7).astype(jnp.float32)
     down = jnp.transpose(along)
-    same = (lane // half) == (row // half)
+    same = ((lane // half) == (row // half)) & (lane % pack_size == row % pack_size)
     before = same & ((along > down) | ((along == down) & (lane < row)))
     rank = jnp.sum(jnp.where(before, 1.0, 0.0), axis=1, keepdims=True)
-    place = rank + ((row // half) * half).astype(jnp.float32)
+    place = rank * pack_size + ((row // half) * half + row % pack_size).astype(jnp.float32)
     at = place == lane.astype(jnp.float32)
     order = jnp.sum(jnp.where(at, row.astype(jnp.float32), 0.0), axis=0, keepdims=True)
     chunks = jnp.sum(jnp.where(at, down, 0.0), axis=0, keepdims=True)
@@ -159,11 +159,11 @@
     order_ref[1:2, :] = chunks.astype(jnp.int32)
 
 
-def build_table(me, page_request_home, lengths):
+def build_table(me, page_request_home, lengths, pack_size):
     per_dev = page_request_home.shape[0]
     requests = lengths.shape[0]
     return pl.pallas_call(
-        functools.partial(table_kernel, per_dev, requests),
+        functools.partial(table_kernel, per_dev, requests, pack_size),
         out_shape=(
             jax.ShapeDtypeStruct((per_dev // 128, 128), jnp.int32),
             jax.ShapeDtypeStruct((2, 128), jnp.int32),
@@ -182,8 +182,6 @@
     per_dev,
     base,
     requests,
-    unroll,
-    priorities,
     order_ref,
     lengths_ref,
     table_in,
@@ -201,18 +199,18 @@
     sem,
     sems,
 ):
-    heads_kv = pages.shape[2]
-    page_size = PAGE_LENGTH * heads_kv * 2
+    columns = pages.shape[-1]
+    heads_kv = columns // HEAD_WIDTH
+    heads = heads_kv * GROUP
+    span = STEP_COUNT * heads
+    pack_size = LANES // span
+    page_size = PAGE_LENGTH * 2
     chunk_size = CHUNK_PAGES * page_size
-    new_rows = STEP_COUNT * heads_kv * 2
-    new_group = 128 // new_rows
-    half = STEP_COUNT * GROUP
-    rows = heads_kv * half
-    heads = heads_kv * GROUP
+    new_rows = STEP_COUNT * 2
+    tokens = requests * STEP_COUNT
     scale = math.log2(math.e) / math.sqrt(HEAD_WIDTH)
-    pairs = PAGE_LENGTH * heads_kv
-    page_rows = pages.reshape(per_dev, pairs, 2, HEAD_WIDTH)
-    inbox_rows = inbox.reshape(req_count, BLOCK * heads_kv, 2, HEAD_WIDTH)
+    page_rows = pages.reshape(per_dev, page_size, columns)
+    inbox_rows = inbox.reshape(req_count, BLOCK * 2, columns)
 
     tab = pltpu.make_async_copy(table_in, table, sem)
     tab.start()
@@ -223,7 +221,7 @@
     row = lax.broadcasted_iota(jnp.int32, (2, 128), 0)
     weight = jnp.where(row == 0, float(DIGIT), 1.0)
     for d in range(req_count):
-        digits = labels_v[d, 0, 0, :, :].astype(jnp.float32) * weight
+        digits = labels_v[d, 0, :, 0:128].astype(jnp.float32) * weight
         labels_w[d : d + 1, :] = jnp.sum(digits, axis=0, keepdims=True).astype(jnp.int32)
     back = pltpu.make_async_copy(labels_w, labels_s, sem)
     back.start()
@@ -236,15 +234,17 @@
             def _():
                 table[lax.shift_right_logical(slot, 7), slot & 127] = per_dev + d * CAP + k
 
-    slots = BUFFERS // unroll
-    steps = requests // unroll
-    flat = buf.reshape(slots, unroll, MAXP * page_size, HEAD_WIDTH)
+    steps = requests // pack_size
+
+    def most_chunks(step):
+        counts = [order_ref[1, base + step * pack_size + u] for u in range(pack_size)]
+        return functools.reduce(jnp.maximum, counts)
 
     def fetch(step):
-        place = lax.rem(step, slots)
-        count = order_ref[1, base + step * unroll]
-        for u in range(unroll):
-            slot = order_ref[0, base + step * unroll + u] * MAXP
+        place = lax.rem(step, SLOTS)
+        count = most_chunks(step)
+        for u in range(pack_size):
+            slot = order_ref[0, base + step * pack_size + u] * MAXP
             line = lax.shift_right_logical(slot, 7)
             at = slot & 127
 
@@ -254,14 +254,13 @@
                 most = functools.reduce(jnp.maximum, sources)
 
                 def target(j):
-                    return buf.at[place, u, pl.ds((c * CHUNK_PAGES + j) * pairs, pairs)]
+                    start = pl.multiple_of(c * chunk_size + j * page_size, page_size)
+                    return buf.at[place, u, pl.ds(start, page_size)]
 
                 @pl.when(most < per_dev)
                 def _():
                     for j in range(CHUNK_PAGES):
-                        pltpu.make_async_copy(page_rows.at[sources[j]], target(j), sems.at[place, u]).start(
-                            priority=j % priorities
-                        )
+                        pltpu.make_async_copy(page_rows.at[sources[j]], target(j), sems.at[place, u]).start()
 
                 @pl.when(most >= per_dev)
                 def _():
@@ -276,62 +275,73 @@
                         def _():
                             e = source - per_dev
                             d = lax.shift_right_logical(e, 1)
-                            k = e - d * CAP
+                            start = pl.multiple_of((e - d * CAP) * page_size, page_size)
                             pltpu.make_async_copy(
-                                inbox_rows.at[d, pl.ds(k * pairs, pairs)], target(j), sems.at[place, u]
+                                inbox_rows.at[d, pl.ds(start, page_size)], target(j), sems.at[place, u]
                             ).start()
 
-    for s in range(min(slots - 1, steps)):
+    for s in range(min(SLOTS - 1, steps)):
         fetch(jnp.int32(s))
 
     def compute(step, n):
-        place = lax.rem(step, slots)
+        place = lax.rem(step, SLOTS)
         width = n * chunk_size
-        for u in range(unroll):
-            whole = buf.at[place, u, pl.ds(0, width // 2)]
+        for u in range(pack_size):
+            whole = buf.at[place, u, pl.ds(0, width)]
             pltpu.make_async_copy(whole, whole, sems.at[place, u]).wait()
-        column = lax.broadcasted_iota(jnp.int32, (1, width), 1)
-        new_column = lax.broadcasted_iota(jnp.int32, (half, 128), 1)
-        new_row = lax.broadcasted_iota(jnp.int32, (half, 128), 0)
-        new_step = (new_column & (new_rows - 1)) // (2 * heads_kv)
-        new_key = new_column & (2 * heads_kv - 1)
-        visible = new_step <= (new_row & (STEP_COUNT - 1))
-        for u in range(unroll):
-            r = order_ref[0, base + step * unroll + u]
-            length = lengths_ref[r]
-            q = q_ref[pl.ds(pl.multiple_of(r * rows, rows), rows), :]
-            kv = flat[place, u, 0:width, :]
-            group = r // new_group
-            new = new_ref[pl.ds(pl.multiple_of(group * 128, 128), 128), :]
-            seen = visible & (new_column // new_rows == r - group * new_group)
-            cached = column < 2 * heads_kv * length
-            whole_s = dot(q, kv, ((1,), (1,)))
-            whole_sn = dot(q, new, ((1,), (1,)))
-            ps, pns = [], []
-            for g in range(heads_kv):
-                key = (column & (2 * heads_kv - 1)) == 2 * g
-                bias = jnp.where(cached & key, 0.0, -jnp.inf)
-                s = whole_s[g * half : (g + 1) * half] * scale + bias
-                sn = whole_sn[g * half : (g + 1) * half] * scale
-                sn = jnp.where(seen & (new_key == 2 * g), sn, -jnp.inf)
-                top = jnp.maximum(jnp.max(s, axis=1, keepdims=True), jnp.max(sn, axis=1, keepdims=True))
-                w = jnp.exp2(s - top)
-                wn = jnp.exp2(sn - top)
-                inverse = 1.0 / (jnp.sum(w, axis=1, keepdims=True) + jnp.sum(wn, axis=1, keepdims=True))
-                ps.append(pltpu.roll(w * inverse, 1, 1).astype(jnp.bfloat16))
-                pns.append(pltpu.roll(wn * inverse, 1, 1).astype(jnp.bfloat16))
-            o = dot(jnp.concatenate(ps, axis=0), kv) + dot(jnp.concatenate(pns, axis=0), new)
-            at = pl.multiple_of((r - base) * STEP_COUNT, STEP_COUNT)
-            for h in range(heads):
-                acc[h, pl.ds(at, STEP_COUNT), :] = o[h * STEP_COUNT : (h + 1) * STEP_COUNT]
+        lane = lax.broadcasted_iota(jnp.int32, (HEAD_WIDTH, LANES), 1)
+        part = lane // span
+        lane_head = (lane % heads) // GROUP
+        one = lax.broadcasted_iota(jnp.int32, (1, LANES), 1)
+        limit = jnp.zeros((1, LANES), jnp.int32)
+        owner = jnp.zeros((1, LANES), jnp.int32)
+        rows, kvs, rights = [], [], []
+        for u in range(pack_size):
+            r = order_ref[0, base + step * pack_size + u]
+            rows.append(r)
+            q = q_ref[:, pl.ds(pl.multiple_of((r // pack_size) * LANES, LANES), LANES)].astype(jnp.float32)
+            own = part == u
+            rights.append(
+                jnp.concatenate(
+                    [jnp.where(own & (lane_head == g), q, 0.0).astype(jnp.bfloat16) for g in range(heads_kv)], axis=0
+                )
+            )
+            kvs.append(buf[place, u, 0:width, :])
+            limit = jnp.where(one // span == u, 2 * lengths_ref[r], limit)
+            owner = jnp.where(one // span == u, r - base, owner)
+        new = new_ref[base * new_rows : (base + requests) * new_rows, :]
+        s = dot(jnp.concatenate(kvs, axis=1), jnp.concatenate(rights, axis=0))
+        sn = dot(new, functools.reduce(jnp.add, rights))
+        row = lax.broadcasted_iota(jnp.int32, (width, LANES), 0)
+        s = jnp.where(((row & 1) == 0) & (row < limit), s * scale, -jnp.inf)
+        row = lax.broadcasted_iota(jnp.int32, sn.shape, 0)
+        step_of = (one % span) // heads
+        seen = ((row & 1) == 0) & (row // new_rows == owner) & ((row % new_rows) // 2 <= step_of)
+        sn = jnp.where(seen, sn * scale, -jnp.inf)
+        top = jnp.maximum(jnp.max(s, axis=0, keepdims=True), jnp.max(sn, axis=0, keepdims=True))
+        w = jnp.exp2(s - top)
+        wn = jnp.exp2(sn - top)
+        inverse = 1.0 / (jnp.sum(w, axis=0, keepdims=True) + jnp.sum(wn, axis=0, keepdims=True))
+        p = jnp.transpose(pltpu.roll(w * inverse, 1, 0)).astype(jnp.bfloat16)
+        pn = jnp.transpose(pltpu.roll(wn * inverse, 1, 0)).astype(jnp.bfloat16)
+        head = (lax.broadcasted_iota(jnp.int32, (span, HEAD_WIDTH), 0) % heads) // GROUP
+        for u in range(pack_size):
+            at = slice(u * span, (u + 1) * span)
+            full = dot(p[at], kvs[u]) + dot(pn[at], new)
+            o = full[:, :HEAD_WIDTH]
+            for g in range(1, heads_kv):
+                o = jnp.where(head == g, full[:, g * HEAD_WIDTH : (g + 1) * HEAD_WIDTH], o)
+            token = (rows[u] - base) * STEP_COUNT
+            for t in range(STEP_COUNT):
+                acc[pl.ds(token + t, heads, stride=tokens), :] = o[t * heads : (t + 1) * heads]
 
     @pl.loop(0, steps)
     def _(step):
-        @pl.when(step + (slots - 1) < steps)
+        @pl.when(step + (SLOTS - 1) < steps)
         def _():
-            fetch(step + (slots - 1))
-
-        count = order_ref[1, base + step * unroll]
+            fetch(step + (SLOTS - 1))
+
+        count = most_chunks(step)
         for n in range(1, CHUNKS + 1):
 
             @pl.when(count == n)
@@ -339,36 +349,36 @@
                 compute(step, n)
 
     for h in range(heads):
-        out_ref[:, h * HEAD_WIDTH : (h + 1) * HEAD_WIDTH] = acc[h].astype(jnp.bfloat16)
+        out_ref[:, h * HEAD_WIDTH : (h + 1) * HEAD_WIDTH] = acc[h * tokens : (h + 1) * tokens].astype(jnp.bfloat16)
 
 
 def attend(part, order, lengths, table, q, new, pages, inbox):
-    per_dev, _, heads_kv, _, _ = pages.shape
+    per_dev, _, _, columns = pages.shape
     req_count = inbox.shape[0]
     requests = lengths.shape[0] // HALVES
-    heads = heads_kv * GROUP
-    extent = MAXP * PAGE_LENGTH * heads_kv * 2
-    unroll = UNROLLS[part]
+    heads = columns // HEAD_WIDTH * GROUP
     tokens = requests * STEP_COUNT
-    return pl.pallas_call(
-        functools.partial(attend_kernel, req_count, per_dev, part * requests, requests, unroll, PRIORITIES[part]),
+    pack_size = LANES // (STEP_COUNT * heads)
+    extent = MAXP * PAGE_LENGTH * 2
+    return pl.pallas_call(
+        functools.partial(attend_kernel, req_count, per_dev, part * requests, requests),
         out_shape=jax.ShapeDtypeStruct((tokens, heads * HEAD_WIDTH), jnp.bfloat16),
-        in_specs=[SMEM, SMEM, HBM, VMEM, VMEM, HBM, HBM],
+        in_specs=[SMEM, SMEM, ANY, VMEM, VMEM, HBM, ANY],
         out_specs=VMEM,
         scratch_shapes=[
             pltpu.SMEM((per_dev // 128, 128), jnp.int32),
-            pltpu.VMEM((req_count, 1, heads_kv, 2, HEAD_WIDTH), jnp.bfloat16),
+            pltpu.VMEM((req_count, 1, 2, columns), jnp.bfloat16),
             pltpu.VMEM((req_count, 128), jnp.int32),
             pltpu.SMEM((req_count, 128), jnp.int32),
-            pltpu.VMEM((BUFFERS // unroll, unroll, extent // 2, 2, HEAD_WIDTH), jnp.bfloat16),
-            pltpu.VMEM((heads, tokens, HEAD_WIDTH), jnp.float32),
+            pltpu.VMEM((SLOTS, pack_size, extent, columns), jnp.bfloat16),
+            pltpu.VMEM((heads * tokens, HEAD_WIDTH), jnp.float32),
             pltpu.SemaphoreType.DMA,
-            pltpu.SemaphoreType.DMA((BUFFERS // unroll, unroll)),
+            pltpu.SemaphoreType.DMA((SLOTS, pack_size)),
         ],
-        compiler_params=params(),
+        compiler_params=params(ATTEND_VMEM),
         cost_estimate=pl.CostEstimate(
             flops=16 * tokens * heads * HEAD_WIDTH * MAXP * PAGE_LENGTH,
-            bytes_accessed=requests * extent * HEAD_WIDTH * 2,
+            bytes_accessed=requests * extent * columns * 2,
             transcendentals=2 * tokens * heads * MAXP * PAGE_LENGTH,
         ),
         name="attend",
@@ -400,13 +410,17 @@
     )(x)
 
 
-def project_kernel(count, roles, tile, where_ref, *refs):
-    xs, (w_ref, down_ref, mask_ref), rest = refs[:count], refs[count : count + 3], refs[count + 3 :]
-    outs, low_ref, x_v = rest[:roles], rest[roles], rest[roles + 1]
-    tokens = xs[0].shape[0]
+def project_kernel(count, roles, tile, counts, where_ref, *refs):
+    xs, (w_ref, down_ref, mask_ref), rest = refs[: len(counts)], refs[len(counts) : len(counts) + 3], refs[len(counts) + 3 :]
+    outs, low_ref, x_v = rest[:-2], rest[-2], rest[-1]
+    tokens = xs[0].shape[-2]
     rows = count * tokens // roles
-    for b in range(count):
-        x_v[pl.ds(pl.multiple_of(where_ref[b] * tokens, tokens), tokens), :] = xs[b][...]
+    b = 0
+    for x_ref, blocks in zip(xs, counts):
+        for k in range(blocks):
+            x = x_ref[...] if len(x_ref.shape) == 2 else x_ref[k]
+            x_v[pl.ds(pl.multiple_of(where_ref[b] * tokens, tokens), tokens), :] = x
+            b = b + 1
     low = dot(x_v[...], down_ref[...], ((1,), (1,)))
     for j in range(roles):
         s = where_ref[count + j]
@@ -416,21 +430,35 @@
     def _(i):
         at = pl.ds(pl.multiple_of(i * tile, tile), tile)
         y = dot(x_v[...], w_ref[:, at]).astype(jnp.bfloat16)
-        for j in range(roles):
-            outs[j][:, at] = y[j * rows : (j + 1) * rows, :]
+        parts = [y[j * rows : (j + 1) * rows, :] for j in range(roles)]
+        if roles == 4:
+            own, pair, two, three = outs
+            own[:, at] = parts[0]
+            pair[0, :, at] = parts[1]
+            pair[1, :, at] = parts[3]
+            two[:, at] = parts[2]
+            three[:, at] = parts[3]
+        else:
+            for j in range(roles):
+                outs[j][:, at] = parts[j]
 
 
 def project(where, xs, w, down, mask, roles):
-    count = len(xs)
+    counts = tuple(1 if len(x.shape) == 2 else x.shape[0] for x in xs)
+    count = sum(counts)
     tokens, width = xs[0].shape
     columns = w.shape[1]
     rows = count * tokens // roles
-    return pl.pallas_call(
-        functools.partial(project_kernel, count, roles, min(256, columns)),
-        out_shape=[jax.ShapeDtypeStruct((rows, columns), jnp.bfloat16)] * roles
-        + [jax.ShapeDtypeStruct((roles, rows, down.shape[0]), jnp.bfloat16)],
-        in_specs=[SMEM] + [VMEM] * (count + 3),
-        out_specs=[VMEM] * (roles + 1),
+    one = jax.ShapeDtypeStruct((rows, columns), jnp.bfloat16)
+    outs = [one] * roles
+    if roles == 4:
+        outs[1] = jax.ShapeDtypeStruct((2, rows, columns), jnp.bfloat16)
+    outs = outs + [jax.ShapeDtypeStruct((roles, rows, down.shape[0]), jnp.bfloat16)]
+    return pl.pallas_call(
+        functools.partial(project_kernel, count, roles, min(256, columns), counts),
+        out_shape=outs,
+        in_specs=[SMEM] + [VMEM] * (len(xs) + 3),
+        out_specs=[VMEM] * len(outs),
         scratch_shapes=[pltpu.VMEM((count * tokens, width), jnp.bfloat16)],
         compiler_params=params(),
         cost_estimate=SMALL,
@@ -438,20 +466,28 @@
     )(where, *xs, w, down, mask)
 
 
-def add_kernel(a_ref, b_ref, o_ref):
-    o_ref[...] = (a_ref[...].astype(jnp.float32) + b_ref[...].astype(jnp.float32)).astype(jnp.bfloat16)
-
-
-def add(a, b):
+def add_kernel(lane_ref, own_ref, passed_ref, o_ref):
+    middle = (lane_ref[0] == 1) | (lane_ref[0] == 2)
+
+    @pl.when(middle)
+    def _():
+        o_ref[...] = (own_ref[...].astype(jnp.float32) + passed_ref[1].astype(jnp.float32)).astype(jnp.bfloat16)
+
+    @pl.when(jnp.logical_not(middle))
+    def _():
+        o_ref[...] = own_ref[...]
+
+
+def add(lane, own, passed):
     return pl.pallas_call(
         add_kernel,
-        out_shape=jax.ShapeDtypeStruct(a.shape, a.dtype),
-        in_specs=[VMEM, VMEM],
+        out_shape=jax.ShapeDtypeStruct(own.shape, own.dtype),
+        in_specs=[SMEM, VMEM, VMEM],
         out_specs=VMEM,
         compiler_params=params(),
         cost_estimate=SMALL,
         name="add",
-    )(a, b)
+    )(lane, own, passed)
 
 
 def adapt_kernel(low_ref, up_ref, o_ref):
@@ -479,7 +515,7 @@
     for h, count in enumerate(counts):
         total = extra_ref[h * rows : (h + 1) * rows, :]
         for term in terms[first : first + count]:
-            total = total + term[...].astype(jnp.float32)
+            total = total + (term[...] if len(term.shape) == 2 else term[0]).astype(jnp.float32)
         first = first + count
         for c in range(cores):
             at = (c * len(counts) + h) * tokens
@@ -514,24 +550,21 @@
     if count != 8:
         whole = lax.all_gather(x, "req", axis=0)
         return [whole[b] for b in range(count)], [jnp.int32(b) for b in range(count)], []
+    near = exchange(x, "req", 1)
     far = [exchange(x, "req", d) for d in (2, 4, 6)]
-    held = [x] + [after(block, *gates) for block in far] if gates else [x] + far
-    near = [exchange(block, "req", 1) for block in held]
-    return held + near, [my_req ^ d for d in (0, 2, 4, 6, 1, 3, 5, 7)], far
+    group = jnp.stack([after(block, *gates) for block in far] if gates else far)
+    return [x, group, near, exchange(group, "req", 1)], [my_req ^ d for d in (0, 2, 4, 6, 1, 3, 5, 7)], far
 
 
 def scatter(blocks):
     if len(blocks) != 4:
         return [lax.psum_scatter(jnp.stack(blocks), "tp", scatter_dimension=0, tiled=False)], blocks[0]
-    own, one, two, three = blocks
-    onward = lax.ppermute(three, "tp", [(0, 1), (3, 2)])
+    own, pair, two, three = blocks
+    lane = lax.axis_index("tp").astype(jnp.int32).reshape(1)
+    pair = exchange(pair, "tp", 1)
     middle = lax.ppermute(three, "tp", [(1, 2), (2, 1)])
-    passed = add(two, onward)
-    return [own, exchange(one, "tp", 1), middle, exchange(passed, "tp", 2)], passed
-
-
-def split_heads(x):
-    return x.reshape(*x.shape[:3], -1, HEAD_WIDTH).transpose(0, 1, 3, 2, 4)
+    passed = add(lane, two, pair)
+    return [own, pair, middle, exchange(passed, "tp", 2)], passed
 
 
 def on_device(
@@ -561,16 +594,14 @@
     outbox = pack(me, page_request_home, request_adapter_index, key_value_pages, req_count)
     inbox = lax.all_to_all(outbox, "req", split_axis=0, concat_axis=0, tiled=True)
 
-    table, order = build_table(me, page_request_home, lengths)
-    q = queries.reshape(requests, STEP_COUNT, heads, HEAD_WIDTH).transpose(0, 2, 1, 3)
-    q = q.reshape(requests * heads * STEP_COUNT, HEAD_WIDTH)
+    table, order = build_table(me, page_request_home, lengths, LANES // (STEP_COUNT * heads))
+    q = queries.reshape(requests * STEP_COUNT * heads, HEAD_WIDTH).T
     up_blocks = split_columns(adapter_up_factor.reshape(own_slots * rank, model), req_count)
-    new = incoming_key_value.reshape(2, requests * STEP_COUNT, -1, HEAD_WIDTH).transpose(1, 2, 0, 3)
-    new = new.reshape(-1, HEAD_WIDTH)
-    pages = split_heads(key_value_pages)
-    inbox_pages = split_heads(inbox)
+    new = incoming_key_value.transpose(1, 0, 2).reshape(-1, columns)
     down = adapter_down_factor.transpose(0, 2, 1).reshape(own_slots * rank, -1)
 
+    up = lax.all_to_all(up_blocks, "req", split_axis=0, concat_axis=0, tiled=True)
+    up = up.reshape(req_count * own_slots * rank, -1)
     slot_count = adapter_storage_slot.shape[0]
     ids = inbox[:, BLOCK - 1, 0, :requests].astype(jnp.int32)
     match = ids[:, :, None] == jnp.arange(slot_count, dtype=jnp.int32)
@@ -580,7 +611,7 @@
     special = tp_count == 4
     roles = [my_lane ^ j if special else jnp.int32(j) for j in range(tp_count)]
     terms, lows, early, gates = [], [], [], []
-    mixed = [attend(h, order, lengths, table, q, new, pages, inbox_pages) for h in range(HALVES)]
+    mixed = [attend(h, order, lengths, table, q, new, key_value_pages, inbox) for h in range(HALVES)]
     gates = [mixed[-1]]
     for h in range(HALVES):
         blocks, origins, far = gather(after(mixed[h], *early), gates)
@@ -592,21 +623,18 @@
         where = jnp.stack(where + roles)
         token_slot = jnp.repeat(slot[:, h * half : (h + 1) * half], STEP_COUNT, axis=1)
         mask = (token_slot.reshape(tp_count, -1)[:, :, None] == mine).astype(jnp.bfloat16)
-        if h:
-            mask = after(mask, passed)
+        mask = after(mask, *([passed] if h else [up]))
         *parts, low = project(where, blocks, output_projection_weight, down, mask, tp_count)
         gates = [low]
         lows.append(low)
         sums, passed = scatter(parts)
         terms.append(sums)
 
-    up = lax.all_to_all(after(up_blocks, lows[0]), "req", split_axis=0, concat_axis=0, tiled=True)
-    up = up.reshape(req_count * own_slots * rank, -1)
-    low = after(jnp.concatenate(lows, axis=1), *terms[0])
+    low = after(jnp.concatenate(lows, axis=1), passed)
     low = lax.all_to_all(low, "tp", split_axis=0, concat_axis=0, tiled=True)
     low = jnp.sum(low.astype(jnp.float32), axis=0).astype(jnp.bfloat16)
     low = after(low, *terms[1][:3])
-    low = lax.all_gather(low, "req", axis=0)
+    low = after(lax.all_gather(low, "req", axis=0), *terms[1])
     return finish(terms, cores, adapt(low, up))
 
 

time: 168 us -> 162 us (0.964)
  waiting for transfers between devices: 35.1 us -> 57.9 us
  Pallas kernels: 58.9 us -> 43.8 us
  local copies, waits for them, and re-layouts: 15.6 us -> 9.21 us
  starting transfers between devices: 41.2 us -> 36.2 us
  blocking collectives: 13.7 us -> 9.22 us
  other arithmetic: 2.07 us -> 4.33 us
    ppermute x18 -> x14, waiting for transfers between devices: 10.9 us -> 38 us  [exchange(): return lax.ppermute(x, axis, [(i, i ^ distance) for i in range(count)])]
    pallas_call x2, Pallas kernels: 41.2 us -> 26.5 us  [attend(): pl.pallas_call(functools.partial(attend_kernel, req_count, per_dev, part...]
    ppermute x2 -> x0, waiting for transfers between devices: 10.6 us -> none  [scatter(): onward = lax.ppermute(three, 'tp', [(0, 1), (3, 2)])]
    unnamed x57 -> x30, local copies, waits for them, and re-layouts: 14.6 us -> 5.29 us
    ppermute x2 -> x0, starting transfers between devices: 6.91 us -> none  [scatter(): onward = lax.ppermute(three, 'tp', [(0, 1), (3, 2)])]
    all_to_all x1, waiting for transfers between devices: 5.2 us -> 11.7 us  [on_device(): low = lax.all_to_all(low, 'tp', split_axis=0, concat_axis=0, tiled=True)]
    all_gather x1, blocking collectives: 13.7 us -> 9.22 us  [on_device(): low = after(lax.all_gather(low, 'req', axis=0), *terms[1])]
    another operation x0 -> x2, other arithmetic: none -> 2.31 us  [gather(): group = jnp.stack([after(block, *gates) for block in far] if gates else far)]
  transfers between devices with their start and end apart: 25 -> 19, of which waited for: 6 -> 8; matrix products, arithmetic and copies ran while one was open for 2% -> 4% of each run, Pallas kernels for 20% -> 21%
where the time goes in v7:
time: 162 us; the launch traced here: 161 us
  waiting for transfers between devices  57.9 us (36%)
  Pallas kernels  43.8 us (27%)
  starting transfers between devices  36.2 us (22%)
  blocking collectives  9.22 us (6%)
  local copies, waits for them, and re-layouts  9.21 us (6%)
  other arithmetic  4.33 us (3%)
    ppermute x14, waiting for transfers between devices, exchange(): return lax.ppermute(x, axis, [(i, i ^ distance) for i in range(count)])  38 us
    pallas_call x2, Pallas kernels, attend(): pl.pallas_call(functools.partial(attend_kernel, req_count, per_dev, part...  26.5 us
    ppermute x14, starting transfers between devices, exchange(): return lax.ppermute(x, axis, [(i, i ^ distance) for i in range(count)])  19.7 us
    all_to_all x1, waiting for transfers between devices, on_device(): low = lax.all_to_all(low, 'tp', split_axis=0, concat_axis=0, tiled=True)  11.7 us
    pallas_call x2, Pallas kernels, project(): pl.pallas_call(functools.partial(project_kernel, count, roles, min(256, c...  10 us
    all_gather x1, blocking collectives, on_device(): low = after(lax.all_gather(low, 'req', axis=0), *terms[1])  9.22 us
    all_to_all x1, waiting for transfers between devices, on_device(): lax.all_to_all(outbox, 'req', split_axis=0, concat_axis=0, tiled=True)  8.24 us
    unnamed x30, local copies, waits for them, and re-layouts  5.29 us
  transfers between devices with their start and end apart: 19, of which 8 were waited for; matrix products, arithmetic and copies ran while one was open for 4% of the time, Pallas kernels for 21%

profile of v7, /device:TPU:0, one launch (start us, length us, event | category | flops | bytes accessed | tf_op | source)
XLA Modules:
  0.0 161.1 jit_solution(16512521203299454530)
XLA Ops:
  0.0 3.7 %pack_outbox.1 = bf16[8,65,2,256]{3,2,1,0:T(2,128)(2,1)} custom-call(s32[1]{0:T(128)} %bitcast.12.me_ref, s32[1,512]{1,0:T(1,128)} %bitcast.39, s32[1,32]{1,0:T(1,128)} %bitcast.45, bf16[512,32,2,256]{3,2,1,0:T(2,128)(2,1)} %pages.5), custom_call_target="tpu_custom_call" | custom-call | flops 1 | bytes 1 | tf_op jit(solution)/shard_map/pack_outbox/pallas_call | solution.py:111
  3.7 5.3 %all-to-all-start = ((bf16[8,65,2,256]{3,2,1,0:T(2,128)(2,1)}), bf16[8,65,2,256]{3,2,1,0:T(2,128)(2,1)S(1)}, u32[]{:S(2)}, u32[]{:S(2)}) async-start(bf16[8,65,2,256]{3,2,1,0:T(2,128)(2,1)} %pack_outbox.1), calls=%async_computation | async-start | bytes 1064960 | tf_op jit(solution)/shard_map/all_to_all | solution.py:595
  10.6 8.2 %all-to-all-done.inbox = bf16[8,65,2,256]{3,2,1,0:T(2,128)(2,1)S(1)} async-done(((bf16[8,65,2,256]{3,2,1,0:T(2,128)(2,1)}), bf16[8,65,2,256]{3,2,1,0:T(2,128)(2,1)S(1)}, u32[]{:S(2)}, u32[]{:S(2)}) %all-to-all-start) | async-done | bytes 532512 | tf_op jit(solution)/shard_map/all_to_all | solution.py:595
  18.8 3.6 %all-to-all-start.1 = ((bf16[8,128,1024]{2,1,0:T(8,128)(2,1)}), bf16[8,128,1024]{2,1,0:T(8,128)(2,1)S(1)}, u32[]{:S(2)}, u32[]{:S(2)}) async-start(bf16[8,128,1024]{2,1,0:T(8,128)(2,1)} %copy-done.2), calls=%async_computation.1 | async-start | bytes 4194304 | tf_op jit(solution)/shard_map/all_to_all | solution.py:603
  26.2 14.0 %attend.2.refs_0_ = bf16[64,2048]{1,0:T(8,128)(2,1)} custom-call(s32[2,128]{1,0:T(2,128)S(1)} %get-tuple-element.29.order_ref, s32[32]{0:T(128)S(1)} %copy-done.10, s32[4,128]{1,0:T(4,128)S(1)} %get-tuple-element.30.table_in, bf16[128,2048]{1,0:T(8,128)(2,1)S(1)} %bitcast.33, bf16[256,256]{1,0:T(8,128)(2,1)S(1)} %reshape.59.new_ref, ...), custom_call_target="tpu_custom_call" | custom-call | flops 1073741824 | bytes 8388608 | tf_op jit(solution)/shard_map/attend/pallas_call | solution.py:363
  40.2 3.3 %collective-permute-start.2 = (bf16[64,2048]{1,0:T(8,128)(2,1)}, bf16[64,2048]{1,0:T(8,128)(2,1)}, u32[]{:S(2)}, u32[]{:S(2)}) collective-permute-start(bf16[64,2048]{1,0:T(8,128)(2,1)} %attend.2.refs_0_), channel_id=1, source_target_pairs={{0,24},{4,28},{8,16},{12,20},{16,8},{20,12},{24,0},{28,4},{1,25},{... | collective-permute-start | bytes 786440 | tf_op jit(solution)/shard_map/ppermute | solution.py:540
  43.5 2.0 %collective-permute-start.1 = (bf16[64,2048]{1,0:T(8,128)(2,1)}, bf16[64,2048]{1,0:T(8,128)(2,1)}, u32[]{:S(2)}, u32[]{:S(2)}) collective-permute-start(bf16[64,2048]{1,0:T(8,128)(2,1)} %attend.2.refs_0_), channel_id=1, source_target_pairs={{0,16},{4,20},{8,24},{12,28},{16,0},{20,4},{24,8},{28,12},{1,17},{... | collective-permute-start | bytes 786440 | tf_op jit(solution)/shard_map/ppermute | solution.py:540
  45.6 12.6 %attend.3.refs_0_ = bf16[64,2048]{1,0:T(8,128)(2,1)} custom-call(s32[2,128]{1,0:T(2,128)S(1)} %get-tuple-element.29.order_ref, s32[32]{0:T(128)S(1)} %copy-done.10, s32[4,128]{1,0:T(4,128)S(1)} %get-tuple-element.30.table_in, bf16[128,2048]{1,0:T(8,128)(2,1)S(1)} %bitcast.34, bf16[256,256]{1,0:T(8,128)(2,1)S(1)} %reshape.59.new_ref, ...), custom_call_target="tpu_custom_call" | custom-call | flops 1073741824 | bytes 8388608 | tf_op jit(solution)/shard_map/attend/pallas_call | solution.py:363
  58.2 2.2 %collective-permute-done.1 = bf16[64,2048]{1,0:T(8,128)(2,1)} collective-permute-done((bf16[64,2048]{1,0:T(8,128)(2,1)}, bf16[64,2048]{1,0:T(8,128)(2,1)}, u32[]{:S(2)}, u32[]{:S(2)}) %collective-permute-start.1) | collective-permute-done | bytes 262176 | tf_op jit(solution)/shard_map/ppermute | solution.py:540
  63.2 2.1 %collective-permute-start.6 = (bf16[64,2048]{1,0:T(8,128)(2,1)}, bf16[64,2048]{1,0:T(8,128)(2,1)}, u32[]{:S(2)}, u32[]{:S(2)}) collective-permute-start(bf16[64,2048]{1,0:T(8,128)(2,1)} %attend.3.refs_0_), channel_id=1, source_target_pairs={{0,16},{4,20},{8,24},{12,28},{16,0},{20,4},{24,8},{28,12},{1,17},{... | collective-permute-start | bytes 786440 | tf_op jit(solution)/shard_map/ppermute | solution.py:540
  66.8 2.2 %copy-done = bf16[2048,1024]{1,0:T(8,128)(2,1)S(1)} copy-done((bf16[2048,1024]{1,0:T(8,128)(2,1)S(1)}, bf16[2048,1024]{1,0:T(8,128)(2,1)}, u32[]{:S(2)}) %copy-start) | copy-done | bytes 4194328
  70.0 5.2 %project.2 = (bf16[128,1024]{1,0:T(8,128)(2,1)S(1)}, bf16[2,128,1024]{2,1,0:T(8,128)(2,1)S(1)}, bf16[128,1024]{1,0:T(8,128)(2,1)S(1)}, bf16[128,1024]{1,0:T(8,128)(2,1)S(1)}, bf16[4,128,128]{2,1,0:T(8,128)(2,1)S(1)}) custom-call(s32[12]{0:T(128)S(1)} %stack.88.where_ref, bf16[64,2048]{1,0:T(8,128)(2,1)} %attend.2.refs_0_, ...), custom_call_target="tpu_custom_call" | custom-call | flops 1 | bytes 1 | tf_op jit(solution)/shard_map/project/pallas_call | solution.py:457
  75.3 2.3 %collective-permute-done.6 = bf16[64,2048]{1,0:T(8,128)(2,1)} collective-permute-done((bf16[64,2048]{1,0:T(8,128)(2,1)}, bf16[64,2048]{1,0:T(8,128)(2,1)}, u32[]{:S(2)}, u32[]{:S(2)}) %collective-permute-start.6) | collective-permute-done | bytes 262176 | tf_op jit(solution)/shard_map/ppermute | solution.py:540
  80.5 12.5 %collective-permute-done.10.passed_ref.refs_1_ = bf16[2,128,1024]{2,1,0:T(8,128)(2,1)S(1)} collective-permute-done((bf16[2,128,1024]{2,1,0:T(8,128)(2,1)S(1)}, bf16[2,128,1024]{2,1,0:T(8,128)(2,1)S(1)}, u32[]{:S(2)}, u32[]{:S(2)}) %collective-permute-start.10) | collective-permute-done | bytes 524320 | tf_op jit(solution)/shard_map/ppermute | solution.py:540
  93.1 4.8 %project.3 = (bf16[128,1024]{1,0:T(8,128)(2,1)S(1)}, bf16[2,128,1024]{2,1,0:T(8,128)(2,1)S(1)}, bf16[128,1024]{1,0:T(8,128)(2,1)S(1)}, bf16[128,1024]{1,0:T(8,128)(2,1)S(1)}, bf16[4,128,128]{2,1,0:T(8,128)(2,1)S(1)}) custom-call(s32[12]{0:T(128)S(1)} %stack.88.where_ref, bf16[64,2048]{1,0:T(8,128)(2,1)} %attend.3.refs_0_, ...), custom_call_target="tpu_custom_call" | custom-call | flops 1 | bytes 1 | tf_op jit(solution)/shard_map/project/pallas_call | solution.py:457
  98.0 1.7 %collective-permute-start.11 = (bf16[2,128,1024]{2,1,0:T(8,128)(2,1)S(1)}, bf16[2,128,1024]{2,1,0:T(8,128)(2,1)S(1)}, u32[]{:S(2)}, u32[]{:S(2)}) collective-permute-start(bf16[2,128,1024]{2,1,0:T(8,128)(2,1)S(1)} %get-tuple-element.45), channel_id=1, source_target_pairs={{0,1},{1,0},{2,3},{3,2},{4,5},{5,4},{6,7},{7,6},{8,9},{9,8},{10,11... | collective-permute-start | bytes 1572872 | tf_op jit(solution)/shard_map/ppermute | solution.py:540
  100.4 11.1 %collective-permute-done.11.passed_ref.refs_5_ = bf16[2,128,1024]{2,1,0:T(8,128)(2,1)S(1)} collective-permute-done((bf16[2,128,1024]{2,1,0:T(8,128)(2,1)S(1)}, bf16[2,128,1024]{2,1,0:T(8,128)(2,1)S(1)}, u32[]{:S(2)}, u32[]{:S(2)}) %collective-permute-start.11) | collective-permute-done | bytes 524320 | tf_op jit(solution)/shard_map/ppermute | solution.py:540
  112.2 4.9 %all-to-all-start.2 = ((bf16[4,256,128]{2,1,0:T(8,128)(2,1)}), bf16[4,256,128]{2,1,0:T(8,128)(2,1)}, u32[]{:S(2)}, u32[]{:S(2)}) async-start(bf16[4,256,128]{2,1,0:T(8,128)(2,1)} %pad_maximum_fusion.2), calls=%async_computation.2 | async-start | bytes 524288 | tf_op jit(solution)/shard_map/all_to_all | solution.py:634
  118.5 4.1 %collective-permute-start.13 = (bf16[128,1024]{1,0:T(8,128)(2,1)}, bf16[128,1024]{1,0:T(8,128)(2,1)}, u32[]{:S(2)}, u32[]{:S(2)}) collective-permute-start(bf16[128,1024]{1,0:T(8,128)(2,1)} %copy-done.8), channel_id=1, source_target_pairs={{0,2},{1,3},{2,0},{3,1},{4,6},{5,7},{6,4},{7,5},{8,10},{9,11},{10,... | collective-permute-start | bytes 786440 | tf_op jit(solution)/shard_map/ppermute | solution.py:540
  123.9 2.3 %collective-permute-start.15 = (bf16[128,1024]{1,0:T(8,128)(2,1)}, bf16[128,1024]{1,0:T(8,128)(2,1)}, u32[]{:S(2)}, u32[]{:S(2)}) collective-permute-start(bf16[128,1024]{1,0:T(8,128)(2,1)} %copy-done.7), channel_id=1, source_target_pairs={{0,2},{1,3},{2,0},{3,1},{4,6},{5,7},{6,4},{7,5},{8,10},{9,11},{10,... | collective-permute-start | bytes 786440 | tf_op jit(solution)/shard_map/ppermute | solution.py:540
  126.3 11.7 %all-to-all-done.2 = bf16[4,256,128]{2,1,0:T(8,128)(2,1)} async-done(((bf16[4,256,128]{2,1,0:T(8,128)(2,1)}), bf16[4,256,128]{2,1,0:T(8,128)(2,1)}, u32[]{:S(2)}, u32[]{:S(2)}) %all-to-all-start.2) | async-done | bytes 262176 | tf_op jit(solution)/shard_map/all_to_all | solution.py:634
  139.0 9.2 %all-gather = bf16[2048,128]{1,0:T(8,128)(2,1)S(1)} all-gather(bf16[256,128]{1,0:T(8,128)(2,1)S(1)} %reduce_sum.22), channel_id=2, replica_groups=mesh['req'=8,'tp'=4] {'req'}, dimensions={0}, use_global_device_ids=true | all-gather | bytes 589824 | tf_op jit(solution)/shard_map/all_gather | solution.py:637
  149.9 8.9 %collective-permute-done.15.refs_3_ = bf16[128,1024]{1,0:T(8,128)(2,1)} collective-permute-done((bf16[128,1024]{1,0:T(8,128)(2,1)}, bf16[128,1024]{1,0:T(8,128)(2,1)}, u32[]{:S(2)}, u32[]{:S(2)}) %collective-permute-start.15) | collective-permute-done | bytes 262176 | tf_op jit(solution)/shard_map/ppermute | solution.py:540
  158.8 2.3 %finish.1 = bf16[256,1024]{1,0:T(8,128)(2,1)} custom-call(f32[256,1024]{1,0:T(8,128)S(1)} %adapt.1.extra_ref, bf16[128,1024]{1,0:T(8,128)(2,1)S(1)} %copy-done.6, bf16[2,128,1024]{2,1,0:T(8,128)(2,1)S(1)} %collective-permute-done.10.passed_ref.refs_1_, bf16[128,1024]{1,0:T(8,128)(2,1)} %collective-permute-done.14.refs_2_, ...), custom_call_target="tpu_custom_call" | custom-call | flops 1 | bytes 1 | tf_op jit(solution)/shard_map/finish/pallas_call | solution.py:527
  (74 shorter events, 20.6 us)
Async XLA Ops:
  3.7 15.1 %all-to-all-start = ((bf16[8,65,2,256]{3,2,1,0:T(2,128)(2,1)}), bf16[8,65,2,256]{3,2,1,0:T(2,128)(2,1)S(1)}, u32[]{:S(2)}, u32[]{:S(2)}) async-start(bf16[8,65,2,256]{3,2,1,0:T(2,128)(2,1)} %pack_outbox.1), calls=%async_computation | async-start | bytes 1064960 | tf_op jit(solution)/shard_map/all_to_all | solution.py:595
  18.8 47.9 %all-to-all-start.1 = ((bf16[8,128,1024]{2,1,0:T(8,128)(2,1)}), bf16[8,128,1024]{2,1,0:T(8,128)(2,1)S(1)}, u32[]{:S(2)}, u32[]{:S(2)}) async-start(bf16[8,128,1024]{2,1,0:T(8,128)(2,1)} %copy-done.2), calls=%async_computation.1 | async-start | bytes 4194304 | tf_op jit(solution)/shard_map/all_to_all | solution.py:603
  40.2 18.0 %collective-permute-start.2 = (bf16[64,2048]{1,0:T(8,128)(2,1)}, bf16[64,2048]{1,0:T(8,128)(2,1)}, u32[]{:S(2)}, u32[]{:S(2)}) collective-permute-start(bf16[64,2048]{1,0:T(8,128)(2,1)} %attend.2.refs_0_), channel_id=1, source_target_pairs={{0,24},{4,28},{8,16},{12,20},{16,8},{20,12},{24,0},{28,4},{1,25},{... | collective-permute-start | bytes 786440 | tf_op jit(solution)/shard_map/ppermute | solution.py:540
  43.5 16.9 %collective-permute-start.1 = (bf16[64,2048]{1,0:T(8,128)(2,1)}, bf16[64,2048]{1,0:T(8,128)(2,1)}, u32[]{:S(2)}, u32[]{:S(2)}) collective-permute-start(bf16[64,2048]{1,0:T(8,128)(2,1)} %attend.2.refs_0_), channel_id=1, source_target_pairs={{0,16},{4,20},{8,24},{12,28},{16,0},{20,4},{24,8},{28,12},{1,17},{... | collective-permute-start | bytes 786440 | tf_op jit(solution)/shard_map/ppermute | solution.py:540
  45.4 14.9 %collective-permute-start = (bf16[64,2048]{1,0:T(8,128)(2,1)}, bf16[64,2048]{1,0:T(8,128)(2,1)}, u32[]{:S(2)}, u32[]{:S(2)}) collective-permute-start(bf16[64,2048]{1,0:T(8,128)(2,1)} %attend.2.refs_0_), channel_id=1, source_target_pairs={{0,8},{4,12},{8,0},{12,4},{16,24},{20,28},{24,16},{28,20},{1,9},{5... | collective-permute-start | bytes 786440 | tf_op jit(solution)/shard_map/ppermute | solution.py:540
  45.5 21.2 %collective-permute-start.3 = (bf16[64,2048]{1,0:T(8,128)(2,1)}, bf16[64,2048]{1,0:T(8,128)(2,1)}, u32[]{:S(2)}, u32[]{:S(2)}) collective-permute-start(bf16[64,2048]{1,0:T(8,128)(2,1)} %attend.2.refs_0_), channel_id=1, source_target_pairs={{0,4},{4,0},{8,12},{12,8},{16,20},{20,16},{24,28},{28,24},{1,5},{5... | collective-permute-start | bytes 786440 | tf_op jit(solution)/shard_map/ppermute | solution.py:540
  61.6 5.2 %collective-permute-start.4 = (bf16[3,64,2048]{2,1,0:T(8,128)(2,1)S(1)}, bf16[3,64,2048]{2,1,0:T(8,128)(2,1)}, u32[]{:S(2)}, u32[]{:S(2)}) collective-permute-start(bf16[3,64,2048]{2,1,0:T(8,128)(2,1)S(1)} %pad_maximum_fusion.refs_1_), channel_id=1, source_target_pairs={{0,4},{4,0},{8,12},{12,8},{16,20},{20,16},{24,28},{28,24},{1,5},{5... | collective-permute-start | bytes 2359304 | tf_op jit(solution)/shard_map/ppermute | solution.py:540
  62.5 12.8 %collective-permute-start.7 = (bf16[64,2048]{1,0:T(8,128)(2,1)}, bf16[64,2048]{1,0:T(8,128)(2,1)S(1)}, u32[]{:S(2)}, u32[]{:S(2)}) collective-permute-start(bf16[64,2048]{1,0:T(8,128)(2,1)} %attend.3.refs_0_), channel_id=1, source_target_pairs={{0,24},{4,28},{8,16},{12,20},{16,8},{20,12},{24,0},{28,4},{1,25},{... | collective-permute-start | bytes 786440 | tf_op jit(solution)/shard_map/ppermute | solution.py:540
  63.2 14.3 %collective-permute-start.6 = (bf16[64,2048]{1,0:T(8,128)(2,1)}, bf16[64,2048]{1,0:T(8,128)(2,1)}, u32[]{:S(2)}, u32[]{:S(2)}) collective-permute-start(bf16[64,2048]{1,0:T(8,128)(2,1)} %attend.3.refs_0_), channel_id=1, source_target_pairs={{0,16},{4,20},{8,24},{12,28},{16,0},{20,4},{24,8},{28,12},{1,17},{... | collective-permute-start | bytes 786440 | tf_op jit(solution)/shard_map/ppermute | solution.py:540
  65.2 12.3 %collective-permute-start.5 = (bf16[64,2048]{1,0:T(8,128)(2,1)}, bf16[64,2048]{1,0:T(8,128)(2,1)}, u32[]{:S(2)}, u32[]{:S(2)}) collective-permute-start(bf16[64,2048]{1,0:T(8,128)(2,1)} %attend.3.refs_0_), channel_id=1, source_target_pairs={{0,8},{4,12},{8,0},{12,4},{16,24},{20,28},{24,16},{28,20},{1,9},{5... | collective-permute-start | bytes 786440 | tf_op jit(solution)/shard_map/ppermute | solution.py:540
  70.0 23.1 %copy-start.1 = (bf16[2048,1024]{1,0:T(8,128)(2,1)S(1)}, bf16[2048,1024]{1,0:T(8,128)(2,1)}, u32[]{:S(2)}) copy-start(bf16[2048,1024]{1,0:T(8,128)(2,1)} %refs_4_.3) | copy-start | bytes 12582916
  75.2 17.9 %copy-start.11 = (bf16[128,1024]{1,0:T(8,128)(2,1)}, bf16[128,1024]{1,0:T(8,128)(2,1)S(1)}, u32[]{:S(2)}) copy-start(bf16[128,1024]{1,0:T(8,128)(2,1)S(1)} %get-tuple-element.52) | copy-start | bytes 786436
  75.2 22.7 %copy-start.5 = (bf16[128,1024]{1,0:T(8,128)(2,1)}, bf16[128,1024]{1,0:T(8,128)(2,1)S(1)}, u32[]{:S(2)}) copy-start(bf16[128,1024]{1,0:T(8,128)(2,1)S(1)} %get-tuple-element.51.refs_0_) | copy-start | bytes 786436
  78.6 14.5 %collective-permute-start.9 = (bf16[3,64,2048]{2,1,0:T(8,128)(2,1)S(1)}, bf16[3,64,2048]{2,1,0:T(8,128)(2,1)S(1)}, u32[]{:S(2)}, u32[]{:S(2)}) collective-permute-start(bf16[3,64,2048]{2,1,0:T(8,128)(2,1)S(1)} %pad_maximum_fusion.1.refs_1_), channel_id=1, source_target_pairs={{0,4},{4,0},{8,12},{12,8},{16,20},{20,16},{24,28},{28,24},{1,5},{5... | collective-permute-start | bytes 2359304 | tf_op jit(solution)/shard_map/ppermute | solution.py:540
  78.7 14.3 %collective-permute-start.10 = (bf16[2,128,1024]{2,1,0:T(8,128)(2,1)S(1)}, bf16[2,128,1024]{2,1,0:T(8,128)(2,1)S(1)}, u32[]{:S(2)}, u32[]{:S(2)}) collective-permute-start(bf16[2,128,1024]{2,1,0:T(8,128)(2,1)S(1)} %get-tuple-element.41), channel_id=1, source_target_pairs={{0,1},{1,0},{2,3},{3,2},{4,5},{5,4},{6,7},{7,6},{8,9},{9,8},{10,11... | collective-permute-start | bytes 1572872 | tf_op jit(solution)/shard_map/ppermute | solution.py:540
  80.4 12.7 %collective-permute-start.8 = (bf16[64,2048]{1,0:T(8,128)(2,1)}, bf16[64,2048]{1,0:T(8,128)(2,1)S(1)}, u32[]{:S(2)}, u32[]{:S(2)}) collective-permute-start(bf16[64,2048]{1,0:T(8,128)(2,1)} %attend.3.refs_0_), channel_id=1, source_target_pairs={{0,4},{4,0},{8,12},{12,8},{16,20},{20,16},{24,28},{28,24},{1,5},{5... | collective-permute-start | bytes 786440 | tf_op jit(solution)/shard_map/ppermute | solution.py:540
  93.1 18.4 %copy-start.7 = (bf16[128,1024]{1,0:T(8,128)(2,1)}, bf16[128,1024]{1,0:T(8,128)(2,1)S(1)}, u32[]{:S(2)}) copy-start(bf16[128,1024]{1,0:T(8,128)(2,1)S(1)} %add.110) | copy-start | bytes 786436
  98.0 13.6 %collective-permute-start.11 = (bf16[2,128,1024]{2,1,0:T(8,128)(2,1)S(1)}, bf16[2,128,1024]{2,1,0:T(8,128)(2,1)S(1)}, u32[]{:S(2)}, u32[]{:S(2)}) collective-permute-start(bf16[2,128,1024]{2,1,0:T(8,128)(2,1)S(1)} %get-tuple-element.45), channel_id=1, source_target_pairs={{0,1},{1,0},{2,3},{3,2},{4,5},{5,4},{6,7},{7,6},{8,9},{9,8},{10,11... | collective-permute-start | bytes 1572872 | tf_op jit(solution)/shard_map/ppermute | solution.py:540
  112.2 25.7 %all-to-all-start.2 = ((bf16[4,256,128]{2,1,0:T(8,128)(2,1)}), bf16[4,256,128]{2,1,0:T(8,128)(2,1)}, u32[]{:S(2)}, u32[]{:S(2)}) async-start(bf16[4,256,128]{2,1,0:T(8,128)(2,1)} %pad_maximum_fusion.2), calls=%async_computation.2 | async-start | bytes 524288 | tf_op jit(solution)/shard_map/all_to_all | solution.py:634
  117.1 21.8 %collective-permute-start.12 = (bf16[128,1024]{1,0:T(8,128)(2,1)}, bf16[128,1024]{1,0:T(8,128)(2,1)}, u32[]{:S(2)}, u32[]{:S(2)}) collective-permute-start(bf16[128,1024]{1,0:T(8,128)(2,1)} %copy-done.12), channel_id=1, source_target_pairs={{1,2},{2,1},{5,6},{6,5},{9,10},{10,9},{13,14},{14,13},{17,18},{18,... | collective-permute-start | bytes 786440 | tf_op jit(solution)/shard_map/ppermute | solution.py:565
  118.5 30.7 %collective-permute-start.13 = (bf16[128,1024]{1,0:T(8,128)(2,1)}, bf16[128,1024]{1,0:T(8,128)(2,1)}, u32[]{:S(2)}, u32[]{:S(2)}) collective-permute-start(bf16[128,1024]{1,0:T(8,128)(2,1)} %copy-done.8), channel_id=1, source_target_pairs={{0,2},{1,3},{2,0},{3,1},{4,6},{5,7},{6,4},{7,5},{8,10},{9,11},{10,... | collective-permute-start | bytes 786440 | tf_op jit(solution)/shard_map/ppermute | solution.py:540
  122.6 27.3 %collective-permute-start.14 = (bf16[128,1024]{1,0:T(8,128)(2,1)}, bf16[128,1024]{1,0:T(8,128)(2,1)}, u32[]{:S(2)}, u32[]{:S(2)}) collective-permute-start(bf16[128,1024]{1,0:T(8,128)(2,1)} %copy-done.11), channel_id=1, source_target_pairs={{1,2},{2,1},{5,6},{6,5},{9,10},{10,9},{13,14},{14,13},{17,18},{18,... | collective-permute-start | bytes 786440 | tf_op jit(solution)/shard_map/ppermute | solution.py:565
  123.9 34.8 %collective-permute-start.15 = (bf16[128,1024]{1,0:T(8,128)(2,1)}, bf16[128,1024]{1,0:T(8,128)(2,1)}, u32[]{:S(2)}, u32[]{:S(2)}) collective-permute-start(bf16[128,1024]{1,0:T(8,128)(2,1)} %copy-done.7), channel_id=1, source_target_pairs={{0,2},{1,3},{2,0},{3,1},{4,6},{5,7},{6,4},{7,5},{8,10},{9,11},{10,... | collective-permute-start | bytes 786440 | tf_op jit(solution)/shard_map/ppermute | solution.py:540
  138.9 19.8 %copy-start.6 = (bf16[128,1024]{1,0:T(8,128)(2,1)S(1)}, bf16[128,1024]{1,0:T(8,128)(2,1)}, u32[]{:S(2)}) copy-start(bf16[128,1024]{1,0:T(8,128)(2,1)} %copy-done.5) | copy-start | bytes 786436
  (10 other events, 80.6 us)

commit v8 on v7

--- a/solution.py
+++ b/solution.py
@@ -212,27 +212,36 @@
     page_rows = pages.reshape(per_dev, page_size, columns)
     inbox_rows = inbox.reshape(req_count, BLOCK * 2, columns)
 
-    tab = pltpu.make_async_copy(table_in, table, sem)
-    tab.start()
-    tab.wait()
-    first = pltpu.make_async_copy(inbox.at[:, pl.ds(BLOCK - 1, 1)], labels_v, sem)
-    first.start()
-    first.wait()
-    row = lax.broadcasted_iota(jnp.int32, (2, 128), 0)
-    weight = jnp.where(row == 0, float(DIGIT), 1.0)
-    for d in range(req_count):
-        digits = labels_v[d, 0, :, 0:128].astype(jnp.float32) * weight
-        labels_w[d : d + 1, :] = jnp.sum(digits, axis=0, keepdims=True).astype(jnp.int32)
-    back = pltpu.make_async_copy(labels_w, labels_s, sem)
-    back.start()
-    back.wait()
-    for d in range(req_count):
-        for k in range(CAP):
-            slot = labels_s[d, LABEL_LANE + k]
-
-            @pl.when(slot >= 0)
-            def _():
-                table[lax.shift_right_logical(slot, 7), slot & 127] = per_dev + d * CAP + k
+    if base == 0:
+        first = pltpu.make_async_copy(inbox.at[:, pl.ds(BLOCK - 1, 1)], labels_v, sem)
+        first.start()
+        first.wait()
+        row = lax.broadcasted_iota(jnp.int32, (2, 128), 0)
+        weight = jnp.where(row == 0, float(DIGIT), 1.0)
+        for d in range(req_count):
+            digits = labels_v[d, 0, :, 0:128].astype(jnp.float32) * weight
+            labels_w[d : d + 1, :] = jnp.sum(digits, axis=0, keepdims=True).astype(jnp.int32)
+        back = pltpu.make_async_copy(labels_w, labels_s, sem)
+        back.start()
+
+        @pl.loop(0, per_dev // 128)
+        def _(i):
+            @pl.loop(0, 128, unroll=8)
+            def _(j):
+                table[i, j] = table_in[i, j]
+
+        back.wait()
+        for d in range(req_count):
+            for k in range(CAP):
+                slot = labels_s[d, LABEL_LANE + k]
+
+                @pl.when(slot >= 0)
+                def _():
+                    table[lax.shift_right_logical(slot, 7), slot & 127] = per_dev + d * CAP + k
+
+    else:
+        table[0, 0] = 0
+        table = table_in
 
     steps = requests // pack_size
 
@@ -362,11 +371,13 @@
     extent = MAXP * PAGE_LENGTH * 2
     return pl.pallas_call(
         functools.partial(attend_kernel, req_count, per_dev, part * requests, requests),
-        out_shape=jax.ShapeDtypeStruct((tokens, heads * HEAD_WIDTH), jnp.bfloat16),
-        in_specs=[SMEM, SMEM, ANY, VMEM, VMEM, HBM, ANY],
-        out_specs=VMEM,
+        out_shape=(
+            jax.ShapeDtypeStruct((tokens, heads * HEAD_WIDTH), jnp.bfloat16),
+            jax.ShapeDtypeStruct(table.shape, jnp.int32),
+        ),
+        in_specs=[SMEM, SMEM, SMEM, VMEM, VMEM, HBM, ANY],
+        out_specs=(VMEM, SMEM),
         scratch_shapes=[
-            pltpu.SMEM((per_dev // 128, 128), jnp.int32),
             pltpu.VMEM((req_count, 1, 2, columns), jnp.bfloat16),
             pltpu.VMEM((req_count, 128), jnp.int32),
             pltpu.SMEM((req_count, 128), jnp.int32),
@@ -410,10 +421,13 @@
     )(x)
 
 
-def project_kernel(count, roles, tile, counts, where_ref, *refs):
-    xs, (w_ref, down_ref, mask_ref), rest = refs[: len(counts)], refs[len(counts) : len(counts) + 3], refs[len(counts) + 3 :]
-    outs, low_ref, x_v = rest[:-2], rest[-2], rest[-1]
+def project_kernel(counts, roles, tile, earlier, where_ref, *refs):
+    xs, refs = refs[: len(counts)], refs[len(counts) :]
+    (w_ref, down_ref, mask_ref), refs = refs[:3], refs[3:]
+    before, refs = refs[:earlier], refs[earlier:]
+    out_ref, lows, x_v, low_v = refs[0], refs[1 : 1 + roles], refs[-2], refs[-1]
     tokens = xs[0].shape[-2]
+    count = sum(counts)
     rows = count * tokens // roles
     b = 0
     for x_ref, blocks in zip(xs, counts):
@@ -421,73 +435,46 @@
             x = x_ref[...] if len(x_ref.shape) == 2 else x_ref[k]
             x_v[pl.ds(pl.multiple_of(where_ref[b] * tokens, tokens), tokens), :] = x
             b = b + 1
-    low = dot(x_v[...], down_ref[...], ((1,), (1,)))
+    low_v[...] = dot(x_v[...], down_ref[...], ((1,), (1,)))
     for j in range(roles):
         s = where_ref[count + j]
-        low_ref[s] = (low[j * rows : (j + 1) * rows] * mask_ref[s].astype(jnp.float32)).astype(jnp.bfloat16)
+        low = low_v[pl.ds(pl.multiple_of(s * rows, rows), rows), :] * mask_ref[s].astype(jnp.float32)
+        start = before[j].shape[0] if earlier else 0
+        if earlier:
+            lows[j][0:start, :] = before[j][...]
+        lows[j][start : start + rows, :] = low.astype(jnp.bfloat16)
 
     @pl.loop(0, w_ref.shape[1] // tile)
     def _(i):
         at = pl.ds(pl.multiple_of(i * tile, tile), tile)
         y = dot(x_v[...], w_ref[:, at]).astype(jnp.bfloat16)
-        parts = [y[j * rows : (j + 1) * rows, :] for j in range(roles)]
-        if roles == 4:
-            own, pair, two, three = outs
-            own[:, at] = parts[0]
-            pair[0, :, at] = parts[1]
-            pair[1, :, at] = parts[3]
-            two[:, at] = parts[2]
-            three[:, at] = parts[3]
-        else:
-            for j in range(roles):
-                outs[j][:, at] = parts[j]
-
-
-def project(where, xs, w, down, mask, roles):
+        for j in range(roles):
+            out_ref[j, :, at] = y[j * rows : (j + 1) * rows, :]
+
+
+def project(where, xs, w, down, mask, roles, before):
     counts = tuple(1 if len(x.shape) == 2 else x.shape[0] for x in xs)
     count = sum(counts)
     tokens, width = xs[0].shape
     columns = w.shape[1]
     rows = count * tokens // roles
-    one = jax.ShapeDtypeStruct((rows, columns), jnp.bfloat16)
-    outs = [one] * roles
-    if roles == 4:
-        outs[1] = jax.ShapeDtypeStruct((2, rows, columns), jnp.bfloat16)
-    outs = outs + [jax.ShapeDtypeStruct((roles, rows, down.shape[0]), jnp.bfloat16)]
-    return pl.pallas_call(
-        functools.partial(project_kernel, count, roles, min(256, columns), counts),
-        out_shape=outs,
-        in_specs=[SMEM] + [VMEM] * (len(xs) + 3),
-        out_specs=[VMEM] * len(outs),
-        scratch_shapes=[pltpu.VMEM((count * tokens, width), jnp.bfloat16)],
+    height = rows + (before[0].shape[0] if before else 0)
+    ranks = down.shape[0]
+    out, *lows = pl.pallas_call(
+        functools.partial(project_kernel, counts, roles, min(256, columns), len(before)),
+        out_shape=[jax.ShapeDtypeStruct((roles, rows, columns), jnp.bfloat16)]
+        + [jax.ShapeDtypeStruct((height, ranks), jnp.bfloat16)] * roles,
+        in_specs=[SMEM] + [VMEM] * (len(xs) + 3 + len(before)),
+        out_specs=[VMEM] * (1 + roles),
+        scratch_shapes=[
+            pltpu.VMEM((count * tokens, width), jnp.bfloat16),
+            pltpu.VMEM((count * tokens, ranks), jnp.float32),
+        ],
         compiler_params=params(),
         cost_estimate=SMALL,
         name="project",
-    )(where, *xs, w, down, mask)
-
-
-def add_kernel(lane_ref, own_ref, passed_ref, o_ref):
-    middle = (lane_ref[0] == 1) | (lane_ref[0] == 2)
-
-    @pl.when(middle)
-    def _():
-        o_ref[...] = (own_ref[...].astype(jnp.float32) + passed_ref[1].astype(jnp.float32)).astype(jnp.bfloat16)
-
-    @pl.when(jnp.logical_not(middle))
-    def _():
-        o_ref[...] = own_ref[...]
-
-
-def add(lane, own, passed):
-    return pl.pallas_call(
-        add_kernel,
-        out_shape=jax.ShapeDtypeStruct(own.shape, own.dtype),
-        in_specs=[SMEM, VMEM, VMEM],
-        out_specs=VMEM,
-        compiler_params=params(),
-        cost_estimate=SMALL,
-        name="add",
-    )(lane, own, passed)
+    )(where, *xs, w, down, mask, *before)
+    return out, lows
 
 
 def adapt_kernel(low_ref, up_ref, o_ref):
@@ -507,32 +494,29 @@
     )(low, up)
 
 
-def finish_kernel(counts, cores, extra_ref, *refs):
-    terms, o_ref = refs[:-1], refs[-1]
-    rows = terms[0].shape[0]
+def finish_kernel(cores, extra_ref, *refs):
+    sums, o_ref = refs[:-1], refs[-1]
+    roles, rows, _ = sums[0].shape
     tokens = rows // cores
-    first = 0
-    for h, count in enumerate(counts):
+    for h, sum_ref in enumerate(sums):
         total = extra_ref[h * rows : (h + 1) * rows, :]
-        for term in terms[first : first + count]:
-            total = total + (term[...] if len(term.shape) == 2 else term[0]).astype(jnp.float32)
-        first = first + count
+        for j in range(roles):
+            total = total + sum_ref[j].astype(jnp.float32)
         for c in range(cores):
-            at = (c * len(counts) + h) * tokens
+            at = (c * len(sums) + h) * tokens
             o_ref[at : at + tokens, :] = total[c * tokens : (c + 1) * tokens].astype(jnp.bfloat16)
 
 
-def finish(terms, cores, extra):
-    flat = [t for half in terms for t in half]
+def finish(sums, cores, extra):
     return pl.pallas_call(
-        functools.partial(finish_kernel, tuple(len(half) for half in terms), cores),
+        functools.partial(finish_kernel, cores),
         out_shape=jax.ShapeDtypeStruct(extra.shape, jnp.bfloat16),
-        in_specs=[VMEM] * (1 + len(flat)),
+        in_specs=[VMEM] * (1 + len(sums)),
         out_specs=VMEM,
         compiler_params=params(),
         cost_estimate=SMALL,
         name="finish",
-    )(extra, *flat)
+    )(extra, *sums)
 
 
 def exchange(x, axis, distance):
@@ -554,17 +538,6 @@
     far = [exchange(x, "req", d) for d in (2, 4, 6)]
     group = jnp.stack([after(block, *gates) for block in far] if gates else far)
     return [x, group, near, exchange(group, "req", 1)], [my_req ^ d for d in (0, 2, 4, 6, 1, 3, 5, 7)], far
-
-
-def scatter(blocks):
-    if len(blocks) != 4:
-        return [lax.psum_scatter(jnp.stack(blocks), "tp", scatter_dimension=0, tiled=False)], blocks[0]
-    own, pair, two, three = blocks
-    lane = lax.axis_index("tp").astype(jnp.int32).reshape(1)
-    pair = exchange(pair, "tp", 1)
-    middle = lax.ppermute(three, "tp", [(1, 2), (2, 1)])
-    passed = add(lane, two, pair)
-    return [own, pair, middle, exchange(passed, "tp", 2)], passed
 
 
 def on_device(
@@ -608,34 +581,28 @@
     slot = jnp.sum(jnp.where(match, adapter_storage_slot, 0), axis=2)
     mine = my_req * own_slots + jnp.arange(own_slots * rank, dtype=jnp.int32) // rank
 
-    special = tp_count == 4
-    roles = [my_lane ^ j if special else jnp.int32(j) for j in range(tp_count)]
-    terms, lows, early, gates = [], [], [], []
-    mixed = [attend(h, order, lengths, table, q, new, key_value_pages, inbox) for h in range(HALVES)]
-    gates = [mixed[-1]]
-    for h in range(HALVES):
-        blocks, origins, far = gather(after(mixed[h], *early), gates)
+    roles = [my_lane ^ j for j in range(tp_count)]
+    first, table = attend(0, order, lengths, table, q, new, key_value_pages, inbox)
+    second, table = attend(1, order, lengths, table, q, new, key_value_pages, inbox)
+    up = lax.all_to_all(after(up_blocks, first), "req", split_axis=0, concat_axis=0, tiled=True)
+    up = up.reshape(req_count * own_slots * rank, -1)
+    sums, lows, early, gates = [], [], [], [second]
+    for h, mixed in enumerate((first, second)):
+        blocks, origins, far = gather(after(mixed, *early), gates)
         early = far
-        where = []
-        for origin in origins:
-            s = origin // cores
-            where.append((s ^ my_lane if special else s) * cores + origin % cores)
-        where = jnp.stack(where + roles)
+        where = jnp.stack(origins + roles)
         token_slot = jnp.repeat(slot[:, h * half : (h + 1) * half], STEP_COUNT, axis=1)
         mask = (token_slot.reshape(tp_count, -1)[:, :, None] == mine).astype(jnp.bfloat16)
-        mask = after(mask, *([passed] if h else [up]))
-        *parts, low = project(where, blocks, output_projection_weight, down, mask, tp_count)
-        gates = [low]
-        lows.append(low)
-        sums, passed = scatter(parts)
-        terms.append(sums)
-
-    low = after(jnp.concatenate(lows, axis=1), passed)
-    low = lax.all_to_all(low, "tp", split_axis=0, concat_axis=0, tiled=True)
-    low = jnp.sum(low.astype(jnp.float32), axis=0).astype(jnp.bfloat16)
-    low = after(low, *terms[1][:3])
-    low = after(lax.all_gather(low, "req", axis=0), *terms[1])
-    return finish(terms, cores, adapt(low, up))
+        if h == 0:
+            mask = after(mask, up)
+        parts, lows = project(where, blocks, output_projection_weight, down, mask, tp_count, lows)
+        gates = [lows[0]]
+        sums.append(lax.all_to_all(parts, "tp", split_axis=0, concat_axis=0, tiled=True))
+
+    terms = [lows[0]] + [exchange(lows[j], "tp", j) for j in range(1, tp_count)]
+    low = functools.reduce(jnp.add, [term.astype(jnp.float32) for term in terms]).astype(jnp.bfloat16)
+    low = lax.all_gather(low, "req", axis=0)
+    return finish(sums, cores, adapt(low, up))
 
 
 def solution(mesh):

time: 162 us -> 177 us (1.093)
  waiting for transfers between devices: 57.9 us -> 70.9 us
  local copies, waits for them, and re-layouts: 9.21 us -> 20.4 us
  starting transfers between devices: 36.2 us -> 31 us
  other arithmetic: 4.33 us -> 1.63 us
    ppermute x14 -> x13, waiting for transfers between devices: 38 us -> 63.8 us  [exchange(): return lax.ppermute(x, axis, [(i, i ^ distance) for i in range(count)])]
    unnamed x30 -> x66, local copies, waits for them, and re-layouts: 5.29 us -> 19.2 us
    all_to_all x2 -> x3, waiting for transfers between devices: 11.7 us -> 0.01 us  [the longest x2 0.01 us: on_device(): lax.all_to_all(parts, 'tp', split_axis=0, concat_axis=0, tiled=True)]
    ppermute x14 -> x13, starting transfers between devices: 19.7 us -> 12.2 us  [exchange(): return lax.ppermute(x, axis, [(i, i ^ distance) for i in range(count)])]
    all_to_all x2 -> x3, starting transfers between devices: 8.48 us -> 13.6 us  [the longest x2 9.96 us: on_device(): lax.all_to_all(parts, 'tp', split_axis=0, concat_axis=0, tiled=True)]
    ppermute x2 -> x0, starting transfers between devices: 2.74 us -> none  [scatter(): middle = lax.ppermute(three, 'tp', [(1, 2), (2, 1)])]
    reshape x2, local copies, waits for them, and re-layouts: 2.28 us -> 0.46 us  [on_device(): q = queries.reshape(requests * STEP_COUNT * heads, HEAD_WIDTH).T]
    pallas_call x5 -> x3, Pallas kernels: 12.3 us -> 11.7 us  [the longest x2 9.44 us: project(): pl.pallas_call(functools.partial(project_kernel, counts, roles, min(256,...]
  transfers between devices with their start and end apart: 19 -> 17, of which waited for: 8 -> 11; matrix products, arithmetic and copies ran while one was open for 4% -> 2% of each run, Pallas kernels for 21% -> 10%
where the time goes in v8:
time: 177 us
  waiting for transfers between devices  70.9 us (40%)
  Pallas kernels  42.5 us (24%)
  starting transfers between devices  31 us (18%)
  local copies, waits for them, and re-layouts  20.4 us (12%)
  blocking collectives  9.77 us (6%)
    ppermute x13, waiting for transfers between devices, exchange(): return lax.ppermute(x, axis, [(i, i ^ distance) for i in range(count)])  63.8 us
    pallas_call x2, Pallas kernels, attend(): pl.pallas_call(functools.partial(attend_kernel, req_count, per_dev, part...  25.7 us
    unnamed x66, local copies, waits for them, and re-layouts  19.2 us
    ppermute x13, starting transfers between devices, exchange(): return lax.ppermute(x, axis, [(i, i ^ distance) for i in range(count)])  12.2 us
    all_to_all x2, starting transfers between devices, on_device(): lax.all_to_all(parts, 'tp', split_axis=0, concat_axis=0, tiled=True)  9.96 us
    all_gather x1, blocking collectives, on_device(): low = lax.all_gather(low, 'req', axis=0)  9.77 us
    pallas_call x2, Pallas kernels, project(): pl.pallas_call(functools.partial(project_kernel, counts, roles, min(256,...  9.44 us
    all_to_all x1, waiting for transfers between devices, on_device(): lax.all_to_all(outbox, 'req', split_axis=0, concat_axis=0, tiled=True)  7.1 us
  transfers between devices with their start and end apart: 17, of which 11 were waited for; matrix products, arithmetic and copies ran while one was open for 2% of the time, Pallas kernels for 10%

profile of v8, /device:TPU:0, one launch (start us, length us, event | category | flops | bytes accessed | tf_op | source)
XLA Modules:
  0.0 176.5 jit_solution(6700186551805673797)
XLA Ops:
  0.0 3.8 %pack_outbox.1 = bf16[8,65,2,256]{3,2,1,0:T(2,128)(2,1)} custom-call(s32[1]{0:T(128)} %bitcast.me_ref, s32[1,512]{1,0:T(1,128)} %bitcast.38, s32[1,32]{1,0:T(1,128)} %bitcast.46, bf16[512,32,2,256]{3,2,1,0:T(2,128)(2,1)} %pages.5), custom_call_target="tpu_custom_call" | custom-call | flops 1 | bytes 1 | tf_op jit(solution)/shard_map/pack_outbox/pallas_call | solution.py:111
  3.8 5.2 %all-to-all-start = ((bf16[8,65,2,256]{3,2,1,0:T(2,128)(2,1)}), bf16[8,65,2,256]{3,2,1,0:T(2,128)(2,1)S(1)}, u32[]{:S(2)}, u32[]{:S(2)}) async-start(bf16[8,65,2,256]{3,2,1,0:T(2,128)(2,1)} %pack_outbox.1), calls=%async_computation | async-start | bytes 1064960 | tf_op jit(solution)/shard_map/all_to_all | solution.py:568
  11.7 7.1 %all-to-all-done.inbox = bf16[8,65,2,256]{3,2,1,0:T(2,128)(2,1)S(1)} async-done(((bf16[8,65,2,256]{3,2,1,0:T(2,128)(2,1)}), bf16[8,65,2,256]{3,2,1,0:T(2,128)(2,1)S(1)}, u32[]{:S(2)}, u32[]{:S(2)}) %all-to-all-start) | async-done | bytes 532512 | tf_op jit(solution)/shard_map/all_to_all | solution.py:568
  18.8 14.2 %attend.2 = (bf16[64,2048]{1,0:T(8,128)(2,1)}, s32[4,128]{1,0:T(4,128)S(1)}) custom-call(s32[2,128]{1,0:T(2,128)S(1)} %get-tuple-element.29.order_ref, s32[32]{0:T(128)S(1)} %copy-done.23, s32[4,128]{1,0:T(4,128)S(1)} %get-tuple-element.30.table_in, bf16[128,2048]{1,0:T(8,128)(2,1)S(1)} %bitcast.32, bf16[256,256]{1,0:T(8,128)(2,1)S(1)} %reshape.54.new_ref, ...), custom_call_target="tpu_custom_call" | custom-call | flops 1073741824 | bytes 8388608 | tf_op jit(solution)/shard_map/attend/pallas_call | solution.py:372
  33.0 3.6 %all-to-all-start.1 = ((bf16[8,128,1024]{2,1,0:T(8,128)(2,1)}), bf16[8,128,1024]{2,1,0:T(8,128)(2,1)S(1)}, u32[]{:S(2)}, u32[]{:S(2)}) async-start(bf16[8,128,1024]{2,1,0:T(8,128)(2,1)} %copy-done.2), calls=%async_computation.1 | async-start | bytes 4194304 | tf_op jit(solution)/shard_map/all_to_all | solution.py:587
  36.7 2.9 %collective-permute-start.2 = (bf16[64,2048]{1,0:T(8,128)(2,1)}, bf16[64,2048]{1,0:T(8,128)(2,1)}, u32[]{:S(2)}, u32[]{:S(2)}) collective-permute-start(bf16[64,2048]{1,0:T(8,128)(2,1)} %get-tuple-element.33.refs_0_), channel_id=1, source_target_pairs={{0,24},{4,28},{8,16},{12,20},{16,8},{20,12},{24,0},{28,4},{1,25},{... | collective-permute-start | bytes 786440 | tf_op jit(solution)/shard_map/ppermute | solution.py:524
  40.4 11.5 %attend.3 = (bf16[64,2048]{1,0:T(8,128)(2,1)S(1)}, s32[4,128]{1,0:T(4,128)}) custom-call(s32[2,128]{1,0:T(2,128)S(1)} %get-tuple-element.29.order_ref, s32[32]{0:T(128)S(1)} %copy-done.23, s32[4,128]{1,0:T(4,128)S(1)} %get-tuple-element.31.table_in, bf16[128,2048]{1,0:T(8,128)(2,1)S(1)} %bitcast.33, bf16[256,256]{1,0:T(8,128)(2,1)S(1)} %reshape.54.new_ref, ...), custom_call_target="tpu_custom_call" | custom-call | flops 1073741824 | bytes 8388608 | tf_op jit(solution)/shard_map/attend/pallas_call | solution.py:372
  51.9 17.5 %collective-permute-done.2 = bf16[64,2048]{1,0:T(8,128)(2,1)} collective-permute-done((bf16[64,2048]{1,0:T(8,128)(2,1)}, bf16[64,2048]{1,0:T(8,128)(2,1)}, u32[]{:S(2)}, u32[]{:S(2)}) %collective-permute-start.2) | collective-permute-done | bytes 262176 | tf_op jit(solution)/shard_map/ppermute | solution.py:524
  69.5 4.1 %collective-permute-done.1 = bf16[64,2048]{1,0:T(8,128)(2,1)} collective-permute-done((bf16[64,2048]{1,0:T(8,128)(2,1)}, bf16[64,2048]{1,0:T(8,128)(2,1)}, u32[]{:S(2)}, u32[]{:S(2)}) %collective-permute-start.1) | collective-permute-done | bytes 262176 | tf_op jit(solution)/shard_map/ppermute | solution.py:524
  75.8 1.6 collective-permute-done.5.refs_3_
  77.4 2.2 %copy-done = bf16[2048,1024]{1,0:T(8,128)(2,1)S(1)} copy-done((bf16[2048,1024]{1,0:T(8,128)(2,1)S(1)}, bf16[2048,1024]{1,0:T(8,128)(2,1)}, u32[]{:S(2)}) %copy-start) | copy-done | bytes 4194328
  80.6 5.1 %project.2 = (bf16[4,128,1024]{2,1,0:T(8,128)(2,1)S(1)}, bf16[128,128]{1,0:T(8,128)(2,1)S(1)}, bf16[128,128]{1,0:T(8,128)(2,1)S(1)}, bf16[128,128]{1,0:T(8,128)(2,1)S(1)}, bf16[128,128]{1,0:T(8,128)(2,1)S(1)}) custom-call(s32[12]{0:T(128)S(1)} %stack.88.where_ref, bf16[64,2048]{1,0:T(8,128)(2,1)} %get-tuple-element.33.refs_0_, ...), custom_call_target="tpu_custom_call" | custom-call | flops 1 | bytes 1 | tf_op jit(solution)/shard_map/project/pallas_call | solution.py:463
  89.2 5.0 %all-to-all-start.2 = ((bf16[4,128,1024]{2,1,0:T(8,128)(2,1)}), bf16[4,128,1024]{2,1,0:T(8,128)(2,1)S(1)}, u32[]{:S(2)}, u32[]{:S(2)}) async-start(bf16[4,128,1024]{2,1,0:T(8,128)(2,1)} %copy-done.8), calls=%async_computation.2 | async-start | bytes 2097152 | tf_op jit(solution)/shard_map/all_to_all | solution.py:600
  97.7 6.6 %collective-permute-done.7 = bf16[64,2048]{1,0:T(8,128)(2,1)S(1)} collective-permute-done((bf16[64,2048]{1,0:T(8,128)(2,1)S(1)}, bf16[64,2048]{1,0:T(8,128)(2,1)S(1)}, u32[]{:S(2)}, u32[]{:S(2)}) %collective-permute-start.7) | collective-permute-done | bytes 262176 | tf_op jit(solution)/shard_map/ppermute | solution.py:524
  104.3 4.5 %collective-permute-done.6 = bf16[64,2048]{1,0:T(8,128)(2,1)S(1)} collective-permute-done((bf16[64,2048]{1,0:T(8,128)(2,1)S(1)}, bf16[64,2048]{1,0:T(8,128)(2,1)S(1)}, u32[]{:S(2)}, u32[]{:S(2)}) %collective-permute-start.6) | collective-permute-done | bytes 262176 | tf_op jit(solution)/shard_map/ppermute | solution.py:524
  109.5 2.1 %collective-permute-done.8.refs_2_ = bf16[64,2048]{1,0:T(8,128)(2,1)S(1)} collective-permute-done((bf16[64,2048]{1,0:T(8,128)(2,1)S(1)}, bf16[64,2048]{1,0:T(8,128)(2,1)S(1)}, u32[]{:S(2)}, u32[]{:S(2)}) %collective-permute-start.8) | collective-permute-done | bytes 262176 | tf_op jit(solution)/shard_map/ppermute | solution.py:524
  111.7 2.2 %copy-done.1 = bf16[2048,1024]{1,0:T(8,128)(2,1)S(1)} copy-done((bf16[2048,1024]{1,0:T(8,128)(2,1)S(1)}, bf16[2048,1024]{1,0:T(8,128)(2,1)}, u32[]{:S(2)}) %copy-start.1) | copy-done | bytes 4194328
  117.9 4.3 %project.3 = (bf16[4,128,1024]{2,1,0:T(8,128)(2,1)S(1)}, bf16[256,128]{1,0:T(8,128)(2,1)S(1)}, bf16[256,128]{1,0:T(8,128)(2,1)S(1)}, bf16[256,128]{1,0:T(8,128)(2,1)S(1)}, bf16[256,128]{1,0:T(8,128)(2,1)S(1)}) custom-call(s32[12]{0:T(128)S(1)} %stack.88.where_ref, bf16[64,2048]{1,0:T(8,128)(2,1)S(1)} %copy-done.11, ...), custom_call_target="tpu_custom_call" | custom-call | flops 1 | bytes 1 | tf_op jit(solution)/shard_map/project/pallas_call | solution.py:463
  125.8 5.0 %all-to-all-start.3 = ((bf16[4,128,1024]{2,1,0:T(8,128)(2,1)}), bf16[4,128,1024]{2,1,0:T(8,128)(2,1)}, u32[]{:S(2)}, u32[]{:S(2)}) async-start(bf16[4,128,1024]{2,1,0:T(8,128)(2,1)} %copy-done.9), calls=%async_computation.3 | async-start | bytes 2097152 | tf_op jit(solution)/shard_map/all_to_all | solution.py:600
  130.8 3.8 %collective-permute-start.12 = (bf16[256,128]{1,0:T(8,128)(2,1)S(1)}, bf16[256,128]{1,0:T(8,128)(2,1)S(1)}, u32[]{:S(2)}, u32[]{:S(2)}) collective-permute-start(bf16[256,128]{1,0:T(8,128)(2,1)S(1)} %copy-done.29), channel_id=1, source_target_pairs={{0,3},{1,2},{2,1},{3,0},{4,7},{5,6},{6,5},{7,4},{8,11},{9,10},{10,... | collective-permute-start | bytes 196616 | tf_op jit(solution)/shard_map/ppermute | solution.py:524
  135.2 19.4 %collective-permute-done.12 = bf16[256,128]{1,0:T(8,128)(2,1)S(1)} collective-permute-done((bf16[256,128]{1,0:T(8,128)(2,1)S(1)}, bf16[256,128]{1,0:T(8,128)(2,1)S(1)}, u32[]{:S(2)}, u32[]{:S(2)}) %collective-permute-start.12) | collective-permute-done | bytes 65568 | tf_op jit(solution)/shard_map/ppermute | solution.py:524
  154.7 7.8 %collective-permute-done.11 = bf16[256,128]{1,0:T(8,128)(2,1)S(1)} collective-permute-done((bf16[256,128]{1,0:T(8,128)(2,1)S(1)}, bf16[256,128]{1,0:T(8,128)(2,1)S(1)}, u32[]{:S(2)}, u32[]{:S(2)}) %collective-permute-start.11) | collective-permute-done | bytes 65568 | tf_op jit(solution)/shard_map/ppermute | solution.py:524
  162.5 9.8 %all-gather = bf16[2048,128]{1,0:T(8,128)(2,1)S(1)} all-gather(bf16[256,128]{1,0:T(8,128)(2,1)S(1)} %add_convert_fusion), channel_id=2, replica_groups=mesh['req'=8,'tp'=4] {'req'}, dimensions={0}, use_global_device_ids=true | all-gather | bytes 589824 | tf_op jit(solution)/shard_map/all_gather | solution.py:604
  174.2 2.3 %finish.1 = bf16[256,1024]{1,0:T(8,128)(2,1)} custom-call(f32[256,1024]{1,0:T(8,128)S(1)} %adapt.1.extra_ref, bf16[4,128,1024]{2,1,0:T(8,128)(2,1)S(1)} %copy-done.4, bf16[4,128,1024]{2,1,0:T(8,128)(2,1)} %all-to-all-done.3.refs_1_), custom_call_target="tpu_custom_call" | custom-call | flops 1 | bytes 1 | tf_op jit(solution)/shard_map/finish/pallas_call | solution.py:511
  (103 shorter events, 24.5 us)
Async XLA Ops:
  0.0 9.0 %copy-start.7 = (bf16[2,64,8192]{2,1,0:T(8,128)(2,1)S(1)}, bf16[2,64,8192]{2,1,0:T(8,128)(2,1)}, u32[]{:S(2)}) copy-start(bf16[2,64,8192]{2,1,0:T(8,128)(2,1)} %param.18) | copy-start | bytes 6291460
  3.8 15.0 %all-to-all-start = ((bf16[8,65,2,256]{3,2,1,0:T(2,128)(2,1)}), bf16[8,65,2,256]{3,2,1,0:T(2,128)(2,1)S(1)}, u32[]{:S(2)}, u32[]{:S(2)}) async-start(bf16[8,65,2,256]{3,2,1,0:T(2,128)(2,1)} %pack_outbox.1), calls=%async_computation | async-start | bytes 1064960 | tf_op jit(solution)/shard_map/all_to_all | solution.py:568
  33.0 42.7 %all-to-all-start.1 = ((bf16[8,128,1024]{2,1,0:T(8,128)(2,1)}), bf16[8,128,1024]{2,1,0:T(8,128)(2,1)S(1)}, u32[]{:S(2)}, u32[]{:S(2)}) async-start(bf16[8,128,1024]{2,1,0:T(8,128)(2,1)} %copy-done.2), calls=%async_computation.1 | async-start | bytes 4194304 | tf_op jit(solution)/shard_map/all_to_all | solution.py:587
  36.7 32.8 %collective-permute-start.2 = (bf16[64,2048]{1,0:T(8,128)(2,1)}, bf16[64,2048]{1,0:T(8,128)(2,1)}, u32[]{:S(2)}, u32[]{:S(2)}) collective-permute-start(bf16[64,2048]{1,0:T(8,128)(2,1)} %get-tuple-element.33.refs_0_), channel_id=1, source_target_pairs={{0,24},{4,28},{8,16},{12,20},{16,8},{20,12},{24,0},{28,4},{1,25},{... | collective-permute-start | bytes 786440 | tf_op jit(solution)/shard_map/ppermute | solution.py:524
  39.5 34.1 %collective-permute-start.1 = (bf16[64,2048]{1,0:T(8,128)(2,1)}, bf16[64,2048]{1,0:T(8,128)(2,1)}, u32[]{:S(2)}, u32[]{:S(2)}) collective-permute-start(bf16[64,2048]{1,0:T(8,128)(2,1)} %get-tuple-element.33.refs_0_), channel_id=1, source_target_pairs={{0,16},{4,20},{8,24},{12,28},{16,0},{20,4},{24,8},{28,12},{1,17},{... | collective-permute-start | bytes 786440 | tf_op jit(solution)/shard_map/ppermute | solution.py:524
  40.0 33.6 %collective-permute-start = (bf16[64,2048]{1,0:T(8,128)(2,1)}, bf16[64,2048]{1,0:T(8,128)(2,1)}, u32[]{:S(2)}, u32[]{:S(2)}) collective-permute-start(bf16[64,2048]{1,0:T(8,128)(2,1)} %get-tuple-element.33.refs_0_), channel_id=1, source_target_pairs={{0,8},{4,12},{8,0},{12,4},{16,24},{20,28},{24,16},{28,20},{1,9},{5... | collective-permute-start | bytes 786440 | tf_op jit(solution)/shard_map/ppermute | solution.py:524
  40.3 35.5 %collective-permute-start.4 = (bf16[64,2048]{1,0:T(8,128)(2,1)}, bf16[64,2048]{1,0:T(8,128)(2,1)}, u32[]{:S(2)}, u32[]{:S(2)}) collective-permute-start(bf16[64,2048]{1,0:T(8,128)(2,1)} %get-tuple-element.33.refs_0_), channel_id=1, source_target_pairs={{0,4},{4,0},{8,12},{12,8},{16,20},{20,16},{24,28},{28,24},{1,5},{5... | collective-permute-start | bytes 786440 | tf_op jit(solution)/shard_map/ppermute | solution.py:524
  40.4 34.6 %copy-start.32 = (s32[16]{0:T(128)S(1)}, s32[16]{0:T(128)}, u32[]{:S(2)}) copy-start(s32[16]{0:T(128)} %param.16) | copy-start | bytes 196
  51.9 23.1 %copy-start.10 = (bf16[64,2048]{1,0:T(8,128)(2,1)}, bf16[64,2048]{1,0:T(8,128)(2,1)S(1)}, u32[]{:S(2)}) copy-start(bf16[64,2048]{1,0:T(8,128)(2,1)S(1)} %get-tuple-element.34.refs_0_) | copy-start | bytes 786436
  74.9 2.5 %collective-permute-start.5 = (bf16[3,64,2048]{2,1,0:T(8,128)(2,1)S(1)}, bf16[3,64,2048]{2,1,0:T(8,128)(2,1)}, u32[]{:S(2)}, u32[]{:S(2)}) collective-permute-start(bf16[3,64,2048]{2,1,0:T(8,128)(2,1)S(1)} %pad_maximum_fusion.refs_1_), channel_id=1, source_target_pairs={{0,4},{4,0},{8,12},{12,8},{16,20},{20,16},{24,28},{28,24},{1,5},{5... | collective-permute-start | bytes 2359304 | tf_op jit(solution)/shard_map/ppermute | solution.py:524
  89.2 36.6 %all-to-all-start.2 = ((bf16[4,128,1024]{2,1,0:T(8,128)(2,1)}), bf16[4,128,1024]{2,1,0:T(8,128)(2,1)S(1)}, u32[]{:S(2)}, u32[]{:S(2)}) async-start(bf16[4,128,1024]{2,1,0:T(8,128)(2,1)} %copy-done.8), calls=%async_computation.2 | async-start | bytes 2097152 | tf_op jit(solution)/shard_map/all_to_all | solution.py:600
  94.2 10.1 %collective-permute-start.7 = (bf16[64,2048]{1,0:T(8,128)(2,1)S(1)}, bf16[64,2048]{1,0:T(8,128)(2,1)S(1)}, u32[]{:S(2)}, u32[]{:S(2)}) collective-permute-start(bf16[64,2048]{1,0:T(8,128)(2,1)S(1)} %copy-done.11), channel_id=1, source_target_pairs={{0,24},{4,28},{8,16},{12,20},{16,8},{20,12},{24,0},{28,4},{1,25},{... | collective-permute-start | bytes 786440 | tf_op jit(solution)/shard_map/ppermute | solution.py:524
  95.7 13.1 %collective-permute-start.6 = (bf16[64,2048]{1,0:T(8,128)(2,1)S(1)}, bf16[64,2048]{1,0:T(8,128)(2,1)S(1)}, u32[]{:S(2)}, u32[]{:S(2)}) collective-permute-start(bf16[64,2048]{1,0:T(8,128)(2,1)S(1)} %copy-done.11), channel_id=1, source_target_pairs={{0,16},{4,20},{8,24},{12,28},{16,0},{20,4},{24,8},{28,12},{1,17},{... | collective-permute-start | bytes 786440 | tf_op jit(solution)/shard_map/ppermute | solution.py:524
  97.1 11.8 %collective-permute-start.3 = (bf16[64,2048]{1,0:T(8,128)(2,1)S(1)}, bf16[64,2048]{1,0:T(8,128)(2,1)S(1)}, u32[]{:S(2)}, u32[]{:S(2)}) collective-permute-start(bf16[64,2048]{1,0:T(8,128)(2,1)S(1)} %copy-done.11), channel_id=1, source_target_pairs={{0,8},{4,12},{8,0},{12,4},{16,24},{20,28},{24,16},{28,20},{1,9},{5... | collective-permute-start | bytes 786440 | tf_op jit(solution)/shard_map/ppermute | solution.py:524
  109.0 2.7 %collective-permute-start.9 = (bf16[3,64,2048]{2,1,0:T(8,128)(2,1)S(1)}, bf16[3,64,2048]{2,1,0:T(8,128)(2,1)S(1)}, u32[]{:S(2)}, u32[]{:S(2)}) collective-permute-start(bf16[3,64,2048]{2,1,0:T(8,128)(2,1)S(1)} %pad_maximum_fusion.1.refs_1_), channel_id=1, source_target_pairs={{0,4},{4,0},{8,12},{12,8},{16,20},{20,16},{24,28},{28,24},{1,5},{5... | collective-permute-start | bytes 2359304 | tf_op jit(solution)/shard_map/ppermute | solution.py:524
  109.0 2.6 %collective-permute-start.8 = (bf16[64,2048]{1,0:T(8,128)(2,1)S(1)}, bf16[64,2048]{1,0:T(8,128)(2,1)S(1)}, u32[]{:S(2)}, u32[]{:S(2)}) collective-permute-start(bf16[64,2048]{1,0:T(8,128)(2,1)S(1)} %copy-done.11), channel_id=1, source_target_pairs={{0,4},{4,0},{8,12},{12,8},{16,20},{20,16},{24,28},{28,24},{1,5},{5... | collective-permute-start | bytes 786440 | tf_op jit(solution)/shard_map/ppermute | solution.py:524
  125.8 46.5 %copy-start.3 = (bf16[4,128,1024]{2,1,0:T(8,128)(2,1)}, bf16[4,128,1024]{2,1,0:T(8,128)(2,1)S(1)}, u32[]{:S(2)}) copy-start(bf16[4,128,1024]{2,1,0:T(8,128)(2,1)S(1)} %all-to-all-done.2.refs_0_) | copy-start | bytes 3145732
  125.8 8.8 %copy-start.27 = (bf16[256,128]{1,0:T(8,128)(2,1)S(1)}, bf16[256,128]{1,0:T(8,128)(2,1)}, u32[]{:S(2)}) copy-start(bf16[256,128]{1,0:T(8,128)(2,1)} %copy-done.26) | copy-start | bytes 196612
  125.8 8.8 %copy-start.25 = (bf16[256,128]{1,0:T(8,128)(2,1)S(1)}, bf16[256,128]{1,0:T(8,128)(2,1)}, u32[]{:S(2)}) copy-start(bf16[256,128]{1,0:T(8,128)(2,1)} %copy-done.24) | copy-start | bytes 196612
  125.8 36.6 %copy-start.13 = (bf16[256,128]{1,0:T(8,128)(2,1)S(1)}, bf16[256,128]{1,0:T(8,128)(2,1)}, u32[]{:S(2)}) copy-start(bf16[256,128]{1,0:T(8,128)(2,1)} %copy-done.12) | copy-start | bytes 196612
  125.8 47.1 %all-to-all-start.3 = ((bf16[4,128,1024]{2,1,0:T(8,128)(2,1)}), bf16[4,128,1024]{2,1,0:T(8,128)(2,1)}, u32[]{:S(2)}, u32[]{:S(2)}) async-start(bf16[4,128,1024]{2,1,0:T(8,128)(2,1)} %copy-done.9), calls=%async_computation.3 | async-start | bytes 2097152 | tf_op jit(solution)/shard_map/all_to_all | solution.py:600
  130.8 23.9 %collective-permute-start.12 = (bf16[256,128]{1,0:T(8,128)(2,1)S(1)}, bf16[256,128]{1,0:T(8,128)(2,1)S(1)}, u32[]{:S(2)}, u32[]{:S(2)}) collective-permute-start(bf16[256,128]{1,0:T(8,128)(2,1)S(1)} %copy-done.29), channel_id=1, source_target_pairs={{0,3},{1,2},{2,1},{3,0},{4,7},{5,6},{6,5},{7,4},{8,11},{9,10},{10,... | collective-permute-start | bytes 196616 | tf_op jit(solution)/shard_map/ppermute | solution.py:524
  134.6 27.8 %collective-permute-start.11 = (bf16[256,128]{1,0:T(8,128)(2,1)S(1)}, bf16[256,128]{1,0:T(8,128)(2,1)S(1)}, u32[]{:S(2)}, u32[]{:S(2)}) collective-permute-start(bf16[256,128]{1,0:T(8,128)(2,1)S(1)} %copy-done.27), channel_id=1, source_target_pairs={{0,2},{1,3},{2,0},{3,1},{4,6},{5,7},{6,4},{7,5},{8,10},{9,11},{10,... | collective-permute-start | bytes 196616 | tf_op jit(solution)/shard_map/ppermute | solution.py:524
  134.6 27.8 %collective-permute-start.10 = (bf16[256,128]{1,0:T(8,128)(2,1)S(1)}, bf16[256,128]{1,0:T(8,128)(2,1)S(1)}, u32[]{:S(2)}, u32[]{:S(2)}) collective-permute-start(bf16[256,128]{1,0:T(8,128)(2,1)S(1)} %copy-done.25), channel_id=1, source_target_pairs={{0,1},{1,0},{2,3},{3,2},{4,5},{5,4},{6,7},{7,6},{8,9},{9,8},{10,11... | collective-permute-start | bytes 196616 | tf_op jit(solution)/shard_map/ppermute | solution.py:524
  (26 other events, 35.1 us)

commit v9 on v7

--- a/solution.py
+++ b/solution.py
@@ -23,8 +23,8 @@
 CHUNKS = MAXP // CHUNK_PAGES
 CHUNK_POSITIONS = CHUNK_PAGES * PAGE_LENGTH
 LANES = 128
+NEW_GROUP = 128 // (2 * STEP_COUNT)
 SLOTS = 6
-HALVES = 2
 VMEM_LIMIT = 24 * 1024 * 1024
 WHOLE_VMEM = 60 * 1024 * 1024
 ATTEND_VMEM = 48 * 1024 * 1024
@@ -142,7 +142,7 @@
         for i in range(tiles):
             total = total + jnp.where(columns[i] == slot, (row + i * 128).astype(jnp.float32), 0.0)
         table_ref[j : j + 1, :] = jnp.sum(total, axis=0, keepdims=True).astype(jnp.int32)
-    half = requests // HALVES
+    half = NEW_GROUP
     len_v[...] = jnp.zeros_like(len_v)
     len_v[:, 0:requests] = lengths_ref[...].astype(jnp.float32)
     along = jnp.broadcast_to(len_v[...], (128, 128))
@@ -180,7 +180,6 @@
 def attend_kernel(
     req_count,
     per_dev,
-    base,
     requests,
     order_ref,
     lengths_ref,
@@ -212,9 +211,6 @@
     page_rows = pages.reshape(per_dev, page_size, columns)
     inbox_rows = inbox.reshape(req_count, BLOCK * 2, columns)
 
-    tab = pltpu.make_async_copy(table_in, table, sem)
-    tab.start()
-    tab.wait()
     first = pltpu.make_async_copy(inbox.at[:, pl.ds(BLOCK - 1, 1)], labels_v, sem)
     first.start()
     first.wait()
@@ -225,6 +221,13 @@
         labels_w[d : d + 1, :] = jnp.sum(digits, axis=0, keepdims=True).astype(jnp.int32)
     back = pltpu.make_async_copy(labels_w, labels_s, sem)
     back.start()
+
+    @pl.loop(0, per_dev // 128)
+    def _(i):
+        @pl.loop(0, 128, unroll=8)
+        def _(j):
+            table[i, j] = table_in[i, j]
+
     back.wait()
     for d in range(req_count):
         for k in range(CAP):
@@ -237,14 +240,14 @@
     steps = requests // pack_size
 
     def most_chunks(step):
-        counts = [order_ref[1, base + step * pack_size + u] for u in range(pack_size)]
+        counts = [order_ref[1, step * pack_size + u] for u in range(pack_size)]
         return functools.reduce(jnp.maximum, counts)
 
     def fetch(step):
         place = lax.rem(step, SLOTS)
         count = most_chunks(step)
         for u in range(pack_size):
-            slot = order_ref[0, base + step * pack_size + u] * MAXP
+            slot = order_ref[0, step * pack_size + u] * MAXP
             line = lax.shift_right_logical(slot, 7)
             at = slot & 127
 
@@ -297,7 +300,7 @@
         owner = jnp.zeros((1, LANES), jnp.int32)
         rows, kvs, rights = [], [], []
         for u in range(pack_size):
-            r = order_ref[0, base + step * pack_size + u]
+            r = order_ref[0, step * pack_size + u]
             rows.append(r)
             q = q_ref[:, pl.ds(pl.multiple_of((r // pack_size) * LANES, LANES), LANES)].astype(jnp.float32)
             own = part == u
@@ -308,8 +311,9 @@
             )
             kvs.append(buf[place, u, 0:width, :])
             limit = jnp.where(one // span == u, 2 * lengths_ref[r], limit)
-            owner = jnp.where(one // span == u, r - base, owner)
-        new = new_ref[base * new_rows : (base + requests) * new_rows, :]
+            owner = jnp.where(one // span == u, r & (NEW_GROUP - 1), owner)
+        group = rows[0] // NEW_GROUP
+        new = new_ref[pl.ds(pl.multiple_of(group * 128, 128), 128), :]
         s = dot(jnp.concatenate(kvs, axis=1), jnp.concatenate(rights, axis=0))
         sn = dot(new, functools.reduce(jnp.add, rights))
         row = lax.broadcasted_iota(jnp.int32, (width, LANES), 0)
@@ -331,7 +335,7 @@
             o = full[:, :HEAD_WIDTH]
             for g in range(1, heads_kv):
                 o = jnp.where(head == g, full[:, g * HEAD_WIDTH : (g + 1) * HEAD_WIDTH], o)
-            token = (rows[u] - base) * STEP_COUNT
+            token = rows[u] * STEP_COUNT
             for t in range(STEP_COUNT):
                 acc[pl.ds(token + t, heads, stride=tokens), :] = o[t * heads : (t + 1) * heads]
 
@@ -352,21 +356,21 @@
         out_ref[:, h * HEAD_WIDTH : (h + 1) * HEAD_WIDTH] = acc[h * tokens : (h + 1) * tokens].astype(jnp.bfloat16)
 
 
-def attend(part, order, lengths, table, q, new, pages, inbox):
+def attend(order, lengths, table, q, new, pages, inbox):
     per_dev, _, _, columns = pages.shape
     req_count = inbox.shape[0]
-    requests = lengths.shape[0] // HALVES
+    requests = lengths.shape[0]
     heads = columns // HEAD_WIDTH * GROUP
     tokens = requests * STEP_COUNT
     pack_size = LANES // (STEP_COUNT * heads)
     extent = MAXP * PAGE_LENGTH * 2
     return pl.pallas_call(
-        functools.partial(attend_kernel, req_count, per_dev, part * requests, requests),
+        functools.partial(attend_kernel, req_count, per_dev, requests),
         out_shape=jax.ShapeDtypeStruct((tokens, heads * HEAD_WIDTH), jnp.bfloat16),
-        in_specs=[SMEM, SMEM, ANY, VMEM, VMEM, HBM, ANY],
+        in_specs=[SMEM, SMEM, SMEM, VMEM, VMEM, HBM, ANY],
         out_specs=VMEM,
         scratch_shapes=[
-            pltpu.SMEM((per_dev // 128, 128), jnp.int32),
+            pltpu.SMEM(table.shape, jnp.int32),
             pltpu.VMEM((req_count, 1, 2, columns), jnp.bfloat16),
             pltpu.VMEM((req_count, 128), jnp.int32),
             pltpu.SMEM((req_count, 128), jnp.int32),
@@ -410,26 +414,47 @@
     )(x)
 
 
-def project_kernel(count, roles, tile, counts, where_ref, *refs):
-    xs, (w_ref, down_ref, mask_ref), rest = refs[: len(counts)], refs[len(counts) : len(counts) + 3], refs[len(counts) + 3 :]
-    outs, low_ref, x_v = rest[:-2], rest[-2], rest[-1]
-    tokens = xs[0].shape[-2]
+def collect_kernel(count, roles, where_ref, *refs):
+    xs, (down_ref, mask_ref), (x_ref, *lows) = refs[:count], refs[count : count + 2], refs[count + 2 :]
+    tokens = xs[0].shape[0]
     rows = count * tokens // roles
-    b = 0
-    for x_ref, blocks in zip(xs, counts):
-        for k in range(blocks):
-            x = x_ref[...] if len(x_ref.shape) == 2 else x_ref[k]
-            x_v[pl.ds(pl.multiple_of(where_ref[b] * tokens, tokens), tokens), :] = x
-            b = b + 1
-    low = dot(x_v[...], down_ref[...], ((1,), (1,)))
+    per_role = count // roles
+    for b in range(count):
+        at = where_ref[b]
+        if roles == 4:
+            at = (at // per_role ^ where_ref[count]) * per_role + at % per_role
+        x_ref[pl.ds(pl.multiple_of(at * tokens, tokens), tokens), :] = xs[b][...]
     for j in range(roles):
         s = where_ref[count + j]
-        low_ref[s] = (low[j * rows : (j + 1) * rows] * mask_ref[s].astype(jnp.float32)).astype(jnp.bfloat16)
+        at = j if roles == 4 else s
+        x = x_ref[pl.ds(pl.multiple_of(at * rows, rows), rows), :]
+        lows[j][...] = (dot(x, down_ref[...], ((1,), (1,))) * mask_ref[s].astype(jnp.float32)).astype(jnp.bfloat16)
+
+
+def collect(where, xs, down, mask, roles):
+    count = len(xs)
+    tokens, width = xs[0].shape
+    rows = count * tokens // roles
+    x, *lows = pl.pallas_call(
+        functools.partial(collect_kernel, count, roles),
+        out_shape=[jax.ShapeDtypeStruct((count * tokens, width), jnp.bfloat16)]
+        + [jax.ShapeDtypeStruct((rows, down.shape[0]), jnp.bfloat16)] * roles,
+        in_specs=[SMEM] + [VMEM] * (count + 2),
+        out_specs=[VMEM] * (1 + roles),
+        compiler_params=params(),
+        cost_estimate=SMALL,
+        name="collect",
+    )(where, *xs, down, mask)
+    return x, lows
+
+
+def project_kernel(roles, tile, x_ref, w_ref, *outs):
+    rows = x_ref.shape[0] // roles
 
     @pl.loop(0, w_ref.shape[1] // tile)
     def _(i):
         at = pl.ds(pl.multiple_of(i * tile, tile), tile)
-        y = dot(x_v[...], w_ref[:, at]).astype(jnp.bfloat16)
+        y = dot(x_ref[...], w_ref[:, at]).astype(jnp.bfloat16)
         parts = [y[j * rows : (j + 1) * rows, :] for j in range(roles)]
         if roles == 4:
             own, pair, two, three = outs
@@ -440,30 +465,26 @@
             three[:, at] = parts[3]
         else:
             for j in range(roles):
-                outs[j][:, at] = parts[j]
-
-
-def project(where, xs, w, down, mask, roles):
-    counts = tuple(1 if len(x.shape) == 2 else x.shape[0] for x in xs)
-    count = sum(counts)
-    tokens, width = xs[0].shape
+                outs[0][j, :, at] = parts[j]
+
+
+def project(x, w, roles):
     columns = w.shape[1]
-    rows = count * tokens // roles
+    rows = x.shape[0] // roles
     one = jax.ShapeDtypeStruct((rows, columns), jnp.bfloat16)
-    outs = [one] * roles
     if roles == 4:
-        outs[1] = jax.ShapeDtypeStruct((2, rows, columns), jnp.bfloat16)
-    outs = outs + [jax.ShapeDtypeStruct((roles, rows, down.shape[0]), jnp.bfloat16)]
-    return pl.pallas_call(
-        functools.partial(project_kernel, count, roles, min(256, columns), counts),
+        outs = [one, jax.ShapeDtypeStruct((2, rows, columns), jnp.bfloat16), one, one]
+    else:
+        outs = [jax.ShapeDtypeStruct((roles, rows, columns), jnp.bfloat16)]
+    return pl.pallas_call(
+        functools.partial(project_kernel, roles, min(256, columns)),
         out_shape=outs,
-        in_specs=[SMEM] + [VMEM] * (len(xs) + 3),
+        in_specs=[VMEM, VMEM],
         out_specs=[VMEM] * len(outs),
-        scratch_shapes=[pltpu.VMEM((count * tokens, width), jnp.bfloat16)],
         compiler_params=params(),
         cost_estimate=SMALL,
         name="project",
-    )(where, *xs, w, down, mask)
+    )(x, w)
 
 
 def add_kernel(lane_ref, own_ref, passed_ref, o_ref):
@@ -507,32 +528,28 @@
     )(low, up)
 
 
-def finish_kernel(counts, cores, extra_ref, *refs):
+def finish_kernel(every, extra_ref, *refs):
     terms, o_ref = refs[:-1], refs[-1]
-    rows = terms[0].shape[0]
-    tokens = rows // cores
-    first = 0
-    for h, count in enumerate(counts):
-        total = extra_ref[h * rows : (h + 1) * rows, :]
-        for term in terms[first : first + count]:
-            total = total + (term[...] if len(term.shape) == 2 else term[0]).astype(jnp.float32)
-        first = first + count
-        for c in range(cores):
-            at = (c * len(counts) + h) * tokens
-            o_ref[at : at + tokens, :] = total[c * tokens : (c + 1) * tokens].astype(jnp.bfloat16)
-
-
-def finish(terms, cores, extra):
-    flat = [t for half in terms for t in half]
-    return pl.pallas_call(
-        functools.partial(finish_kernel, tuple(len(half) for half in terms), cores),
+    total = extra_ref[...]
+    for term in terms:
+        if len(term.shape) == 2:
+            total = total + term[...].astype(jnp.float32)
+        else:
+            for j in range(term.shape[0] if every else 1):
+                total = total + term[j].astype(jnp.float32)
+    o_ref[...] = total.astype(jnp.bfloat16)
+
+
+def finish(terms, every, extra):
+    return pl.pallas_call(
+        functools.partial(finish_kernel, every),
         out_shape=jax.ShapeDtypeStruct(extra.shape, jnp.bfloat16),
-        in_specs=[VMEM] * (1 + len(flat)),
+        in_specs=[VMEM] * (1 + len(terms)),
         out_specs=VMEM,
         compiler_params=params(),
         cost_estimate=SMALL,
         name="finish",
-    )(extra, *flat)
+    )(extra, *terms)
 
 
 def exchange(x, axis, distance):
@@ -544,27 +561,26 @@
     return lax.optimization_barrier((x, *others))[0]
 
 
-def gather(x, gates):
+def gather(x):
     my_req = lax.axis_index("req").astype(jnp.int32)
     count = lax.axis_size("req")
     if count != 8:
         whole = lax.all_gather(x, "req", axis=0)
-        return [whole[b] for b in range(count)], [jnp.int32(b) for b in range(count)], []
-    near = exchange(x, "req", 1)
-    far = [exchange(x, "req", d) for d in (2, 4, 6)]
-    group = jnp.stack([after(block, *gates) for block in far] if gates else far)
-    return [x, group, near, exchange(group, "req", 1)], [my_req ^ d for d in (0, 2, 4, 6, 1, 3, 5, 7)], far
-
-
-def scatter(blocks):
-    if len(blocks) != 4:
-        return [lax.psum_scatter(jnp.stack(blocks), "tp", scatter_dimension=0, tiled=False)], blocks[0]
-    own, pair, two, three = blocks
+        return [whole[b] for b in range(count)], [jnp.int32(b) for b in range(count)]
+    held = [x] + [exchange(x, "req", d) for d in (2, 4, 6)]
+    near = [exchange(block, "req", 1) for block in held]
+    return held + near, [my_req ^ d for d in (0, 2, 4, 6, 1, 3, 5, 7)]
+
+
+def scatter(parts):
+    if len(parts) == 1:
+        return [lax.all_to_all(parts[0], "tp", split_axis=0, concat_axis=0, tiled=True)], parts[0]
+    own, pair, two, three = parts
     lane = lax.axis_index("tp").astype(jnp.int32).reshape(1)
     pair = exchange(pair, "tp", 1)
     middle = lax.ppermute(three, "tp", [(1, 2), (2, 1)])
-    passed = add(lane, two, pair)
-    return [own, pair, middle, exchange(passed, "tp", 2)], passed
+    passed = add(lane, after(two, middle), pair)
+    return [own, pair, middle, exchange(passed, "tp", 2)], middle
 
 
 def on_device(
@@ -585,11 +601,9 @@
     my_lane = lax.axis_index("tp").astype(jnp.int32)
     me = my_req.reshape(1)
     requests = lengths.shape[0]
-    half = requests // HALVES
     columns = key_value_pages.shape[-1]
     heads = columns // HEAD_WIDTH * GROUP
     own_slots, rank, model = adapter_up_factor.shape
-    cores = req_count // tp_count
 
     outbox = pack(me, page_request_home, request_adapter_index, key_value_pages, req_count)
     inbox = lax.all_to_all(outbox, "req", split_axis=0, concat_axis=0, tiled=True)
@@ -608,34 +622,22 @@
     slot = jnp.sum(jnp.where(match, adapter_storage_slot, 0), axis=2)
     mine = my_req * own_slots + jnp.arange(own_slots * rank, dtype=jnp.int32) // rank
 
-    special = tp_count == 4
-    roles = [my_lane ^ j if special else jnp.int32(j) for j in range(tp_count)]
-    terms, lows, early, gates = [], [], [], []
-    mixed = [attend(h, order, lengths, table, q, new, key_value_pages, inbox) for h in range(HALVES)]
-    gates = [mixed[-1]]
-    for h in range(HALVES):
-        blocks, origins, far = gather(after(mixed[h], *early), gates)
-        early = far
-        where = []
-        for origin in origins:
-            s = origin // cores
-            where.append((s ^ my_lane if special else s) * cores + origin % cores)
-        where = jnp.stack(where + roles)
-        token_slot = jnp.repeat(slot[:, h * half : (h + 1) * half], STEP_COUNT, axis=1)
-        mask = (token_slot.reshape(tp_count, -1)[:, :, None] == mine).astype(jnp.bfloat16)
-        mask = after(mask, *([passed] if h else [up]))
-        *parts, low = project(where, blocks, output_projection_weight, down, mask, tp_count)
-        gates = [low]
-        lows.append(low)
-        sums, passed = scatter(parts)
-        terms.append(sums)
-
-    low = after(jnp.concatenate(lows, axis=1), passed)
-    low = lax.all_to_all(low, "tp", split_axis=0, concat_axis=0, tiled=True)
-    low = jnp.sum(low.astype(jnp.float32), axis=0).astype(jnp.bfloat16)
-    low = after(low, *terms[1][:3])
-    low = after(lax.all_gather(low, "req", axis=0), *terms[1])
-    return finish(terms, cores, adapt(low, up))
+    roles = [my_lane ^ j for j in range(tp_count)]
+    mixed = attend(order, lengths, table, q, new, key_value_pages, inbox)
+    blocks, origins = gather(mixed)
+    where = jnp.stack(origins + roles)
+    token_slot = jnp.repeat(slot, STEP_COUNT, axis=1)
+    mask = (token_slot.reshape(tp_count, -1)[:, :, None] == mine).astype(jnp.bfloat16)
+    up = lax.all_to_all(after(up_blocks, table, q, new), "req", split_axis=0, concat_axis=0, tiled=True)
+    up = up.reshape(req_count * own_slots * rank, -1)
+    mask = after(mask, up)
+    x, lows = collect(where, blocks, down, mask, tp_count)
+    parts = project(x, output_projection_weight, tp_count)
+    terms, moved = scatter(parts)
+    low = [lows[0]] + [exchange(lows[j], "tp", j) for j in range(1, tp_count)]
+    low = functools.reduce(jnp.add, [term.astype(jnp.float32) for term in low]).astype(jnp.bfloat16)
+    low = lax.all_gather(after(low, moved), "req", axis=0)
+    return finish(terms, tp_count != 4, adapt(low, up))
 
 
 def solution(mesh):

time: 162 us -> 156 us (0.963)
  waiting for transfers between devices: 57.9 us -> 74.6 us
  starting transfers between devices: 36.2 us -> 23.6 us
  other arithmetic: 4.33 us -> 0.35 us
  Pallas kernels: 43.8 us -> 40.7 us
  local copies, waits for them, and re-layouts: 9.21 us -> 6.23 us
    ppermute x14 -> x12, waiting for transfers between devices: 38 us -> 69.2 us  [exchange(): return lax.ppermute(x, axis, [(i, i ^ distance) for i in range(count)])]
    all_to_all x2 -> x1, waiting for transfers between devices: 11.7 us -> 0.01 us  [on_device(): lax.all_to_all(after(up_blocks, table, q, new), 'req', split_axis=0, conc...]
    ppermute x14 -> x12, starting transfers between devices: 19.7 us -> 14 us  [exchange(): return lax.ppermute(x, axis, [(i, i ^ distance) for i in range(count)])]
    all_to_all x2 -> x1, starting transfers between devices: 8.48 us -> 3.6 us  [on_device(): lax.all_to_all(after(up_blocks, table, q, new), 'req', split_axis=0, conc...]
    pallas_call x5 -> x4, Pallas kernels: 38.8 us -> 35.7 us  [the longest x1 26 us: attend(): pl.pallas_call(functools.partial(attend_kernel, req_count, per_dev, reque...]
    all_to_all x1, waiting for transfers between devices: 8.24 us -> 5.42 us  [on_device(): lax.all_to_all(outbox, 'req', split_axis=0, concat_axis=0, tiled=True)]
    another operation x2 -> x0, other arithmetic: 2.31 us -> none  [gather(): group = jnp.stack([after(block, *gates) for block in far] if gates else far)]
    ppermute x2 -> x1, starting transfers between devices: 2.74 us -> 0.68 us  [scatter(): middle = lax.ppermute(three, 'tp', [(1, 2), (2, 1)])]
  transfers between devices with their start and end apart: 19 -> 15, of which waited for: 8 -> 8; matrix products, arithmetic and copies ran while one was open for 4% -> 2% of each run, Pallas kernels for 21% -> 18%
where the time goes in v9:
time: 156 us; the launch traced here: 155 us
  waiting for transfers between devices  74.6 us (48%)
  Pallas kernels  40.7 us (26%)
  starting transfers between devices  23.6 us (15%)
  blocking collectives  9.24 us (6%)
  local copies, waits for them, and re-layouts  6.23 us (4%)
    ppermute x12, waiting for transfers between devices, exchange(): return lax.ppermute(x, axis, [(i, i ^ distance) for i in range(count)])  69.2 us
    pallas_call x1, Pallas kernels, attend(): pl.pallas_call(functools.partial(attend_kernel, req_count, per_dev, reque...  26 us
    ppermute x12, starting transfers between devices, exchange(): return lax.ppermute(x, axis, [(i, i ^ distance) for i in range(count)])  14 us
    all_gather x1, blocking collectives, on_device(): low = lax.all_gather(after(low, moved), 'req', axis=0)  9.24 us
    all_to_all x1, waiting for transfers between devices, on_device(): lax.all_to_all(outbox, 'req', split_axis=0, concat_axis=0, tiled=True)  5.42 us
    all_to_all x1, starting transfers between devices, on_device(): lax.all_to_all(outbox, 'req', split_axis=0, concat_axis=0, tiled=True)  5.3 us
    pallas_call x1, Pallas kernels, project(): pl.pallas_call(functools.partial(project_kernel, roles, min(256, columns)...  5.1 us
    pallas_call x1, Pallas kernels, pack(): pl.pallas_call(functools.partial(pack_kernel, req_count, per_dev), out_sh...  3.72 us
  transfers between devices with their start and end apart: 15, of which 8 were waited for; matrix products, arithmetic and copies ran while one was open for 2% of the time, Pallas kernels for 18%

profile of v9, /device:TPU:0, one launch (start us, length us, event | category | flops | bytes accessed | tf_op | source)
XLA Modules:
  0.0 155.0 jit_solution(14798103691443443322)
XLA Ops:
  0.0 3.7 %pack_outbox.1 = bf16[8,65,2,256]{3,2,1,0:T(2,128)(2,1)} custom-call(s32[1]{0:T(128)} %bitcast.me_ref, s32[1,512]{1,0:T(1,128)} %bitcast.30, s32[1,32]{1,0:T(1,128)} %bitcast.35, bf16[512,32,2,256]{3,2,1,0:T(2,128)(2,1)} %pages.3), custom_call_target="tpu_custom_call" | custom-call | flops 1 | bytes 1 | tf_op jit(solution)/shard_map/pack_outbox/pallas_call | solution.py:111
  3.8 5.3 %all-to-all-start = ((bf16[8,65,2,256]{3,2,1,0:T(2,128)(2,1)}), bf16[8,65,2,256]{3,2,1,0:T(2,128)(2,1)S(1)}, u32[]{:S(2)}, u32[]{:S(2)}) async-start(bf16[8,65,2,256]{3,2,1,0:T(2,128)(2,1)} %pack_outbox.1), calls=%async_computation | async-start | bytes 1064960 | tf_op jit(solution)/shard_map/all_to_all | solution.py:609
  9.3 1.3 copy-done
  11.2 1.3 reshape.53
  13.5 5.4 %all-to-all-done.inbox = bf16[8,65,2,256]{3,2,1,0:T(2,128)(2,1)S(1)} async-done(((bf16[8,65,2,256]{3,2,1,0:T(2,128)(2,1)}), bf16[8,65,2,256]{3,2,1,0:T(2,128)(2,1)S(1)}, u32[]{:S(2)}, u32[]{:S(2)}) %all-to-all-start) | async-done | bytes 532512 | tf_op jit(solution)/shard_map/all_to_all | solution.py:609
  18.9 3.6 %all-to-all-start.1 = ((bf16[8,128,1024]{2,1,0:T(8,128)(2,1)}), bf16[8,128,1024]{2,1,0:T(8,128)(2,1)S(1)}, u32[]{:S(2)}, u32[]{:S(2)}) async-start(bf16[8,128,1024]{2,1,0:T(8,128)(2,1)} %copy-done), calls=%async_computation.1 | async-start | bytes 4194304 | tf_op jit(solution)/shard_map/all_to_all | solution.py:631
  23.6 26.0 %attend.1.refs_0_ = bf16[128,2048]{1,0:T(8,128)(2,1)S(1)} custom-call(s32[2,128]{1,0:T(2,128)S(1)} %get-tuple-element.20.order_ref, s32[32]{0:T(128)S(1)} %copy-done.6, s32[4,128]{1,0:T(4,128)S(1)} %get-tuple-element.21.table_in, bf16[128,2048]{1,0:T(8,128)(2,1)S(1)} %bitcast.26, bf16[256,256]{1,0:T(8,128)(2,1)S(1)} %reshape.54.new_ref, ...), custom_call_target="tpu_custom_call" | custom-call | flops 2147483648 | bytes 16777216 | tf_op jit(solution)/shard_map/attend/pallas_call | solution.py:367
  49.7 3.2 %collective-permute-start.1 = (bf16[128,2048]{1,0:T(8,128)(2,1)S(1)}, bf16[128,2048]{1,0:T(8,128)(2,1)}, u32[]{:S(2)}, u32[]{:S(2)}) collective-permute-start(bf16[128,2048]{1,0:T(8,128)(2,1)S(1)} %attend.1.refs_0_), channel_id=1, source_target_pairs={{0,16},{4,20},{8,24},{12,28},{16,0},{20,4},{24,8},{28,12},{1,17},{... | collective-permute-start | bytes 1572872 | tf_op jit(solution)/shard_map/ppermute | solution.py:557
  52.9 1.4 collective-permute-start
  54.4 11.1 %collective-permute-done.2.refs_3_ = bf16[128,2048]{1,0:T(8,128)(2,1)} collective-permute-done((bf16[128,2048]{1,0:T(8,128)(2,1)S(1)}, bf16[128,2048]{1,0:T(8,128)(2,1)}, u32[]{:S(2)}, u32[]{:S(2)}) %collective-permute-start.2) | collective-permute-done | bytes 524320 | tf_op jit(solution)/shard_map/ppermute | solution.py:557
  65.5 10.1 %collective-permute-done.1.refs_2_ = bf16[128,2048]{1,0:T(8,128)(2,1)} collective-permute-done((bf16[128,2048]{1,0:T(8,128)(2,1)S(1)}, bf16[128,2048]{1,0:T(8,128)(2,1)}, u32[]{:S(2)}, u32[]{:S(2)}) %collective-permute-start.1) | collective-permute-done | bytes 524320 | tf_op jit(solution)/shard_map/ppermute | solution.py:557
  76.8 1.2 collective-permute-done.5.refs_6_
  78.7 1.0 copy-done.4
  79.7 3.5 %collect.1 = (bf16[1024,2048]{1,0:T(8,128)(2,1)S(1)}, bf16[256,128]{1,0:T(8,128)(2,1)S(1)}, bf16[256,128]{1,0:T(8,128)(2,1)S(1)}, bf16[256,128]{1,0:T(8,128)(2,1)S(1)}, bf16[256,128]{1,0:T(8,128)(2,1)S(1)}) custom-call(s32[12]{0:T(128)S(1)} %stack.51.where_ref, bf16[128,2048]{1,0:T(8,128)(2,1)S(1)} %attend.1.refs_0_, ...), custom_call_target="tpu_custom_call" | custom-call | flops 1 | bytes 1 | tf_op jit(solution)/shard_map/collect/pallas_call | solution.py:438
  83.2 5.1 %project.1 = (bf16[256,1024]{1,0:T(8,128)(2,1)S(1)}, bf16[2,256,1024]{2,1,0:T(8,128)(2,1)S(1)}, bf16[256,1024]{1,0:T(8,128)(2,1)S(1)}, bf16[256,1024]{1,0:T(8,128)(2,1)S(1)}) custom-call(bf16[1024,2048]{1,0:T(8,128)(2,1)S(1)} %get-tuple-element.28.x_ref, bf16[2048,1024]{1,0:T(8,128)(2,1)S(1)} %copy-done.1), custom_call_target="tpu_custom_call" | custom-call | flops 1 | bytes 1 | tf_op jit(solution)/shard_map/project/pallas_call | solution.py:479
  88.3 1.6 %collective-permute-start.11 = (bf16[2,256,1024]{2,1,0:T(8,128)(2,1)S(1)}, bf16[2,256,1024]{2,1,0:T(8,128)(2,1)S(1)}, u32[]{:S(2)}, u32[]{:S(2)}) collective-permute-start(bf16[2,256,1024]{2,1,0:T(8,128)(2,1)S(1)} %get-tuple-element.32), channel_id=1, source_target_pairs={{0,1},{1,0},{2,3},{3,2},{4,5},{5,4},{6,7},{7,6},{8,9},{9,8},{10,11... | collective-permute-start | bytes 3145736 | tf_op jit(solution)/shard_map/ppermute | solution.py:557
  90.7 22.9 %collective-permute-done.11.passed_ref.refs_1_ = bf16[2,256,1024]{2,1,0:T(8,128)(2,1)S(1)} collective-permute-done((bf16[2,256,1024]{2,1,0:T(8,128)(2,1)S(1)}, bf16[2,256,1024]{2,1,0:T(8,128)(2,1)S(1)}, u32[]{:S(2)}, u32[]{:S(2)}) %collective-permute-start.11) | collective-permute-done | bytes 1048608 | tf_op jit(solution)/shard_map/ppermute | solution.py:557
  113.6 2.7 %collective-permute-start.12 = (bf16[256,1024]{1,0:T(8,128)(2,1)S(1)}, bf16[256,1024]{1,0:T(8,128)(2,1)S(1)}, u32[]{:S(2)}, u32[]{:S(2)}) collective-permute-start(bf16[256,1024]{1,0:T(8,128)(2,1)S(1)} %add.35), channel_id=1, source_target_pairs={{0,2},{1,3},{2,0},{3,1},{4,6},{5,7},{6,4},{7,5},{8,10},{9,11},{10,... | collective-permute-start | bytes 1572872 | tf_op jit(solution)/shard_map/ppermute | solution.py:557
  116.4 1.5 collective-permute-start.7
  118.3 2.5 %collective-permute-start.9 = (bf16[256,128]{1,0:T(8,128)(2,1)S(1)}, bf16[256,128]{1,0:T(8,128)(2,1)S(1)}, u32[]{:S(2)}, u32[]{:S(2)}) collective-permute-start(bf16[256,128]{1,0:T(8,128)(2,1)S(1)} %get-tuple-element.27), channel_id=1, source_target_pairs={{0,3},{1,2},{2,1},{3,0},{4,7},{5,6},{6,5},{7,4},{8,11},{9,10},{10,... | collective-permute-start | bytes 196616 | tf_op jit(solution)/shard_map/ppermute | solution.py:557
  120.8 9.1 %collective-permute-done.7 = bf16[256,128]{1,0:T(8,128)(2,1)S(1)} collective-permute-done((bf16[256,128]{1,0:T(8,128)(2,1)S(1)}, bf16[256,128]{1,0:T(8,128)(2,1)S(1)}, u32[]{:S(2)}, u32[]{:S(2)}) %collective-permute-start.7) | collective-permute-done | bytes 65568 | tf_op jit(solution)/shard_map/ppermute | solution.py:557
  129.9 14.0 %collective-permute-done.8 = bf16[256,128]{1,0:T(8,128)(2,1)S(1)} collective-permute-done((bf16[256,128]{1,0:T(8,128)(2,1)S(1)}, bf16[256,128]{1,0:T(8,128)(2,1)S(1)}, u32[]{:S(2)}, u32[]{:S(2)}) %collective-permute-start.8) | collective-permute-done | bytes 65568 | tf_op jit(solution)/shard_map/ppermute | solution.py:557
  144.0 9.2 %all-gather = bf16[2048,128]{1,0:T(8,128)(2,1)S(1)} all-gather(bf16[256,128]{1,0:T(8,128)(2,1)S(1)} %add_convert_fusion), channel_id=2, replica_groups=mesh['req'=8,'tp'=4] {'req'}, dimensions={0}, use_global_device_ids=true | all-gather | bytes 589824 | tf_op jit(solution)/shard_map/all_gather | solution.py:639
  153.9 1.1 finish.1
  (46 shorter events, 6.7 us)
Async XLA Ops:
  0.0 9.1 %copy-start.3 = (bf16[2,64,8192]{2,1,0:T(8,128)(2,1)S(1)}, bf16[2,64,8192]{2,1,0:T(8,128)(2,1)}, u32[]{:S(2)}) copy-start(bf16[2,64,8192]{2,1,0:T(8,128)(2,1)} %param.18) | copy-start | bytes 6291460
  3.7 6.9 %copy-start.5 = (s32[512]{0:T(512)S(1)}, s32[512]{0:T(512)}, u32[]{:S(2)}) copy-start(s32[512]{0:T(512)} %param.13) | copy-start | bytes 6148
  3.7 6.9 %copy-start.6 = (s32[32]{0:T(128)S(1)}, s32[32]{0:T(128)}, u32[]{:S(2)}) copy-start(s32[32]{0:T(128)} %lengths_ref.1) | copy-start | bytes 388
  3.8 7.2 %copy-start.7 = (bf16[2,128,256]{2,1,0:T(8,128)(2,1)S(1)}, bf16[2,128,256]{2,1,0:T(8,128)(2,1)}, u32[]{:S(2)}) copy-start(bf16[2,128,256]{2,1,0:T(8,128)(2,1)} %param.11) | copy-start | bytes 393220
  3.8 15.1 %all-to-all-start = ((bf16[8,65,2,256]{3,2,1,0:T(2,128)(2,1)}), bf16[8,65,2,256]{3,2,1,0:T(2,128)(2,1)S(1)}, u32[]{:S(2)}, u32[]{:S(2)}) async-start(bf16[8,65,2,256]{3,2,1,0:T(2,128)(2,1)} %pack_outbox.1), calls=%async_computation | async-start | bytes 1064960 | tf_op jit(solution)/shard_map/all_to_all | solution.py:609
  9.3 1.3 copy-start
  18.9 57.8 %all-to-all-start.1 = ((bf16[8,128,1024]{2,1,0:T(8,128)(2,1)}), bf16[8,128,1024]{2,1,0:T(8,128)(2,1)S(1)}, u32[]{:S(2)}, u32[]{:S(2)}) async-start(bf16[8,128,1024]{2,1,0:T(8,128)(2,1)} %copy-done), calls=%async_computation.1 | async-start | bytes 4194304 | tf_op jit(solution)/shard_map/all_to_all | solution.py:631
  22.5 1.0 copy-start.2
  23.6 52.6 %copy-start.8 = (s32[16]{0:T(128)S(1)}, s32[16]{0:T(128)}, u32[]{:S(2)}) copy-start(s32[16]{0:T(128)} %param.16) | copy-start | bytes 196
  49.6 15.9 %collective-permute-start.2 = (bf16[128,2048]{1,0:T(8,128)(2,1)S(1)}, bf16[128,2048]{1,0:T(8,128)(2,1)}, u32[]{:S(2)}, u32[]{:S(2)}) collective-permute-start(bf16[128,2048]{1,0:T(8,128)(2,1)S(1)} %attend.1.refs_0_), channel_id=1, source_target_pairs={{0,24},{4,28},{8,16},{12,20},{16,8},{20,12},{24,0},{28,4},{1,25},{... | collective-permute-start | bytes 1572872 | tf_op jit(solution)/shard_map/ppermute | solution.py:557
  49.7 26.0 %collective-permute-start.1 = (bf16[128,2048]{1,0:T(8,128)(2,1)S(1)}, bf16[128,2048]{1,0:T(8,128)(2,1)}, u32[]{:S(2)}, u32[]{:S(2)}) collective-permute-start(bf16[128,2048]{1,0:T(8,128)(2,1)S(1)} %attend.1.refs_0_), channel_id=1, source_target_pairs={{0,16},{4,20},{8,24},{12,28},{16,0},{20,4},{24,8},{28,12},{1,17},{... | collective-permute-start | bytes 1572872 | tf_op jit(solution)/shard_map/ppermute | solution.py:557
  52.9 22.8 %collective-permute-start = (bf16[128,2048]{1,0:T(8,128)(2,1)S(1)}, bf16[128,2048]{1,0:T(8,128)(2,1)}, u32[]{:S(2)}, u32[]{:S(2)}) collective-permute-start(bf16[128,2048]{1,0:T(8,128)(2,1)S(1)} %attend.1.refs_0_), channel_id=1, source_target_pairs={{0,8},{4,12},{8,0},{12,4},{16,24},{20,28},{24,16},{28,20},{1,9},{5... | collective-permute-start | bytes 1572872 | tf_op jit(solution)/shard_map/ppermute | solution.py:557
  54.4 22.4 %collective-permute-start.3 = (bf16[128,2048]{1,0:T(8,128)(2,1)S(1)}, bf16[128,2048]{1,0:T(8,128)(2,1)}, u32[]{:S(2)}, u32[]{:S(2)}) collective-permute-start(bf16[128,2048]{1,0:T(8,128)(2,1)S(1)} %attend.1.refs_0_), channel_id=1, source_target_pairs={{0,4},{4,0},{8,12},{12,8},{16,20},{20,16},{24,28},{28,24},{1,5},{5... | collective-permute-start | bytes 1572872 | tf_op jit(solution)/shard_map/ppermute | solution.py:557
  65.5 11.2 %collective-permute-start.6 = (bf16[128,2048]{1,0:T(8,128)(2,1)}, bf16[128,2048]{1,0:T(8,128)(2,1)}, u32[]{:S(2)}, u32[]{:S(2)}) collective-permute-start(bf16[128,2048]{1,0:T(8,128)(2,1)} %collective-permute-done.2.refs_3_), channel_id=1, source_target_pairs={{0,4},{4,0},{8,12},{12,8},{16,20},{20,16},{24,28},{28,24},{1,5},{5... | collective-permute-start | bytes 1572872 | tf_op jit(solution)/shard_map/ppermute | solution.py:557
  75.7 2.3 %collective-permute-start.5 = (bf16[128,2048]{1,0:T(8,128)(2,1)}, bf16[128,2048]{1,0:T(8,128)(2,1)}, u32[]{:S(2)}, u32[]{:S(2)}) collective-permute-start(bf16[128,2048]{1,0:T(8,128)(2,1)} %collective-permute-done.1.refs_2_), channel_id=1, source_target_pairs={{0,4},{4,0},{8,12},{12,8},{16,20},{20,16},{24,28},{28,24},{1,5},{5... | collective-permute-start | bytes 1572872 | tf_op jit(solution)/shard_map/ppermute | solution.py:557
  75.7 3.0 %collective-permute-start.4 = (bf16[128,2048]{1,0:T(8,128)(2,1)}, bf16[128,2048]{1,0:T(8,128)(2,1)}, u32[]{:S(2)}, u32[]{:S(2)}) collective-permute-start(bf16[128,2048]{1,0:T(8,128)(2,1)} %collective-permute-done.refs_1_), channel_id=1, source_target_pairs={{0,4},{4,0},{8,12},{12,8},{16,20},{20,16},{24,28},{28,24},{1,5},{5... | collective-permute-start | bytes 1572872 | tf_op jit(solution)/shard_map/ppermute | solution.py:557
  76.7 6.5 %copy-start.1 = (bf16[2048,1024]{1,0:T(8,128)(2,1)S(1)}, bf16[2048,1024]{1,0:T(8,128)(2,1)}, u32[]{:S(2)}) copy-start(bf16[2048,1024]{1,0:T(8,128)(2,1)} %w_ref.1) | copy-start | bytes 12582916
  78.7 1.0 copy-start.4
  88.3 25.3 %collective-permute-start.11 = (bf16[2,256,1024]{2,1,0:T(8,128)(2,1)S(1)}, bf16[2,256,1024]{2,1,0:T(8,128)(2,1)S(1)}, u32[]{:S(2)}, u32[]{:S(2)}) collective-permute-start(bf16[2,256,1024]{2,1,0:T(8,128)(2,1)S(1)} %get-tuple-element.32), channel_id=1, source_target_pairs={{0,1},{1,0},{2,3},{3,2},{4,5},{5,4},{6,7},{7,6},{8,9},{9,8},{10,11... | collective-permute-start | bytes 3145736 | tf_op jit(solution)/shard_map/ppermute | solution.py:557
  90.0 0.7 collective-permute-start.10
  113.6 40.3 %collective-permute-start.12 = (bf16[256,1024]{1,0:T(8,128)(2,1)S(1)}, bf16[256,1024]{1,0:T(8,128)(2,1)S(1)}, u32[]{:S(2)}, u32[]{:S(2)}) collective-permute-start(bf16[256,1024]{1,0:T(8,128)(2,1)S(1)} %add.35), channel_id=1, source_target_pairs={{0,2},{1,3},{2,0},{3,1},{4,6},{5,7},{6,4},{7,5},{8,10},{9,11},{10,... | collective-permute-start | bytes 1572872 | tf_op jit(solution)/shard_map/ppermute | solution.py:557
  116.4 13.5 %collective-permute-start.7 = (bf16[256,128]{1,0:T(8,128)(2,1)S(1)}, bf16[256,128]{1,0:T(8,128)(2,1)S(1)}, u32[]{:S(2)}, u32[]{:S(2)}) collective-permute-start(bf16[256,128]{1,0:T(8,128)(2,1)S(1)} %get-tuple-element.25), channel_id=1, source_target_pairs={{0,1},{1,0},{2,3},{3,2},{4,5},{5,4},{6,7},{7,6},{8,9},{9,8},{10,11... | collective-permute-start | bytes 196616 | tf_op jit(solution)/shard_map/ppermute | solution.py:557
  117.9 26.1 %collective-permute-start.8 = (bf16[256,128]{1,0:T(8,128)(2,1)S(1)}, bf16[256,128]{1,0:T(8,128)(2,1)S(1)}, u32[]{:S(2)}, u32[]{:S(2)}) collective-permute-start(bf16[256,128]{1,0:T(8,128)(2,1)S(1)} %get-tuple-element.26), channel_id=1, source_target_pairs={{0,2},{1,3},{2,0},{3,1},{4,6},{5,7},{6,4},{7,5},{8,10},{9,11},{10,... | collective-permute-start | bytes 196616 | tf_op jit(solution)/shard_map/ppermute | solution.py:557
  118.3 25.6 %collective-permute-start.9 = (bf16[256,128]{1,0:T(8,128)(2,1)S(1)}, bf16[256,128]{1,0:T(8,128)(2,1)S(1)}, u32[]{:S(2)}, u32[]{:S(2)}) collective-permute-start(bf16[256,128]{1,0:T(8,128)(2,1)S(1)} %get-tuple-element.27), channel_id=1, source_target_pairs={{0,3},{1,2},{2,1},{3,0},{4,7},{5,6},{6,5},{7,4},{8,11},{9,10},{10,... | collective-permute-start | bytes 196616 | tf_op jit(solution)/shard_map/ppermute | solution.py:557

commit v10 on v9

--- a/solution.py
+++ b/solution.py
@@ -23,6 +23,7 @@
 CHUNKS = MAXP // CHUNK_PAGES
 CHUNK_POSITIONS = CHUNK_PAGES * PAGE_LENGTH
 LANES = 128
+PARTS = 2
 NEW_GROUP = 128 // (2 * STEP_COUNT)
 SLOTS = 6
 VMEM_LIMIT = 24 * 1024 * 1024
@@ -243,45 +244,57 @@
         counts = [order_ref[1, step * pack_size + u] for u in range(pack_size)]
         return functools.reduce(jnp.maximum, counts)
 
+    def page_count(step, u):
+        length = lengths_ref[order_ref[0, step * pack_size + u]]
+        return lax.shift_right_logical(length + (PAGE_LENGTH - 1), PAGE_LENGTH.bit_length() - 1)
+
     def fetch(step):
         place = lax.rem(step, SLOTS)
-        count = most_chunks(step)
         for u in range(pack_size):
             slot = order_ref[0, step * pack_size + u] * MAXP
             line = lax.shift_right_logical(slot, 7)
             at = slot & 127
 
-            @pl.loop(0, count)
+            def target(j):
+                return buf.at[place, u, pl.ds(pl.multiple_of(j * page_size, page_size), page_size)]
+
+            def copy(source, j):
+                @pl.when(source < per_dev)
+                def _():
+                    pltpu.make_async_copy(page_rows.at[source], target(j), sems.at[place, u]).start()
+
+                @pl.when(source >= per_dev)
+                def _():
+                    e = source - per_dev
+                    d = lax.shift_right_logical(e, 1)
+                    start = pl.multiple_of((e - d * CAP) * page_size, page_size)
+                    pltpu.make_async_copy(
+                        inbox_rows.at[d, pl.ds(start, page_size)], target(j), sems.at[place, u]
+                    ).start()
+
+            count = page_count(step, u)
+            full = lax.shift_right_logical(count, 2)
+
+            @pl.loop(0, full)
             def _(c):
                 sources = [table[line, at + c * CHUNK_PAGES + j] for j in range(CHUNK_PAGES)]
                 most = functools.reduce(jnp.maximum, sources)
 
-                def target(j):
-                    start = pl.multiple_of(c * chunk_size + j * page_size, page_size)
-                    return buf.at[place, u, pl.ds(start, page_size)]
-
                 @pl.when(most < per_dev)
                 def _():
                     for j in range(CHUNK_PAGES):
-                        pltpu.make_async_copy(page_rows.at[sources[j]], target(j), sems.at[place, u]).start()
+                        pltpu.make_async_copy(
+                            page_rows.at[sources[j]], target(c * CHUNK_PAGES + j), sems.at[place, u]
+                        ).start()
 
                 @pl.when(most >= per_dev)
                 def _():
                     for j in range(CHUNK_PAGES):
-                        source = sources[j]
-
-                        @pl.when(source < per_dev)
-                        def _():
-                            pltpu.make_async_copy(page_rows.at[source], target(j), sems.at[place, u]).start()
-
-                        @pl.when(source >= per_dev)
-                        def _():
-                            e = source - per_dev
-                            d = lax.shift_right_logical(e, 1)
-                            start = pl.multiple_of((e - d * CAP) * page_size, page_size)
-                            pltpu.make_async_copy(
-                                inbox_rows.at[d, pl.ds(start, page_size)], target(j), sems.at[place, u]
-                            ).start()
+                        copy(sources[j], c * CHUNK_PAGES + j)
+
+            @pl.loop(full * CHUNK_PAGES, count)
+            def _(j):
+                copy(table[line, at + j], j)
 
     for s in range(min(SLOTS - 1, steps)):
         fetch(jnp.int32(s))
@@ -290,8 +303,19 @@
         place = lax.rem(step, SLOTS)
         width = n * chunk_size
         for u in range(pack_size):
-            whole = buf.at[place, u, pl.ds(0, width)]
-            pltpu.make_async_copy(whole, whole, sems.at[place, u]).wait()
+            one = buf.at[place, u, pl.ds(0, page_size)]
+            count = page_count(step, u)
+
+            @pl.loop(0, count)
+            def _(_):
+                pltpu.make_async_copy(one, one, sems.at[place, u]).wait()
+
+            @pl.loop(count, n * CHUNK_PAGES)
+            def _(j):
+                buf[place, u, pl.ds(pl.multiple_of(j * page_size, page_size), page_size), :] = jnp.zeros(
+                    (page_size, columns), jnp.bfloat16
+                )
+
         lane = lax.broadcasted_iota(jnp.int32, (HEAD_WIDTH, LANES), 1)
         part = lane // span
         lane_head = (lane % heads) // GROUP
@@ -450,30 +474,37 @@
 
 def project_kernel(roles, tile, x_ref, w_ref, *outs):
     rows = x_ref.shape[0] // roles
-
-    @pl.loop(0, w_ref.shape[1] // tile)
-    def _(i):
-        at = pl.ds(pl.multiple_of(i * tile, tile), tile)
-        y = dot(x_ref[...], w_ref[:, at]).astype(jnp.bfloat16)
-        parts = [y[j * rows : (j + 1) * rows, :] for j in range(roles)]
-        if roles == 4:
-            own, pair, two, three = outs
-            own[:, at] = parts[0]
-            pair[0, :, at] = parts[1]
-            pair[1, :, at] = parts[3]
-            two[:, at] = parts[2]
-            three[:, at] = parts[3]
-        else:
-            for j in range(roles):
-                outs[0][j, :, at] = parts[j]
+    columns = w_ref.shape[1]
+    count = PARTS if roles == 4 else 1
+    width = columns // count
+    for c in range(count):
+
+        @pl.loop(0, width // tile)
+        def _(i):
+            inner = pl.ds(pl.multiple_of(i * tile, tile), tile)
+            at = pl.ds(pl.multiple_of(c * width + i * tile, tile), tile)
+            y = dot(x_ref[...], w_ref[:, at]).astype(jnp.bfloat16)
+            parts = [y[j * rows : (j + 1) * rows, :] for j in range(roles)]
+            if roles == 4:
+                own, three, pair, two = outs[0], outs[1], outs[2 + c], outs[2 + count + c]
+                own[:, at] = parts[0]
+                three[:, at] = parts[3]
+                pair[0, :, inner] = parts[1]
+                pair[1, :, inner] = parts[3]
+                two[:, inner] = parts[2]
+            else:
+                for j in range(roles):
+                    outs[0][j, :, at] = parts[j]
 
 
 def project(x, w, roles):
     columns = w.shape[1]
     rows = x.shape[0] // roles
-    one = jax.ShapeDtypeStruct((rows, columns), jnp.bfloat16)
     if roles == 4:
-        outs = [one, jax.ShapeDtypeStruct((2, rows, columns), jnp.bfloat16), one, one]
+        one = jax.ShapeDtypeStruct((rows, columns), jnp.bfloat16)
+        outs = [one, one]
+        outs = outs + [jax.ShapeDtypeStruct((2, rows, columns // PARTS), jnp.bfloat16)] * PARTS
+        outs = outs + [jax.ShapeDtypeStruct((rows, columns // PARTS), jnp.bfloat16)] * PARTS
     else:
         outs = [jax.ShapeDtypeStruct((roles, rows, columns), jnp.bfloat16)]
     return pl.pallas_call(
@@ -528,28 +559,36 @@
     )(low, up)
 
 
-def finish_kernel(every, extra_ref, *refs):
-    terms, o_ref = refs[:-1], refs[-1]
+def finish_kernel(whole, extra_ref, *refs):
+    terms, parts, o_ref = refs[:whole], refs[whole:-1], refs[-1]
     total = extra_ref[...]
     for term in terms:
         if len(term.shape) == 2:
             total = total + term[...].astype(jnp.float32)
         else:
-            for j in range(term.shape[0] if every else 1):
+            for j in range(term.shape[0]):
                 total = total + term[j].astype(jnp.float32)
-    o_ref[...] = total.astype(jnp.bfloat16)
-
-
-def finish(terms, every, extra):
+    if not parts:
+        o_ref[...] = total.astype(jnp.bfloat16)
+    width = total.shape[1] // PARTS
+    for c in range(PARTS if parts else 0):
+        at = slice(c * width, (c + 1) * width)
+        piece = total[:, at]
+        for term in parts[c::PARTS]:
+            piece = piece + (term[...] if len(term.shape) == 2 else term[0]).astype(jnp.float32)
+        o_ref[:, at] = piece.astype(jnp.bfloat16)
+
+
+def finish(terms, parts, extra):
     return pl.pallas_call(
-        functools.partial(finish_kernel, every),
+        functools.partial(finish_kernel, len(terms)),
         out_shape=jax.ShapeDtypeStruct(extra.shape, jnp.bfloat16),
-        in_specs=[VMEM] * (1 + len(terms)),
+        in_specs=[VMEM] * (1 + len(terms) + len(parts)),
         out_specs=VMEM,
         compiler_params=params(),
         cost_estimate=SMALL,
         name="finish",
-    )(extra, *terms)
+    )(extra, *terms, *parts)
 
 
 def exchange(x, axis, distance):
@@ -572,15 +611,19 @@
     return held + near, [my_req ^ d for d in (0, 2, 4, 6, 1, 3, 5, 7)]
 
 
-def scatter(parts):
-    if len(parts) == 1:
-        return [lax.all_to_all(parts[0], "tp", split_axis=0, concat_axis=0, tiled=True)], parts[0]
-    own, pair, two, three = parts
+def scatter(made, low):
+    if len(made) == 1:
+        moved = lax.all_to_all(made[0], "tp", split_axis=0, concat_axis=0, tiled=True)
+        return [moved], [], made[0]
+    own, three, pairs, twos = made[0], made[1], made[2 : 2 + PARTS], made[2 + PARTS :]
     lane = lax.axis_index("tp").astype(jnp.int32).reshape(1)
-    pair = exchange(pair, "tp", 1)
-    middle = lax.ppermute(three, "tp", [(1, 2), (2, 1)])
-    passed = add(lane, after(two, middle), pair)
-    return [own, pair, middle, exchange(passed, "tp", 2)], middle
+    pairs = [exchange(after(pair, low), "tp", 1) for pair in pairs]
+    middle = lax.ppermute(after(three, low), "tp", [(1, 2), (2, 1)])
+    passed, gates = [], [middle]
+    for pair, two in zip(pairs, twos):
+        passed.append(exchange(add(lane, after(two, *gates), pair), "tp", 2))
+        gates = [passed[-1]]
+    return [own, middle], pairs + passed, middle
 
 
 def on_device(
@@ -632,12 +675,11 @@
     up = up.reshape(req_count * own_slots * rank, -1)
     mask = after(mask, up)
     x, lows = collect(where, blocks, down, mask, tp_count)
-    parts = project(x, output_projection_weight, tp_count)
-    terms, moved = scatter(parts)
     low = [lows[0]] + [exchange(lows[j], "tp", j) for j in range(1, tp_count)]
     low = functools.reduce(jnp.add, [term.astype(jnp.float32) for term in low]).astype(jnp.bfloat16)
+    terms, parts, moved = scatter(project(x, output_projection_weight, tp_count), low)
     low = lax.all_gather(after(low, moved), "req", axis=0)
-    return finish(terms, tp_count != 4, adapt(low, up))
+    return finish(terms, parts, adapt(low, up))
 
 
 def solution(mesh):

time: 156 us -> 142 us (0.910)
  waiting for transfers between devices: 74.6 us -> 56.6 us
  starting transfers between devices: 23.6 us -> 27.7 us
    ppermute x12 -> x14, waiting for transfers between devices: 69.2 us -> 51.2 us  [exchange(): return lax.ppermute(x, axis, [(i, i ^ distance) for i in range(count)])]
    ppermute x12 -> x14, starting transfers between devices: 14 us -> 18.2 us  [exchange(): return lax.ppermute(x, axis, [(i, i ^ distance) for i in range(count)])]
  transfers between devices with their start and end apart: 15 -> 17, of which waited for: 8 -> 10; matrix products, arithmetic and copies ran while one was open for 2% -> 2% of each run, Pallas kernels for 18% -> 23%
where the time goes in v10:
time: 142 us
  waiting for transfers between devices  56.6 us (40%)
  Pallas kernels  41.2 us (29%)
  starting transfers between devices  27.7 us (20%)
  blocking collectives  9.97 us (7%)
  local copies, waits for them, and re-layouts  6.25 us (4%)
    ppermute x14, waiting for transfers between devices, exchange(): return lax.ppermute(x, axis, [(i, i ^ distance) for i in range(count)])  51.2 us
    pallas_call x1, Pallas kernels, attend(): pl.pallas_call(functools.partial(attend_kernel, req_count, per_dev, reque...  26.4 us
    ppermute x14, starting transfers between devices, exchange(): return lax.ppermute(x, axis, [(i, i ^ distance) for i in range(count)])  18.2 us
    all_gather x1, blocking collectives, on_device(): low = lax.all_gather(after(low, moved), 'req', axis=0)  9.97 us
    all_to_all x1, waiting for transfers between devices, on_device(): lax.all_to_all(outbox, 'req', split_axis=0, concat_axis=0, tiled=True)  5.41 us
    all_to_all x1, starting transfers between devices, on_device(): lax.all_to_all(outbox, 'req', split_axis=0, concat_axis=0, tiled=True)  5.17 us
    pallas_call x1, Pallas kernels, project(): pl.pallas_call(functools.partial(project_kernel, roles, min(256, columns)...  5.09 us
    pallas_call x1, Pallas kernels, pack(): pl.pallas_call(functools.partial(pack_kernel, req_count, per_dev), out_sh...  3.85 us
  transfers between devices with their start and end apart: 17, of which 10 were waited for; matrix products, arithmetic and copies ran while one was open for 2% of the time, Pallas kernels for 23%

profile of v10, /device:TPU:0, one launch (start us, length us, event | category | flops | bytes accessed | tf_op | source)
XLA Modules:
  0.0 142.3 jit_solution(7814523807360924853)
XLA Ops:
  0.0 3.9 %pack_outbox.1 = bf16[8,65,2,256]{3,2,1,0:T(2,128)(2,1)} custom-call(s32[1]{0:T(128)} %bitcast.me_ref, s32[1,512]{1,0:T(1,128)} %bitcast.30, s32[1,32]{1,0:T(1,128)} %bitcast.35, bf16[512,32,2,256]{3,2,1,0:T(2,128)(2,1)} %pages.3), custom_call_target="tpu_custom_call" | custom-call | flops 1 | bytes 1 | tf_op jit(solution)/shard_map/pack_outbox/pallas_call | solution.py:112
  3.9 5.2 %all-to-all-start = ((bf16[8,65,2,256]{3,2,1,0:T(2,128)(2,1)}), bf16[8,65,2,256]{3,2,1,0:T(2,128)(2,1)S(1)}, u32[]{:S(2)}, u32[]{:S(2)}) async-start(bf16[8,65,2,256]{3,2,1,0:T(2,128)(2,1)} %pack_outbox.1), calls=%async_computation | async-start | bytes 1064960 | tf_op jit(solution)/shard_map/all_to_all | solution.py:652
  9.3 1.3 copy-done
  11.2 1.3 reshape.53
  13.5 5.4 %all-to-all-done.inbox = bf16[8,65,2,256]{3,2,1,0:T(2,128)(2,1)S(1)} async-done(((bf16[8,65,2,256]{3,2,1,0:T(2,128)(2,1)}), bf16[8,65,2,256]{3,2,1,0:T(2,128)(2,1)S(1)}, u32[]{:S(2)}, u32[]{:S(2)}) %all-to-all-start) | async-done | bytes 532512 | tf_op jit(solution)/shard_map/all_to_all | solution.py:652
  18.9 3.6 %all-to-all-start.1 = ((bf16[8,128,1024]{2,1,0:T(8,128)(2,1)}), bf16[8,128,1024]{2,1,0:T(8,128)(2,1)S(1)}, u32[]{:S(2)}, u32[]{:S(2)}) async-start(bf16[8,128,1024]{2,1,0:T(8,128)(2,1)} %copy-done), calls=%async_computation.1 | async-start | bytes 4194304 | tf_op jit(solution)/shard_map/all_to_all | solution.py:674
  23.6 26.4 %attend.1.refs_0_ = bf16[128,2048]{1,0:T(8,128)(2,1)S(1)} custom-call(s32[2,128]{1,0:T(2,128)S(1)} %get-tuple-element.26.order_ref, s32[32]{0:T(128)S(1)} %copy-done.6, s32[4,128]{1,0:T(4,128)S(1)} %get-tuple-element.27.table_in, bf16[128,2048]{1,0:T(8,128)(2,1)S(1)} %bitcast.26, bf16[256,256]{1,0:T(8,128)(2,1)S(1)} %reshape.54.new_ref, ...), custom_call_target="tpu_custom_call" | custom-call | flops 2147483648 | bytes 16777216 | tf_op jit(solution)/shard_map/attend/pallas_call | solution.py:391
  50.0 3.6 %collective-permute-start.2 = (bf16[128,2048]{1,0:T(8,128)(2,1)S(1)}, bf16[128,2048]{1,0:T(8,128)(2,1)}, u32[]{:S(2)}, u32[]{:S(2)}) collective-permute-start(bf16[128,2048]{1,0:T(8,128)(2,1)S(1)} %attend.1.refs_0_), channel_id=1, source_target_pairs={{0,24},{4,28},{8,16},{12,20},{16,8},{20,12},{24,0},{28,4},{1,25},{... | collective-permute-start | bytes 1572872 | tf_op jit(solution)/shard_map/ppermute | solution.py:596
  53.6 1.6 %collective-permute-start.1 = (bf16[128,2048]{1,0:T(8,128)(2,1)S(1)}, bf16[128,2048]{1,0:T(8,128)(2,1)}, u32[]{:S(2)}, u32[]{:S(2)}) collective-permute-start(bf16[128,2048]{1,0:T(8,128)(2,1)S(1)} %attend.1.refs_0_), channel_id=1, source_target_pairs={{0,16},{4,20},{8,24},{12,28},{16,0},{20,4},{24,8},{28,12},{1,17},{... | collective-permute-start | bytes 1572872 | tf_op jit(solution)/shard_map/ppermute | solution.py:596
  55.2 1.4 collective-permute-start
  56.8 9.5 %collective-permute-done.2.refs_3_ = bf16[128,2048]{1,0:T(8,128)(2,1)} collective-permute-done((bf16[128,2048]{1,0:T(8,128)(2,1)S(1)}, bf16[128,2048]{1,0:T(8,128)(2,1)}, u32[]{:S(2)}, u32[]{:S(2)}) %collective-permute-start.2) | collective-permute-done | bytes 524320 | tf_op jit(solution)/shard_map/ppermute | solution.py:596
  66.6 11.1 %collective-permute-done.1.refs_2_ = bf16[128,2048]{1,0:T(8,128)(2,1)} collective-permute-done((bf16[128,2048]{1,0:T(8,128)(2,1)S(1)}, bf16[128,2048]{1,0:T(8,128)(2,1)}, u32[]{:S(2)}, u32[]{:S(2)}) %collective-permute-start.1) | collective-permute-done | bytes 524320 | tf_op jit(solution)/shard_map/ppermute | solution.py:596
  80.0 1.1 collective-permute-done.4.refs_5_
  81.0 1.0 copy-done.4
  82.1 3.5 %collect.1 = (bf16[1024,2048]{1,0:T(8,128)(2,1)S(1)}, bf16[256,128]{1,0:T(8,128)(2,1)S(1)}, bf16[256,128]{1,0:T(8,128)(2,1)S(1)}, bf16[256,128]{1,0:T(8,128)(2,1)S(1)}, bf16[256,128]{1,0:T(8,128)(2,1)S(1)}) custom-call(s32[12]{0:T(128)S(1)} %stack.51.where_ref, bf16[128,2048]{1,0:T(8,128)(2,1)S(1)} %attend.1.refs_0_, ...), custom_call_target="tpu_custom_call" | custom-call | flops 1 | bytes 1 | tf_op jit(solution)/shard_map/collect/pallas_call | solution.py:462
  85.6 1.6 %collective-permute-start.7 = (bf16[256,128]{1,0:T(8,128)(2,1)S(1)}, bf16[256,128]{1,0:T(8,128)(2,1)S(1)}, u32[]{:S(2)}, u32[]{:S(2)}) collective-permute-start(bf16[256,128]{1,0:T(8,128)(2,1)S(1)} %get-tuple-element.31), channel_id=1, source_target_pairs={{0,1},{1,0},{2,3},{3,2},{4,5},{5,4},{6,7},{7,6},{8,9},{9,8},{10,11... | collective-permute-start | bytes 196616 | tf_op jit(solution)/shard_map/ppermute | solution.py:596
  87.2 2.6 %collective-permute-start.8 = (bf16[256,128]{1,0:T(8,128)(2,1)S(1)}, bf16[256,128]{1,0:T(8,128)(2,1)S(1)}, u32[]{:S(2)}, u32[]{:S(2)}) collective-permute-start(bf16[256,128]{1,0:T(8,128)(2,1)S(1)} %get-tuple-element.32), channel_id=1, source_target_pairs={{0,2},{1,3},{2,0},{3,1},{4,6},{5,7},{6,4},{7,5},{8,10},{9,11},{10,... | collective-permute-start | bytes 196616 | tf_op jit(solution)/shard_map/ppermute | solution.py:596
  90.0 5.1 %project.1 = (bf16[256,1024]{1,0:T(8,128)(2,1)S(1)}, bf16[256,1024]{1,0:T(8,128)(2,1)S(1)}, bf16[2,256,512]{2,1,0:T(8,128)(2,1)S(1)}, bf16[2,256,512]{2,1,0:T(8,...) custom-call(bf16[1024,2048]{1,0:T(8,128)(2,1)S(1)} %get-tuple-element.34.x_ref, ...), custom_call_target="tpu_custom_call" | custom-call | flops 1 | bytes 1 | tf_op jit(solution)/shard_map/project/pallas_call | solution.py:510
  96.7 3.6 %collective-permute-start.11 = (bf16[2,256,512]{2,1,0:T(8,128)(2,1)S(1)}, bf16[2,256,512]{2,1,0:T(8,128)(2,1)S(1)}, u32[]{:S(2)}, u32[]{:S(2)}) collective-permute-start(bf16[2,256,512]{2,1,0:T(8,128)(2,1)S(1)} %get-tuple-element.40), channel_id=1, source_target_pairs={{0,1},{1,0},{2,3},{3,2},{4,5},{5,4},{6,7},{7,6},{8,9},{9,8},{10,11... | collective-permute-start | bytes 1572872 | tf_op jit(solution)/shard_map/ppermute | solution.py:596
  100.4 15.6 %collective-permute-done.11.passed_ref.refs_2_ = bf16[2,256,512]{2,1,0:T(8,128)(2,1)S(1)} collective-permute-done((bf16[2,256,512]{2,1,0:T(8,128)(2,1)S(1)}, bf16[2,256,512]{2,1,0:T(8,128)(2,1)S(1)}, u32[]{:S(2)}, u32[]{:S(2)}) %collective-permute-start.11) | collective-permute-done | bytes 524320 | tf_op jit(solution)/shard_map/ppermute | solution.py:596
  116.1 10.9 %collective-permute-done.13.refs_4_ = bf16[256,512]{1,0:T(8,128)(2,1)S(1)} collective-permute-done((bf16[256,512]{1,0:T(8,128)(2,1)S(1)}, bf16[256,512]{1,0:T(8,128)(2,1)S(1)}, u32[]{:S(2)}, u32[]{:S(2)}) %collective-permute-start.13) | collective-permute-done | bytes 262176 | tf_op jit(solution)/shard_map/ppermute | solution.py:596
  127.7 2.8 %collective-permute-start.14 = (bf16[256,512]{1,0:T(8,128)(2,1)S(1)}, bf16[256,512]{1,0:T(8,128)(2,1)S(1)}, u32[]{:S(2)}, u32[]{:S(2)}) collective-permute-start(bf16[256,512]{1,0:T(8,128)(2,1)S(1)} %add.37), channel_id=1, source_target_pairs={{0,2},{1,3},{2,0},{3,1},{4,6},{5,7},{6,4},{7,5},{8,10},{9,11},{10,... | collective-permute-start | bytes 786440 | tf_op jit(solution)/shard_map/ppermute | solution.py:596
  130.5 10.0 %all-gather = bf16[2048,128]{1,0:T(8,128)(2,1)S(1)} all-gather(bf16[256,128]{1,0:T(8,128)(2,1)S(1)} %add_convert_fusion), channel_id=2, replica_groups=mesh['req'=8,'tp'=4] {'req'}, dimensions={0}, use_global_device_ids=true | all-gather | bytes 589824 | tf_op jit(solution)/shard_map/all_gather | solution.py:681
  141.2 1.1 finish.1
  (51 shorter events, 9.0 us)
Async XLA Ops:
  0.0 9.1 %copy-start.3 = (bf16[2,64,8192]{2,1,0:T(8,128)(2,1)S(1)}, bf16[2,64,8192]{2,1,0:T(8,128)(2,1)}, u32[]{:S(2)}) copy-start(bf16[2,64,8192]{2,1,0:T(8,128)(2,1)} %param.18) | copy-start | bytes 6291460
  3.9 6.8 %copy-start.5 = (s32[512]{0:T(512)S(1)}, s32[512]{0:T(512)}, u32[]{:S(2)}) copy-start(s32[512]{0:T(512)} %param.13) | copy-start | bytes 6148
  3.9 6.8 %copy-start.6 = (s32[32]{0:T(128)S(1)}, s32[32]{0:T(128)}, u32[]{:S(2)}) copy-start(s32[32]{0:T(128)} %lengths_ref.1) | copy-start | bytes 388
  3.9 7.1 %copy-start.7 = (bf16[2,128,256]{2,1,0:T(8,128)(2,1)S(1)}, bf16[2,128,256]{2,1,0:T(8,128)(2,1)}, u32[]{:S(2)}) copy-start(bf16[2,128,256]{2,1,0:T(8,128)(2,1)} %param.11) | copy-start | bytes 393220
  3.9 15.0 %all-to-all-start = ((bf16[8,65,2,256]{3,2,1,0:T(2,128)(2,1)}), bf16[8,65,2,256]{3,2,1,0:T(2,128)(2,1)S(1)}, u32[]{:S(2)}, u32[]{:S(2)}) async-start(bf16[8,65,2,256]{3,2,1,0:T(2,128)(2,1)} %pack_outbox.1), calls=%async_computation | async-start | bytes 1064960 | tf_op jit(solution)/shard_map/all_to_all | solution.py:652
  9.3 1.3 copy-start
  18.9 60.4 %all-to-all-start.1 = ((bf16[8,128,1024]{2,1,0:T(8,128)(2,1)}), bf16[8,128,1024]{2,1,0:T(8,128)(2,1)S(1)}, u32[]{:S(2)}, u32[]{:S(2)}) async-start(bf16[8,128,1024]{2,1,0:T(8,128)(2,1)} %copy-done), calls=%async_computation.1 | async-start | bytes 4194304 | tf_op jit(solution)/shard_map/all_to_all | solution.py:674
  23.6 55.2 %copy-start.8 = (s32[16]{0:T(128)S(1)}, s32[16]{0:T(128)}, u32[]{:S(2)}) copy-start(s32[16]{0:T(128)} %param.16) | copy-start | bytes 196
  50.0 16.3 %collective-permute-start.2 = (bf16[128,2048]{1,0:T(8,128)(2,1)S(1)}, bf16[128,2048]{1,0:T(8,128)(2,1)}, u32[]{:S(2)}, u32[]{:S(2)}) collective-permute-start(bf16[128,2048]{1,0:T(8,128)(2,1)S(1)} %attend.1.refs_0_), channel_id=1, source_target_pairs={{0,24},{4,28},{8,16},{12,20},{16,8},{20,12},{24,0},{28,4},{1,25},{... | collective-permute-start | bytes 1572872 | tf_op jit(solution)/shard_map/ppermute | solution.py:596
  53.6 24.1 %collective-permute-start.1 = (bf16[128,2048]{1,0:T(8,128)(2,1)S(1)}, bf16[128,2048]{1,0:T(8,128)(2,1)}, u32[]{:S(2)}, u32[]{:S(2)}) collective-permute-start(bf16[128,2048]{1,0:T(8,128)(2,1)S(1)} %attend.1.refs_0_), channel_id=1, source_target_pairs={{0,16},{4,20},{8,24},{12,28},{16,0},{20,4},{24,8},{28,12},{1,17},{... | collective-permute-start | bytes 1572872 | tf_op jit(solution)/shard_map/ppermute | solution.py:596
  55.2 23.5 %collective-permute-start = (bf16[128,2048]{1,0:T(8,128)(2,1)S(1)}, bf16[128,2048]{1,0:T(8,128)(2,1)}, u32[]{:S(2)}, u32[]{:S(2)}) collective-permute-start(bf16[128,2048]{1,0:T(8,128)(2,1)S(1)} %attend.1.refs_0_), channel_id=1, source_target_pairs={{0,8},{4,12},{8,0},{12,4},{16,24},{20,28},{24,16},{28,20},{1,9},{5... | collective-permute-start | bytes 1572872 | tf_op jit(solution)/shard_map/ppermute | solution.py:596
  56.7 22.6 %collective-permute-start.3 = (bf16[128,2048]{1,0:T(8,128)(2,1)S(1)}, bf16[128,2048]{1,0:T(8,128)(2,1)}, u32[]{:S(2)}, u32[]{:S(2)}) collective-permute-start(bf16[128,2048]{1,0:T(8,128)(2,1)S(1)} %attend.1.refs_0_), channel_id=1, source_target_pairs={{0,4},{4,0},{8,12},{12,8},{16,20},{20,16},{24,28},{28,24},{1,5},{5... | collective-permute-start | bytes 1572872 | tf_op jit(solution)/shard_map/ppermute | solution.py:596
  66.2 13.1 %collective-permute-start.6 = (bf16[128,2048]{1,0:T(8,128)(2,1)}, bf16[128,2048]{1,0:T(8,128)(2,1)}, u32[]{:S(2)}, u32[]{:S(2)}) collective-permute-start(bf16[128,2048]{1,0:T(8,128)(2,1)} %collective-permute-done.2.refs_3_), channel_id=1, source_target_pairs={{0,4},{4,0},{8,12},{12,8},{16,20},{20,16},{24,28},{28,24},{1,5},{5... | collective-permute-start | bytes 1572872 | tf_op jit(solution)/shard_map/ppermute | solution.py:596
  77.7 2.3 %collective-permute-start.5 = (bf16[128,2048]{1,0:T(8,128)(2,1)}, bf16[128,2048]{1,0:T(8,128)(2,1)}, u32[]{:S(2)}, u32[]{:S(2)}) collective-permute-start(bf16[128,2048]{1,0:T(8,128)(2,1)} %collective-permute-done.1.refs_2_), channel_id=1, source_target_pairs={{0,4},{4,0},{8,12},{12,8},{16,20},{20,16},{24,28},{28,24},{1,5},{5... | collective-permute-start | bytes 1572872 | tf_op jit(solution)/shard_map/ppermute | solution.py:596
  78.8 2.3 %collective-permute-start.4 = (bf16[128,2048]{1,0:T(8,128)(2,1)}, bf16[128,2048]{1,0:T(8,128)(2,1)}, u32[]{:S(2)}, u32[]{:S(2)}) collective-permute-start(bf16[128,2048]{1,0:T(8,128)(2,1)} %collective-permute-done.refs_1_), channel_id=1, source_target_pairs={{0,4},{4,0},{8,12},{12,8},{16,20},{20,16},{24,28},{28,24},{1,5},{5... | collective-permute-start | bytes 1572872 | tf_op jit(solution)/shard_map/ppermute | solution.py:596
  79.3 10.7 %copy-start.1 = (bf16[2048,1024]{1,0:T(8,128)(2,1)S(1)}, bf16[2048,1024]{1,0:T(8,128)(2,1)}, u32[]{:S(2)}) copy-start(bf16[2048,1024]{1,0:T(8,128)(2,1)} %w_ref.1) | copy-start | bytes 12582916
  85.6 9.6 %collective-permute-start.7 = (bf16[256,128]{1,0:T(8,128)(2,1)S(1)}, bf16[256,128]{1,0:T(8,128)(2,1)S(1)}, u32[]{:S(2)}, u32[]{:S(2)}) collective-permute-start(bf16[256,128]{1,0:T(8,128)(2,1)S(1)} %get-tuple-element.31), channel_id=1, source_target_pairs={{0,1},{1,0},{2,3},{3,2},{4,5},{5,4},{6,7},{7,6},{8,9},{9,8},{10,11... | collective-permute-start | bytes 196616 | tf_op jit(solution)/shard_map/ppermute | solution.py:596
  87.2 7.9 %collective-permute-start.8 = (bf16[256,128]{1,0:T(8,128)(2,1)S(1)}, bf16[256,128]{1,0:T(8,128)(2,1)S(1)}, u32[]{:S(2)}, u32[]{:S(2)}) collective-permute-start(bf16[256,128]{1,0:T(8,128)(2,1)S(1)} %get-tuple-element.32), channel_id=1, source_target_pairs={{0,2},{1,3},{2,0},{3,1},{4,6},{5,7},{6,4},{7,5},{8,10},{9,11},{10,... | collective-permute-start | bytes 196616 | tf_op jit(solution)/shard_map/ppermute | solution.py:596
  89.8 6.2 %collective-permute-start.9 = (bf16[256,128]{1,0:T(8,128)(2,1)S(1)}, bf16[256,128]{1,0:T(8,128)(2,1)S(1)}, u32[]{:S(2)}, u32[]{:S(2)}) collective-permute-start(bf16[256,128]{1,0:T(8,128)(2,1)S(1)} %get-tuple-element.33), channel_id=1, source_target_pairs={{0,3},{1,2},{2,1},{3,0},{4,7},{5,6},{6,5},{7,4},{8,11},{9,10},{10,... | collective-permute-start | bytes 196616 | tf_op jit(solution)/shard_map/ppermute | solution.py:596
  96.0 4.4 %collective-permute-start.10 = (bf16[256,1024]{1,0:T(8,128)(2,1)S(1)}, bf16[256,1024]{1,0:T(8,128)(2,1)S(1)}, u32[]{:S(2)}, u32[]{:S(2)}) collective-permute-start(bf16[256,1024]{1,0:T(8,128)(2,1)S(1)} %get-tuple-element.36), channel_id=1, source_target_pairs={{1,2},{2,1},{5,6},{6,5},{9,10},{10,9},{13,14},{14,13},{17,18},{18,... | collective-permute-start | bytes 1572872 | tf_op jit(solution)/shard_map/ppermute | solution.py:621
  96.7 19.3 %collective-permute-start.11 = (bf16[2,256,512]{2,1,0:T(8,128)(2,1)S(1)}, bf16[2,256,512]{2,1,0:T(8,128)(2,1)S(1)}, u32[]{:S(2)}, u32[]{:S(2)}) collective-permute-start(bf16[2,256,512]{2,1,0:T(8,128)(2,1)S(1)} %get-tuple-element.40), channel_id=1, source_target_pairs={{0,1},{1,0},{2,3},{3,2},{4,5},{5,4},{6,7},{7,6},{8,9},{9,8},{10,11... | collective-permute-start | bytes 1572872 | tf_op jit(solution)/shard_map/ppermute | solution.py:596
  100.3 27.4 %collective-permute-start.12 = (bf16[2,256,512]{2,1,0:T(8,128)(2,1)S(1)}, bf16[2,256,512]{2,1,0:T(8,128)(2,1)S(1)}, u32[]{:S(2)}, u32[]{:S(2)}) collective-permute-start(bf16[2,256,512]{2,1,0:T(8,128)(2,1)S(1)} %get-tuple-element.42), channel_id=1, source_target_pairs={{0,1},{1,0},{2,3},{3,2},{4,5},{5,4},{6,7},{7,6},{8,9},{9,8},{10,11... | collective-permute-start | bytes 1572872 | tf_op jit(solution)/shard_map/ppermute | solution.py:596
  116.0 11.0 %collective-permute-start.13 = (bf16[256,512]{1,0:T(8,128)(2,1)S(1)}, bf16[256,512]{1,0:T(8,128)(2,1)S(1)}, u32[]{:S(2)}, u32[]{:S(2)}) collective-permute-start(bf16[256,512]{1,0:T(8,128)(2,1)S(1)} %add.36), channel_id=1, source_target_pairs={{0,2},{1,3},{2,0},{3,1},{4,6},{5,7},{6,4},{7,5},{8,10},{9,11},{10,... | collective-permute-start | bytes 786440 | tf_op jit(solution)/shard_map/ppermute | solution.py:596
  127.7 13.4 %collective-permute-start.14 = (bf16[256,512]{1,0:T(8,128)(2,1)S(1)}, bf16[256,512]{1,0:T(8,128)(2,1)S(1)}, u32[]{:S(2)}, u32[]{:S(2)}) collective-permute-start(bf16[256,512]{1,0:T(8,128)(2,1)S(1)} %add.37), channel_id=1, source_target_pairs={{0,2},{1,3},{2,0},{3,1},{4,6},{5,7},{6,4},{7,5},{8,10},{9,11},{10,... | collective-permute-start | bytes 786440 | tf_op jit(solution)/shard_map/ppermute | solution.py:596
  (2 other events, 2.1 us)

commit v11 on v10

--- a/solution.py
+++ b/solution.py
@@ -25,7 +25,8 @@
 LANES = 128
 PARTS = 2
 NEW_GROUP = 128 // (2 * STEP_COUNT)
-SLOTS = 6
+SLOTS = 4
+PACKS = 2
 VMEM_LIMIT = 24 * 1024 * 1024
 WHOLE_VMEM = 60 * 1024 * 1024
 ATTEND_VMEM = 48 * 1024 * 1024
@@ -238,63 +239,52 @@
             def _():
                 table[lax.shift_right_logical(slot, 7), slot & 127] = per_dev + d * CAP + k
 
-    steps = requests // pack_size
+    batch = PACKS * pack_size
+    steps = requests // batch
 
     def most_chunks(step):
-        counts = [order_ref[1, step * pack_size + u] for u in range(pack_size)]
+        counts = [order_ref[1, step * batch + u] for u in range(batch)]
         return functools.reduce(jnp.maximum, counts)
-
-    def page_count(step, u):
-        length = lengths_ref[order_ref[0, step * pack_size + u]]
-        return lax.shift_right_logical(length + (PAGE_LENGTH - 1), PAGE_LENGTH.bit_length() - 1)
 
     def fetch(step):
         place = lax.rem(step, SLOTS)
-        for u in range(pack_size):
-            slot = order_ref[0, step * pack_size + u] * MAXP
+        count = most_chunks(step)
+        for u in range(batch):
+            slot = order_ref[0, step * batch + u] * MAXP
             line = lax.shift_right_logical(slot, 7)
             at = slot & 127
 
-            def target(j):
-                return buf.at[place, u, pl.ds(pl.multiple_of(j * page_size, page_size), page_size)]
-
-            def copy(source, j):
-                @pl.when(source < per_dev)
-                def _():
-                    pltpu.make_async_copy(page_rows.at[source], target(j), sems.at[place, u]).start()
-
-                @pl.when(source >= per_dev)
-                def _():
-                    e = source - per_dev
-                    d = lax.shift_right_logical(e, 1)
-                    start = pl.multiple_of((e - d * CAP) * page_size, page_size)
-                    pltpu.make_async_copy(
-                        inbox_rows.at[d, pl.ds(start, page_size)], target(j), sems.at[place, u]
-                    ).start()
-
-            count = page_count(step, u)
-            full = lax.shift_right_logical(count, 2)
-
-            @pl.loop(0, full)
+            @pl.loop(0, count)
             def _(c):
                 sources = [table[line, at + c * CHUNK_PAGES + j] for j in range(CHUNK_PAGES)]
                 most = functools.reduce(jnp.maximum, sources)
 
+                def target(j):
+                    start = pl.multiple_of(c * chunk_size + j * page_size, page_size)
+                    return buf.at[place, u, pl.ds(start, page_size)]
+
                 @pl.when(most < per_dev)
                 def _():
                     for j in range(CHUNK_PAGES):
-                        pltpu.make_async_copy(
-                            page_rows.at[sources[j]], target(c * CHUNK_PAGES + j), sems.at[place, u]
-                        ).start()
+                        pltpu.make_async_copy(page_rows.at[sources[j]], target(j), sems.at[place, u]).start()
 
                 @pl.when(most >= per_dev)
                 def _():
                     for j in range(CHUNK_PAGES):
-                        copy(sources[j], c * CHUNK_PAGES + j)
-
-            @pl.loop(full * CHUNK_PAGES, count)
-            def _(j):
-                copy(table[line, at + j], j)
+                        source = sources[j]
+
+                        @pl.when(source < per_dev)
+                        def _():
+                            pltpu.make_async_copy(page_rows.at[source], target(j), sems.at[place, u]).start()
+
+                        @pl.when(source >= per_dev)
+                        def _():
+                            e = source - per_dev
+                            d = lax.shift_right_logical(e, 1)
+                            start = pl.multiple_of((e - d * CAP) * page_size, page_size)
+                            pltpu.make_async_copy(
+                                inbox_rows.at[d, pl.ds(start, page_size)], target(j), sems.at[place, u]
+                            ).start()
 
     for s in range(min(SLOTS - 1, steps)):
         fetch(jnp.int32(s))
@@ -302,20 +292,13 @@
     def compute(step, n):
         place = lax.rem(step, SLOTS)
         width = n * chunk_size
-        for u in range(pack_size):
-            one = buf.at[place, u, pl.ds(0, page_size)]
-            count = page_count(step, u)
-
-            @pl.loop(0, count)
-            def _(_):
-                pltpu.make_async_copy(one, one, sems.at[place, u]).wait()
-
-            @pl.loop(count, n * CHUNK_PAGES)
-            def _(j):
-                buf[place, u, pl.ds(pl.multiple_of(j * page_size, page_size), page_size), :] = jnp.zeros(
-                    (page_size, columns), jnp.bfloat16
-                )
-
+        for u in range(batch):
+            whole = buf.at[place, u, pl.ds(0, width)]
+            pltpu.make_async_copy(whole, whole, sems.at[place, u]).wait()
+        for v in range(PACKS):
+            attend_pack(step, place, width, v)
+
+    def attend_pack(step, place, width, v):
         lane = lax.broadcasted_iota(jnp.int32, (HEAD_WIDTH, LANES), 1)
         part = lane // span
         lane_head = (lane % heads) // GROUP
@@ -324,7 +307,7 @@
         owner = jnp.zeros((1, LANES), jnp.int32)
         rows, kvs, rights = [], [], []
         for u in range(pack_size):
-            r = order_ref[0, step * pack_size + u]
+            r = order_ref[0, step * batch + v * pack_size + u]
             rows.append(r)
             q = q_ref[:, pl.ds(pl.multiple_of((r // pack_size) * LANES, LANES), LANES)].astype(jnp.float32)
             own = part == u
@@ -333,7 +316,7 @@
                     [jnp.where(own & (lane_head == g), q, 0.0).astype(jnp.bfloat16) for g in range(heads_kv)], axis=0
                 )
             )
-            kvs.append(buf[place, u, 0:width, :])
+            kvs.append(buf[place, v * pack_size + u, 0:width, :])
             limit = jnp.where(one // span == u, 2 * lengths_ref[r], limit)
             owner = jnp.where(one // span == u, r & (NEW_GROUP - 1), owner)
         group = rows[0] // NEW_GROUP
@@ -398,10 +381,10 @@
             pltpu.VMEM((req_count, 1, 2, columns), jnp.bfloat16),
             pltpu.VMEM((req_count, 128), jnp.int32),
             pltpu.SMEM((req_count, 128), jnp.int32),
-            pltpu.VMEM((SLOTS, pack_size, extent, columns), jnp.bfloat16),
+            pltpu.VMEM((SLOTS, PACKS * pack_size, extent, columns), jnp.bfloat16),
             pltpu.VMEM((heads * tokens, HEAD_WIDTH), jnp.float32),
             pltpu.SemaphoreType.DMA,
-            pltpu.SemaphoreType.DMA((SLOTS, pack_size)),
+            pltpu.SemaphoreType.DMA((SLOTS, PACKS * pack_size)),
         ],
         compiler_params=params(ATTEND_VMEM),
         cost_estimate=pl.CostEstimate(
@@ -614,16 +597,17 @@
 def scatter(made, low):
     if len(made) == 1:
         moved = lax.all_to_all(made[0], "tp", split_axis=0, concat_axis=0, tiled=True)
-        return [moved], [], made[0]
+        return [moved], [], lax.all_gather(low, "req", axis=0)
     own, three, pairs, twos = made[0], made[1], made[2 : 2 + PARTS], made[2 + PARTS :]
     lane = lax.axis_index("tp").astype(jnp.int32).reshape(1)
-    pairs = [exchange(after(pair, low), "tp", 1) for pair in pairs]
     middle = lax.ppermute(after(three, low), "tp", [(1, 2), (2, 1)])
-    passed, gates = [], [middle]
-    for pair, two in zip(pairs, twos):
-        passed.append(exchange(add(lane, after(two, *gates), pair), "tp", 2))
-        gates = [passed[-1]]
-    return [own, middle], pairs + passed, middle
+    gathered = lax.all_gather(after(low, middle), "req", axis=0)
+    moved, passed = [], []
+    for c in range(PARTS):
+        moved.append(exchange(after(pairs[c], *([middle] if c else [low])), "tp", 1))
+        two = after(twos[c], *([passed[-1], gathered] if c else [middle]))
+        passed.append(exchange(add(lane, two, moved[c]), "tp", 2))
+    return [own, middle], moved + passed, gathered
 
 
 def on_device(
@@ -677,8 +661,7 @@
     x, lows = collect(where, blocks, down, mask, tp_count)
     low = [lows[0]] + [exchange(lows[j], "tp", j) for j in range(1, tp_count)]
     low = functools.reduce(jnp.add, [term.astype(jnp.float32) for term in low]).astype(jnp.bfloat16)
-    terms, parts, moved = scatter(project(x, output_projection_weight, tp_count), low)
-    low = lax.all_gather(after(low, moved), "req", axis=0)
+    terms, parts, low = scatter(project(x, output_projection_weight, tp_count), low)
     return finish(terms, parts, adapt(low, up))
 
 

time: 142 us -> 140 us (0.986)
  waiting for transfers between devices: 56.6 us -> 38.1 us
  starting transfers between devices: 27.7 us -> 44.8 us
    ppermute x14, waiting for transfers between devices: 51.2 us -> 32.7 us  [exchange(): return lax.ppermute(x, axis, [(i, i ^ distance) for i in range(count)])]
    ppermute x14, starting transfers between devices: 18.2 us -> 35.2 us  [exchange(): return lax.ppermute(x, axis, [(i, i ^ distance) for i in range(count)])]
where the time goes in v11:
time: 140 us
  starting transfers between devices  44.8 us (32%)
  Pallas kernels  40.8 us (29%)
  waiting for transfers between devices  38.1 us (27%)
  blocking collectives  9.64 us (7%)
  local copies, waits for them, and re-layouts  6.25 us (4%)
    ppermute x14, starting transfers between devices, exchange(): return lax.ppermute(x, axis, [(i, i ^ distance) for i in range(count)])  35.2 us
    ppermute x14, waiting for transfers between devices, exchange(): return lax.ppermute(x, axis, [(i, i ^ distance) for i in range(count)])  32.7 us
    pallas_call x1, Pallas kernels, attend(): pl.pallas_call(functools.partial(attend_kernel, req_count, per_dev, reque...  26.1 us
    all_gather x1, blocking collectives, scatter(): gathered = lax.all_gather(after(low, middle), 'req', axis=0)  9.64 us
    all_to_all x1, waiting for transfers between devices, on_device(): lax.all_to_all(outbox, 'req', split_axis=0, concat_axis=0, tiled=True)  5.41 us
    all_to_all x1, starting transfers between devices, on_device(): lax.all_to_all(outbox, 'req', split_axis=0, concat_axis=0, tiled=True)  5.33 us
    pallas_call x1, Pallas kernels, project(): pl.pallas_call(functools.partial(project_kernel, roles, min(256, columns)...  5.1 us
    pallas_call x1, Pallas kernels, pack(): pl.pallas_call(functools.partial(pack_kernel, req_count, per_dev), out_sh...  3.76 us
  transfers between devices with their start and end apart: 17, of which 10 were waited for; matrix products, arithmetic and copies ran while one was open for 2% of the time, Pallas kernels for 23%

profile of v11, /device:TPU:0, one launch (start us, length us, event | category | flops | bytes accessed | tf_op | source)
XLA Modules:
  0.0 140.2 jit_solution(11944057033082713936)
XLA Ops:
  0.0 3.8 %pack_outbox.1 = bf16[8,65,2,256]{3,2,1,0:T(2,128)(2,1)} custom-call(s32[1]{0:T(128)} %bitcast.me_ref, s32[1,512]{1,0:T(1,128)} %bitcast.30, s32[1,32]{1,0:T(1,128)} %bitcast.35, bf16[512,32,2,256]{3,2,1,0:T(2,128)(2,1)} %pages.3), custom_call_target="tpu_custom_call" | custom-call | flops 1 | bytes 1 | tf_op jit(solution)/shard_map/pack_outbox/pallas_call | solution.py:113
  3.8 5.3 %all-to-all-start = ((bf16[8,65,2,256]{3,2,1,0:T(2,128)(2,1)}), bf16[8,65,2,256]{3,2,1,0:T(2,128)(2,1)S(1)}, u32[]{:S(2)}, u32[]{:S(2)}) async-start(bf16[8,65,2,256]{3,2,1,0:T(2,128)(2,1)} %pack_outbox.1), calls=%async_computation | async-start | bytes 1064960 | tf_op jit(solution)/shard_map/all_to_all | solution.py:636
  9.4 1.3 copy-done
  11.3 1.3 reshape.53
  13.6 5.4 %all-to-all-done.inbox = bf16[8,65,2,256]{3,2,1,0:T(2,128)(2,1)S(1)} async-done(((bf16[8,65,2,256]{3,2,1,0:T(2,128)(2,1)}), bf16[8,65,2,256]{3,2,1,0:T(2,128)(2,1)S(1)}, u32[]{:S(2)}, u32[]{:S(2)}) %all-to-all-start) | async-done | bytes 532512 | tf_op jit(solution)/shard_map/all_to_all | solution.py:636
  19.0 3.6 %all-to-all-start.1 = ((bf16[8,128,1024]{2,1,0:T(8,128)(2,1)}), bf16[8,128,1024]{2,1,0:T(8,128)(2,1)S(1)}, u32[]{:S(2)}, u32[]{:S(2)}) async-start(bf16[8,128,1024]{2,1,0:T(8,128)(2,1)} %copy-done), calls=%async_computation.1 | async-start | bytes 4194304 | tf_op jit(solution)/shard_map/all_to_all | solution.py:658
  23.6 26.1 %attend.1.refs_0_ = bf16[128,2048]{1,0:T(8,128)(2,1)S(1)} custom-call(s32[2,128]{1,0:T(2,128)S(1)} %get-tuple-element.26.order_ref, s32[32]{0:T(128)S(1)} %copy-done.6, s32[4,128]{1,0:T(4,128)S(1)} %get-tuple-element.27.table_in, bf16[128,2048]{1,0:T(8,128)(2,1)S(1)} %bitcast.27, bf16[256,256]{1,0:T(8,128)(2,1)S(1)} %reshape.54.new_ref, ...), custom_call_target="tpu_custom_call" | custom-call | flops 2147483648 | bytes 16777216 | tf_op jit(solution)/shard_map/attend/pallas_call | solution.py:374
  49.8 3.4 %collective-permute-start.1 = (bf16[128,2048]{1,0:T(8,128)(2,1)S(1)}, bf16[128,2048]{1,0:T(8,128)(2,1)}, u32[]{:S(2)}, u32[]{:S(2)}) collective-permute-start(bf16[128,2048]{1,0:T(8,128)(2,1)S(1)} %attend.1.refs_0_), channel_id=1, source_target_pairs={{0,16},{4,20},{8,24},{12,28},{16,0},{20,4},{24,8},{28,12},{1,17},{... | collective-permute-start | bytes 1572872 | tf_op jit(solution)/shard_map/ppermute | solution.py:579
  53.4 2.9 %collective-permute-start.3 = (bf16[128,2048]{1,0:T(8,128)(2,1)S(1)}, bf16[128,2048]{1,0:T(8,128)(2,1)}, u32[]{:S(2)}, u32[]{:S(2)}) collective-permute-start(bf16[128,2048]{1,0:T(8,128)(2,1)S(1)} %attend.1.refs_0_), channel_id=1, source_target_pairs={{0,4},{4,0},{8,12},{12,8},{16,20},{20,16},{24,28},{28,24},{1,5},{5... | collective-permute-start | bytes 1572872 | tf_op jit(solution)/shard_map/ppermute | solution.py:579
  56.2 6.8 %collective-permute-done.2.refs_3_ = bf16[128,2048]{1,0:T(8,128)(2,1)} collective-permute-done((bf16[128,2048]{1,0:T(8,128)(2,1)S(1)}, bf16[128,2048]{1,0:T(8,128)(2,1)}, u32[]{:S(2)}, u32[]{:S(2)}) %collective-permute-start.2) | collective-permute-done | bytes 524320 | tf_op jit(solution)/shard_map/ppermute | solution.py:579
  63.0 5.1 %collective-permute-start.6 = (bf16[128,2048]{1,0:T(8,128)(2,1)}, bf16[128,2048]{1,0:T(8,128)(2,1)}, u32[]{:S(2)}, u32[]{:S(2)}) collective-permute-start(bf16[128,2048]{1,0:T(8,128)(2,1)} %collective-permute-done.2.refs_3_), channel_id=1, source_target_pairs={{0,4},{4,0},{8,12},{12,8},{16,20},{20,16},{24,28},{28,24},{1,5},{5... | collective-permute-start | bytes 1572872 | tf_op jit(solution)/shard_map/ppermute | solution.py:579
  68.1 8.6 %collective-permute-done.1.refs_2_ = bf16[128,2048]{1,0:T(8,128)(2,1)} collective-permute-done((bf16[128,2048]{1,0:T(8,128)(2,1)S(1)}, bf16[128,2048]{1,0:T(8,128)(2,1)}, u32[]{:S(2)}, u32[]{:S(2)}) %collective-permute-start.1) | collective-permute-done | bytes 524320 | tf_op jit(solution)/shard_map/ppermute | solution.py:579
  77.8 1.2 collective-permute-done.5.refs_6_
  80.8 3.5 %collect.1 = (bf16[1024,2048]{1,0:T(8,128)(2,1)S(1)}, bf16[256,128]{1,0:T(8,128)(2,1)S(1)}, bf16[256,128]{1,0:T(8,128)(2,1)S(1)}, bf16[256,128]{1,0:T(8,128)(2,1)S(1)}, bf16[256,128]{1,0:T(8,128)(2,1)S(1)}) custom-call(s32[12]{0:T(128)S(1)} %stack.51.where_ref, bf16[128,2048]{1,0:T(8,128)(2,1)S(1)} %attend.1.refs_0_, ...), custom_call_target="tpu_custom_call" | custom-call | flops 1 | bytes 1 | tf_op jit(solution)/shard_map/collect/pallas_call | solution.py:445
  84.3 1.6 %collective-permute-start.7 = (bf16[256,128]{1,0:T(8,128)(2,1)S(1)}, bf16[256,128]{1,0:T(8,128)(2,1)S(1)}, u32[]{:S(2)}, u32[]{:S(2)}) collective-permute-start(bf16[256,128]{1,0:T(8,128)(2,1)S(1)} %get-tuple-element.31), channel_id=1, source_target_pairs={{0,1},{1,0},{2,3},{3,2},{4,5},{5,4},{6,7},{7,6},{8,9},{9,8},{10,11... | collective-permute-start | bytes 196616 | tf_op jit(solution)/shard_map/ppermute | solution.py:579
  85.9 2.6 %collective-permute-start.8 = (bf16[256,128]{1,0:T(8,128)(2,1)S(1)}, bf16[256,128]{1,0:T(8,128)(2,1)S(1)}, u32[]{:S(2)}, u32[]{:S(2)}) collective-permute-start(bf16[256,128]{1,0:T(8,128)(2,1)S(1)} %get-tuple-element.32), channel_id=1, source_target_pairs={{0,2},{1,3},{2,0},{3,1},{4,6},{5,7},{6,4},{7,5},{8,10},{9,11},{10,... | collective-permute-start | bytes 196616 | tf_op jit(solution)/shard_map/ppermute | solution.py:579
  88.7 5.1 %project.1 = (bf16[256,1024]{1,0:T(8,128)(2,1)S(1)}, bf16[256,1024]{1,0:T(8,128)(2,1)S(1)}, bf16[2,256,512]{2,1,0:T(8,128)(2,1)S(1)}, bf16[2,256,512]{2,1,0:T(8,...) custom-call(bf16[1024,2048]{1,0:T(8,128)(2,1)S(1)} %get-tuple-element.34.x_ref, ...), custom_call_target="tpu_custom_call" | custom-call | flops 1 | bytes 1 | tf_op jit(solution)/shard_map/project/pallas_call | solution.py:493
  95.4 3.6 %collective-permute-start.11 = (bf16[2,256,512]{2,1,0:T(8,128)(2,1)S(1)}, bf16[2,256,512]{2,1,0:T(8,128)(2,1)S(1)}, u32[]{:S(2)}, u32[]{:S(2)}) collective-permute-start(bf16[2,256,512]{2,1,0:T(8,128)(2,1)S(1)} %get-tuple-element.40), channel_id=1, source_target_pairs={{0,1},{1,0},{2,3},{3,2},{4,5},{5,4},{6,7},{7,6},{8,9},{9,8},{10,11... | collective-permute-start | bytes 1572872 | tf_op jit(solution)/shard_map/ppermute | solution.py:579
  99.0 11.0 %collective-permute-start.12 = (bf16[2,256,512]{2,1,0:T(8,128)(2,1)S(1)}, bf16[2,256,512]{2,1,0:T(8,128)(2,1)S(1)}, u32[]{:S(2)}, u32[]{:S(2)}) collective-permute-start(bf16[2,256,512]{2,1,0:T(8,128)(2,1)S(1)} %get-tuple-element.42), channel_id=1, source_target_pairs={{0,1},{1,0},{2,3},{3,2},{4,5},{5,4},{6,7},{7,6},{8,9},{9,8},{10,11... | collective-permute-start | bytes 1572872 | tf_op jit(solution)/shard_map/ppermute | solution.py:579
  110.3 1.2 collective-permute-start.13
  111.5 9.6 %all-gather = bf16[2048,128]{1,0:T(8,128)(2,1)S(1)} all-gather(bf16[256,128]{1,0:T(8,128)(2,1)S(1)} %add_convert_fusion), channel_id=2, replica_groups=mesh['req'=8,'tp'=4] {'req'}, dimensions={0}, use_global_device_ids=true | all-gather | bytes 589824 | tf_op jit(solution)/shard_map/all_gather | solution.py:604
  121.1 4.6 %collective-permute-done.13.refs_4_ = bf16[256,512]{1,0:T(8,128)(2,1)S(1)} collective-permute-done((bf16[256,512]{1,0:T(8,128)(2,1)S(1)}, bf16[256,512]{1,0:T(8,128)(2,1)S(1)}, u32[]{:S(2)}, u32[]{:S(2)}) %collective-permute-start.13) | collective-permute-done | bytes 262176 | tf_op jit(solution)/shard_map/ppermute | solution.py:579
  126.4 2.8 %collective-permute-start.14 = (bf16[256,512]{1,0:T(8,128)(2,1)S(1)}, bf16[256,512]{1,0:T(8,128)(2,1)S(1)}, u32[]{:S(2)}, u32[]{:S(2)}) collective-permute-start(bf16[256,512]{1,0:T(8,128)(2,1)S(1)} %add.37), channel_id=1, source_target_pairs={{0,2},{1,3},{2,0},{3,1},{4,6},{5,7},{6,4},{7,5},{8,10},{9,11},{10,... | collective-permute-start | bytes 786440 | tf_op jit(solution)/shard_map/ppermute | solution.py:579
  129.9 9.2 %collective-permute-done.14.refs_5_ = bf16[256,512]{1,0:T(8,128)(2,1)S(1)} collective-permute-done((bf16[256,512]{1,0:T(8,128)(2,1)S(1)}, bf16[256,512]{1,0:T(8,128)(2,1)S(1)}, u32[]{:S(2)}, u32[]{:S(2)}) %collective-permute-start.14) | collective-permute-done | bytes 262176 | tf_op jit(solution)/shard_map/ppermute | solution.py:579
  (51 shorter events, 10.4 us)
Async XLA Ops:
  0.0 9.1 %copy-start.3 = (bf16[2,64,8192]{2,1,0:T(8,128)(2,1)S(1)}, bf16[2,64,8192]{2,1,0:T(8,128)(2,1)}, u32[]{:S(2)}) copy-start(bf16[2,64,8192]{2,1,0:T(8,128)(2,1)} %param.18) | copy-start | bytes 6291460
  3.8 7.0 %copy-start.5 = (s32[512]{0:T(512)S(1)}, s32[512]{0:T(512)}, u32[]{:S(2)}) copy-start(s32[512]{0:T(512)} %param.13) | copy-start | bytes 6148
  3.8 6.9 %copy-start.6 = (s32[32]{0:T(128)S(1)}, s32[32]{0:T(128)}, u32[]{:S(2)}) copy-start(s32[32]{0:T(128)} %lengths_ref.1) | copy-start | bytes 388
  3.8 7.2 %copy-start.7 = (bf16[2,128,256]{2,1,0:T(8,128)(2,1)S(1)}, bf16[2,128,256]{2,1,0:T(8,128)(2,1)}, u32[]{:S(2)}) copy-start(bf16[2,128,256]{2,1,0:T(8,128)(2,1)} %param.11) | copy-start | bytes 393220
  3.8 15.2 %all-to-all-start = ((bf16[8,65,2,256]{3,2,1,0:T(2,128)(2,1)}), bf16[8,65,2,256]{3,2,1,0:T(2,128)(2,1)S(1)}, u32[]{:S(2)}, u32[]{:S(2)}) async-start(bf16[8,65,2,256]{3,2,1,0:T(2,128)(2,1)} %pack_outbox.1), calls=%async_computation | async-start | bytes 1064960 | tf_op jit(solution)/shard_map/all_to_all | solution.py:636
  9.4 1.3 copy-start
  19.0 58.8 %all-to-all-start.1 = ((bf16[8,128,1024]{2,1,0:T(8,128)(2,1)}), bf16[8,128,1024]{2,1,0:T(8,128)(2,1)S(1)}, u32[]{:S(2)}, u32[]{:S(2)}) async-start(bf16[8,128,1024]{2,1,0:T(8,128)(2,1)} %copy-done), calls=%async_computation.1 | async-start | bytes 4194304 | tf_op jit(solution)/shard_map/all_to_all | solution.py:658
  23.6 53.6 %copy-start.8 = (s32[16]{0:T(128)S(1)}, s32[16]{0:T(128)}, u32[]{:S(2)}) copy-start(s32[16]{0:T(128)} %param.16) | copy-start | bytes 196
  49.7 13.3 %collective-permute-start.2 = (bf16[128,2048]{1,0:T(8,128)(2,1)S(1)}, bf16[128,2048]{1,0:T(8,128)(2,1)}, u32[]{:S(2)}, u32[]{:S(2)}) collective-permute-start(bf16[128,2048]{1,0:T(8,128)(2,1)S(1)} %attend.1.refs_0_), channel_id=1, source_target_pairs={{0,24},{4,28},{8,16},{12,20},{16,8},{20,12},{24,0},{28,4},{1,25},{... | collective-permute-start | bytes 1572872 | tf_op jit(solution)/shard_map/ppermute | solution.py:579
  49.8 26.9 %collective-permute-start.1 = (bf16[128,2048]{1,0:T(8,128)(2,1)S(1)}, bf16[128,2048]{1,0:T(8,128)(2,1)}, u32[]{:S(2)}, u32[]{:S(2)}) collective-permute-start(bf16[128,2048]{1,0:T(8,128)(2,1)S(1)} %attend.1.refs_0_), channel_id=1, source_target_pairs={{0,16},{4,20},{8,24},{12,28},{16,0},{20,4},{24,8},{28,12},{1,17},{... | collective-permute-start | bytes 1572872 | tf_op jit(solution)/shard_map/ppermute | solution.py:579
  53.2 23.7 %collective-permute-start = (bf16[128,2048]{1,0:T(8,128)(2,1)S(1)}, bf16[128,2048]{1,0:T(8,128)(2,1)}, u32[]{:S(2)}, u32[]{:S(2)}) collective-permute-start(bf16[128,2048]{1,0:T(8,128)(2,1)S(1)} %attend.1.refs_0_), channel_id=1, source_target_pairs={{0,8},{4,12},{8,0},{12,4},{16,24},{20,28},{24,16},{28,20},{1,9},{5... | collective-permute-start | bytes 1572872 | tf_op jit(solution)/shard_map/ppermute | solution.py:579
  53.4 24.4 %collective-permute-start.3 = (bf16[128,2048]{1,0:T(8,128)(2,1)S(1)}, bf16[128,2048]{1,0:T(8,128)(2,1)}, u32[]{:S(2)}, u32[]{:S(2)}) collective-permute-start(bf16[128,2048]{1,0:T(8,128)(2,1)S(1)} %attend.1.refs_0_), channel_id=1, source_target_pairs={{0,4},{4,0},{8,12},{12,8},{16,20},{20,16},{24,28},{28,24},{1,5},{5... | collective-permute-start | bytes 1572872 | tf_op jit(solution)/shard_map/ppermute | solution.py:579
  63.0 14.8 %collective-permute-start.6 = (bf16[128,2048]{1,0:T(8,128)(2,1)}, bf16[128,2048]{1,0:T(8,128)(2,1)}, u32[]{:S(2)}, u32[]{:S(2)}) collective-permute-start(bf16[128,2048]{1,0:T(8,128)(2,1)} %collective-permute-done.2.refs_3_), channel_id=1, source_target_pairs={{0,4},{4,0},{8,12},{12,8},{16,20},{20,16},{24,28},{28,24},{1,5},{5... | collective-permute-start | bytes 1572872 | tf_op jit(solution)/shard_map/ppermute | solution.py:579
  76.7 2.3 %collective-permute-start.5 = (bf16[128,2048]{1,0:T(8,128)(2,1)}, bf16[128,2048]{1,0:T(8,128)(2,1)}, u32[]{:S(2)}, u32[]{:S(2)}) collective-permute-start(bf16[128,2048]{1,0:T(8,128)(2,1)} %collective-permute-done.1.refs_2_), channel_id=1, source_target_pairs={{0,4},{4,0},{8,12},{12,8},{16,20},{20,16},{24,28},{28,24},{1,5},{5... | collective-permute-start | bytes 1572872 | tf_op jit(solution)/shard_map/ppermute | solution.py:579
  76.8 2.9 %collective-permute-start.4 = (bf16[128,2048]{1,0:T(8,128)(2,1)}, bf16[128,2048]{1,0:T(8,128)(2,1)}, u32[]{:S(2)}, u32[]{:S(2)}) collective-permute-start(bf16[128,2048]{1,0:T(8,128)(2,1)} %collective-permute-done.refs_1_), channel_id=1, source_target_pairs={{0,4},{4,0},{8,12},{12,8},{16,20},{20,16},{24,28},{28,24},{1,5},{5... | collective-permute-start | bytes 1572872 | tf_op jit(solution)/shard_map/ppermute | solution.py:579
  77.8 10.9 %copy-start.1 = (bf16[2048,1024]{1,0:T(8,128)(2,1)S(1)}, bf16[2048,1024]{1,0:T(8,128)(2,1)}, u32[]{:S(2)}) copy-start(bf16[2048,1024]{1,0:T(8,128)(2,1)} %w_ref.1) | copy-start | bytes 12582916
  84.3 9.6 %collective-permute-start.7 = (bf16[256,128]{1,0:T(8,128)(2,1)S(1)}, bf16[256,128]{1,0:T(8,128)(2,1)S(1)}, u32[]{:S(2)}, u32[]{:S(2)}) collective-permute-start(bf16[256,128]{1,0:T(8,128)(2,1)S(1)} %get-tuple-element.31), channel_id=1, source_target_pairs={{0,1},{1,0},{2,3},{3,2},{4,5},{5,4},{6,7},{7,6},{8,9},{9,8},{10,11... | collective-permute-start | bytes 196616 | tf_op jit(solution)/shard_map/ppermute | solution.py:579
  85.9 7.9 %collective-permute-start.8 = (bf16[256,128]{1,0:T(8,128)(2,1)S(1)}, bf16[256,128]{1,0:T(8,128)(2,1)S(1)}, u32[]{:S(2)}, u32[]{:S(2)}) collective-permute-start(bf16[256,128]{1,0:T(8,128)(2,1)S(1)} %get-tuple-element.32), channel_id=1, source_target_pairs={{0,2},{1,3},{2,0},{3,1},{4,6},{5,7},{6,4},{7,5},{8,10},{9,11},{10,... | collective-permute-start | bytes 196616 | tf_op jit(solution)/shard_map/ppermute | solution.py:579
  88.5 6.2 %collective-permute-start.9 = (bf16[256,128]{1,0:T(8,128)(2,1)S(1)}, bf16[256,128]{1,0:T(8,128)(2,1)S(1)}, u32[]{:S(2)}, u32[]{:S(2)}) collective-permute-start(bf16[256,128]{1,0:T(8,128)(2,1)S(1)} %get-tuple-element.33), channel_id=1, source_target_pairs={{0,3},{1,2},{2,1},{3,0},{4,7},{5,6},{6,5},{7,4},{8,11},{9,10},{10,... | collective-permute-start | bytes 196616 | tf_op jit(solution)/shard_map/ppermute | solution.py:579
  94.7 4.3 %collective-permute-start.10 = (bf16[256,1024]{1,0:T(8,128)(2,1)S(1)}, bf16[256,1024]{1,0:T(8,128)(2,1)S(1)}, u32[]{:S(2)}, u32[]{:S(2)}) collective-permute-start(bf16[256,1024]{1,0:T(8,128)(2,1)S(1)} %get-tuple-element.36), channel_id=1, source_target_pairs={{1,2},{2,1},{5,6},{6,5},{9,10},{10,9},{13,14},{14,13},{17,18},{18,... | collective-permute-start | bytes 1572872 | tf_op jit(solution)/shard_map/ppermute | solution.py:603
  95.4 14.8 %collective-permute-start.11 = (bf16[2,256,512]{2,1,0:T(8,128)(2,1)S(1)}, bf16[2,256,512]{2,1,0:T(8,128)(2,1)S(1)}, u32[]{:S(2)}, u32[]{:S(2)}) collective-permute-start(bf16[2,256,512]{2,1,0:T(8,128)(2,1)S(1)} %get-tuple-element.40), channel_id=1, source_target_pairs={{0,1},{1,0},{2,3},{3,2},{4,5},{5,4},{6,7},{7,6},{8,9},{9,8},{10,11... | collective-permute-start | bytes 1572872 | tf_op jit(solution)/shard_map/ppermute | solution.py:579
  99.0 27.4 %collective-permute-start.12 = (bf16[2,256,512]{2,1,0:T(8,128)(2,1)S(1)}, bf16[2,256,512]{2,1,0:T(8,128)(2,1)S(1)}, u32[]{:S(2)}, u32[]{:S(2)}) collective-permute-start(bf16[2,256,512]{2,1,0:T(8,128)(2,1)S(1)} %get-tuple-element.42), channel_id=1, source_target_pairs={{0,1},{1,0},{2,3},{3,2},{4,5},{5,4},{6,7},{7,6},{8,9},{9,8},{10,11... | collective-permute-start | bytes 1572872 | tf_op jit(solution)/shard_map/ppermute | solution.py:579
  110.3 15.4 %collective-permute-start.13 = (bf16[256,512]{1,0:T(8,128)(2,1)S(1)}, bf16[256,512]{1,0:T(8,128)(2,1)S(1)}, u32[]{:S(2)}, u32[]{:S(2)}) collective-permute-start(bf16[256,512]{1,0:T(8,128)(2,1)S(1)} %add.36), channel_id=1, source_target_pairs={{0,2},{1,3},{2,0},{3,1},{4,6},{5,7},{6,4},{7,5},{8,10},{9,11},{10,... | collective-permute-start | bytes 786440 | tf_op jit(solution)/shard_map/ppermute | solution.py:579
  126.4 12.7 %collective-permute-start.14 = (bf16[256,512]{1,0:T(8,128)(2,1)S(1)}, bf16[256,512]{1,0:T(8,128)(2,1)S(1)}, u32[]{:S(2)}, u32[]{:S(2)}) collective-permute-start(bf16[256,512]{1,0:T(8,128)(2,1)S(1)} %add.37), channel_id=1, source_target_pairs={{0,2},{1,3},{2,0},{3,1},{4,6},{5,7},{6,4},{7,5},{8,10},{9,11},{10,... | collective-permute-start | bytes 786440 | tf_op jit(solution)/shard_map/ppermute | solution.py:579
  (2 other events, 2.1 us)

commit v12 on v11

--- a/solution.py
+++ b/solution.py
@@ -25,8 +25,8 @@
 LANES = 128
 PARTS = 2
 NEW_GROUP = 128 // (2 * STEP_COUNT)
-SLOTS = 4
-PACKS = 2
+SLOTS = 6
+PACKS = 1
 VMEM_LIMIT = 24 * 1024 * 1024
 WHOLE_VMEM = 60 * 1024 * 1024
 ATTEND_VMEM = 48 * 1024 * 1024
@@ -597,17 +597,16 @@
 def scatter(made, low):
     if len(made) == 1:
         moved = lax.all_to_all(made[0], "tp", split_axis=0, concat_axis=0, tiled=True)
-        return [moved], [], lax.all_gather(low, "req", axis=0)
+        return [moved], [], lax.all_gather(low, "req", axis=0), low
     own, three, pairs, twos = made[0], made[1], made[2 : 2 + PARTS], made[2 + PARTS :]
     lane = lax.axis_index("tp").astype(jnp.int32).reshape(1)
     middle = lax.ppermute(after(three, low), "tp", [(1, 2), (2, 1)])
-    gathered = lax.all_gather(after(low, middle), "req", axis=0)
     moved, passed = [], []
     for c in range(PARTS):
         moved.append(exchange(after(pairs[c], *([middle] if c else [low])), "tp", 1))
-        two = after(twos[c], *([passed[-1], gathered] if c else [middle]))
-        passed.append(exchange(add(lane, two, moved[c]), "tp", 2))
-    return [own, middle], moved + passed, gathered
+        passed.append(exchange(add(lane, after(twos[c], middle), moved[c]), "tp", 2))
+    gathered = lax.all_gather(after(low, *moved), "req", axis=0)
+    return [own, middle], moved + passed, gathered, middle
 
 
 def on_device(
@@ -655,13 +654,12 @@
     where = jnp.stack(origins + roles)
     token_slot = jnp.repeat(slot, STEP_COUNT, axis=1)
     mask = (token_slot.reshape(tp_count, -1)[:, :, None] == mine).astype(jnp.bfloat16)
-    up = lax.all_to_all(after(up_blocks, table, q, new), "req", split_axis=0, concat_axis=0, tiled=True)
-    up = up.reshape(req_count * own_slots * rank, -1)
-    mask = after(mask, up)
     x, lows = collect(where, blocks, down, mask, tp_count)
     low = [lows[0]] + [exchange(lows[j], "tp", j) for j in range(1, tp_count)]
     low = functools.reduce(jnp.add, [term.astype(jnp.float32) for term in low]).astype(jnp.bfloat16)
-    terms, parts, low = scatter(project(x, output_projection_weight, tp_count), low)
+    terms, parts, low, middle = scatter(project(x, output_projection_weight, tp_count), low)
+    up = lax.all_to_all(after(up_blocks, middle), "req", split_axis=0, concat_axis=0, tiled=True)
+    up = up.reshape(req_count * own_slots * rank, -1)
     return finish(terms, parts, adapt(low, up))
 
 

time: 140 us -> 157 us (1.12); the launches traced: 140 us -> 156 us
  waiting for transfers between devices: 38.1 us -> 60.9 us
  starting transfers between devices: 44.8 us -> 34.6 us
    ppermute x14, waiting for transfers between devices: 32.7 us -> 52.1 us  [exchange(): return lax.ppermute(x, axis, [(i, i ^ distance) for i in range(count)])]
    ppermute x14, starting transfers between devices: 35.2 us -> 25.1 us  [exchange(): return lax.ppermute(x, axis, [(i, i ^ distance) for i in range(count)])]
    all_to_all x1, waiting for transfers between devices: 5.41 us -> 8.8 us  [on_device(): lax.all_to_all(outbox, 'req', split_axis=0, concat_axis=0, tiled=True)]
    unnamed x18 -> x36, local copies, waits for them, and re-layouts: 3.45 us -> 6.38 us
    reshape x2, local copies, waits for them, and re-layouts: 2.3 us -> 0.46 us  [on_device(): q = queries.reshape(requests * STEP_COUNT * heads, HEAD_WIDTH).T]
  transfers between devices with their start and end apart: 17 -> 17, of which waited for: 10 -> 9; matrix products, arithmetic and copies ran while one was open for 2% -> 1% of each run, Pallas kernels for 23% -> 5%
where the time goes in v12:
time: 157 us; the launch traced here: 156 us
  waiting for transfers between devices  60.9 us (39%)
  Pallas kernels  42 us (27%)
  starting transfers between devices  34.6 us (22%)
  blocking collectives  10 us (6%)
  local copies, waits for them, and re-layouts  7.34 us (5%)
    ppermute x14, waiting for transfers between devices, exchange(): return lax.ppermute(x, axis, [(i, i ^ distance) for i in range(count)])  52.1 us
    pallas_call x1, Pallas kernels, attend(): pl.pallas_call(functools.partial(attend_kernel, req_count, per_dev, reque...  25.5 us
    ppermute x14, starting transfers between devices, exchange(): return lax.ppermute(x, axis, [(i, i ^ distance) for i in range(count)])  25.1 us
    all_gather x1, blocking collectives, scatter(): gathered = lax.all_gather(after(low, *moved), 'req', axis=0)  10 us
    all_to_all x1, waiting for transfers between devices, on_device(): lax.all_to_all(outbox, 'req', split_axis=0, concat_axis=0, tiled=True)  8.8 us
    unnamed x36, local copies, waits for them, and re-layouts  6.38 us
    all_to_all x1, starting transfers between devices, on_device(): lax.all_to_all(outbox, 'req', split_axis=0, concat_axis=0, tiled=True)  5.23 us
    pallas_call x1, Pallas kernels, project(): pl.pallas_call(functools.partial(project_kernel, roles, min(256, columns)...  5.09 us
  transfers between devices with their start and end apart: 17, of which 9 were waited for; matrix products, arithmetic and copies ran while one was open for 1% of the time, Pallas kernels for 5%

profile of v12, /device:TPU:0, one launch (start us, length us, event | category | flops | bytes accessed | tf_op | source)
XLA Modules:
  0.0 155.5 jit_solution(2560302050457794201)
XLA Ops:
  0.0 3.7 %pack_outbox.1 = bf16[8,65,2,256]{3,2,1,0:T(2,128)(2,1)} custom-call(s32[1]{0:T(128)} %bitcast.me_ref, s32[1,512]{1,0:T(1,128)} %bitcast.30, s32[1,32]{1,0:T(1,128)} %bitcast.35, bf16[512,32,2,256]{3,2,1,0:T(2,128)(2,1)} %pages.3), custom_call_target="tpu_custom_call" | custom-call | flops 1 | bytes 1 | tf_op jit(solution)/shard_map/pack_outbox/pallas_call | solution.py:113
  3.7 5.2 %all-to-all-start = ((bf16[8,65,2,256]{3,2,1,0:T(2,128)(2,1)}), bf16[8,65,2,256]{3,2,1,0:T(2,128)(2,1)S(1)}, u32[]{:S(2)}, u32[]{:S(2)}) async-start(bf16[8,65,2,256]{3,2,1,0:T(2,128)(2,1)} %pack_outbox.1), calls=%async_computation | async-start | bytes 1064960 | tf_op jit(solution)/shard_map/all_to_all | solution.py:635
  9.9 8.8 %all-to-all-done.inbox = bf16[8,65,2,256]{3,2,1,0:T(2,128)(2,1)S(1)} async-done(((bf16[8,65,2,256]{3,2,1,0:T(2,128)(2,1)}), bf16[8,65,2,256]{3,2,1,0:T(2,128)(2,1)S(1)}, u32[]{:S(2)}, u32[]{:S(2)}) %all-to-all-start) | async-done | bytes 532512 | tf_op jit(solution)/shard_map/all_to_all | solution.py:635
  18.7 25.5 %attend.1.refs_0_ = bf16[128,2048]{1,0:T(8,128)(2,1)S(1)} custom-call(s32[2,128]{1,0:T(2,128)S(1)} %get-tuple-element.25.order_ref, s32[32]{0:T(128)S(1)} %copy-done.13, s32[4,128]{1,0:T(4,128)S(1)} %get-tuple-element.26.table_in, bf16[128,2048]{1,0:T(8,128)(2,1)S(1)} %bitcast.26, bf16[256,256]{1,0:T(8,128)(2,1)S(1)} %reshape.54.new_ref, ...), custom_call_target="tpu_custom_call" | custom-call | flops 2147483648 | bytes 16777216 | tf_op jit(solution)/shard_map/attend/pallas_call | solution.py:374
  44.2 1.2 collective-permute-start
  45.4 2.3 %collective-permute-start.2 = (bf16[128,2048]{1,0:T(8,128)(2,1)S(1)}, bf16[128,2048]{1,0:T(8,128)(2,1)S(1)}, u32[]{:S(2)}, u32[]{:S(2)}) collective-permute-start(bf16[128,2048]{1,0:T(8,128)(2,1)S(1)} %attend.1.refs_0_), channel_id=1, source_target_pairs={{0,24},{4,28},{8,16},{12,20},{16,8},{20,12},{24,0},{28,4},{1,25},{... | collective-permute-start | bytes 1572872 | tf_op jit(solution)/shard_map/ppermute | solution.py:579
  48.0 11.2 %collective-permute-done.refs_1_ = bf16[128,2048]{1,0:T(8,128)(2,1)S(1)} collective-permute-done((bf16[128,2048]{1,0:T(8,128)(2,1)S(1)}, bf16[128,2048]{1,0:T(8,128)(2,1)S(1)}, u32[]{:S(2)}, u32[]{:S(2)}) %collective-permute-start) | collective-permute-done | bytes 524320 | tf_op jit(solution)/shard_map/ppermute | solution.py:579
  59.2 9.2 %collective-permute-done.1.refs_2_ = bf16[128,2048]{1,0:T(8,128)(2,1)S(1)} collective-permute-done((bf16[128,2048]{1,0:T(8,128)(2,1)S(1)}, bf16[128,2048]{1,0:T(8,128)(2,1)S(1)}, u32[]{:S(2)}, u32[]{:S(2)}) %collective-permute-start.1) | collective-permute-done | bytes 524320 | tf_op jit(solution)/shard_map/ppermute | solution.py:579
  71.2 3.0 %collect.1 = (bf16[1024,2048]{1,0:T(8,128)(2,1)S(1)}, bf16[256,128]{1,0:T(8,128)(2,1)S(1)}, bf16[256,128]{1,0:T(8,128)(2,1)S(1)}, bf16[256,128]{1,0:T(8,128)(2,1)S(1)}, bf16[256,128]{1,0:T(8,128)(2,1)S(1)}) custom-call(s32[12]{0:T(128)S(1)} %stack.51.where_ref, bf16[128,2048]{1,0:T(8,128)(2,1)S(1)} %attend.1.refs_0_, ...), custom_call_target="tpu_custom_call" | custom-call | flops 1 | bytes 1 | tf_op jit(solution)/shard_map/collect/pallas_call | solution.py:445
  74.2 1.6 %collective-permute-start.7 = (bf16[256,128]{1,0:T(8,128)(2,1)S(1)}, bf16[256,128]{1,0:T(8,128)(2,1)S(1)}, u32[]{:S(2)}, u32[]{:S(2)}) collective-permute-start(bf16[256,128]{1,0:T(8,128)(2,1)S(1)} %get-tuple-element.28), channel_id=1, source_target_pairs={{0,1},{1,0},{2,3},{3,2},{4,5},{5,4},{6,7},{7,6},{8,9},{9,8},{10,11... | collective-permute-start | bytes 196616 | tf_op jit(solution)/shard_map/ppermute | solution.py:579
  75.8 2.6 %collective-permute-start.8 = (bf16[256,128]{1,0:T(8,128)(2,1)S(1)}, bf16[256,128]{1,0:T(8,128)(2,1)S(1)}, u32[]{:S(2)}, u32[]{:S(2)}) collective-permute-start(bf16[256,128]{1,0:T(8,128)(2,1)S(1)} %get-tuple-element.29), channel_id=1, source_target_pairs={{0,2},{1,3},{2,0},{3,1},{4,6},{5,7},{6,4},{7,5},{8,10},{9,11},{10,... | collective-permute-start | bytes 196616 | tf_op jit(solution)/shard_map/ppermute | solution.py:579
  78.7 5.1 %project.1 = (bf16[256,1024]{1,0:T(8,128)(2,1)S(1)}, bf16[256,1024]{1,0:T(8,128)(2,1)S(1)}, bf16[2,256,512]{2,1,0:T(8,128)(2,1)S(1)}, bf16[2,256,512]{2,1,0:T(8,...) custom-call(bf16[1024,2048]{1,0:T(8,128)(2,1)S(1)} %get-tuple-element.31.x_ref, ...), custom_call_target="tpu_custom_call" | custom-call | flops 1 | bytes 1 | tf_op jit(solution)/shard_map/project/pallas_call | solution.py:493
  85.6 1.3 copy-done
  87.8 3.6 %all-to-all-start.1 = ((bf16[8,128,1024]{2,1,0:T(8,128)(2,1)}), bf16[8,128,1024]{2,1,0:T(8,128)(2,1)S(1)}, u32[]{:S(2)}, u32[]{:S(2)}) async-start(bf16[8,128,1024]{2,1,0:T(8,128)(2,1)} %copy-done), calls=%async_computation.1 | async-start | bytes 4194304 | tf_op jit(solution)/shard_map/all_to_all | solution.py:661
  91.4 13.1 %collective-permute-start.10 = (bf16[2,256,512]{2,1,0:T(8,128)(2,1)}, bf16[2,256,512]{2,1,0:T(8,128)(2,1)S(1)}, u32[]{:S(2)}, u32[]{:S(2)}) collective-permute-start(bf16[2,256,512]{2,1,0:T(8,128)(2,1)} %copy-done.14), channel_id=1, source_target_pairs={{0,1},{1,0},{2,3},{3,2},{4,5},{5,4},{6,7},{7,6},{8,9},{9,8},{10,11... | collective-permute-start | bytes 1572872 | tf_op jit(solution)/shard_map/ppermute | solution.py:579
  104.6 12.8 %collective-permute-done.10.passed_ref.refs_2_ = bf16[2,256,512]{2,1,0:T(8,128)(2,1)S(1)} collective-permute-done((bf16[2,256,512]{2,1,0:T(8,128)(2,1)}, bf16[2,256,512]{2,1,0:T(8,128)(2,1)S(1)}, u32[]{:S(2)}, u32[]{:S(2)}) %collective-permute-start.10) | collective-permute-done | bytes 524320 | tf_op jit(solution)/shard_map/ppermute | solution.py:579
  118.1 3.0 %collective-permute-start.13 = (bf16[256,512]{1,0:T(8,128)(2,1)}, bf16[256,512]{1,0:T(8,128)(2,1)S(1)}, u32[]{:S(2)}, u32[]{:S(2)}) collective-permute-start(bf16[256,512]{1,0:T(8,128)(2,1)} %add.36), channel_id=1, source_target_pairs={{0,2},{1,3},{2,0},{3,1},{4,6},{5,7},{6,4},{7,5},{8,10},{9,11},{10,... | collective-permute-start | bytes 786440 | tf_op jit(solution)/shard_map/ppermute | solution.py:579
  121.0 12.9 %collective-permute-done.12.passed_ref.refs_3_ = bf16[2,256,512]{2,1,0:T(8,128)(2,1)S(1)} collective-permute-done((bf16[2,256,512]{2,1,0:T(8,128)(2,1)S(1)}, bf16[2,256,512]{2,1,0:T(8,128)(2,1)S(1)}, u32[]{:S(2)}, u32[]{:S(2)}) %collective-permute-start.12) | collective-permute-done | bytes 524320 | tf_op jit(solution)/shard_map/ppermute | solution.py:579
  136.2 10.0 %all-gather = bf16[2048,128]{1,0:T(8,128)(2,1)S(1)} all-gather(bf16[256,128]{1,0:T(8,128)(2,1)S(1)} %add_convert_fusion), channel_id=2, replica_groups=mesh['req'=8,'tp'=4] {'req'}, dimensions={0}, use_global_device_ids=true | all-gather | bytes 589824 | tf_op jit(solution)/shard_map/all_gather | solution.py:608
  146.9 3.4 %collective-permute-done.14.refs_5_ = bf16[256,512]{1,0:T(8,128)(2,1)} collective-permute-done((bf16[256,512]{1,0:T(8,128)(2,1)}, bf16[256,512]{1,0:T(8,128)(2,1)}, u32[]{:S(2)}, u32[]{:S(2)}) %collective-permute-start.14) | collective-permute-done | bytes 262176 | tf_op jit(solution)/shard_map/ppermute | solution.py:579
  150.4 1.0 copy-done.4
  151.4 1.0 copy-done.7
  152.4 1.0 copy-done.9
  153.5 2.0 %finish.1 = bf16[256,1024]{1,0:T(8,128)(2,1)} custom-call(f32[256,1024]{1,0:T(8,128)S(1)} %adapt.1.extra_ref, bf16[256,1024]{1,0:T(8,128)(2,1)S(1)} %copy-done.7, bf16[256,1024]{1,0:T(8,128)(2,1)S(1)} %copy-done.9, bf16[2,256,512]{2,1,0:T(8,128)(2,1)S(1)} %collective-permute-done.10.passed_ref.refs_2_, bf16[2,256,512]{2,1,0:T(8,128)(2,1)S(1)} %copy-done.4, ...), custom_call_target="tpu_custom_call" | custom-call | flops 1 | bytes 1 | tf_op jit(solution)/shard_map/finish/pallas_call | solution.py:566
  (69 shorter events, 10.4 us)
Async XLA Ops:
  0.0 8.9 %copy-start.12 = (s32[512]{0:T(512)S(1)}, s32[512]{0:T(512)}, u32[]{:S(2)}) copy-start(s32[512]{0:T(512)} %param.13) | copy-start | bytes 6148
  0.0 8.9 %copy-start.13 = (s32[32]{0:T(128)S(1)}, s32[32]{0:T(128)}, u32[]{:S(2)}) copy-start(s32[32]{0:T(128)} %lengths_ref.1) | copy-start | bytes 388
  0.0 9.2 %copy-start.15 = (bf16[128,2048]{1,0:T(8,128)(2,1)S(1)}, bf16[128,2048]{1,0:T(8,128)(2,1)}, u32[]{:S(2)}) copy-start(bf16[128,2048]{1,0:T(8,128)(2,1)} %param.10) | copy-start | bytes 1572868
  0.0 9.7 %copy-start.16 = (bf16[2,128,256]{2,1,0:T(8,128)(2,1)S(1)}, bf16[2,128,256]{2,1,0:T(8,128)(2,1)}, u32[]{:S(2)}) copy-start(bf16[2,128,256]{2,1,0:T(8,128)(2,1)} %param.11) | copy-start | bytes 393220
  3.7 15.1 %all-to-all-start = ((bf16[8,65,2,256]{3,2,1,0:T(2,128)(2,1)}), bf16[8,65,2,256]{3,2,1,0:T(2,128)(2,1)S(1)}, u32[]{:S(2)}, u32[]{:S(2)}) async-start(bf16[8,65,2,256]{3,2,1,0:T(2,128)(2,1)} %pack_outbox.1), calls=%async_computation | async-start | bytes 1064960 | tf_op jit(solution)/shard_map/all_to_all | solution.py:635
  18.7 50.1 %copy-start.17 = (s32[16]{0:T(128)S(1)}, s32[16]{0:T(128)}, u32[]{:S(2)}) copy-start(s32[16]{0:T(128)} %param.16) | copy-start | bytes 196
  18.7 52.4 %copy-start.5 = (bf16[2,2048,64]{1,2,0:T(8,128)(2,1)S(1)}, bf16[2,2048,64]{1,2,0:T(8,128)(2,1)}, u32[]{:S(2)}) copy-start(bf16[2,2048,64]{1,2,0:T(8,128)(2,1)} %param.17) | copy-start | bytes 1572868
  44.2 14.9 %collective-permute-start = (bf16[128,2048]{1,0:T(8,128)(2,1)S(1)}, bf16[128,2048]{1,0:T(8,128)(2,1)S(1)}, u32[]{:S(2)}, u32[]{:S(2)}) collective-permute-start(bf16[128,2048]{1,0:T(8,128)(2,1)S(1)} %attend.1.refs_0_), channel_id=1, source_target_pairs={{0,8},{4,12},{8,0},{12,4},{16,24},{20,28},{24,16},{28,20},{1,9},{5... | collective-permute-start | bytes 1572872 | tf_op jit(solution)/shard_map/ppermute | solution.py:579
  45.4 22.9 %collective-permute-start.1 = (bf16[128,2048]{1,0:T(8,128)(2,1)S(1)}, bf16[128,2048]{1,0:T(8,128)(2,1)S(1)}, u32[]{:S(2)}, u32[]{:S(2)}) collective-permute-start(bf16[128,2048]{1,0:T(8,128)(2,1)S(1)} %attend.1.refs_0_), channel_id=1, source_target_pairs={{0,16},{4,20},{8,24},{12,28},{16,0},{20,4},{24,8},{28,12},{1,17},{... | collective-permute-start | bytes 1572872 | tf_op jit(solution)/shard_map/ppermute | solution.py:579
  45.4 22.9 %collective-permute-start.2 = (bf16[128,2048]{1,0:T(8,128)(2,1)S(1)}, bf16[128,2048]{1,0:T(8,128)(2,1)S(1)}, u32[]{:S(2)}, u32[]{:S(2)}) collective-permute-start(bf16[128,2048]{1,0:T(8,128)(2,1)S(1)} %attend.1.refs_0_), channel_id=1, source_target_pairs={{0,24},{4,28},{8,16},{12,20},{16,8},{20,12},{24,0},{28,4},{1,25},{... | collective-permute-start | bytes 1572872 | tf_op jit(solution)/shard_map/ppermute | solution.py:579
  47.9 21.5 %collective-permute-start.3 = (bf16[128,2048]{1,0:T(8,128)(2,1)S(1)}, bf16[128,2048]{1,0:T(8,128)(2,1)}, u32[]{:S(2)}, u32[]{:S(2)}) collective-permute-start(bf16[128,2048]{1,0:T(8,128)(2,1)S(1)} %attend.1.refs_0_), channel_id=1, source_target_pairs={{0,4},{4,0},{8,12},{12,8},{16,20},{20,16},{24,28},{28,24},{1,5},{5... | collective-permute-start | bytes 1572872 | tf_op jit(solution)/shard_map/ppermute | solution.py:579
  59.2 10.3 %collective-permute-start.4 = (bf16[128,2048]{1,0:T(8,128)(2,1)S(1)}, bf16[128,2048]{1,0:T(8,128)(2,1)}, u32[]{:S(2)}, u32[]{:S(2)}) collective-permute-start(bf16[128,2048]{1,0:T(8,128)(2,1)S(1)} %collective-permute-done.refs_1_), channel_id=1, source_target_pairs={{0,4},{4,0},{8,12},{12,8},{16,20},{20,16},{24,28},{28,24},{1,5},{5... | collective-permute-start | bytes 1572872 | tf_op jit(solution)/shard_map/ppermute | solution.py:579
  68.4 2.0 %collective-permute-start.5 = (bf16[128,2048]{1,0:T(8,128)(2,1)S(1)}, bf16[128,2048]{1,0:T(8,128)(2,1)}, u32[]{:S(2)}, u32[]{:S(2)}) collective-permute-start(bf16[128,2048]{1,0:T(8,128)(2,1)S(1)} %collective-permute-done.1.refs_2_), channel_id=1, source_target_pairs={{0,4},{4,0},{8,12},{12,8},{16,20},{20,16},{24,28},{28,24},{1,5},{5... | collective-permute-start | bytes 1572872 | tf_op jit(solution)/shard_map/ppermute | solution.py:579
  68.4 2.8 %collective-permute-start.6 = (bf16[128,2048]{1,0:T(8,128)(2,1)S(1)}, bf16[128,2048]{1,0:T(8,128)(2,1)}, u32[]{:S(2)}, u32[]{:S(2)}) collective-permute-start(bf16[128,2048]{1,0:T(8,128)(2,1)S(1)} %collective-permute-done.2.refs_3_), channel_id=1, source_target_pairs={{0,4},{4,0},{8,12},{12,8},{16,20},{20,16},{24,28},{28,24},{1,5},{5... | collective-permute-start | bytes 1572872 | tf_op jit(solution)/shard_map/ppermute | solution.py:579
  69.2 9.4 %copy-start.1 = (bf16[2048,1024]{1,0:T(8,128)(2,1)S(1)}, bf16[2048,1024]{1,0:T(8,128)(2,1)}, u32[]{:S(2)}) copy-start(bf16[2048,1024]{1,0:T(8,128)(2,1)} %w_ref.1) | copy-start | bytes 12582916
  74.2 9.6 %collective-permute-start.7 = (bf16[256,128]{1,0:T(8,128)(2,1)S(1)}, bf16[256,128]{1,0:T(8,128)(2,1)S(1)}, u32[]{:S(2)}, u32[]{:S(2)}) collective-permute-start(bf16[256,128]{1,0:T(8,128)(2,1)S(1)} %get-tuple-element.28), channel_id=1, source_target_pairs={{0,1},{1,0},{2,3},{3,2},{4,5},{5,4},{6,7},{7,6},{8,9},{9,8},{10,11... | collective-permute-start | bytes 196616 | tf_op jit(solution)/shard_map/ppermute | solution.py:579
  75.8 8.0 %collective-permute-start.8 = (bf16[256,128]{1,0:T(8,128)(2,1)S(1)}, bf16[256,128]{1,0:T(8,128)(2,1)S(1)}, u32[]{:S(2)}, u32[]{:S(2)}) collective-permute-start(bf16[256,128]{1,0:T(8,128)(2,1)S(1)} %get-tuple-element.29), channel_id=1, source_target_pairs={{0,2},{1,3},{2,0},{3,1},{4,6},{5,7},{6,4},{7,5},{8,10},{9,11},{10,... | collective-permute-start | bytes 196616 | tf_op jit(solution)/shard_map/ppermute | solution.py:579
  78.4 6.2 %collective-permute-start.9 = (bf16[256,128]{1,0:T(8,128)(2,1)S(1)}, bf16[256,128]{1,0:T(8,128)(2,1)S(1)}, u32[]{:S(2)}, u32[]{:S(2)}) collective-permute-start(bf16[256,128]{1,0:T(8,128)(2,1)S(1)} %get-tuple-element.30), channel_id=1, source_target_pairs={{0,3},{1,2},{2,1},{3,0},{4,7},{5,6},{6,5},{7,4},{8,11},{9,10},{10,... | collective-permute-start | bytes 196616 | tf_op jit(solution)/shard_map/ppermute | solution.py:579
  84.6 2.3 %collective-permute-start.11 = (bf16[256,1024]{1,0:T(8,128)(2,1)S(1)}, bf16[256,1024]{1,0:T(8,128)(2,1)S(1)}, u32[]{:S(2)}, u32[]{:S(2)}) collective-permute-start(bf16[256,1024]{1,0:T(8,128)(2,1)S(1)} %get-tuple-element.36), channel_id=1, source_target_pairs={{1,2},{2,1},{5,6},{6,5},{9,10},{10,9},{13,14},{14,13},{17,18},{18,... | collective-permute-start | bytes 1572872 | tf_op jit(solution)/shard_map/ppermute | solution.py:603
  87.8 58.4 %all-to-all-start.1 = ((bf16[8,128,1024]{2,1,0:T(8,128)(2,1)}), bf16[8,128,1024]{2,1,0:T(8,128)(2,1)S(1)}, u32[]{:S(2)}, u32[]{:S(2)}) async-start(bf16[8,128,1024]{2,1,0:T(8,128)(2,1)} %copy-done), calls=%async_computation.1 | async-start | bytes 4194304 | tf_op jit(solution)/shard_map/all_to_all | solution.py:661
  91.4 26.0 %collective-permute-start.10 = (bf16[2,256,512]{2,1,0:T(8,128)(2,1)}, bf16[2,256,512]{2,1,0:T(8,128)(2,1)S(1)}, u32[]{:S(2)}, u32[]{:S(2)}) collective-permute-start(bf16[2,256,512]{2,1,0:T(8,128)(2,1)} %copy-done.14), channel_id=1, source_target_pairs={{0,1},{1,0},{2,3},{3,2},{4,5},{5,4},{6,7},{7,6},{8,9},{9,8},{10,11... | collective-permute-start | bytes 1572872 | tf_op jit(solution)/shard_map/ppermute | solution.py:579
  104.5 29.5 %collective-permute-start.12 = (bf16[2,256,512]{2,1,0:T(8,128)(2,1)S(1)}, bf16[2,256,512]{2,1,0:T(8,128)(2,1)S(1)}, u32[]{:S(2)}, u32[]{:S(2)}) collective-permute-start(bf16[2,256,512]{2,1,0:T(8,128)(2,1)S(1)} %get-tuple-element.37), channel_id=1, source_target_pairs={{0,1},{1,0},{2,3},{3,2},{4,5},{5,4},{6,7},{7,6},{8,9},{9,8},{10,11... | collective-permute-start | bytes 1572872 | tf_op jit(solution)/shard_map/ppermute | solution.py:579
  118.1 28.8 %collective-permute-start.13 = (bf16[256,512]{1,0:T(8,128)(2,1)}, bf16[256,512]{1,0:T(8,128)(2,1)S(1)}, u32[]{:S(2)}, u32[]{:S(2)}) collective-permute-start(bf16[256,512]{1,0:T(8,128)(2,1)} %add.36), channel_id=1, source_target_pairs={{0,2},{1,3},{2,0},{3,1},{4,6},{5,7},{6,4},{7,5},{8,10},{9,11},{10,... | collective-permute-start | bytes 786440 | tf_op jit(solution)/shard_map/ppermute | solution.py:579
  135.8 14.6 %collective-permute-start.14 = (bf16[256,512]{1,0:T(8,128)(2,1)}, bf16[256,512]{1,0:T(8,128)(2,1)}, u32[]{:S(2)}, u32[]{:S(2)}) collective-permute-start(bf16[256,512]{1,0:T(8,128)(2,1)} %add.37), channel_id=1, source_target_pairs={{0,2},{1,3},{2,0},{3,1},{4,6},{5,7},{6,4},{7,5},{8,10},{9,11},{10,... | collective-permute-start | bytes 786440 | tf_op jit(solution)/shard_map/ppermute | solution.py:579
  (11 other events, 19.3 us)

commit v13 on v11

--- a/solution.py
+++ b/solution.py
@@ -25,8 +25,8 @@
 LANES = 128
 PARTS = 2
 NEW_GROUP = 128 // (2 * STEP_COUNT)
-SLOTS = 4
-PACKS = 2
+SLOTS = 6
+PACKS = 1
 VMEM_LIMIT = 24 * 1024 * 1024
 WHOLE_VMEM = 60 * 1024 * 1024
 ATTEND_VMEM = 48 * 1024 * 1024
@@ -601,12 +601,11 @@
     own, three, pairs, twos = made[0], made[1], made[2 : 2 + PARTS], made[2 + PARTS :]
     lane = lax.axis_index("tp").astype(jnp.int32).reshape(1)
     middle = lax.ppermute(after(three, low), "tp", [(1, 2), (2, 1)])
-    gathered = lax.all_gather(after(low, middle), "req", axis=0)
     moved, passed = [], []
     for c in range(PARTS):
         moved.append(exchange(after(pairs[c], *([middle] if c else [low])), "tp", 1))
-        two = after(twos[c], *([passed[-1], gathered] if c else [middle]))
-        passed.append(exchange(add(lane, two, moved[c]), "tp", 2))
+        passed.append(exchange(add(lane, after(twos[c], middle), moved[c]), "tp", 2))
+    gathered = lax.all_gather(after(low, *moved), "req", axis=0)
     return [own, middle], moved + passed, gathered
 
 

time: 140 us -> 140 us (level)
  waiting for transfers between devices: 38.1 us -> 48.8 us
  starting transfers between devices: 44.8 us -> 35.4 us
    ppermute x14, waiting for transfers between devices: 32.7 us -> 43.4 us  [exchange(): return lax.ppermute(x, axis, [(i, i ^ distance) for i in range(count)])]
    ppermute x14, starting transfers between devices: 35.2 us -> 25.8 us  [exchange(): return lax.ppermute(x, axis, [(i, i ^ distance) for i in range(count)])]
  transfers between devices with their start and end apart: 17 -> 17, of which waited for: 10 -> 9; matrix products, arithmetic and copies ran while one was open for 2% -> 2% of each run, Pallas kernels for 23% -> 23%
where the time goes in v13:
time: 140 us
  waiting for transfers between devices  48.8 us (35%)
  Pallas kernels  40.1 us (29%)
  starting transfers between devices  35.4 us (25%)
  blocking collectives  8.7 us (6%)
  local copies, waits for them, and re-layouts  6.25 us (4%)
    ppermute x14, waiting for transfers between devices, exchange(): return lax.ppermute(x, axis, [(i, i ^ distance) for i in range(count)])  43.4 us
    ppermute x14, starting transfers between devices, exchange(): return lax.ppermute(x, axis, [(i, i ^ distance) for i in range(count)])  25.8 us
    pallas_call x1, Pallas kernels, attend(): pl.pallas_call(functools.partial(attend_kernel, req_count, per_dev, reque...  25.4 us
    all_gather x1, blocking collectives, scatter(): gathered = lax.all_gather(after(low, *moved), 'req', axis=0)  8.7 us
    all_to_all x1, waiting for transfers between devices, on_device(): lax.all_to_all(outbox, 'req', split_axis=0, concat_axis=0, tiled=True)  5.41 us
    all_to_all x1, starting transfers between devices, on_device(): lax.all_to_all(outbox, 'req', split_axis=0, concat_axis=0, tiled=True)  5.28 us
    pallas_call x1, Pallas kernels, project(): pl.pallas_call(functools.partial(project_kernel, roles, min(256, columns)...  5.1 us
    pallas_call x1, Pallas kernels, pack(): pl.pallas_call(functools.partial(pack_kernel, req_count, per_dev), out_sh...  3.79 us
  transfers between devices with their start and end apart: 17, of which 9 were waited for; matrix products, arithmetic and copies ran while one was open for 2% of the time, Pallas kernels for 23%

profile of v13, /device:TPU:0, one launch (start us, length us, event | category | flops | bytes accessed | tf_op | source)
XLA Modules:
  0.0 139.8 jit_solution(12845471255854625967)
XLA Ops:
  0.0 3.8 %pack_outbox.1 = bf16[8,65,2,256]{3,2,1,0:T(2,128)(2,1)} custom-call(s32[1]{0:T(128)} %bitcast.me_ref, s32[1,512]{1,0:T(1,128)} %bitcast.30, s32[1,32]{1,0:T(1,128)} %bitcast.35, bf16[512,32,2,256]{3,2,1,0:T(2,128)(2,1)} %pages.3), custom_call_target="tpu_custom_call" | custom-call | flops 1 | bytes 1 | tf_op jit(solution)/shard_map/pack_outbox/pallas_call | solution.py:113
  3.8 5.3 %all-to-all-start = ((bf16[8,65,2,256]{3,2,1,0:T(2,128)(2,1)}), bf16[8,65,2,256]{3,2,1,0:T(2,128)(2,1)S(1)}, u32[]{:S(2)}, u32[]{:S(2)}) async-start(bf16[8,65,2,256]{3,2,1,0:T(2,128)(2,1)} %pack_outbox.1), calls=%async_computation | async-start | bytes 1064960 | tf_op jit(solution)/shard_map/all_to_all | solution.py:635
  9.4 1.3 copy-done
  11.2 1.3 reshape.53
  13.5 5.4 %all-to-all-done.inbox = bf16[8,65,2,256]{3,2,1,0:T(2,128)(2,1)S(1)} async-done(((bf16[8,65,2,256]{3,2,1,0:T(2,128)(2,1)}), bf16[8,65,2,256]{3,2,1,0:T(2,128)(2,1)S(1)}, u32[]{:S(2)}, u32[]{:S(2)}) %all-to-all-start) | async-done | bytes 532512 | tf_op jit(solution)/shard_map/all_to_all | solution.py:635
  18.9 3.6 %all-to-all-start.1 = ((bf16[8,128,1024]{2,1,0:T(8,128)(2,1)}), bf16[8,128,1024]{2,1,0:T(8,128)(2,1)S(1)}, u32[]{:S(2)}, u32[]{:S(2)}) async-start(bf16[8,128,1024]{2,1,0:T(8,128)(2,1)} %copy-done), calls=%async_computation.1 | async-start | bytes 4194304 | tf_op jit(solution)/shard_map/all_to_all | solution.py:657
  22.6 1.0 copy-done.2
  23.6 25.4 %attend.1.refs_0_ = bf16[128,2048]{1,0:T(8,128)(2,1)S(1)} custom-call(s32[2,128]{1,0:T(2,128)S(1)} %get-tuple-element.26.order_ref, s32[32]{0:T(128)S(1)} %copy-done.6, s32[4,128]{1,0:T(4,128)S(1)} %get-tuple-element.27.table_in, bf16[128,2048]{1,0:T(8,128)(2,1)S(1)} %bitcast.26, bf16[256,256]{1,0:T(8,128)(2,1)S(1)} %reshape.54.new_ref, ...), custom_call_target="tpu_custom_call" | custom-call | flops 2147483648 | bytes 16777216 | tf_op jit(solution)/shard_map/attend/pallas_call | solution.py:374
  49.0 4.2 %collective-permute-start.2 = (bf16[128,2048]{1,0:T(8,128)(2,1)S(1)}, bf16[128,2048]{1,0:T(8,128)(2,1)}, u32[]{:S(2)}, u32[]{:S(2)}) collective-permute-start(bf16[128,2048]{1,0:T(8,128)(2,1)S(1)} %attend.1.refs_0_), channel_id=1, source_target_pairs={{0,24},{4,28},{8,16},{12,20},{16,8},{20,12},{24,0},{28,4},{1,25},{... | collective-permute-start | bytes 1572872 | tf_op jit(solution)/shard_map/ppermute | solution.py:579
  54.0 12.1 %collective-permute-done.2.refs_3_ = bf16[128,2048]{1,0:T(8,128)(2,1)} collective-permute-done((bf16[128,2048]{1,0:T(8,128)(2,1)S(1)}, bf16[128,2048]{1,0:T(8,128)(2,1)}, u32[]{:S(2)}, u32[]{:S(2)}) %collective-permute-start.2) | collective-permute-done | bytes 524320 | tf_op jit(solution)/shard_map/ppermute | solution.py:579
  66.1 10.5 %collective-permute-done.1.refs_2_ = bf16[128,2048]{1,0:T(8,128)(2,1)} collective-permute-done((bf16[128,2048]{1,0:T(8,128)(2,1)S(1)}, bf16[128,2048]{1,0:T(8,128)(2,1)}, u32[]{:S(2)}, u32[]{:S(2)}) %collective-permute-start.1) | collective-permute-done | bytes 524320 | tf_op jit(solution)/shard_map/ppermute | solution.py:579
  77.7 1.2 collective-permute-done.5.refs_6_
  79.6 1.0 copy-done.4
  80.6 3.5 %collect.1 = (bf16[1024,2048]{1,0:T(8,128)(2,1)S(1)}, bf16[256,128]{1,0:T(8,128)(2,1)S(1)}, bf16[256,128]{1,0:T(8,128)(2,1)S(1)}, bf16[256,128]{1,0:T(8,128)(2,1)S(1)}, bf16[256,128]{1,0:T(8,128)(2,1)S(1)}) custom-call(s32[12]{0:T(128)S(1)} %stack.51.where_ref, bf16[128,2048]{1,0:T(8,128)(2,1)S(1)} %attend.1.refs_0_, ...), custom_call_target="tpu_custom_call" | custom-call | flops 1 | bytes 1 | tf_op jit(solution)/shard_map/collect/pallas_call | solution.py:445
  84.1 1.6 %collective-permute-start.7 = (bf16[256,128]{1,0:T(8,128)(2,1)S(1)}, bf16[256,128]{1,0:T(8,128)(2,1)S(1)}, u32[]{:S(2)}, u32[]{:S(2)}) collective-permute-start(bf16[256,128]{1,0:T(8,128)(2,1)S(1)} %get-tuple-element.31), channel_id=1, source_target_pairs={{0,1},{1,0},{2,3},{3,2},{4,5},{5,4},{6,7},{7,6},{8,9},{9,8},{10,11... | collective-permute-start | bytes 196616 | tf_op jit(solution)/shard_map/ppermute | solution.py:579
  85.8 2.6 %collective-permute-start.8 = (bf16[256,128]{1,0:T(8,128)(2,1)S(1)}, bf16[256,128]{1,0:T(8,128)(2,1)S(1)}, u32[]{:S(2)}, u32[]{:S(2)}) collective-permute-start(bf16[256,128]{1,0:T(8,128)(2,1)S(1)} %get-tuple-element.32), channel_id=1, source_target_pairs={{0,2},{1,3},{2,0},{3,1},{4,6},{5,7},{6,4},{7,5},{8,10},{9,11},{10,... | collective-permute-start | bytes 196616 | tf_op jit(solution)/shard_map/ppermute | solution.py:579
  88.6 5.1 %project.1 = (bf16[256,1024]{1,0:T(8,128)(2,1)S(1)}, bf16[256,1024]{1,0:T(8,128)(2,1)S(1)}, bf16[2,256,512]{2,1,0:T(8,128)(2,1)S(1)}, bf16[2,256,512]{2,1,0:T(8,...) custom-call(bf16[1024,2048]{1,0:T(8,128)(2,1)S(1)} %get-tuple-element.34.x_ref, ...), custom_call_target="tpu_custom_call" | custom-call | flops 1 | bytes 1 | tf_op jit(solution)/shard_map/project/pallas_call | solution.py:493
  95.3 3.6 %collective-permute-start.10 = (bf16[2,256,512]{2,1,0:T(8,128)(2,1)S(1)}, bf16[2,256,512]{2,1,0:T(8,128)(2,1)S(1)}, u32[]{:S(2)}, u32[]{:S(2)}) collective-permute-start(bf16[2,256,512]{2,1,0:T(8,128)(2,1)S(1)} %get-tuple-element.36), channel_id=1, source_target_pairs={{0,1},{1,0},{2,3},{3,2},{4,5},{5,4},{6,7},{7,6},{8,9},{9,8},{10,11... | collective-permute-start | bytes 1572872 | tf_op jit(solution)/shard_map/ppermute | solution.py:579
  98.9 11.0 %collective-permute-start.12 = (bf16[2,256,512]{2,1,0:T(8,128)(2,1)S(1)}, bf16[2,256,512]{2,1,0:T(8,128)(2,1)S(1)}, u32[]{:S(2)}, u32[]{:S(2)}) collective-permute-start(bf16[2,256,512]{2,1,0:T(8,128)(2,1)S(1)} %get-tuple-element.40), channel_id=1, source_target_pairs={{0,1},{1,0},{2,3},{3,2},{4,5},{5,4},{6,7},{7,6},{8,9},{9,8},{10,11... | collective-permute-start | bytes 1572872 | tf_op jit(solution)/shard_map/ppermute | solution.py:579
  110.1 1.2 collective-permute-start.13
  111.3 14.9 %collective-permute-done.12.passed_ref.refs_3_ = bf16[2,256,512]{2,1,0:T(8,128)(2,1)S(1)} collective-permute-done((bf16[2,256,512]{2,1,0:T(8,128)(2,1)S(1)}, bf16[2,256,512]{2,1,0:T(8,128)(2,1)S(1)}, u32[]{:S(2)}, u32[]{:S(2)}) %collective-permute-start.12) | collective-permute-done | bytes 524320 | tf_op jit(solution)/shard_map/ppermute | solution.py:579
  126.4 8.7 %all-gather = bf16[2048,128]{1,0:T(8,128)(2,1)S(1)} all-gather(bf16[256,128]{1,0:T(8,128)(2,1)S(1)} %add_convert_fusion), channel_id=2, replica_groups=mesh['req'=8,'tp'=4] {'req'}, dimensions={0}, use_global_device_ids=true | all-gather | bytes 589824 | tf_op jit(solution)/shard_map/all_gather | solution.py:608
  135.8 2.9 %collective-permute-done.14.refs_5_ = bf16[256,512]{1,0:T(8,128)(2,1)S(1)} collective-permute-done((bf16[256,512]{1,0:T(8,128)(2,1)S(1)}, bf16[256,512]{1,0:T(8,128)(2,1)S(1)}, u32[]{:S(2)}, u32[]{:S(2)}) %collective-permute-start.14) | collective-permute-done | bytes 262176 | tf_op jit(solution)/shard_map/ppermute | solution.py:579
  138.7 1.1 finish.1
  (51 shorter events, 7.1 us)
Async XLA Ops:
  0.0 9.1 %copy-start.3 = (bf16[2,64,8192]{2,1,0:T(8,128)(2,1)S(1)}, bf16[2,64,8192]{2,1,0:T(8,128)(2,1)}, u32[]{:S(2)}) copy-start(bf16[2,64,8192]{2,1,0:T(8,128)(2,1)} %param.18) | copy-start | bytes 6291460
  3.8 6.9 %copy-start.5 = (s32[512]{0:T(512)S(1)}, s32[512]{0:T(512)}, u32[]{:S(2)}) copy-start(s32[512]{0:T(512)} %param.13) | copy-start | bytes 6148
  3.8 6.9 %copy-start.6 = (s32[32]{0:T(128)S(1)}, s32[32]{0:T(128)}, u32[]{:S(2)}) copy-start(s32[32]{0:T(128)} %lengths_ref.1) | copy-start | bytes 388
  3.8 7.2 %copy-start.7 = (bf16[2,128,256]{2,1,0:T(8,128)(2,1)S(1)}, bf16[2,128,256]{2,1,0:T(8,128)(2,1)}, u32[]{:S(2)}) copy-start(bf16[2,128,256]{2,1,0:T(8,128)(2,1)} %param.11) | copy-start | bytes 393220
  3.8 15.1 %all-to-all-start = ((bf16[8,65,2,256]{3,2,1,0:T(2,128)(2,1)}), bf16[8,65,2,256]{3,2,1,0:T(2,128)(2,1)S(1)}, u32[]{:S(2)}, u32[]{:S(2)}) async-start(bf16[8,65,2,256]{3,2,1,0:T(2,128)(2,1)} %pack_outbox.1), calls=%async_computation | async-start | bytes 1064960 | tf_op jit(solution)/shard_map/all_to_all | solution.py:635
  9.4 1.3 copy-start
  18.9 58.7 %all-to-all-start.1 = ((bf16[8,128,1024]{2,1,0:T(8,128)(2,1)}), bf16[8,128,1024]{2,1,0:T(8,128)(2,1)S(1)}, u32[]{:S(2)}, u32[]{:S(2)}) async-start(bf16[8,128,1024]{2,1,0:T(8,128)(2,1)} %copy-done), calls=%async_computation.1 | async-start | bytes 4194304 | tf_op jit(solution)/shard_map/all_to_all | solution.py:657
  23.6 53.5 %copy-start.8 = (s32[16]{0:T(128)S(1)}, s32[16]{0:T(128)}, u32[]{:S(2)}) copy-start(s32[16]{0:T(128)} %param.16) | copy-start | bytes 196
  49.0 17.0 %collective-permute-start.2 = (bf16[128,2048]{1,0:T(8,128)(2,1)S(1)}, bf16[128,2048]{1,0:T(8,128)(2,1)}, u32[]{:S(2)}, u32[]{:S(2)}) collective-permute-start(bf16[128,2048]{1,0:T(8,128)(2,1)S(1)} %attend.1.refs_0_), channel_id=1, source_target_pairs={{0,24},{4,28},{8,16},{12,20},{16,8},{20,12},{24,0},{28,4},{1,25},{... | collective-permute-start | bytes 1572872 | tf_op jit(solution)/shard_map/ppermute | solution.py:579
  53.2 23.4 %collective-permute-start.1 = (bf16[128,2048]{1,0:T(8,128)(2,1)S(1)}, bf16[128,2048]{1,0:T(8,128)(2,1)}, u32[]{:S(2)}, u32[]{:S(2)}) collective-permute-start(bf16[128,2048]{1,0:T(8,128)(2,1)S(1)} %attend.1.refs_0_), channel_id=1, source_target_pairs={{0,16},{4,20},{8,24},{12,28},{16,0},{20,4},{24,8},{28,12},{1,17},{... | collective-permute-start | bytes 1572872 | tf_op jit(solution)/shard_map/ppermute | solution.py:579
  53.2 23.4 %collective-permute-start = (bf16[128,2048]{1,0:T(8,128)(2,1)S(1)}, bf16[128,2048]{1,0:T(8,128)(2,1)}, u32[]{:S(2)}, u32[]{:S(2)}) collective-permute-start(bf16[128,2048]{1,0:T(8,128)(2,1)S(1)} %attend.1.refs_0_), channel_id=1, source_target_pairs={{0,8},{4,12},{8,0},{12,4},{16,24},{20,28},{24,16},{28,20},{1,9},{5... | collective-permute-start | bytes 1572872 | tf_op jit(solution)/shard_map/ppermute | solution.py:579
  53.9 23.7 %collective-permute-start.3 = (bf16[128,2048]{1,0:T(8,128)(2,1)S(1)}, bf16[128,2048]{1,0:T(8,128)(2,1)}, u32[]{:S(2)}, u32[]{:S(2)}) collective-permute-start(bf16[128,2048]{1,0:T(8,128)(2,1)S(1)} %attend.1.refs_0_), channel_id=1, source_target_pairs={{0,4},{4,0},{8,12},{12,8},{16,20},{20,16},{24,28},{28,24},{1,5},{5... | collective-permute-start | bytes 1572872 | tf_op jit(solution)/shard_map/ppermute | solution.py:579
  66.0 11.6 %collective-permute-start.6 = (bf16[128,2048]{1,0:T(8,128)(2,1)}, bf16[128,2048]{1,0:T(8,128)(2,1)}, u32[]{:S(2)}, u32[]{:S(2)}) collective-permute-start(bf16[128,2048]{1,0:T(8,128)(2,1)} %collective-permute-done.2.refs_3_), channel_id=1, source_target_pairs={{0,4},{4,0},{8,12},{12,8},{16,20},{20,16},{24,28},{28,24},{1,5},{5... | collective-permute-start | bytes 1572872 | tf_op jit(solution)/shard_map/ppermute | solution.py:579
  76.6 2.3 %collective-permute-start.5 = (bf16[128,2048]{1,0:T(8,128)(2,1)}, bf16[128,2048]{1,0:T(8,128)(2,1)}, u32[]{:S(2)}, u32[]{:S(2)}) collective-permute-start(bf16[128,2048]{1,0:T(8,128)(2,1)} %collective-permute-done.1.refs_2_), channel_id=1, source_target_pairs={{0,4},{4,0},{8,12},{12,8},{16,20},{20,16},{24,28},{28,24},{1,5},{5... | collective-permute-start | bytes 1572872 | tf_op jit(solution)/shard_map/ppermute | solution.py:579
  76.6 3.0 %collective-permute-start.4 = (bf16[128,2048]{1,0:T(8,128)(2,1)}, bf16[128,2048]{1,0:T(8,128)(2,1)}, u32[]{:S(2)}, u32[]{:S(2)}) collective-permute-start(bf16[128,2048]{1,0:T(8,128)(2,1)} %collective-permute-done.refs_1_), channel_id=1, source_target_pairs={{0,4},{4,0},{8,12},{12,8},{16,20},{20,16},{24,28},{28,24},{1,5},{5... | collective-permute-start | bytes 1572872 | tf_op jit(solution)/shard_map/ppermute | solution.py:579
  77.6 10.9 %copy-start.1 = (bf16[2048,1024]{1,0:T(8,128)(2,1)S(1)}, bf16[2048,1024]{1,0:T(8,128)(2,1)}, u32[]{:S(2)}) copy-start(bf16[2048,1024]{1,0:T(8,128)(2,1)} %w_ref.1) | copy-start | bytes 12582916
  84.1 9.6 %collective-permute-start.7 = (bf16[256,128]{1,0:T(8,128)(2,1)S(1)}, bf16[256,128]{1,0:T(8,128)(2,1)S(1)}, u32[]{:S(2)}, u32[]{:S(2)}) collective-permute-start(bf16[256,128]{1,0:T(8,128)(2,1)S(1)} %get-tuple-element.31), channel_id=1, source_target_pairs={{0,1},{1,0},{2,3},{3,2},{4,5},{5,4},{6,7},{7,6},{8,9},{9,8},{10,11... | collective-permute-start | bytes 196616 | tf_op jit(solution)/shard_map/ppermute | solution.py:579
  85.8 7.9 %collective-permute-start.8 = (bf16[256,128]{1,0:T(8,128)(2,1)S(1)}, bf16[256,128]{1,0:T(8,128)(2,1)S(1)}, u32[]{:S(2)}, u32[]{:S(2)}) collective-permute-start(bf16[256,128]{1,0:T(8,128)(2,1)S(1)} %get-tuple-element.32), channel_id=1, source_target_pairs={{0,2},{1,3},{2,0},{3,1},{4,6},{5,7},{6,4},{7,5},{8,10},{9,11},{10,... | collective-permute-start | bytes 196616 | tf_op jit(solution)/shard_map/ppermute | solution.py:579
  88.4 6.2 %collective-permute-start.9 = (bf16[256,128]{1,0:T(8,128)(2,1)S(1)}, bf16[256,128]{1,0:T(8,128)(2,1)S(1)}, u32[]{:S(2)}, u32[]{:S(2)}) collective-permute-start(bf16[256,128]{1,0:T(8,128)(2,1)S(1)} %get-tuple-element.33), channel_id=1, source_target_pairs={{0,3},{1,2},{2,1},{3,0},{4,7},{5,6},{6,5},{7,4},{8,11},{9,10},{10,... | collective-permute-start | bytes 196616 | tf_op jit(solution)/shard_map/ppermute | solution.py:579
  94.6 4.3 %collective-permute-start.11 = (bf16[256,1024]{1,0:T(8,128)(2,1)S(1)}, bf16[256,1024]{1,0:T(8,128)(2,1)S(1)}, u32[]{:S(2)}, u32[]{:S(2)}) collective-permute-start(bf16[256,1024]{1,0:T(8,128)(2,1)S(1)} %get-tuple-element.39), channel_id=1, source_target_pairs={{1,2},{2,1},{5,6},{6,5},{9,10},{10,9},{13,14},{14,13},{17,18},{18,... | collective-permute-start | bytes 1572872 | tf_op jit(solution)/shard_map/ppermute | solution.py:603
  95.3 14.8 %collective-permute-start.10 = (bf16[2,256,512]{2,1,0:T(8,128)(2,1)S(1)}, bf16[2,256,512]{2,1,0:T(8,128)(2,1)S(1)}, u32[]{:S(2)}, u32[]{:S(2)}) collective-permute-start(bf16[2,256,512]{2,1,0:T(8,128)(2,1)S(1)} %get-tuple-element.36), channel_id=1, source_target_pairs={{0,1},{1,0},{2,3},{3,2},{4,5},{5,4},{6,7},{7,6},{8,9},{9,8},{10,11... | collective-permute-start | bytes 1572872 | tf_op jit(solution)/shard_map/ppermute | solution.py:579
  98.9 27.4 %collective-permute-start.12 = (bf16[2,256,512]{2,1,0:T(8,128)(2,1)S(1)}, bf16[2,256,512]{2,1,0:T(8,128)(2,1)S(1)}, u32[]{:S(2)}, u32[]{:S(2)}) collective-permute-start(bf16[2,256,512]{2,1,0:T(8,128)(2,1)S(1)} %get-tuple-element.40), channel_id=1, source_target_pairs={{0,1},{1,0},{2,3},{3,2},{4,5},{5,4},{6,7},{7,6},{8,9},{9,8},{10,11... | collective-permute-start | bytes 1572872 | tf_op jit(solution)/shard_map/ppermute | solution.py:579
  110.1 25.7 %collective-permute-start.13 = (bf16[256,512]{1,0:T(8,128)(2,1)S(1)}, bf16[256,512]{1,0:T(8,128)(2,1)S(1)}, u32[]{:S(2)}, u32[]{:S(2)}) collective-permute-start(bf16[256,512]{1,0:T(8,128)(2,1)S(1)} %add.36), channel_id=1, source_target_pairs={{0,2},{1,3},{2,0},{3,1},{4,6},{5,7},{6,4},{7,5},{8,10},{9,11},{10,... | collective-permute-start | bytes 786440 | tf_op jit(solution)/shard_map/ppermute | solution.py:579
  126.3 12.4 %collective-permute-start.14 = (bf16[256,512]{1,0:T(8,128)(2,1)S(1)}, bf16[256,512]{1,0:T(8,128)(2,1)S(1)}, u32[]{:S(2)}, u32[]{:S(2)}) collective-permute-start(bf16[256,512]{1,0:T(8,128)(2,1)S(1)} %add.37), channel_id=1, source_target_pairs={{0,2},{1,3},{2,0},{3,1},{4,6},{5,7},{6,4},{7,5},{8,10},{9,11},{10,... | collective-permute-start | bytes 786440 | tf_op jit(solution)/shard_map/ppermute | solution.py:579
  (2 other events, 2.1 us)
